TPU v7x, 256 devices: a whole 4x4x8 slice. The times are simulated.
256 devices in a mesh: gx: 32 (over x, z), gy: 8 (over y, core).
Axes of the slice: x: 4, y: 4, z: 8, core: 2. Of those that a mesh axis runs over, the one named last changes fastest.
Arguments:
- forcing: float32 [3, 256, 128, 512], P(None, 'gx', 'gy'), may hold values from -6.5 to 6.5
- phase_ids: int32 [256, 128, 512], P('gx', 'gy'), may hold values from 0 to 3
Outputs:
- velocity: float32 [3, 256, 128, 512], P(None, 'gx', 'gy')
All inputs are finite; a program needn't handle non-finite values.
Results may differ from a plain program's by a relative error of at most 0.0003.
Values sent between devices are 32-bit elements; how exact they have to be, the bound alone decides.
No kernel may reach another device: no remote copies, remote signals or barrier semaphores. Data moves between devices by JAX's collectives and lax.ppermute only.
A program may use at most 128 MiB of HBM per device.

v0:
```python
import jax
import jax.numpy as jnp
from jax import lax
from jax.sharding import PartitionSpec as P

COARSE_SWEEPS = 6


viscosities = (0.2, 0.6, 1.5, 4.0)
relax_weight = 2.0 / 3.0


def extended(array, sides, width):
    for axis, dim in sides:
        size, length = (lax.axis_size(axis), array.shape[dim])
        up = [(i, (i + 1) % size) for i in range(size - 1)]
        down = [(j, i) for i, j in up]
        last = lax.slice_in_dim(array, length - width, length, axis=dim)
        initial = lax.slice_in_dim(array, 0, width, axis=dim)
        before = lax.ppermute(last, axis, up)
        after = lax.ppermute(initial, axis, down)
        array = jnp.concatenate([before, array, after], axis=dim)
    return array


def lookup(phase_ids):
    viscosity = jnp.zeros(phase_ids.shape, jnp.float32)
    for material, visc_value in enumerate(viscosities):
        viscosity = viscosity + jnp.where(
            phase_ids == material, jnp.float32(visc_value), jnp.float32(0.0)
        )
    return viscosity


def restrict(values):
    extent = values.shape
    leading = extent[:-3]
    blocks = values.reshape(leading + (extent[-3] // 2, 2, extent[-2] // 2, 2, extent[-1] // 2, 2))
    return jnp.mean(blocks, axis=(-5, -3, -1))


def prolong(values):
    return jnp.repeat(jnp.repeat(jnp.repeat(values, 2, axis=-3), 2, axis=-2), 2, axis=-1)


def face_set(wide_visc, spacing):
    center = wide_visc[1:-1, 1:-1, :]
    z_padded = jnp.pad(center, ((0, 0), (0, 0), (1, 1)))
    besides = (
        wide_visc[2:, 1:-1, :],
        wide_visc[:-2, 1:-1, :],
        wide_visc[1:-1, 2:, :],
        wide_visc[1:-1, :-2, :],
        z_padded[:, :, 2:],
        z_padded[:, :, :-2],
    )
    coeffs = tuple(
        (jnp.where(beside > 0.0, 0.5 * (center + beside), center) / spacing for beside in besides)
    )
    diagonal = coeffs[0]
    for entry in coeffs[1:]:
        diagonal = diagonal + entry
    inside = center > 0.0
    inverse = jnp.where(inside, 1.0 / jnp.where(inside, diagonal, 1.0), 0.0)
    return (coeffs, inverse)


def crop_set(level_set):
    coeffs, inverse = level_set
    return (tuple((entry[1:-1, 1:-1, :] for entry in coeffs)), inverse[1:-1, 1:-1, :])


def apply_operator(wide_field, coeffs):
    center = wide_field[..., 1:-1, 1:-1, :]
    padding = [(0, 0)] * (center.ndim - 1) + [(1, 1)]
    z_padded = jnp.pad(center, padding)
    besides = (
        wide_field[..., 2:, 1:-1, :],
        wide_field[..., :-2, 1:-1, :],
        wide_field[..., 1:-1, 2:, :],
        wide_field[..., 1:-1, :-2, :],
        z_padded[..., 2:],
        z_padded[..., :-2],
    )
    summed = jnp.zeros_like(center)
    for face_coeff, beside in zip(coeffs, besides):
        summed = summed + face_coeff * (center - beside)
    return summed


def rim_field(current):
    return extended(current, (("gx", 1), ("gy", 2)), 1)


def jacobi_sweep(current, source, level_set):
    coeffs, inverse = level_set
    return current + relax_weight * (source - apply_operator(rim_field(current), coeffs)) * inverse


def per_device(forcing, phase_ids):
    viscosity = lookup(phase_ids)
    wide_sets = []
    for level_index in range(2):
        wide_visc = extended(viscosity, (("gx", 0), ("gy", 1)), 2)
        wide_sets.append(face_set(wide_visc, 4.0**level_index))
        viscosity = restrict(viscosity)
    narrow_sets = [crop_set(entry) for entry in wide_sets]

    def descend(source, level_index):
        coeffs, inverse = narrow_sets[level_index]
        current = relax_weight * source * inverse
        current = jacobi_sweep(current, source, narrow_sets[level_index])
        residual = source - apply_operator(rim_field(current), coeffs)
        return (current, restrict(residual), source)

    def ascend(current, source, level_index):
        current = jacobi_sweep(current, source, narrow_sets[level_index])
        return jacobi_sweep(current, source, narrow_sets[level_index])

    fine_velocity, source_one, wide_zero = descend(forcing, 0)
    middle_velocity, source_two, wide_one = descend(source_one, 1)
    wide_visc = extended(viscosity, (("gx", 0), ("gy", 1)), 1)
    coarse_set = face_set(wide_visc, 16.0)
    coarse = relax_weight * source_two * coarse_set[1]
    for repeat in range(COARSE_SWEEPS - 1):
        coarse = jacobi_sweep(coarse, source_two, coarse_set)
    middle_velocity = ascend(middle_velocity + prolong(coarse), source_one, 1)
    fine_velocity = ascend(fine_velocity + prolong(middle_velocity), forcing, 0)
    return fine_velocity


def solution(mesh):
    return jax.shard_map(
        per_device,
        mesh=mesh,
        in_specs=(P(None, "gx", "gy", None), P("gx", "gy", None)),
        out_specs=P(None, "gx", "gy", None),
        check_vma=False,
    )
```

profile of v0, /device:TPU:15, one launch (start us, length us, event | category | flops | bytes accessed | tf_op | source)
XLA Modules:
  0.0 424.4 jit_solution(10337076495502430074)
XLA Ops:
  1.1 7.8 %collective-permute-start.1 = (f32[2,16,512]{2,1,0:T(8,128)S(1)}, f32[2,16,512]{2,1,0:T(8,128)S(1)}, u32[]{:S(2)}, u32[]{:S(2)}) collective-permute-start(f32[2,16,512]{2,1,0:T(8,128)S(1)} %get-tuple-element.46), channel_id=1, source_target_pairs={{8,0},{16,8},{24,16},{32,24},{40,32},{48,40},{56,48},{64,56},{72,6... | collective-permute-start | bytes 196616 | tf_op jit(solution)/shard_map/ppermute | solution.py:21
  10.8 18.1 %reshape.53 = f32[4,2,8,2,256,2]{5,4,3,2,1,0:T(8,128)} reshape(f32[8,16,512]{2,1,0:T(8,128)S(1)} %select_add_fusion) | data formatting | bytes 524288 | tf_op jit(solution)/shard_map/reshape | solution.py:38
  28.9 7.0 %reduce_sum.37 = f32[4,8,256]{2,1,0:T(8,128)S(1)} reduce(f32[4,2,8,2,256,2]{5,4,3,2,1,0:T(8,128)} %reshape.53, f32[]{:T(128)} %constant.21.clone.1), dimensions={1,3,5}, to_apply=%region_1.2 | reduce | flops 57344 | bytes 294916 | tf_op jit(solution)/shard_map/reduce_sum | solution.py:39
  35.9 5.5 %collective-permute-start.13 = (f32[2,8,256]{2,1,0:T(8,128)S(1)}, f32[2,8,256]{2,1,0:T(8,128)S(1)}, u32[]{:S(2)}, u32[]{:S(2)}) collective-permute-start(f32[2,8,256]{2,1,0:T(8,128)S(1)} %get-tuple-element.73), channel_id=1, source_target_pairs={{8,0},{16,8},{24,16},{32,24},{40,32},{48,40},{56,48},{64,56},{72,6... | collective-permute-start | bytes 49160 | tf_op jit(solution)/shard_map/ppermute | solution.py:21
  48.0 4.6 %collective-permute-start.15 = (f32[8,2,256]{2,1,0:T(2,128)S(1)}, f32[8,2,256]{2,1,0:T(2,128)S(1)}, u32[]{:S(2)}, u32[]{:S(2)}) collective-permute-start(f32[8,2,256]{2,1,0:T(2,128)S(1)} %get-tuple-element.71), channel_id=1, source_target_pairs={{1,0},{2,1},{3,2},{4,3},{5,4},{6,5},{7,6},{9,8},{10,9},{11,10},{12... | collective-permute-start | bytes 49160 | tf_op jit(solution)/shard_map/ppermute | solution.py:21
  52.5 3.1 collective-permute-start.14
  57.6 3.6 collective-permute-start.2
  66.0 3.0 collective-permute-start.5
  69.8 3.7 collective-permute-done.5
  73.6 5.7 %collective-permute-start.7 = (f32[3,10,1,512]{3,2,1,0:T(1,128)S(1)}, f32[3,10,1,512]{3,2,1,0:T(1,128)S(1)}, u32[]{:S(2)}, u32[]{:S(2)}) collective-permute-start(f32[3,10,1,512]{3,2,1,0:T(1,128)S(1)} %get-tuple-element.26), channel_id=1, source_target_pairs={{0,1},{1,2},{2,3},{3,4},{4,5},{5,6},{6,7},{8,9},{9,10},{10,11},{11... | collective-permute-start | bytes 184328 | tf_op jit(solution)/shard_map/ppermute | solution.py:20
  81.5 3.4 collective-permute-done.6
  87.6 3.4 collective-permute-start.9
  91.6 3.7 collective-permute-done.9
  95.5 3.4 collective-permute-start.11
  101.5 3.0 collective-permute-done.10
  106.1 52.4 %reshape.52 = f32[3,4,2,8,2,256,2]{6,5,4,3,2,1,0:T(8,128)} reshape(f32[3,8,16,512]{3,2,1,0:T(8,128)} %fusion.13) | data formatting | bytes 1572864 | tf_op jit(solution)/shard_map/reshape | solution.py:38
  158.4 17.8 %reduce_sum.36 = f32[3,4,8,256]{3,2,1,0:T(8,128)S(1)} reduce(f32[3,4,2,8,2,256,2]{6,5,4,3,2,1,0:T(8,128)} %reshape.52, f32[]{:T(128)} %constant.21.clone.1), dimensions={2,4,6}, to_apply=%region_0.1 | reduce | flops 172032 | bytes 884740 | tf_op jit(solution)/shard_map/reduce_sum | solution.py:39
  179.0 3.4 collective-permute-start.17
  184.3 5.5 %collective-permute-start.24 = (f32[1,4,128]{2,1,0:T(4,128)S(1)}, f32[1,4,128]{2,1,0:T(4,128)S(1)}, u32[]{:S(2)}, u32[]{:S(2)}) collective-permute-start(f32[1,4,128]{2,1,0:T(4,128)S(1)} %get-tuple-element.100), channel_id=1, source_target_pairs={{8,0},{16,8},{24,16},{32,24},{40,32},{48,40},{56,48},{64,56},{72,6... | collective-permute-start | bytes 6152 | tf_op jit(solution)/shard_map/ppermute | solution.py:21
  189.8 3.0 collective-permute-start.19
  196.9 3.4 collective-permute-start.27
  205.8 3.4 collective-permute-start.21
  212.5 3.6 collective-permute-start.23
  222.7 8.4 %reshape.54 = f32[3,2,2,4,2,128,2]{6,5,4,3,2,1,0:T(8,128)} reshape(f32[3,4,8,256]{3,2,1,0:T(8,128)} %fusion.97) | data formatting | bytes 196608 | tf_op jit(solution)/shard_map/reshape | solution.py:38
  231.1 3.3 reduce_sum.38
  237.0 3.4 collective-permute-start.29
  240.4 3.1 collective-permute-done.29
  243.5 3.1 collective-permute-start.31
  254.2 3.4 collective-permute-start.33
  257.6 3.1 collective-permute-done.33
  260.7 3.1 collective-permute-start.35
  265.8 3.0 collective-permute-done.34
  271.5 3.4 collective-permute-start.37
  274.9 3.1 collective-permute-done.37
  278.0 3.1 collective-permute-start.39
  283.1 3.0 collective-permute-done.38
  288.8 3.4 collective-permute-start.41
  292.2 3.1 collective-permute-done.41
  295.3 3.1 collective-permute-start.43
  300.3 3.0 collective-permute-done.42
  306.1 3.4 collective-permute-start.45
  309.5 3.1 collective-permute-done.45
  312.6 3.1 collective-permute-start.47
  317.6 3.0 collective-permute-done.46
  324.0 2.8 broadcast_in_dim.48
  332.2 3.4 collective-permute-start.49
  335.6 3.3 collective-permute-done.49
  338.9 3.1 collective-permute-start.51
  344.0 3.1 collective-permute-done.50
  350.0 3.4 collective-permute-start.53
  353.4 3.3 collective-permute-done.53
  356.7 3.1 collective-permute-start.55
  361.8 3.1 collective-permute-done.54
  370.1 3.2 copy.216
  373.3 4.9 %broadcast_in_dim.51 = f32[3,8,16,256,2]{2,1,4,3,0:T(8,128)} broadcast(f32[3,8,16,256]{2,1,3,0:T(8,128)} %copy.216), dimensions={0,1,2,3} | broadcast | bytes 1179648 | tf_op jit(solution)/shard_map/broadcast_in_dim | solution.py:43
  378.2 5.2 %copy.217 = f32[3,8,16,512]{3,2,1,0:T(8,128)} copy(f32[3,8,16,512]{2,1,3,0:T(8,128)} %bitcast.14) | data formatting | bytes 1572864 | tf_op jit(solution)/shard_map/reshape | solution.py:43
  386.7 3.4 collective-permute-start.57
  390.1 4.0 collective-permute-done.57
  394.3 3.8 collective-permute-start.59
  400.1 3.6 collective-permute-done.58
  406.4 3.4 collective-permute-start.61
  409.9 4.0 collective-permute-done.61
  414.0 3.1 collective-permute-start.63
  419.0 3.6 collective-permute-done.62
  (167 shorter events, 109.7 us)
Async XLA Ops:
  1.1 54.6 %collective-permute-start.1 = (f32[2,16,512]{2,1,0:T(8,128)S(1)}, f32[2,16,512]{2,1,0:T(8,128)S(1)}, u32[]{:S(2)}, u32[]{:S(2)}) collective-permute-start(f32[2,16,512]{2,1,0:T(8,128)S(1)} %get-tuple-element.46), channel_id=1, source_target_pairs={{8,0},{16,8},{24,16},{32,24},{40,32},{48,40},{56,48},{64,56},{72,6... | collective-permute-start | bytes 196616 | tf_op jit(solution)/shard_map/ppermute | solution.py:21
  8.8 46.8 %collective-permute-start = (f32[2,16,512]{2,1,0:T(8,128)S(1)}, f32[2,16,512]{2,1,0:T(8,128)S(1)}, u32[]{:S(2)}, u32[]{:S(2)}) collective-permute-start(f32[2,16,512]{2,1,0:T(8,128)S(1)} %get-tuple-element.45), channel_id=1, source_target_pairs={{0,8},{8,16},{16,24},{24,32},{32,40},{40,48},{48,56},{56,64},{64,7... | collective-permute-start | bytes 196616 | tf_op jit(solution)/shard_map/ppermute | solution.py:20
  35.9 9.8 %collective-permute-start.13 = (f32[2,8,256]{2,1,0:T(8,128)S(1)}, f32[2,8,256]{2,1,0:T(8,128)S(1)}, u32[]{:S(2)}, u32[]{:S(2)}) collective-permute-start(f32[2,8,256]{2,1,0:T(8,128)S(1)} %get-tuple-element.73), channel_id=1, source_target_pairs={{8,0},{16,8},{24,16},{32,24},{40,32},{48,40},{56,48},{64,56},{72,6... | collective-permute-start | bytes 49160 | tf_op jit(solution)/shard_map/ppermute | solution.py:21
  41.4 6.6 %collective-permute-start.12 = (f32[2,8,256]{2,1,0:T(8,128)S(1)}, f32[2,8,256]{2,1,0:T(8,128)S(1)}, u32[]{:S(2)}, u32[]{:S(2)}) collective-permute-start(f32[2,8,256]{2,1,0:T(8,128)S(1)} %get-tuple-element.72), channel_id=1, source_target_pairs={{0,8},{8,16},{16,24},{24,32},{32,40},{40,48},{48,56},{56,64},{64,7... | collective-permute-start | bytes 49160 | tf_op jit(solution)/shard_map/ppermute | solution.py:20
  48.0 13.3 %collective-permute-start.15 = (f32[8,2,256]{2,1,0:T(2,128)S(1)}, f32[8,2,256]{2,1,0:T(2,128)S(1)}, u32[]{:S(2)}, u32[]{:S(2)}) collective-permute-start(f32[8,2,256]{2,1,0:T(2,128)S(1)} %get-tuple-element.71), channel_id=1, source_target_pairs={{1,0},{2,1},{3,2},{4,3},{5,4},{6,5},{7,6},{9,8},{10,9},{11,10},{12... | collective-permute-start | bytes 49160 | tf_op jit(solution)/shard_map/ppermute | solution.py:21
  52.5 8.8 %collective-permute-start.14 = (f32[8,2,256]{2,1,0:T(2,128)S(1)}, f32[8,2,256]{2,1,0:T(2,128)S(1)}, u32[]{:S(2)}, u32[]{:S(2)}) collective-permute-start(f32[8,2,256]{2,1,0:T(2,128)S(1)} %get-tuple-element.70), channel_id=1, source_target_pairs={{0,1},{1,2},{2,3},{3,4},{4,5},{5,6},{6,7},{8,9},{9,10},{10,11},{11... | collective-permute-start | bytes 49160 | tf_op jit(solution)/shard_map/ppermute | solution.py:20
  55.7 5.6 %collective-permute-start.3 = (f32[12,2,512]{2,1,0:T(2,128)S(1)}, f32[12,2,512]{2,1,0:T(2,128)S(1)}, u32[]{:S(2)}, u32[]{:S(2)}) collective-permute-start(f32[12,2,512]{2,1,0:T(2,128)S(1)} %get-tuple-element.44), channel_id=1, source_target_pairs={{1,0},{2,1},{3,2},{4,3},{5,4},{6,5},{7,6},{9,8},{10,9},{11,10},{12... | collective-permute-start | bytes 147464 | tf_op jit(solution)/shard_map/ppermute | solution.py:21
  57.6 4.8 %collective-permute-start.2 = (f32[12,2,512]{2,1,0:T(2,128)S(1)}, f32[12,2,512]{2,1,0:T(2,128)S(1)}, u32[]{:S(2)}, u32[]{:S(2)}) collective-permute-start(f32[12,2,512]{2,1,0:T(2,128)S(1)} %get-tuple-element.43), channel_id=1, source_target_pairs={{0,1},{1,2},{2,3},{3,4},{4,5},{5,6},{6,7},{8,9},{9,10},{10,11},{11... | collective-permute-start | bytes 147464 | tf_op jit(solution)/shard_map/ppermute | solution.py:20
  63.7 6.1 %collective-permute-start.4 = (f32[3,1,16,512]{3,2,1,0:T(8,128)S(1)}, f32[3,1,16,512]{3,2,1,0:T(8,128)S(1)}, u32[]{:S(2)}, u32[]{:S(2)}) collective-permute-start(f32[3,1,16,512]{3,2,1,0:T(8,128)S(1)} %get-tuple-element.35), channel_id=1, source_target_pairs={{8,0},{16,8},{24,16},{32,24},{40,32},{48,40},{56,48},{64,56},{72,6... | collective-permute-start | bytes 294920 | tf_op jit(solution)/shard_map/ppermute | solution.py:21
  66.0 7.5 %collective-permute-start.5 = (f32[3,1,16,512]{3,2,1,0:T(8,128)S(1)}, f32[3,1,16,512]{3,2,1,0:T(8,128)S(1)}, u32[]{:S(2)}, u32[]{:S(2)}) collective-permute-start(f32[3,1,16,512]{3,2,1,0:T(8,128)S(1)} %get-tuple-element.34), channel_id=1, source_target_pairs={{0,8},{8,16},{16,24},{24,32},{32,40},{40,48},{48,56},{56,64},{64,7... | collective-permute-start | bytes 294920 | tf_op jit(solution)/shard_map/ppermute | solution.py:20
  73.6 7.9 %collective-permute-start.7 = (f32[3,10,1,512]{3,2,1,0:T(1,128)S(1)}, f32[3,10,1,512]{3,2,1,0:T(1,128)S(1)}, u32[]{:S(2)}, u32[]{:S(2)}) collective-permute-start(f32[3,10,1,512]{3,2,1,0:T(1,128)S(1)} %get-tuple-element.26), channel_id=1, source_target_pairs={{0,1},{1,2},{2,3},{3,4},{4,5},{5,6},{6,7},{8,9},{9,10},{10,11},{11... | collective-permute-start | bytes 184328 | tf_op jit(solution)/shard_map/ppermute | solution.py:20
  79.3 5.5 %collective-permute-start.6 = (f32[3,10,1,512]{3,2,1,0:T(1,128)S(1)}, f32[3,10,1,512]{3,2,1,0:T(1,128)S(1)}, u32[]{:S(2)}, u32[]{:S(2)}) collective-permute-start(f32[3,10,1,512]{3,2,1,0:T(1,128)S(1)} %get-tuple-element.25), channel_id=1, source_target_pairs={{1,0},{2,1},{3,2},{4,3},{5,4},{6,5},{7,6},{9,8},{10,9},{11,10},{12... | collective-permute-start | bytes 184328 | tf_op jit(solution)/shard_map/ppermute | solution.py:21
  85.7 5.9 %collective-permute-start.8 = (f32[3,1,16,512]{3,2,1,0:T(8,128)S(1)}, f32[3,1,16,512]{3,2,1,0:T(8,128)S(1)}, u32[]{:S(2)}, u32[]{:S(2)}) collective-permute-start(f32[3,1,16,512]{3,2,1,0:T(8,128)S(1)} %get-tuple-element.33), channel_id=1, source_target_pairs={{8,0},{16,8},{24,16},{32,24},{40,32},{48,40},{56,48},{64,56},{72,6... | collective-permute-start | bytes 294920 | tf_op jit(solution)/shard_map/ppermute | solution.py:21
  87.6 7.8 %collective-permute-start.9 = (f32[3,1,16,512]{3,2,1,0:T(8,128)S(1)}, f32[3,1,16,512]{3,2,1,0:T(8,128)S(1)}, u32[]{:S(2)}, u32[]{:S(2)}) collective-permute-start(f32[3,1,16,512]{3,2,1,0:T(8,128)S(1)} %get-tuple-element.32), channel_id=1, source_target_pairs={{0,8},{8,16},{16,24},{24,32},{32,40},{40,48},{48,56},{56,64},{64,7... | collective-permute-start | bytes 294920 | tf_op jit(solution)/shard_map/ppermute | solution.py:20
  95.5 6.0 %collective-permute-start.11 = (f32[3,10,1,512]{3,2,1,0:T(1,128)S(1)}, f32[3,10,1,512]{3,2,1,0:T(1,128)S(1)}, u32[]{:S(2)}, u32[]{:S(2)}) collective-permute-start(f32[3,10,1,512]{3,2,1,0:T(1,128)S(1)} %get-tuple-element.24), channel_id=1, source_target_pairs={{0,1},{1,2},{2,3},{3,4},{4,5},{5,6},{6,7},{8,9},{9,10},{10,11},{11... | collective-permute-start | bytes 184328 | tf_op jit(solution)/shard_map/ppermute | solution.py:20
  98.9 5.5 %collective-permute-start.10 = (f32[3,10,1,512]{3,2,1,0:T(1,128)S(1)}, f32[3,10,1,512]{3,2,1,0:T(1,128)S(1)}, u32[]{:S(2)}, u32[]{:S(2)}) collective-permute-start(f32[3,10,1,512]{3,2,1,0:T(1,128)S(1)} %get-tuple-element.23), channel_id=1, source_target_pairs={{1,0},{2,1},{3,2},{4,3},{5,4},{6,5},{7,6},{9,8},{10,9},{11,10},{12... | collective-permute-start | bytes 184328 | tf_op jit(solution)/shard_map/ppermute | solution.py:21
  177.0 12.7 %collective-permute-start.16 = (f32[3,1,8,256]{3,2,1,0:T(8,128)S(1)}, f32[3,1,8,256]{3,2,1,0:T(8,128)S(1)}, u32[]{:S(2)}, u32[]{:S(2)}) collective-permute-start(f32[3,1,8,256]{3,2,1,0:T(8,128)S(1)} %get-tuple-element.67), channel_id=1, source_target_pairs={{8,0},{16,8},{24,16},{32,24},{40,32},{48,40},{56,48},{64,56},{72,6... | collective-permute-start | bytes 73736 | tf_op jit(solution)/shard_map/ppermute | solution.py:21
  179.0 10.8 %collective-permute-start.17 = (f32[3,1,8,256]{3,2,1,0:T(8,128)S(1)}, f32[3,1,8,256]{3,2,1,0:T(8,128)S(1)}, u32[]{:S(2)}, u32[]{:S(2)}) collective-permute-start(f32[3,1,8,256]{3,2,1,0:T(8,128)S(1)} %get-tuple-element.66), channel_id=1, source_target_pairs={{0,8},{8,16},{16,24},{24,32},{32,40},{40,48},{48,56},{56,64},{64,7... | collective-permute-start | bytes 73736 | tf_op jit(solution)/shard_map/ppermute | solution.py:20
  182.3 12.4 %collective-permute-start.25 = (f32[1,4,128]{2,1,0:T(4,128)S(1)}, f32[1,4,128]{2,1,0:T(4,128)S(1)}, u32[]{:S(2)}, u32[]{:S(2)}) collective-permute-start(f32[1,4,128]{2,1,0:T(4,128)S(1)} %get-tuple-element.101), channel_id=1, source_target_pairs={{0,8},{8,16},{16,24},{24,32},{32,40},{40,48},{48,56},{56,64},{64,7... | collective-permute-start | bytes 6152 | tf_op jit(solution)/shard_map/ppermute | solution.py:20
  184.3 10.5 %collective-permute-start.24 = (f32[1,4,128]{2,1,0:T(4,128)S(1)}, f32[1,4,128]{2,1,0:T(4,128)S(1)}, u32[]{:S(2)}, u32[]{:S(2)}) collective-permute-start(f32[1,4,128]{2,1,0:T(4,128)S(1)} %get-tuple-element.100), channel_id=1, source_target_pairs={{8,0},{16,8},{24,16},{32,24},{40,32},{48,40},{56,48},{64,56},{72,6... | collective-permute-start | bytes 6152 | tf_op jit(solution)/shard_map/ppermute | solution.py:21
  189.8 13.1 %collective-permute-start.19 = (f32[3,6,1,256]{3,2,1,0:T(1,128)S(1)}, f32[3,6,1,256]{3,2,1,0:T(1,128)S(1)}, u32[]{:S(2)}, u32[]{:S(2)}) collective-permute-start(f32[3,6,1,256]{3,2,1,0:T(1,128)S(1)} %get-tuple-element.55), channel_id=1, source_target_pairs={{0,1},{1,2},{2,3},{3,4},{4,5},{5,6},{6,7},{8,9},{9,10},{10,11},{11... | collective-permute-start | bytes 55304 | tf_op jit(solution)/shard_map/ppermute | solution.py:20
  192.8 10.1 %collective-permute-start.18 = (f32[3,6,1,256]{3,2,1,0:T(1,128)S(1)}, f32[3,6,1,256]{3,2,1,0:T(1,128)S(1)}, u32[]{:S(2)}, u32[]{:S(2)}) collective-permute-start(f32[3,6,1,256]{3,2,1,0:T(1,128)S(1)} %get-tuple-element.54), channel_id=1, source_target_pairs={{1,0},{2,1},{3,2},{4,3},{5,4},{6,5},{7,6},{9,8},{10,9},{11,10},{12... | collective-permute-start | bytes 55304 | tf_op jit(solution)/shard_map/ppermute | solution.py:21
  194.8 14.4 %collective-permute-start.26 = (f32[4,1,128]{2,1,0:T(1,128)S(1)}, f32[4,1,128]{2,1,0:T(1,128)S(1)}, u32[]{:S(2)}, u32[]{:S(2)}) collective-permute-start(f32[4,1,128]{2,1,0:T(1,128)S(1)} %get-tuple-element.95), channel_id=1, source_target_pairs={{1,0},{2,1},{3,2},{4,3},{5,4},{6,5},{7,6},{9,8},{10,9},{11,10},{12... | collective-permute-start | bytes 6152 | tf_op jit(solution)/shard_map/ppermute | solution.py:21
  196.9 12.3 %collective-permute-start.27 = (f32[4,1,128]{2,1,0:T(1,128)S(1)}, f32[4,1,128]{2,1,0:T(1,128)S(1)}, u32[]{:S(2)}, u32[]{:S(2)}) collective-permute-start(f32[4,1,128]{2,1,0:T(1,128)S(1)} %get-tuple-element.94), channel_id=1, source_target_pairs={{0,1},{1,2},{2,3},{3,4},{4,5},{5,6},{6,7},{8,9},{9,10},{10,11},{11... | collective-permute-start | bytes 6152 | tf_op jit(solution)/shard_map/ppermute | solution.py:20
  203.9 6.0 %collective-permute-start.20 = (f32[3,1,8,256]{3,2,1,0:T(8,128)S(1)}, f32[3,1,8,256]{3,2,1,0:T(8,128)S(1)}, u32[]{:S(2)}, u32[]{:S(2)}) collective-permute-start(f32[3,1,8,256]{3,2,1,0:T(8,128)S(1)} %get-tuple-element.62), channel_id=1, source_target_pairs={{8,0},{16,8},{24,16},{32,24},{40,32},{48,40},{56,48},{64,56},{72,6... | collective-permute-start | bytes 73736 | tf_op jit(solution)/shard_map/ppermute | solution.py:21
  205.8 6.7 %collective-permute-start.21 = (f32[3,1,8,256]{3,2,1,0:T(8,128)S(1)}, f32[3,1,8,256]{3,2,1,0:T(8,128)S(1)}, u32[]{:S(2)}, u32[]{:S(2)}) collective-permute-start(f32[3,1,8,256]{3,2,1,0:T(8,128)S(1)} %get-tuple-element.61), channel_id=1, source_target_pairs={{0,8},{8,16},{16,24},{24,32},{32,40},{40,48},{48,56},{56,64},{64,7... | collective-permute-start | bytes 73736 | tf_op jit(solution)/shard_map/ppermute | solution.py:20
  212.5 6.3 %collective-permute-start.23 = (f32[3,6,1,256]{3,2,1,0:T(1,128)S(1)}, f32[3,6,1,256]{3,2,1,0:T(1,128)S(1)}, u32[]{:S(2)}, u32[]{:S(2)}) collective-permute-start(f32[3,6,1,256]{3,2,1,0:T(1,128)S(1)} %get-tuple-element.53), channel_id=1, source_target_pairs={{0,1},{1,2},{2,3},{3,4},{4,5},{5,6},{6,7},{8,9},{9,10},{10,11},{11... | collective-permute-start | bytes 55304 | tf_op jit(solution)/shard_map/ppermute | solution.py:20
  216.1 5.1 %collective-permute-start.22 = (f32[3,6,1,256]{3,2,1,0:T(1,128)S(1)}, f32[3,6,1,256]{3,2,1,0:T(1,128)S(1)}, u32[]{:S(2)}, u32[]{:S(2)}) collective-permute-start(f32[3,6,1,256]{3,2,1,0:T(1,128)S(1)} %get-tuple-element.52), channel_id=1, source_target_pairs={{1,0},{2,1},{3,2},{4,3},{5,4},{6,5},{7,6},{9,8},{10,9},{11,10},{12... | collective-permute-start | bytes 55304 | tf_op jit(solution)/shard_map/ppermute | solution.py:21
  235.1 5.3 %collective-permute-start.28 = (f32[3,1,4,128]{3,2,1,0:T(4,128)S(1)}, f32[3,1,4,128]{3,2,1,0:T(4,128)S(1)}, u32[]{:S(2)}, u32[]{:S(2)}) collective-permute-start(f32[3,1,4,128]{3,2,1,0:T(4,128)S(1)} %get-tuple-element.93), channel_id=1, source_target_pairs={{8,0},{16,8},{24,16},{32,24},{40,32},{48,40},{56,48},{64,56},{72,6... | collective-permute-start | bytes 18440 | tf_op jit(solution)/shard_map/ppermute | solution.py:21
  237.0 6.5 %collective-permute-start.29 = (f32[3,1,4,128]{3,2,1,0:T(4,128)S(1)}, f32[3,1,4,128]{3,2,1,0:T(4,128)S(1)}, u32[]{:S(2)}, u32[]{:S(2)}) collective-permute-start(f32[3,1,4,128]{3,2,1,0:T(4,128)S(1)} %get-tuple-element.92), channel_id=1, source_target_pairs={{0,8},{8,16},{16,24},{24,32},{32,40},{40,48},{48,56},{56,64},{64,7... | collective-permute-start | bytes 18440 | tf_op jit(solution)/shard_map/ppermute | solution.py:20
  243.5 5.9 %collective-permute-start.31 = (f32[3,4,1,128]{3,2,1,0:T(1,128)S(1)}, f32[3,4,1,128]{3,2,1,0:T(1,128)S(1)}, u32[]{:S(2)}, u32[]{:S(2)}) collective-permute-start(f32[3,4,1,128]{3,2,1,0:T(1,128)S(1)} %get-tuple-element.83), channel_id=1, source_target_pairs={{0,1},{1,2},{2,3},{3,4},{4,5},{5,6},{6,7},{8,9},{9,10},{10,11},{11... | collective-permute-start | bytes 18440 | tf_op jit(solution)/shard_map/ppermute | solution.py:20
  246.6 4.9 %collective-permute-start.30 = (f32[3,4,1,128]{3,2,1,0:T(1,128)S(1)}, f32[3,4,1,128]{3,2,1,0:T(1,128)S(1)}, u32[]{:S(2)}, u32[]{:S(2)}) collective-permute-start(f32[3,4,1,128]{3,2,1,0:T(1,128)S(1)} %get-tuple-element.82), channel_id=1, source_target_pairs={{1,0},{2,1},{3,2},{4,3},{5,4},{6,5},{7,6},{9,8},{10,9},{11,10},{12... | collective-permute-start | bytes 18440 | tf_op jit(solution)/shard_map/ppermute | solution.py:21
  252.3 5.3 %collective-permute-start.32 = (f32[3,1,4,128]{3,2,1,0:T(4,128)S(1)}, f32[3,1,4,128]{3,2,1,0:T(4,128)S(1)}, u32[]{:S(2)}, u32[]{:S(2)}) collective-permute-start(f32[3,1,4,128]{3,2,1,0:T(4,128)S(1)} %get-tuple-element.91), channel_id=1, source_target_pairs={{8,0},{16,8},{24,16},{32,24},{40,32},{48,40},{56,48},{64,56},{72,6... | collective-permute-start | bytes 18440 | tf_op jit(solution)/shard_map/ppermute | solution.py:21
  254.2 6.5 %collective-permute-start.33 = (f32[3,1,4,128]{3,2,1,0:T(4,128)S(1)}, f32[3,1,4,128]{3,2,1,0:T(4,128)S(1)}, u32[]{:S(2)}, u32[]{:S(2)}) collective-permute-start(f32[3,1,4,128]{3,2,1,0:T(4,128)S(1)} %get-tuple-element.90), channel_id=1, source_target_pairs={{0,8},{8,16},{16,24},{24,32},{32,40},{40,48},{48,56},{56,64},{64,7... | collective-permute-start | bytes 18440 | tf_op jit(solution)/shard_map/ppermute | solution.py:20
  260.7 5.0 %collective-permute-start.35 = (f32[3,4,1,128]{3,2,1,0:T(1,128)S(1)}, f32[3,4,1,128]{3,2,1,0:T(1,128)S(1)}, u32[]{:S(2)}, u32[]{:S(2)}) collective-permute-start(f32[3,4,1,128]{3,2,1,0:T(1,128)S(1)} %get-tuple-element.81), channel_id=1, source_target_pairs={{0,1},{1,2},{2,3},{3,4},{4,5},{5,6},{6,7},{8,9},{9,10},{10,11},{11... | collective-permute-start | bytes 18440 | tf_op jit(solution)/shard_map/ppermute | solution.py:20
  263.8 4.9 %collective-permute-start.34 = (f32[3,4,1,128]{3,2,1,0:T(1,128)S(1)}, f32[3,4,1,128]{3,2,1,0:T(1,128)S(1)}, u32[]{:S(2)}, u32[]{:S(2)}) collective-permute-start(f32[3,4,1,128]{3,2,1,0:T(1,128)S(1)} %get-tuple-element.80), channel_id=1, source_target_pairs={{1,0},{2,1},{3,2},{4,3},{5,4},{6,5},{7,6},{9,8},{10,9},{11,10},{12... | collective-permute-start | bytes 18440 | tf_op jit(solution)/shard_map/ppermute | solution.py:21
  269.6 5.3 %collective-permute-start.36 = (f32[3,1,4,128]{3,2,1,0:T(4,128)S(1)}, f32[3,1,4,128]{3,2,1,0:T(4,128)S(1)}, u32[]{:S(2)}, u32[]{:S(2)}) collective-permute-start(f32[3,1,4,128]{3,2,1,0:T(4,128)S(1)} %get-tuple-element.89), channel_id=1, source_target_pairs={{8,0},{16,8},{24,16},{32,24},{40,32},{48,40},{56,48},{64,56},{72,6... | collective-permute-start | bytes 18440 | tf_op jit(solution)/shard_map/ppermute | solution.py:21
  271.5 6.5 %collective-permute-start.37 = (f32[3,1,4,128]{3,2,1,0:T(4,128)S(1)}, f32[3,1,4,128]{3,2,1,0:T(4,128)S(1)}, u32[]{:S(2)}, u32[]{:S(2)}) collective-permute-start(f32[3,1,4,128]{3,2,1,0:T(4,128)S(1)} %get-tuple-element.88), channel_id=1, source_target_pairs={{0,8},{8,16},{16,24},{24,32},{32,40},{40,48},{48,56},{56,64},{64,7... | collective-permute-start | bytes 18440 | tf_op jit(solution)/shard_map/ppermute | solution.py:20
  278.0 5.0 %collective-permute-start.39 = (f32[3,4,1,128]{3,2,1,0:T(1,128)S(1)}, f32[3,4,1,128]{3,2,1,0:T(1,128)S(1)}, u32[]{:S(2)}, u32[]{:S(2)}) collective-permute-start(f32[3,4,1,128]{3,2,1,0:T(1,128)S(1)} %get-tuple-element.79), channel_id=1, source_target_pairs={{0,1},{1,2},{2,3},{3,4},{4,5},{5,6},{6,7},{8,9},{9,10},{10,11},{11... | collective-permute-start | bytes 18440 | tf_op jit(solution)/shard_map/ppermute | solution.py:20
  281.1 4.9 %collective-permute-start.38 = (f32[3,4,1,128]{3,2,1,0:T(1,128)S(1)}, f32[3,4,1,128]{3,2,1,0:T(1,128)S(1)}, u32[]{:S(2)}, u32[]{:S(2)}) collective-permute-start(f32[3,4,1,128]{3,2,1,0:T(1,128)S(1)} %get-tuple-element.78), channel_id=1, source_target_pairs={{1,0},{2,1},{3,2},{4,3},{5,4},{6,5},{7,6},{9,8},{10,9},{11,10},{12... | collective-permute-start | bytes 18440 | tf_op jit(solution)/shard_map/ppermute | solution.py:21
  286.9 5.3 %collective-permute-start.40 = (f32[3,1,4,128]{3,2,1,0:T(4,128)S(1)}, f32[3,1,4,128]{3,2,1,0:T(4,128)S(1)}, u32[]{:S(2)}, u32[]{:S(2)}) collective-permute-start(f32[3,1,4,128]{3,2,1,0:T(4,128)S(1)} %get-tuple-element.87), channel_id=1, source_target_pairs={{8,0},{16,8},{24,16},{32,24},{40,32},{48,40},{56,48},{64,56},{72,6... | collective-permute-start | bytes 18440 | tf_op jit(solution)/shard_map/ppermute | solution.py:21
  288.8 6.5 %collective-permute-start.41 = (f32[3,1,4,128]{3,2,1,0:T(4,128)S(1)}, f32[3,1,4,128]{3,2,1,0:T(4,128)S(1)}, u32[]{:S(2)}, u32[]{:S(2)}) collective-permute-start(f32[3,1,4,128]{3,2,1,0:T(4,128)S(1)} %get-tuple-element.86), channel_id=1, source_target_pairs={{0,8},{8,16},{16,24},{24,32},{32,40},{40,48},{48,56},{56,64},{64,7... | collective-permute-start | bytes 18440 | tf_op jit(solution)/shard_map/ppermute | solution.py:20
  295.3 5.0 %collective-permute-start.43 = (f32[3,4,1,128]{3,2,1,0:T(1,128)S(1)}, f32[3,4,1,128]{3,2,1,0:T(1,128)S(1)}, u32[]{:S(2)}, u32[]{:S(2)}) collective-permute-start(f32[3,4,1,128]{3,2,1,0:T(1,128)S(1)} %get-tuple-element.77), channel_id=1, source_target_pairs={{0,1},{1,2},{2,3},{3,4},{4,5},{5,6},{6,7},{8,9},{9,10},{10,11},{11... | collective-permute-start | bytes 18440 | tf_op jit(solution)/shard_map/ppermute | solution.py:20
  298.4 4.9 %collective-permute-start.42 = (f32[3,4,1,128]{3,2,1,0:T(1,128)S(1)}, f32[3,4,1,128]{3,2,1,0:T(1,128)S(1)}, u32[]{:S(2)}, u32[]{:S(2)}) collective-permute-start(f32[3,4,1,128]{3,2,1,0:T(1,128)S(1)} %get-tuple-element.76), channel_id=1, source_target_pairs={{1,0},{2,1},{3,2},{4,3},{5,4},{6,5},{7,6},{9,8},{10,9},{11,10},{12... | collective-permute-start | bytes 18440 | tf_op jit(solution)/shard_map/ppermute | solution.py:21
  304.1 5.3 %collective-permute-start.44 = (f32[3,1,4,128]{3,2,1,0:T(4,128)S(1)}, f32[3,1,4,128]{3,2,1,0:T(4,128)S(1)}, u32[]{:S(2)}, u32[]{:S(2)}) collective-permute-start(f32[3,1,4,128]{3,2,1,0:T(4,128)S(1)} %get-tuple-element.85), channel_id=1, source_target_pairs={{8,0},{16,8},{24,16},{32,24},{40,32},{48,40},{56,48},{64,56},{72,6... | collective-permute-start | bytes 18440 | tf_op jit(solution)/shard_map/ppermute | solution.py:21
  306.1 6.5 %collective-permute-start.45 = (f32[3,1,4,128]{3,2,1,0:T(4,128)S(1)}, f32[3,1,4,128]{3,2,1,0:T(4,128)S(1)}, u32[]{:S(2)}, u32[]{:S(2)}) collective-permute-start(f32[3,1,4,128]{3,2,1,0:T(4,128)S(1)} %get-tuple-element.84), channel_id=1, source_target_pairs={{0,8},{8,16},{16,24},{24,32},{32,40},{40,48},{48,56},{56,64},{64,7... | collective-permute-start | bytes 18440 | tf_op jit(solution)/shard_map/ppermute | solution.py:20
  312.6 5.0 %collective-permute-start.47 = (f32[3,4,1,128]{3,2,1,0:T(1,128)S(1)}, f32[3,4,1,128]{3,2,1,0:T(1,128)S(1)}, u32[]{:S(2)}, u32[]{:S(2)}) collective-permute-start(f32[3,4,1,128]{3,2,1,0:T(1,128)S(1)} %get-tuple-element.75), channel_id=1, source_target_pairs={{0,1},{1,2},{2,3},{3,4},{4,5},{5,6},{6,7},{8,9},{9,10},{10,11},{11... | collective-permute-start | bytes 18440 | tf_op jit(solution)/shard_map/ppermute | solution.py:20
  315.7 4.9 %collective-permute-start.46 = (f32[3,4,1,128]{3,2,1,0:T(1,128)S(1)}, f32[3,4,1,128]{3,2,1,0:T(1,128)S(1)}, u32[]{:S(2)}, u32[]{:S(2)}) collective-permute-start(f32[3,4,1,128]{3,2,1,0:T(1,128)S(1)} %get-tuple-element.74), channel_id=1, source_target_pairs={{1,0},{2,1},{3,2},{4,3},{5,4},{6,5},{7,6},{9,8},{10,9},{11,10},{12... | collective-permute-start | bytes 18440 | tf_op jit(solution)/shard_map/ppermute | solution.py:21
  330.3 5.3 %collective-permute-start.48 = (f32[3,1,8,256]{3,2,1,0:T(8,128)S(1)}, f32[3,1,8,256]{3,2,1,0:T(8,128)S(1)}, u32[]{:S(2)}, u32[]{:S(2)}) collective-permute-start(f32[3,1,8,256]{3,2,1,0:T(8,128)S(1)} %get-tuple-element.60), channel_id=1, source_target_pairs={{8,0},{16,8},{24,16},{32,24},{40,32},{48,40},{56,48},{64,56},{72,6... | collective-permute-start | bytes 73736 | tf_op jit(solution)/shard_map/ppermute | solution.py:21
  332.2 6.7 %collective-permute-start.49 = (f32[3,1,8,256]{3,2,1,0:T(8,128)S(1)}, f32[3,1,8,256]{3,2,1,0:T(8,128)S(1)}, u32[]{:S(2)}, u32[]{:S(2)}) collective-permute-start(f32[3,1,8,256]{3,2,1,0:T(8,128)S(1)} %get-tuple-element.59), channel_id=1, source_target_pairs={{0,8},{8,16},{16,24},{24,32},{32,40},{40,48},{48,56},{56,64},{64,7... | collective-permute-start | bytes 73736 | tf_op jit(solution)/shard_map/ppermute | solution.py:20
  338.9 5.0 %collective-permute-start.51 = (f32[3,6,1,256]{3,2,1,0:T(1,128)S(1)}, f32[3,6,1,256]{3,2,1,0:T(1,128)S(1)}, u32[]{:S(2)}, u32[]{:S(2)}) collective-permute-start(f32[3,6,1,256]{3,2,1,0:T(1,128)S(1)} %get-tuple-element.51), channel_id=1, source_target_pairs={{0,1},{1,2},{2,3},{3,4},{4,5},{5,6},{6,7},{8,9},{9,10},{10,11},{11... | collective-permute-start | bytes 55304 | tf_op jit(solution)/shard_map/ppermute | solution.py:20
  342.0 5.1 %collective-permute-start.50 = (f32[3,6,1,256]{3,2,1,0:T(1,128)S(1)}, f32[3,6,1,256]{3,2,1,0:T(1,128)S(1)}, u32[]{:S(2)}, u32[]{:S(2)}) collective-permute-start(f32[3,6,1,256]{3,2,1,0:T(1,128)S(1)} %get-tuple-element.50), channel_id=1, source_target_pairs={{1,0},{2,1},{3,2},{4,3},{5,4},{6,5},{7,6},{9,8},{10,9},{11,10},{12... | collective-permute-start | bytes 55304 | tf_op jit(solution)/shard_map/ppermute | solution.py:21
  348.1 5.3 %collective-permute-start.52 = (f32[3,1,8,256]{3,2,1,0:T(8,128)S(1)}, f32[3,1,8,256]{3,2,1,0:T(8,128)S(1)}, u32[]{:S(2)}, u32[]{:S(2)}) collective-permute-start(f32[3,1,8,256]{3,2,1,0:T(8,128)S(1)} %get-tuple-element.58), channel_id=1, source_target_pairs={{8,0},{16,8},{24,16},{32,24},{40,32},{48,40},{56,48},{64,56},{72,6... | collective-permute-start | bytes 73736 | tf_op jit(solution)/shard_map/ppermute | solution.py:21
  350.0 6.7 %collective-permute-start.53 = (f32[3,1,8,256]{3,2,1,0:T(8,128)S(1)}, f32[3,1,8,256]{3,2,1,0:T(8,128)S(1)}, u32[]{:S(2)}, u32[]{:S(2)}) collective-permute-start(f32[3,1,8,256]{3,2,1,0:T(8,128)S(1)} %get-tuple-element.57), channel_id=1, source_target_pairs={{0,8},{8,16},{16,24},{24,32},{32,40},{40,48},{48,56},{56,64},{64,7... | collective-permute-start | bytes 73736 | tf_op jit(solution)/shard_map/ppermute | solution.py:20
  356.7 5.0 %collective-permute-start.55 = (f32[3,6,1,256]{3,2,1,0:T(1,128)S(1)}, f32[3,6,1,256]{3,2,1,0:T(1,128)S(1)}, u32[]{:S(2)}, u32[]{:S(2)}) collective-permute-start(f32[3,6,1,256]{3,2,1,0:T(1,128)S(1)} %get-tuple-element.49), channel_id=1, source_target_pairs={{0,1},{1,2},{2,3},{3,4},{4,5},{5,6},{6,7},{8,9},{9,10},{10,11},{11... | collective-permute-start | bytes 55304 | tf_op jit(solution)/shard_map/ppermute | solution.py:20
  359.8 5.1 %collective-permute-start.54 = (f32[3,6,1,256]{3,2,1,0:T(1,128)S(1)}, f32[3,6,1,256]{3,2,1,0:T(1,128)S(1)}, u32[]{:S(2)}, u32[]{:S(2)}) collective-permute-start(f32[3,6,1,256]{3,2,1,0:T(1,128)S(1)} %get-tuple-element.48), channel_id=1, source_target_pairs={{1,0},{2,1},{3,2},{4,3},{5,4},{6,5},{7,6},{9,8},{10,9},{11,10},{12... | collective-permute-start | bytes 55304 | tf_op jit(solution)/shard_map/ppermute | solution.py:21
  384.7 5.4 %collective-permute-start.56 = (f32[3,1,16,512]{3,2,1,0:T(8,128)S(1)}, f32[3,1,16,512]{3,2,1,0:T(8,128)S(1)}, u32[]{:S(2)}, u32[]{:S(2)}) collective-permute-start(f32[3,1,16,512]{3,2,1,0:T(8,128)S(1)} %get-tuple-element.31), channel_id=1, source_target_pairs={{8,0},{16,8},{24,16},{32,24},{40,32},{48,40},{56,48},{64,56},{72,6... | collective-permute-start | bytes 294920 | tf_op jit(solution)/shard_map/ppermute | solution.py:21
  386.7 7.5 %collective-permute-start.57 = (f32[3,1,16,512]{3,2,1,0:T(8,128)S(1)}, f32[3,1,16,512]{3,2,1,0:T(8,128)S(1)}, u32[]{:S(2)}, u32[]{:S(2)}) collective-permute-start(f32[3,1,16,512]{3,2,1,0:T(8,128)S(1)} %get-tuple-element.30), channel_id=1, source_target_pairs={{0,8},{8,16},{16,24},{24,32},{32,40},{40,48},{48,56},{56,64},{64,7... | collective-permute-start | bytes 294920 | tf_op jit(solution)/shard_map/ppermute | solution.py:20
  394.3 5.8 %collective-permute-start.59 = (f32[3,10,1,512]{3,2,1,0:T(1,128)S(1)}, f32[3,10,1,512]{3,2,1,0:T(1,128)S(1)}, u32[]{:S(2)}, u32[]{:S(2)}) collective-permute-start(f32[3,10,1,512]{3,2,1,0:T(1,128)S(1)} %get-tuple-element.22), channel_id=1, source_target_pairs={{0,1},{1,2},{2,3},{3,4},{4,5},{5,6},{6,7},{8,9},{9,10},{10,11},{11... | collective-permute-start | bytes 184328 | tf_op jit(solution)/shard_map/ppermute | solution.py:20
  398.1 5.5 %collective-permute-start.58 = (f32[3,10,1,512]{3,2,1,0:T(1,128)S(1)}, f32[3,10,1,512]{3,2,1,0:T(1,128)S(1)}, u32[]{:S(2)}, u32[]{:S(2)}) collective-permute-start(f32[3,10,1,512]{3,2,1,0:T(1,128)S(1)} %get-tuple-element.21), channel_id=1, source_target_pairs={{1,0},{2,1},{3,2},{4,3},{5,4},{6,5},{7,6},{9,8},{10,9},{11,10},{12... | collective-permute-start | bytes 184328 | tf_op jit(solution)/shard_map/ppermute | solution.py:21
  404.5 5.4 %collective-permute-start.60 = (f32[3,1,16,512]{3,2,1,0:T(8,128)S(1)}, f32[3,1,16,512]{3,2,1,0:T(8,128)S(1)}, u32[]{:S(2)}, u32[]{:S(2)}) collective-permute-start(f32[3,1,16,512]{3,2,1,0:T(8,128)S(1)} %get-tuple-element.29), channel_id=1, source_target_pairs={{8,0},{16,8},{24,16},{32,24},{40,32},{48,40},{56,48},{64,56},{72,6... | collective-permute-start | bytes 294920 | tf_op jit(solution)/shard_map/ppermute | solution.py:21
  406.4 7.5 %collective-permute-start.61 = (f32[3,1,16,512]{3,2,1,0:T(8,128)S(1)}, f32[3,1,16,512]{3,2,1,0:T(8,128)S(1)}, u32[]{:S(2)}, u32[]{:S(2)}) collective-permute-start(f32[3,1,16,512]{3,2,1,0:T(8,128)S(1)} %get-tuple-element.28), channel_id=1, source_target_pairs={{0,8},{8,16},{16,24},{24,32},{32,40},{40,48},{48,56},{56,64},{64,7... | collective-permute-start | bytes 294920 | tf_op jit(solution)/shard_map/ppermute | solution.py:20
  414.0 5.0 %collective-permute-start.63 = (f32[3,10,1,512]{3,2,1,0:T(1,128)S(1)}, f32[3,10,1,512]{3,2,1,0:T(1,128)S(1)}, u32[]{:S(2)}, u32[]{:S(2)}) collective-permute-start(f32[3,10,1,512]{3,2,1,0:T(1,128)S(1)} %get-tuple-element.20), channel_id=1, source_target_pairs={{0,1},{1,2},{2,3},{3,4},{4,5},{5,6},{6,7},{8,9},{9,10},{10,11},{11... | collective-permute-start | bytes 184328 | tf_op jit(solution)/shard_map/ppermute | solution.py:20
  417.1 5.5 %collective-permute-start.62 = (f32[3,10,1,512]{3,2,1,0:T(1,128)S(1)}, f32[3,10,1,512]{3,2,1,0:T(1,128)S(1)}, u32[]{:S(2)}, u32[]{:S(2)}) collective-permute-start(f32[3,10,1,512]{3,2,1,0:T(1,128)S(1)} %get-tuple-element.19), channel_id=1, source_target_pairs={{1,0},{2,1},{3,2},{4,3},{5,4},{6,5},{7,6},{9,8},{10,9},{11,10},{12... | collective-permute-start | bytes 184328 | tf_op jit(solution)/shard_map/ppermute | solution.py:21
  (6 other events, 256.5 us)
where the time goes:
time: 428 us; the launch traced here: 424 us
  starting transfers between devices  181 us (42%)
  local copies, waits for them, and re-layouts  109 us (25%)
  waiting for transfers between devices  80.3 us (19%)
  other arithmetic  52.5 us (12%)
    ppermute x32, starting transfers between devices, extended(): before = lax.ppermute(last, axis, up)  103 us
    reshape x3, local copies, waits for them, and re-layouts, restrict(): values.reshape(leading + (extent[-3] // 2, 2, extent[-2] // 2, 2, extent[...  78.8 us
    ppermute x32, starting transfers between devices, extended(): after = lax.ppermute(initial, axis, down)  77.8 us
    ppermute x32, waiting for transfers between devices, extended(): before = lax.ppermute(last, axis, up)  43.7 us
    ppermute x32, waiting for transfers between devices, extended(): after = lax.ppermute(initial, axis, down)  36.6 us
    reduce_sum x4, other arithmetic, restrict(): return jnp.mean(blocks, axis=(-5, -3, -1))  28.3 us
    add x11, other arithmetic, jacobi_sweep(): current + relax_weight * (source - apply_operator(rim_field(current), coe...  10.1 us
  transfers between devices with their start and end apart: 64, of which 28 were waited for; matrix products, arithmetic and copies ran while one was open for 8% of the time, Pallas kernels for 0%

commit v1 on v0

v1 whole, which is shorter than its diff:
```python
import functools

import jax
import jax.numpy as jnp
from jax import lax
from jax.experimental import pallas as pl
from jax.experimental.pallas import tpu as pltpu
from jax.sharding import PartitionSpec as P

F32 = jnp.float32
BF16 = jnp.bfloat16
WEIGHT = 2.0 / 3.0
VMEM_LIMIT = 40 * 1024 * 1024


def materials(ids):
    eta = jnp.where(ids == 3, F32(4.0), F32(0.0))
    eta = jnp.where(ids == 2, F32(1.5), eta)
    eta = jnp.where(ids == 1, F32(0.6), eta)
    return jnp.where(ids == 0, F32(0.2), eta)


def lanes_of(shape):
    return lax.broadcasted_iota(jnp.int32, shape, len(shape) - 1)


def next_row(v):
    return pltpu.roll(v, v.shape[0] - 1, 0)


def last_row(v):
    return pltpu.roll(v, 1, 0)


def next_lane(v):
    return pltpu.roll(v, v.shape[1] - 1, 1)


def last_lane(v):
    return pltpu.roll(v, 1, 1)


def split_dot(rows, matrix):
    high = rows.astype(BF16)
    low = (rows - high.astype(F32)).astype(BF16)
    return jnp.dot(high, matrix, preferred_element_type=F32) + jnp.dot(
        low, matrix, preferred_element_type=F32
    )


def pair_matrix(fine):
    shape = (fine, fine // 2)
    row = lax.broadcasted_iota(jnp.int32, shape, 0)
    col = lax.broadcasted_iota(jnp.int32, shape, 1)
    return jnp.where((row == 2 * col) | (row == 2 * col + 1), F32(1), F32(0)).astype(BF16)


def copy_matrix(coarse):
    shape = (coarse, 2 * coarse)
    row = lax.broadcasted_iota(jnp.int32, shape, 0)
    col = lax.broadcasted_iota(jnp.int32, shape, 1)
    return jnp.where((col == 2 * row) | (col == 2 * row + 1), F32(1), F32(0)).astype(BF16)


YP, YM, ZP, ZM, DG, EI = range(6)


def coefficients(eta, cx, cf, layers, scale):
    half = 0.5 * scale

    def face(i, _):
        cx[i] = half * (eta[i] + eta[i + 1])
        return 0

    lax.fori_loop(0, layers + 1, face, 0)

    def body(i, _):
        here = eta[i + 1]
        lane = lanes_of(here.shape)
        first = lane == 0
        final = lane == here.shape[1] - 1
        yp, ym = next_row(here), last_row(here)
        zp, zm = next_lane(here), last_lane(here)
        cf[YP, i] = half * (here + yp)
        cf[YM, i] = half * (here + ym)
        cf[ZP, i] = jnp.where(final, 0.0, half * (here + zp))
        cf[ZM, i] = jnp.where(first, 0.0, half * (here + zm))

        def ghost(q):
            return jnp.where(q > 0.0, q, here)

        around = ghost(yp) + ghost(ym) + ghost(eta[i]) + ghost(eta[i + 2])
        around = around + jnp.where(final, here, zp) + jnp.where(first, here, zm)
        diag = scale * (3.0 * here + 0.5 * around)
        cf[DG, i] = diag
        cf[EI, i] = jnp.where(here > 0.0, WEIGHT / diag, 0.0)
        return 0

    lax.fori_loop(0, layers, body, 0)


def gather_sum(v, comp, i, cx, cf, k):
    here = v[comp, i]
    total = cx[k] * v[comp, i - 1] + cx[k + 1] * v[comp, i + 1]
    total = total + cf[YP, k] * next_row(here) + cf[YM, k] * last_row(here)
    total = total + cf[ZP, k] * next_lane(here) + cf[ZM, k] * last_lane(here)
    return here, total


def sweep(v, vo, g, go, cx, cf, co, out, oo, low, high):
    vo, go, co, oo = vo + low, go + low, co + low, oo + low

    def body(n, _):
        for comp in range(3):
            here, total = gather_sum(v, comp, n + vo, cx, cf, n + co)
            out[comp, n + oo] = (1.0 / 3.0) * here + cf[EI, n + co] * (g[comp, n + go] + total)
        return 0

    lax.fori_loop(0, high - low, body, 0)


def residual(v, vo, g, go, cx, cf, co, comp, x):
    here, total = gather_sum(v, comp, x + vo, cx, cf, x + co)
    return g[comp, x + go] - cf[DG, x + co] * here + total


def pack_fine_x(f, ids, up, down):
    for c in range(3):
        for k in range(3):
            up[3 * c + k] = f[c, 5 + k]
            down[3 * c + k] = f[c, k]
    for k in range(4):
        up[9 + k] = materials(ids[4 + k])
        down[9 + k] = materials(ids[k])


def fine_source(f, low, high, c, x):
    if x < 0:
        return low[3 * c + x + 3]
    if x < 8:
        return f[c, x]
    return high[3 * c + x - 8]


def fine_eta(ids, low, high, x):
    if x < 0:
        return low[9 + x + 4]
    if x < 8:
        return materials(ids[x])
    return high[9 + x - 8]


def pack_fine_y(f, ids, low, high, up, down):
    for i in range(14):
        rows = [fine_source(f, low, high, c, i - 3) for c in range(3)]
        for out, at in ((up, 13), (down, 0)):
            out[i, 0:3] = rows[0][at : at + 3]
            out[i, 3:6] = rows[1][at : at + 3]
            out[i, 6:8] = rows[2][at : at + 2]
            out[14 + i // 8, i % 8 : i % 8 + 1] = rows[2][at + 2 : at + 3]
    for out in (up, down):
        out[15, 6:8] = jnp.zeros((2, f.shape[-1]), F32)
    for j in range(16):
        eta = fine_eta(ids, low, high, j - 4)
        at = 4 * (j % 2)
        up[16 + j // 2, at : at + 4] = eta[12:16]
        down[16 + j // 2, at : at + 4] = eta[0:4]


def fine_down(f, ids, xlow, xhigh, ylow, yhigh, v0, g, cx, cf, f1, eta1, up, down, eta, va, pairs, rest):
    nz = f.shape[-1]
    blank = jnp.zeros((1, nz), F32)
    for c in range(3):
        for i in range(14):
            g[c, i, 4:20] = fine_source(f, xlow, xhigh, c, i - 3)
            for side, at in ((ylow, 1), (yhigh, 20)):
                if c < 2:
                    g[c, i, at : at + 3] = side[i, 3 * c : 3 * c + 3]
                else:
                    g[c, i, at : at + 2] = side[i, 6:8]
                    g[c, i, at + 2 : at + 3] = side[14 + i // 8, i % 8 : i % 8 + 1]
            g[c, i, 0:1] = blank
            g[c, i, 23:24] = blank
    for j in range(16):
        eta[j, 4:20] = fine_eta(ids, xlow, xhigh, j - 4)
        at = 4 * (j % 2)
        eta[j, 0:4] = ylow[16 + j // 2, at : at + 4]
        eta[j, 20:24] = yhigh[16 + j // 2, at : at + 4]

    coefficients(eta, cx, cf, 14, 1.0)

    def start(i, _):
        for c in range(3):
            va[c, i] = cf[EI, i] * g[c, i]
        return 0

    lax.fori_loop(0, 14, start, 0)
    sweep(va, 3, g, 3, cx, cf, 3, v0, 2, -2, 10)

    def down_pair(k, _):
        for c in range(3):
            x = 2 * k
            total = residual(v0, 2, g, 3, cx, cf, 3, c, x) + residual(v0, 2, g, 3, cx, cf, 3, c, x + 1)
            put_plane(pairs, c * 4 + k, total)
        return 0

    lax.fori_loop(0, 4, down_pair, 0)

    def eta_pair(k, _):
        put_plane(pairs, 12 + k, eta[2 * k + 2] + eta[2 * k + 3])
        return 0

    lax.fori_loop(0, 6, eta_pair, 0)
    for n in range(18):
        row_pairs(pairs, n, 4, 8, rest, n * 8)
    coarse = split_dot(rest[...], pair_matrix(nz)) * 0.125
    for n in range(12):
        block = coarse[n * 8 : n * 8 + 8]
        f1[n // 4, n % 4] = block
        up[n] = block
        down[n] = block
    for n in range(6):
        block = coarse[96 + n * 8 : 96 + n * 8 + 8]
        eta1[n] = block
        if n < 5:
            up[12 + n] = block
        if n > 0:
            down[12 + n - 1] = block


def lane_blocks(planes, nz):
    width = min(nz, 128)
    return (planes, nz // width, 24, width)


def put_plane(ref, n, value):
    width = ref.shape[-1]
    for b in range(ref.shape[1]):
        ref[n, b] = value[:, b * width : b * width + width]


def row_pairs(ref, n, at, count, out, row):
    width = ref.shape[-1]
    for b in range(ref.shape[1]):
        total = ref[n, b, pl.ds(at, count, stride=2), :] + ref[n, b, pl.ds(at + 1, count, stride=2), :]
        out[row : row + count, b * width : b * width + width] = total


def row_copies(ref, n, value):
    width = ref.shape[-1]
    count = value.shape[0]
    for b in range(ref.shape[1]):
        block = value[:, b * width : b * width + width]
        ref[n, b, pl.ds(0, count, stride=2), :] = block
        ref[n, b, pl.ds(1, count, stride=2), :] = block


def get_plane(ref, n):
    return jnp.concatenate([ref[n, b] for b in range(ref.shape[1])], axis=1)


def pack_middle_y(f1, eta1, low, high, up, down):
    def source(c, x):
        if x < 0:
            return low[4 * c + x + 4]
        if x < 4:
            return f1[c, x]
        return high[4 * c + x - 4]

    def viscosity(x):
        if x < 0:
            return low[12 + x + 5]
        if x < 4:
            return eta1[x + 1]
        return high[12 + x - 4]

    for i in range(12):
        rows = [source(c, i - 4) for c in range(3)]
        for out, at in ((up, 4), (down, 0)):
            out[i, 0:4] = rows[0][at : at + 4]
            out[i, 4:8] = rows[1][at : at + 4]
            out[12 + i + 1, 0:4] = rows[2][at : at + 4]
    for out in (up, down):
        out[12, 0:4] = jnp.zeros((4, f1.shape[-1]), F32)
        out[25, 0:4] = jnp.zeros((4, f1.shape[-1]), F32)
        out[27, 6:8] = jnp.zeros((2, f1.shape[-1]), F32)
    for j in range(14):
        eta = viscosity(j - 5)
        up[12 + j, 4:8] = eta[4:8]
        down[12 + j, 4:8] = eta[0:4]
        up[26 + j // 8, j % 8 : j % 8 + 1] = eta[3:4]
        down[26 + j // 8, j % 8 : j % 8 + 1] = eta[4:5]


def middle_down(f1, eta1, xlow, xhigh, ylow, yhigh, v1, g, cx, cf, own, up, down, far_up, far_down, eta, va, pairs, rest):
    nz = f1.shape[-1]
    blank = jnp.zeros((4, nz), F32)

    def source(c, x):
        if x < 0:
            return xlow[4 * c + x + 4]
        if x < 4:
            return f1[c, x]
        return xhigh[4 * c + x - 4]

    def viscosity(x):
        if x < 0:
            return xlow[12 + x + 5]
        if x < 4:
            return eta1[x + 1]
        return xhigh[12 + x - 4]

    for c in range(3):
        for i in range(12):
            g[c, i, 8:16] = source(c, i - 4)
            g[c, i, 0:4] = blank
            g[c, i, 20:24] = blank
            for side, at in ((ylow, 4), (yhigh, 16)):
                if c < 2:
                    g[c, i, at : at + 4] = side[i, 4 * c : 4 * c + 4]
                else:
                    g[c, i, at : at + 4] = side[13 + i, 0:4]
    for j in range(14):
        eta[j, 0:4] = blank
        eta[j, 20:24] = blank
        eta[j, 8:16] = viscosity(j - 5)
        eta[j, 4:8] = ylow[12 + j, 4:8]
        eta[j, 3:4] = ylow[26 + j // 8, j % 8 : j % 8 + 1]
        eta[j, 16:20] = yhigh[12 + j, 4:8]
        eta[j, 20:21] = yhigh[26 + j // 8, j % 8 : j % 8 + 1]

    coefficients(eta, cx, cf, 12, 0.25)

    plane = jnp.zeros((24, nz), F32)
    for c in range(3):
        for i in (0, 13):
            va[c, i] = plane
            v1[c, i] = plane

    def start(i, _):
        for c in range(3):
            va[c, i + 1] = cf[EI, i] * g[c, i]
        return 0

    lax.fori_loop(0, 12, start, 0)
    sweep(va, 5, g, 4, cx, cf, 4, v1, 5, -4, 8)

    def down_pair(k, _):
        for c in range(3):
            x = 2 * k
            total = residual(v1, 1, g, 0, cx, cf, 0, c, x) + residual(v1, 1, g, 0, cx, cf, 0, c, x + 1)
            put_plane(pairs, c * 6 + k, total)
        return 0

    lax.fori_loop(0, 6, down_pair, 0)

    def eta_pair(k, _):
        put_plane(pairs, 18 + k, eta[2 * k + 1] + eta[2 * k + 2])
        return 0

    lax.fori_loop(0, 6, eta_pair, 0)
    for k in range(6):
        for c in range(3):
            row_pairs(pairs, c * 6 + k, 8, 4, rest, 16 * k + 4 * c)
        row_pairs(pairs, 18 + k, 8, 4, rest, 16 * k + 12)
    coarse = split_dot(rest[...], pair_matrix(nz)) * 0.125
    for k in range(6):
        own[k] = coarse[16 * k : 16 * k + 16]
    for t in range(4):
        source_rows = own[t + 1, 0:12]
        up[t, 0:12] = source_rows
        up[t, 12:16] = own[t, 12:16]
        down[t, 0:12] = source_rows
        down[t, 12:16] = own[t + 2, 12:16]
        if t < 2:
            far_up[t, 0:12] = source_rows
            far_up[t, 12:16] = own[t, 12:16]
        else:
            far_down[t - 2, 0:12] = source_rows
            far_down[t - 2, 12:16] = own[t + 2, 12:16]


def pack_coarse_y(own, low2, low3, high2, high3, strip):
    strip[0, 0:12] = jnp.zeros((12, own.shape[-1]), F32)
    strip[17, 0:12] = jnp.zeros((12, own.shape[-1]), F32)
    for t in range(2):
        strip[1 + t, 0:12] = low3[t, 0:12]
        strip[t, 12:16] = low3[t, 12:16]
        strip[15 + t, 0:12] = high3[t, 0:12]
        strip[16 + t, 12:16] = high3[t, 12:16]
    for t in range(4):
        strip[3 + t, 0:12] = low2[t, 0:12]
        strip[2 + t, 12:16] = low2[t, 12:16]
        strip[7 + t, 0:12] = own[1 + t, 0:12]
        strip[11 + t, 0:12] = high2[t, 0:12]
        strip[12 + t, 12:16] = high2[t, 12:16]
    for t in range(6):
        strip[6 + t, 12:16] = own[t, 12:16]
    for plane, outer, mine in ((6, 5, 0), (11, 12, 5)):
        inside = strip[outer, 12:16] > 0.0
        for c in range(3):
            rows = slice(4 * c, 4 * c + 4)
            strip[plane, rows] = jnp.where(inside, strip[plane, rows], own[mine, rows])


def ascend(
    mid, ym1, ym2, yp1, yp2, v1, g1, cx1, cf1, v0, g0, cx0, cf0, out,
    eta2, g2, cx2, cf2, va2, vb2, rows2, wide1, va1, vb1, rows1, wide0, va0, vb0,
):
    nz2, nz1, nz0 = mid.shape[-1], v1.shape[-1], v0.shape[-1]
    blank = jnp.zeros((4, nz2), F32)
    for j in range(18):
        for n, side in enumerate((ym2, ym1, mid, yp1, yp2)):
            eta2[j, 4 * n : 4 * n + 4] = side[j, 12:16]
        eta2[j, 20:24] = blank
    for i in range(16):
        for c in range(3):
            for n, side in enumerate((ym2, ym1, mid, yp1, yp2)):
                g2[c, i, 4 * n : 4 * n + 4] = side[i + 1, 4 * c : 4 * c + 4]
            g2[c, i, 20:24] = blank
    coefficients(eta2, cx2, cf2, 16, 0.0625)

    def start(i, _):
        for c in range(3):
            va2[c, i] = cf2[EI, i] * g2[c, i]
        return 0

    lax.fori_loop(0, 16, start, 0)
    source, target = va2, vb2
    for s in range(1, 6):
        sweep(source, 0, g2, 0, cx2, cf2, 0, target, 0, s, 16 - s)
        source, target = target, source

    for c in range(3):
        for k in range(6):
            rows2[(c * 6 + k) * 16 : (c * 6 + k) * 16 + 16] = source[c, 5 + k, 4:20]
    spread = split_dot(rows2[...], copy_matrix(nz2))
    for n in range(18):
        block = spread[n * 16 : n * 16 + 12]
        row_copies(wide1, n, block)
    for c in range(3):
        for i in range(10):
            va1[c, i] = v1[c, i + 2] + get_plane(wide1, c * 6 + (i - 3) // 2 + 2)
    sweep(va1, 3, g1, 4, cx1, cf1, 4, vb1, 3, -2, 6)
    sweep(vb1, 3, g1, 4, cx1, cf1, 4, va1, 3, -1, 5)

    for c in range(3):
        for k in range(6):
            rows1[(c * 6 + k) * 16 : (c * 6 + k) * 16 + 16] = va1[c, 2 + k, 6:22]
    spread = split_dot(rows1[...], copy_matrix(nz1))
    for n in range(18):
        block = spread[n * 16 : n * 16 + 12]
        row_copies(wide0, n, block)

    def correct(k, _):
        for c in range(3):
            block = get_plane(wide0, c * 6 + k)
            va0[c, 2 * k] = v0[c, 2 * k] + block
            va0[c, 2 * k + 1] = v0[c, 2 * k + 1] + block
        return 0

    lax.fori_loop(0, 6, correct, 0)
    sweep(va0, 2, g0, 3, cx0, cf0, 3, vb0, 2, -1, 9)

    def final(x, _):
        for c in range(3):
            here, total = gather_sum(vb0, c, x + 2, cx0, cf0, x + 3)
            value = (1.0 / 3.0) * here + cf0[EI, x + 3] * (g0[c, x + 3] + total)
            out[c, x] = value[4:20]
        return 0

    lax.fori_loop(0, 8, final, 0)


def call(body, outs, *args, scratch=()):
    vmem = pl.BlockSpec(memory_space=pltpu.VMEM)
    return pl.pallas_call(
        body,
        out_shape=[jax.ShapeDtypeStruct(shape, F32) for shape in outs],
        in_specs=[vmem] * len(args),
        out_specs=[vmem] * len(outs),
        scratch_shapes=[pltpu.VMEM(shape, F32) for shape in scratch],
        compiler_params=pltpu.CompilerParams(vmem_limit_bytes=VMEM_LIMIT),
    )(*args)


def moved(array, axis, step):
    size = lax.axis_size(axis)
    pairs = [(i, i + step) for i in range(size) if 0 <= i + step < size]
    if not pairs:
        return jnp.zeros_like(array)
    return lax.ppermute(array, axis, pairs)


def per_device(forcing, phase_ids):
    z0 = forcing.shape[-1]
    z1, z2 = z0 // 2, z0 // 4
    up, down = call(pack_fine_x, [(13, 16, z0)] * 2, forcing, phase_ids)
    xlow, xhigh = moved(up, "gx", 1), moved(down, "gx", -1)
    up, down = call(pack_fine_y, [(24, 8, z0)] * 2, forcing, phase_ids, xlow, xhigh)
    ylow, yhigh = moved(up, "gy", 1), moved(down, "gy", -1)
    v0, g0, cx0, cf0, f1, eta1, up, down = call(
        fine_down,
        [(3, 12, 24, z0), (3, 14, 24, z0), (15, 24, z0), (6, 14, 24, z0), (3, 4, 8, z1), (6, 8, z1), (17, 8, z1), (17, 8, z1)],
        forcing, phase_ids, xlow, xhigh, ylow, yhigh,
        scratch=[(16, 24, z0), (3, 14, 24, z0), lane_blocks(18, z0), (144, z0)],
    )
    xlow, xhigh = moved(up, "gx", 1), moved(down, "gx", -1)
    up, down = call(pack_middle_y, [(28, 8, z1)] * 2, f1, eta1, xlow, xhigh)
    ylow, yhigh = moved(up, "gy", 1), moved(down, "gy", -1)
    v1, g1, cx1, cf1, own, up, down, far_up, far_down = call(
        middle_down,
        [(3, 14, 24, z1), (3, 12, 24, z1), (13, 24, z1), (6, 12, 24, z1), (6, 16, z2), (4, 16, z2), (4, 16, z2), (2, 16, z2), (2, 16, z2)],
        f1, eta1, xlow, xhigh, ylow, yhigh,
        scratch=[(14, 24, z1), (3, 14, 24, z1), lane_blocks(24, z1), (96, z1)],
    )
    low2, high2 = moved(up, "gx", 2), moved(down, "gx", -2)
    low3, high3 = moved(far_up, "gx", 3), moved(far_down, "gx", -3)
    (strip,) = call(pack_coarse_y, [(18, 16, z2)], own, low2, low3, high2, high3)
    ym1, yp1 = moved(strip, "gy", 1), moved(strip, "gy", -1)
    ym2, yp2 = moved(strip, "gy", 2), moved(strip, "gy", -2)
    (velocity,) = call(
        ascend,
        [forcing.shape],
        strip, ym1, ym2, yp1, yp2, v1, g1, cx1, cf1, v0, g0, cx0, cf0,
        scratch=[
            (18, 24, z2), (3, 16, 24, z2), (17, 24, z2), (6, 16, 24, z2), (3, 16, 24, z2), (3, 16, 24, z2),
            (288, z2), lane_blocks(18, z1), (3, 10, 24, z1), (3, 10, 24, z1),
            (288, z1), lane_blocks(18, z0), (3, 12, 24, z0), (3, 12, 24, z0),
        ],
    )
    return velocity


def solution(mesh):
    return jax.shard_map(
        per_device,
        mesh=mesh,
        in_specs=(P(None, "gx", "gy", None), P("gx", "gy", None)),
        out_specs=P(None, "gx", "gy", None),
        check_vma=False,
    )
```

time: 428 us -> 112 us (0.26)
  the two profiles are of different devices: /device:TPU:15 before, /device:TPU:1 now
where the time goes in v1:
time: 112 us; the launch traced here: 111 us
  starting transfers between devices  48.3 us (43%)
  waiting for transfers between devices  36.8 us (33%)
  Pallas kernels  23.5 us (21%)
  local copies, waits for them, and re-layouts  2.08 us (2%)
    ppermute x16, starting transfers between devices, moved(): return lax.ppermute(array, axis, pairs)  48.3 us
    ppermute x16, waiting for transfers between devices, moved(): return lax.ppermute(array, axis, pairs)  36.8 us
    pallas_call x7, Pallas kernels, call(): pl.pallas_call(body, out_shape=[jax.ShapeDtypeStruct(shape, F32) for shap...  23.5 us
  transfers between devices with their start and end apart: 16, of which 10 were waited for; matrix products, arithmetic and copies ran while one was open for 0% of the time, Pallas kernels for 0%

profile of v1, /device:TPU:1, one launch (start us, length us, event | category | flops | bytes accessed | tf_op | source)
XLA Modules:
  0.0 110.9 jit_solution(17742884560882502170)
XLA Ops:
  0.0 0.0 copy-start
  0.0 1.1 %copy-done = f32[3,8,16,512]{3,2,1,0:T(8,128)S(1)} copy-done((f32[3,8,16,512]{3,2,1,0:T(8,128)S(1)}, f32[3,8,16,512]{3,2,1,0:T(8,128)}, u32[]{:S(2)}) %copy-start) | copy-done | bytes 786456
  1.1 0.0 copy-start.1
  1.1 0.9 copy-done.1
  2.1 0.1 shard_map.28
  2.2 4.4 %collective-permute-start = (f32[13,16,512]{2,1,0:T(8,128)S(1)}, f32[13,16,512]{2,1,0:T(8,128)S(1)}, u32[]{:S(2)}, u32[]{:S(2)}) collective-permute-start(f32[13,16,512]{2,1,0:T(8,128)S(1)} %get-tuple-element.28), channel_id=1, source_target_pairs={{0,8},{8,16},{16,24},{24,32},{32,40},{40,48},{48,56},{56,64},{64,7... | collective-permute-start | bytes 1277960 | tf_op jit(solution)/shard_map/ppermute | solution.py:492
  6.6 1.3 %collective-permute-start.1 = (f32[13,16,512]{2,1,0:T(8,128)S(1)}, f32[13,16,512]{2,1,0:T(8,128)S(1)}, u32[]{:S(2)}, u32[]{:S(2)}) collective-permute-start(f32[13,16,512]{2,1,0:T(8,128)S(1)} %get-tuple-element.29), channel_id=1, source_target_pairs={{8,0},{16,8},{24,16},{32,24},{40,32},{48,40},{56,48},{64,56},{72,6... | collective-permute-start | bytes 1277960 | tf_op jit(solution)/shard_map/ppermute | solution.py:492
  7.9 7.1 %collective-permute-done.low.xlow = f32[13,16,512]{2,1,0:T(8,128)S(1)} collective-permute-done((f32[13,16,512]{2,1,0:T(8,128)S(1)}, f32[13,16,512]{2,1,0:T(8,128)S(1)}, u32[]{:S(2)}, u32[]{:S(2)}) %collective-permute-start) | collective-permute-done | bytes 426016 | tf_op jit(solution)/shard_map/ppermute | solution.py:492
  15.0 4.2 %collective-permute-done.1.high.xhigh = f32[13,16,512]{2,1,0:T(8,128)S(1)} collective-permute-done((f32[13,16,512]{2,1,0:T(8,128)S(1)}, f32[13,16,512]{2,1,0:T(8,128)S(1)}, u32[]{:S(2)}, u32[]{:S(2)}) %collective-permute-start.1) | collective-permute-done | bytes 426016 | tf_op jit(solution)/shard_map/ppermute | solution.py:492
  19.2 0.2 shard_map.29
  19.4 4.8 %collective-permute-start.2 = (f32[24,8,512]{2,1,0:T(8,128)S(1)}, f32[24,8,512]{2,1,0:T(8,128)S(1)}, u32[]{:S(2)}, u32[]{:S(2)}) collective-permute-start(f32[24,8,512]{2,1,0:T(8,128)S(1)} %get-tuple-element.30), channel_id=1, source_target_pairs={{0,1},{1,2},{2,3},{3,4},{4,5},{5,6},{6,7},{8,9},{9,10},{10,11},{11... | collective-permute-start | bytes 1179656 | tf_op jit(solution)/shard_map/ppermute | solution.py:492
  24.2 1.9 %collective-permute-start.3 = (f32[24,8,512]{2,1,0:T(8,128)S(1)}, f32[24,8,512]{2,1,0:T(8,128)S(1)}, u32[]{:S(2)}, u32[]{:S(2)}) collective-permute-start(f32[24,8,512]{2,1,0:T(8,128)S(1)} %get-tuple-element.31), channel_id=1, source_target_pairs={{1,0},{2,1},{3,2},{4,3},{5,4},{6,5},{7,6},{9,8},{10,9},{11,10},{12... | collective-permute-start | bytes 1179656 | tf_op jit(solution)/shard_map/ppermute | solution.py:492
  26.1 2.8 %collective-permute-done.2.ylow = f32[24,8,512]{2,1,0:T(8,128)S(1)} collective-permute-done((f32[24,8,512]{2,1,0:T(8,128)S(1)}, f32[24,8,512]{2,1,0:T(8,128)S(1)}, u32[]{:S(2)}, u32[]{:S(2)}) %collective-permute-start.2) | collective-permute-done | bytes 393248 | tf_op jit(solution)/shard_map/ppermute | solution.py:492
  28.9 4.4 %collective-permute-done.3.yhigh = f32[24,8,512]{2,1,0:T(8,128)S(1)} collective-permute-done((f32[24,8,512]{2,1,0:T(8,128)S(1)}, f32[24,8,512]{2,1,0:T(8,128)S(1)}, u32[]{:S(2)}, u32[]{:S(2)}) %collective-permute-start.3) | collective-permute-done | bytes 393248 | tf_op jit(solution)/shard_map/ppermute | solution.py:492
  33.3 5.9 %shard_map.30 = (f32[3,12,24,512]{3,2,1,0:T(8,128)S(1)}, f32[3,14,24,512]{3,2,1,0:T(8,128)S(1)}, f32[15,24,512]{2,1,0:T(8,128)S(1)}, f32[6,14,24,512]{3,2,1,0:T(...) custom-call(f32[3,8,16,512]{3,2,1,0:T(8,128)S(1)} %copy-done, ...), custom_call_target="tpu_custom_call" | custom-call | tf_op jit(solution)/shard_map/pallas_call | solution.py:477
  39.2 3.5 %collective-permute-start.4 = (f32[17,8,256]{2,1,0:T(8,128)S(1)}, f32[17,8,256]{2,1,0:T(8,128)S(1)}, u32[]{:S(2)}, u32[]{:S(2)}) collective-permute-start(f32[17,8,256]{2,1,0:T(8,128)S(1)} %get-tuple-element.34), channel_id=1, source_target_pairs={{0,8},{8,16},{16,24},{24,32},{32,40},{40,48},{48,56},{56,64},{64,7... | collective-permute-start | bytes 417800 | tf_op jit(solution)/shard_map/ppermute | solution.py:492
  42.8 1.3 %collective-permute-start.5 = (f32[17,8,256]{2,1,0:T(8,128)S(1)}, f32[17,8,256]{2,1,0:T(8,128)S(1)}, u32[]{:S(2)}, u32[]{:S(2)}) collective-permute-start(f32[17,8,256]{2,1,0:T(8,128)S(1)} %get-tuple-element.35), channel_id=1, source_target_pairs={{8,0},{16,8},{24,16},{32,24},{40,32},{48,40},{56,48},{64,56},{72,6... | collective-permute-start | bytes 417800 | tf_op jit(solution)/shard_map/ppermute | solution.py:492
  44.1 0.7 collective-permute-done.4.low.xlow
  44.8 5.2 %collective-permute-done.5.high.xhigh = f32[17,8,256]{2,1,0:T(8,128)S(1)} collective-permute-done((f32[17,8,256]{2,1,0:T(8,128)S(1)}, f32[17,8,256]{2,1,0:T(8,128)S(1)}, u32[]{:S(2)}, u32[]{:S(2)}) %collective-permute-start.5) | collective-permute-done | bytes 139296 | tf_op jit(solution)/shard_map/ppermute | solution.py:492
  50.0 0.1 shard_map.31
  50.1 3.5 %collective-permute-start.6 = (f32[28,8,256]{2,1,0:T(8,128)S(1)}, f32[28,8,256]{2,1,0:T(8,128)S(1)}, u32[]{:S(2)}, u32[]{:S(2)}) collective-permute-start(f32[28,8,256]{2,1,0:T(8,128)S(1)} %get-tuple-element.36), channel_id=1, source_target_pairs={{0,1},{1,2},{2,3},{3,4},{4,5},{5,6},{6,7},{8,9},{9,10},{10,11},{11... | collective-permute-start | bytes 688136 | tf_op jit(solution)/shard_map/ppermute | solution.py:492
  53.6 1.9 %collective-permute-start.7 = (f32[28,8,256]{2,1,0:T(8,128)S(1)}, f32[28,8,256]{2,1,0:T(8,128)S(1)}, u32[]{:S(2)}, u32[]{:S(2)}) collective-permute-start(f32[28,8,256]{2,1,0:T(8,128)S(1)} %get-tuple-element.37), channel_id=1, source_target_pairs={{1,0},{2,1},{3,2},{4,3},{5,4},{6,5},{7,6},{9,8},{10,9},{11,10},{12... | collective-permute-start | bytes 688136 | tf_op jit(solution)/shard_map/ppermute | solution.py:492
  55.5 1.0 collective-permute-done.6.ylow
  56.5 4.4 %collective-permute-done.7.yhigh = f32[28,8,256]{2,1,0:T(8,128)S(1)} collective-permute-done((f32[28,8,256]{2,1,0:T(8,128)S(1)}, f32[28,8,256]{2,1,0:T(8,128)S(1)}, u32[]{:S(2)}, u32[]{:S(2)}) %collective-permute-start.7) | collective-permute-done | bytes 229408 | tf_op jit(solution)/shard_map/ppermute | solution.py:492
  60.9 4.1 %shard_map.32 = (f32[3,14,24,256]{3,2,1,0:T(8,128)S(1)}, f32[3,12,24,256]{3,2,1,0:T(8,128)S(1)}, f32[13,24,256]{2,1,0:T(8,128)S(1)}, f32[6,12,24,256]{3,2,1,0:T(...) custom-call(f32[3,4,8,256]{3,2,1,0:T(8,128)S(1)} %get-tuple-element., ...), custom_call_target="tpu_custom_call" | custom-call | tf_op jit(solution)/shard_map/pallas_call | solution.py:477
  65.0 6.3 %collective-permute-start.8 = (f32[4,16,128]{2,1,0:T(8,128)S(1)}, f32[4,16,128]{2,1,0:T(8,128)S(1)}, u32[]{:S(2)}, u32[]{:S(2)}) collective-permute-start(f32[4,16,128]{2,1,0:T(8,128)S(1)} %get-tuple-element.39), channel_id=1, source_target_pairs={{0,16},{8,24},{16,32},{24,40},{32,48},{40,56},{48,64},{56,72},{64,... | collective-permute-start | bytes 98312 | tf_op jit(solution)/shard_map/ppermute | solution.py:492
  71.4 1.3 %collective-permute-start.10 = (f32[4,16,128]{2,1,0:T(8,128)S(1)}, f32[4,16,128]{2,1,0:T(8,128)S(1)}, u32[]{:S(2)}, u32[]{:S(2)}) collective-permute-start(f32[4,16,128]{2,1,0:T(8,128)S(1)} %get-tuple-element.41), channel_id=1, source_target_pairs={{16,0},{24,8},{32,16},{40,24},{48,32},{56,40},{64,48},{72,56},{80,... | collective-permute-start | bytes 98312 | tf_op jit(solution)/shard_map/ppermute | solution.py:492
  72.7 5.2 %collective-permute-start.9 = (f32[2,16,128]{2,1,0:T(8,128)S(1)}, f32[2,16,128]{2,1,0:T(8,128)S(1)}, u32[]{:S(2)}, u32[]{:S(2)}) collective-permute-start(f32[2,16,128]{2,1,0:T(8,128)S(1)} %get-tuple-element.40), channel_id=1, source_target_pairs={{0,24},{8,32},{16,40},{24,48},{32,56},{40,64},{48,72},{56,80},{64,... | collective-permute-start | bytes 49160 | tf_op jit(solution)/shard_map/ppermute | solution.py:492
  77.9 1.3 %collective-permute-start.11 = (f32[2,16,128]{2,1,0:T(8,128)S(1)}, f32[2,16,128]{2,1,0:T(8,128)S(1)}, u32[]{:S(2)}, u32[]{:S(2)}) collective-permute-start(f32[2,16,128]{2,1,0:T(8,128)S(1)} %get-tuple-element.42), channel_id=1, source_target_pairs={{24,0},{32,8},{40,16},{48,24},{56,32},{64,40},{72,48},{80,56},{88,... | collective-permute-start | bytes 49160 | tf_op jit(solution)/shard_map/ppermute | solution.py:492
  79.2 0.0 collective-permute-done.9.low3
  79.2 5.0 %collective-permute-done.11.high3 = f32[2,16,128]{2,1,0:T(8,128)S(1)} collective-permute-done((f32[2,16,128]{2,1,0:T(8,128)S(1)}, f32[2,16,128]{2,1,0:T(8,128)S(1)}, u32[]{:S(2)}, u32[]{:S(2)}) %collective-permute-start.11) | collective-permute-done | bytes 16416 | tf_op jit(solution)/shard_map/ppermute | solution.py:492
  84.2 0.0 collective-permute-done.8.low2
  84.2 0.0 collective-permute-done.10.high2
  84.2 1.3 %collective-permute-start.15 = (f32[18,16,128]{2,1,0:T(8,128)S(1)}, f32[18,16,128]{2,1,0:T(8,128)S(1)}, u32[]{:S(2)}, u32[]{:S(2)}) collective-permute-start(f32[18,16,128]{2,1,0:T(8,128)S(1)} %shard_map.33.mid), channel_id=1, source_target_pairs={{2,0},{3,1},{4,2},{5,3},{6,4},{7,5},{10,8},{11,9},{12,10},{13,11},... | collective-permute-start | bytes 442376 | tf_op jit(solution)/shard_map/ppermute | solution.py:492
  85.5 1.9 %collective-permute-start.14 = (f32[18,16,128]{2,1,0:T(8,128)S(1)}, f32[18,16,128]{2,1,0:T(8,128)S(1)}, u32[]{:S(2)}, u32[]{:S(2)}) collective-permute-start(f32[18,16,128]{2,1,0:T(8,128)S(1)} %shard_map.33.mid), channel_id=1, source_target_pairs={{1,0},{2,1},{3,2},{4,3},{5,4},{6,5},{7,6},{9,8},{10,9},{11,10},{12... | collective-permute-start | bytes 442376 | tf_op jit(solution)/shard_map/ppermute | solution.py:492
  87.4 4.5 %collective-permute-start.13 = (f32[18,16,128]{2,1,0:T(8,128)S(1)}, f32[18,16,128]{2,1,0:T(8,128)S(1)}, u32[]{:S(2)}, u32[]{:S(2)}) collective-permute-start(f32[18,16,128]{2,1,0:T(8,128)S(1)} %shard_map.33.mid), channel_id=1, source_target_pairs={{0,2},{1,3},{2,4},{3,5},{4,6},{5,7},{8,10},{9,11},{10,12},{11,13},... | collective-permute-start | bytes 442376 | tf_op jit(solution)/shard_map/ppermute | solution.py:492
  91.9 3.8 %collective-permute-start.12 = (f32[18,16,128]{2,1,0:T(8,128)S(1)}, f32[18,16,128]{2,1,0:T(8,128)S(1)}, u32[]{:S(2)}, u32[]{:S(2)}) collective-permute-start(f32[18,16,128]{2,1,0:T(8,128)S(1)} %shard_map.33.mid), channel_id=1, source_target_pairs={{0,1},{1,2},{2,3},{3,4},{4,5},{5,6},{6,7},{8,9},{9,10},{10,11},{11... | collective-permute-start | bytes 442376 | tf_op jit(solution)/shard_map/ppermute | solution.py:492
  95.7 0.0 collective-permute-done.15.yp2
  95.7 0.0 collective-permute-done.14.yp1
  95.8 0.0 collective-permute-done.13.ym2
  95.8 2.0 %collective-permute-done.12.ym1 = f32[18,16,128]{2,1,0:T(8,128)S(1)} collective-permute-done((f32[18,16,128]{2,1,0:T(8,128)S(1)}, f32[18,16,128]{2,1,0:T(8,128)S(1)}, u32[]{:S(2)}, u32[]{:S(2)}) %collective-permute-start.12) | collective-permute-done | bytes 147488 | tf_op jit(solution)/shard_map/ppermute | solution.py:492
  97.8 13.1 %shard_map.34 = f32[3,8,16,512]{3,2,1,0:T(8,128)} custom-call(f32[18,16,128]{2,1,0:T(8,128)S(1)} %shard_map.33.mid, f32[18,16,128]{2,1,0:T(8,128)S(1)} %collective-permute-done.12.ym1, f32[18,16,128]{2,1,0:T(8,128)S(1)} %collective-permute-done.13.ym2, f32[18,16,128]{2,1,0:T(8,128)S(1)} %collective-permute-done.14.yp1, ...), custom_call_target="tpu_custom_call" | custom-call | tf_op jit(solution)/shard_map/pallas_call | solution.py:477
  (1 shorter events, 0.0 us)
Async XLA Ops:
  0.0 1.1 %copy-start = (f32[3,8,16,512]{3,2,1,0:T(8,128)S(1)}, f32[3,8,16,512]{3,2,1,0:T(8,128)}, u32[]{:S(2)}) copy-start(f32[3,8,16,512]{3,2,1,0:T(8,128)} %f.5) | copy-start | bytes 2359300
  1.1 0.9 copy-start.1
  2.2 12.8 %collective-permute-start = (f32[13,16,512]{2,1,0:T(8,128)S(1)}, f32[13,16,512]{2,1,0:T(8,128)S(1)}, u32[]{:S(2)}, u32[]{:S(2)}) collective-permute-start(f32[13,16,512]{2,1,0:T(8,128)S(1)} %get-tuple-element.28), channel_id=1, source_target_pairs={{0,8},{8,16},{16,24},{24,32},{32,40},{40,48},{48,56},{56,64},{64,7... | collective-permute-start | bytes 1277960 | tf_op jit(solution)/shard_map/ppermute | solution.py:492
  6.6 12.6 %collective-permute-start.1 = (f32[13,16,512]{2,1,0:T(8,128)S(1)}, f32[13,16,512]{2,1,0:T(8,128)S(1)}, u32[]{:S(2)}, u32[]{:S(2)}) collective-permute-start(f32[13,16,512]{2,1,0:T(8,128)S(1)} %get-tuple-element.29), channel_id=1, source_target_pairs={{8,0},{16,8},{24,16},{32,24},{40,32},{48,40},{56,48},{64,56},{72,6... | collective-permute-start | bytes 1277960 | tf_op jit(solution)/shard_map/ppermute | solution.py:492
  19.4 9.5 %collective-permute-start.2 = (f32[24,8,512]{2,1,0:T(8,128)S(1)}, f32[24,8,512]{2,1,0:T(8,128)S(1)}, u32[]{:S(2)}, u32[]{:S(2)}) collective-permute-start(f32[24,8,512]{2,1,0:T(8,128)S(1)} %get-tuple-element.30), channel_id=1, source_target_pairs={{0,1},{1,2},{2,3},{3,4},{4,5},{5,6},{6,7},{8,9},{9,10},{10,11},{11... | collective-permute-start | bytes 1179656 | tf_op jit(solution)/shard_map/ppermute | solution.py:492
  24.2 9.1 %collective-permute-start.3 = (f32[24,8,512]{2,1,0:T(8,128)S(1)}, f32[24,8,512]{2,1,0:T(8,128)S(1)}, u32[]{:S(2)}, u32[]{:S(2)}) collective-permute-start(f32[24,8,512]{2,1,0:T(8,128)S(1)} %get-tuple-element.31), channel_id=1, source_target_pairs={{1,0},{2,1},{3,2},{4,3},{5,4},{6,5},{7,6},{9,8},{10,9},{11,10},{12... | collective-permute-start | bytes 1179656 | tf_op jit(solution)/shard_map/ppermute | solution.py:492
  39.2 5.6 %collective-permute-start.4 = (f32[17,8,256]{2,1,0:T(8,128)S(1)}, f32[17,8,256]{2,1,0:T(8,128)S(1)}, u32[]{:S(2)}, u32[]{:S(2)}) collective-permute-start(f32[17,8,256]{2,1,0:T(8,128)S(1)} %get-tuple-element.34), channel_id=1, source_target_pairs={{0,8},{8,16},{16,24},{24,32},{32,40},{40,48},{48,56},{56,64},{64,7... | collective-permute-start | bytes 417800 | tf_op jit(solution)/shard_map/ppermute | solution.py:492
  42.8 7.2 %collective-permute-start.5 = (f32[17,8,256]{2,1,0:T(8,128)S(1)}, f32[17,8,256]{2,1,0:T(8,128)S(1)}, u32[]{:S(2)}, u32[]{:S(2)}) collective-permute-start(f32[17,8,256]{2,1,0:T(8,128)S(1)} %get-tuple-element.35), channel_id=1, source_target_pairs={{8,0},{16,8},{24,16},{32,24},{40,32},{48,40},{56,48},{64,56},{72,6... | collective-permute-start | bytes 417800 | tf_op jit(solution)/shard_map/ppermute | solution.py:492
  50.1 6.5 %collective-permute-start.6 = (f32[28,8,256]{2,1,0:T(8,128)S(1)}, f32[28,8,256]{2,1,0:T(8,128)S(1)}, u32[]{:S(2)}, u32[]{:S(2)}) collective-permute-start(f32[28,8,256]{2,1,0:T(8,128)S(1)} %get-tuple-element.36), channel_id=1, source_target_pairs={{0,1},{1,2},{2,3},{3,4},{4,5},{5,6},{6,7},{8,9},{9,10},{10,11},{11... | collective-permute-start | bytes 688136 | tf_op jit(solution)/shard_map/ppermute | solution.py:492
  53.6 7.3 %collective-permute-start.7 = (f32[28,8,256]{2,1,0:T(8,128)S(1)}, f32[28,8,256]{2,1,0:T(8,128)S(1)}, u32[]{:S(2)}, u32[]{:S(2)}) collective-permute-start(f32[28,8,256]{2,1,0:T(8,128)S(1)} %get-tuple-element.37), channel_id=1, source_target_pairs={{1,0},{2,1},{3,2},{4,3},{5,4},{6,5},{7,6},{9,8},{10,9},{11,10},{12... | collective-permute-start | bytes 688136 | tf_op jit(solution)/shard_map/ppermute | solution.py:492
  65.0 19.2 %collective-permute-start.8 = (f32[4,16,128]{2,1,0:T(8,128)S(1)}, f32[4,16,128]{2,1,0:T(8,128)S(1)}, u32[]{:S(2)}, u32[]{:S(2)}) collective-permute-start(f32[4,16,128]{2,1,0:T(8,128)S(1)} %get-tuple-element.39), channel_id=1, source_target_pairs={{0,16},{8,24},{16,32},{24,40},{32,48},{40,56},{48,64},{56,72},{64,... | collective-permute-start | bytes 98312 | tf_op jit(solution)/shard_map/ppermute | solution.py:492
  71.4 12.8 %collective-permute-start.10 = (f32[4,16,128]{2,1,0:T(8,128)S(1)}, f32[4,16,128]{2,1,0:T(8,128)S(1)}, u32[]{:S(2)}, u32[]{:S(2)}) collective-permute-start(f32[4,16,128]{2,1,0:T(8,128)S(1)} %get-tuple-element.41), channel_id=1, source_target_pairs={{16,0},{24,8},{32,16},{40,24},{48,32},{56,40},{64,48},{72,56},{80,... | collective-permute-start | bytes 98312 | tf_op jit(solution)/shard_map/ppermute | solution.py:492
  72.7 6.5 %collective-permute-start.9 = (f32[2,16,128]{2,1,0:T(8,128)S(1)}, f32[2,16,128]{2,1,0:T(8,128)S(1)}, u32[]{:S(2)}, u32[]{:S(2)}) collective-permute-start(f32[2,16,128]{2,1,0:T(8,128)S(1)} %get-tuple-element.40), channel_id=1, source_target_pairs={{0,24},{8,32},{16,40},{24,48},{32,56},{40,64},{48,72},{56,80},{64,... | collective-permute-start | bytes 49160 | tf_op jit(solution)/shard_map/ppermute | solution.py:492
  77.9 6.3 %collective-permute-start.11 = (f32[2,16,128]{2,1,0:T(8,128)S(1)}, f32[2,16,128]{2,1,0:T(8,128)S(1)}, u32[]{:S(2)}, u32[]{:S(2)}) collective-permute-start(f32[2,16,128]{2,1,0:T(8,128)S(1)} %get-tuple-element.42), channel_id=1, source_target_pairs={{24,0},{32,8},{40,16},{48,24},{56,32},{64,40},{72,48},{80,56},{88,... | collective-permute-start | bytes 49160 | tf_op jit(solution)/shard_map/ppermute | solution.py:492
  84.2 11.5 %collective-permute-start.15 = (f32[18,16,128]{2,1,0:T(8,128)S(1)}, f32[18,16,128]{2,1,0:T(8,128)S(1)}, u32[]{:S(2)}, u32[]{:S(2)}) collective-permute-start(f32[18,16,128]{2,1,0:T(8,128)S(1)} %shard_map.33.mid), channel_id=1, source_target_pairs={{2,0},{3,1},{4,2},{5,3},{6,4},{7,5},{10,8},{11,9},{12,10},{13,11},... | collective-permute-start | bytes 442376 | tf_op jit(solution)/shard_map/ppermute | solution.py:492
  85.5 10.2 %collective-permute-start.14 = (f32[18,16,128]{2,1,0:T(8,128)S(1)}, f32[18,16,128]{2,1,0:T(8,128)S(1)}, u32[]{:S(2)}, u32[]{:S(2)}) collective-permute-start(f32[18,16,128]{2,1,0:T(8,128)S(1)} %shard_map.33.mid), channel_id=1, source_target_pairs={{1,0},{2,1},{3,2},{4,3},{5,4},{6,5},{7,6},{9,8},{10,9},{11,10},{12... | collective-permute-start | bytes 442376 | tf_op jit(solution)/shard_map/ppermute | solution.py:492
  87.4 8.3 %collective-permute-start.13 = (f32[18,16,128]{2,1,0:T(8,128)S(1)}, f32[18,16,128]{2,1,0:T(8,128)S(1)}, u32[]{:S(2)}, u32[]{:S(2)}) collective-permute-start(f32[18,16,128]{2,1,0:T(8,128)S(1)} %shard_map.33.mid), channel_id=1, source_target_pairs={{0,2},{1,3},{2,4},{3,5},{4,6},{5,7},{8,10},{9,11},{10,12},{11,13},... | collective-permute-start | bytes 442376 | tf_op jit(solution)/shard_map/ppermute | solution.py:492
  91.9 5.9 %collective-permute-start.12 = (f32[18,16,128]{2,1,0:T(8,128)S(1)}, f32[18,16,128]{2,1,0:T(8,128)S(1)}, u32[]{:S(2)}, u32[]{:S(2)}) collective-permute-start(f32[18,16,128]{2,1,0:T(8,128)S(1)} %shard_map.33.mid), channel_id=1, source_target_pairs={{0,1},{1,2},{2,3},{3,4},{4,5},{5,6},{6,7},{8,9},{9,10},{10,11},{11... | collective-permute-start | bytes 442376 | tf_op jit(solution)/shard_map/ppermute | solution.py:492

commit v2 on v1

--- a/solution.py
+++ b/solution.py
@@ -11,6 +11,7 @@
 BF16 = jnp.bfloat16
 WEIGHT = 2.0 / 3.0
 VMEM_LIMIT = 40 * 1024 * 1024
+U0, U1, U2 = 2, 4, 16
 
 
 def materials(ids):
@@ -38,6 +39,25 @@
 
 def last_lane(v):
     return pltpu.roll(v, 1, 1)
+
+
+def planes(count, body, unroll):
+    steps = count // unroll if unroll < count else 0
+
+    def step(n, _):
+        for k in range(unroll):
+            body(n * unroll + k)
+        return 0
+
+    if steps > 0:
+        lax.fori_loop(0, steps, step, 0)
+    for i in range(steps * unroll, count):
+        body(i)
+
+
+def kept(axis, step, value):
+    place = lax.axis_index(axis) - step
+    return jnp.where((place >= 0) & (place < lax.axis_size(axis)), value, 0.0)
 
 
 def split_dot(rows, matrix):
@@ -65,16 +85,15 @@
 YP, YM, ZP, ZM, DG, EI = range(6)
 
 
-def coefficients(eta, cx, cf, layers, scale):
+def coefficients(eta, cx, cf, layers, scale, unroll):
     half = 0.5 * scale
 
-    def face(i, _):
+    def face(i):
         cx[i] = half * (eta[i] + eta[i + 1])
-        return 0
-
-    lax.fori_loop(0, layers + 1, face, 0)
-
-    def body(i, _):
+
+    planes(layers + 1, face, unroll)
+
+    def body(i):
         here = eta[i + 1]
         lane = lanes_of(here.shape)
         first = lane == 0
@@ -94,9 +113,8 @@
         diag = scale * (3.0 * here + 0.5 * around)
         cf[DG, i] = diag
         cf[EI, i] = jnp.where(here > 0.0, WEIGHT / diag, 0.0)
-        return 0
-
-    lax.fori_loop(0, layers, body, 0)
+
+    planes(layers, body, unroll)
 
 
 def gather_sum(v, comp, i, cx, cf, k):
@@ -107,16 +125,15 @@
     return here, total
 
 
-def sweep(v, vo, g, go, cx, cf, co, out, oo, low, high):
+def sweep(v, vo, g, go, cx, cf, co, out, oo, low, high, unroll):
     vo, go, co, oo = vo + low, go + low, co + low, oo + low
 
-    def body(n, _):
+    def body(n):
         for comp in range(3):
             here, total = gather_sum(v, comp, n + vo, cx, cf, n + co)
             out[comp, n + oo] = (1.0 / 3.0) * here + cf[EI, n + co] * (g[comp, n + go] + total)
-        return 0
-
-    lax.fori_loop(0, high - low, body, 0)
+
+    planes(high - low, body, unroll)
 
 
 def residual(v, vo, g, go, cx, cf, co, comp, x):
@@ -187,30 +204,27 @@
         eta[j, 0:4] = ylow[16 + j // 2, at : at + 4]
         eta[j, 20:24] = yhigh[16 + j // 2, at : at + 4]
 
-    coefficients(eta, cx, cf, 14, 1.0)
-
-    def start(i, _):
+    coefficients(eta, cx, cf, 14, 1.0, U0)
+
+    def start(i):
         for c in range(3):
             va[c, i] = cf[EI, i] * g[c, i]
-        return 0
-
-    lax.fori_loop(0, 14, start, 0)
-    sweep(va, 3, g, 3, cx, cf, 3, v0, 2, -2, 10)
-
-    def down_pair(k, _):
+
+    planes(14, start, U0)
+    sweep(va, 3, g, 3, cx, cf, 3, v0, 2, -2, 10, U0)
+
+    def down_pair(k):
         for c in range(3):
             x = 2 * k
             total = residual(v0, 2, g, 3, cx, cf, 3, c, x) + residual(v0, 2, g, 3, cx, cf, 3, c, x + 1)
             put_plane(pairs, c * 4 + k, total)
-        return 0
-
-    lax.fori_loop(0, 4, down_pair, 0)
-
-    def eta_pair(k, _):
+
+    planes(4, down_pair, U0)
+
+    def eta_pair(k):
         put_plane(pairs, 12 + k, eta[2 * k + 2] + eta[2 * k + 3])
-        return 0
-
-    lax.fori_loop(0, 6, eta_pair, 0)
+
+    planes(6, eta_pair, U0)
     for n in range(18):
         row_pairs(pairs, n, 4, 8, rest, n * 8)
     coarse = split_dot(rest[...], pair_matrix(nz)) * 0.125
@@ -262,17 +276,17 @@
 def pack_middle_y(f1, eta1, low, high, up, down):
     def source(c, x):
         if x < 0:
-            return low[4 * c + x + 4]
+            return kept("gx", 1, low[4 * c + x + 4])
         if x < 4:
             return f1[c, x]
-        return high[4 * c + x - 4]
+        return kept("gx", -1, high[4 * c + x - 4])
 
     def viscosity(x):
         if x < 0:
-            return low[12 + x + 5]
+            return kept("gx", 1, low[12 + x + 5])
         if x < 4:
             return eta1[x + 1]
-        return high[12 + x - 4]
+        return kept("gx", -1, high[12 + x - 4])
 
     for i in range(12):
         rows = [source(c, i - 4) for c in range(3)]
@@ -298,38 +312,36 @@
 
     def source(c, x):
         if x < 0:
-            return xlow[4 * c + x + 4]
+            return kept("gx", 1, xlow[4 * c + x + 4])
         if x < 4:
             return f1[c, x]
-        return xhigh[4 * c + x - 4]
+        return kept("gx", -1, xhigh[4 * c + x - 4])
 
     def viscosity(x):
         if x < 0:
-            return xlow[12 + x + 5]
+            return kept("gx", 1, xlow[12 + x + 5])
         if x < 4:
             return eta1[x + 1]
-        return xhigh[12 + x - 4]
+        return kept("gx", -1, xhigh[12 + x - 4])
 
     for c in range(3):
         for i in range(12):
             g[c, i, 8:16] = source(c, i - 4)
             g[c, i, 0:4] = blank
             g[c, i, 20:24] = blank
-            for side, at in ((ylow, 4), (yhigh, 16)):
-                if c < 2:
-                    g[c, i, at : at + 4] = side[i, 4 * c : 4 * c + 4]
-                else:
-                    g[c, i, at : at + 4] = side[13 + i, 0:4]
+            for side, at, step in ((ylow, 4, 1), (yhigh, 16, -1)):
+                rows = side[i, 4 * c : 4 * c + 4] if c < 2 else side[13 + i, 0:4]
+                g[c, i, at : at + 4] = kept("gy", step, rows)
     for j in range(14):
         eta[j, 0:4] = blank
         eta[j, 20:24] = blank
         eta[j, 8:16] = viscosity(j - 5)
-        eta[j, 4:8] = ylow[12 + j, 4:8]
-        eta[j, 3:4] = ylow[26 + j // 8, j % 8 : j % 8 + 1]
-        eta[j, 16:20] = yhigh[12 + j, 4:8]
-        eta[j, 20:21] = yhigh[26 + j // 8, j % 8 : j % 8 + 1]
-
-    coefficients(eta, cx, cf, 12, 0.25)
+        eta[j, 4:8] = kept("gy", 1, ylow[12 + j, 4:8])
+        eta[j, 3:4] = kept("gy", 1, ylow[26 + j // 8, j % 8 : j % 8 + 1])
+        eta[j, 16:20] = kept("gy", -1, yhigh[12 + j, 4:8])
+        eta[j, 20:21] = kept("gy", -1, yhigh[26 + j // 8, j % 8 : j % 8 + 1])
+
+    coefficients(eta, cx, cf, 12, 0.25, U1)
 
     plane = jnp.zeros((24, nz), F32)
     for c in range(3):
@@ -337,28 +349,25 @@
             va[c, i] = plane
             v1[c, i] = plane
 
-    def start(i, _):
+    def start(i):
         for c in range(3):
             va[c, i + 1] = cf[EI, i] * g[c, i]
-        return 0
-
-    lax.fori_loop(0, 12, start, 0)
-    sweep(va, 5, g, 4, cx, cf, 4, v1, 5, -4, 8)
-
-    def down_pair(k, _):
+
+    planes(12, start, U1)
+    sweep(va, 5, g, 4, cx, cf, 4, v1, 5, -4, 8, U1)
+
+    def down_pair(k):
         for c in range(3):
             x = 2 * k
             total = residual(v1, 1, g, 0, cx, cf, 0, c, x) + residual(v1, 1, g, 0, cx, cf, 0, c, x + 1)
             put_plane(pairs, c * 6 + k, total)
-        return 0
-
-    lax.fori_loop(0, 6, down_pair, 0)
-
-    def eta_pair(k, _):
+
+    planes(6, down_pair, U1)
+
+    def eta_pair(k):
         put_plane(pairs, 18 + k, eta[2 * k + 1] + eta[2 * k + 2])
-        return 0
-
-    lax.fori_loop(0, 6, eta_pair, 0)
+
+    planes(6, eta_pair, U1)
     for k in range(6):
         for c in range(3):
             row_pairs(pairs, c * 6 + k, 8, 4, rest, 16 * k + 4 * c)
@@ -384,16 +393,20 @@
     strip[0, 0:12] = jnp.zeros((12, own.shape[-1]), F32)
     strip[17, 0:12] = jnp.zeros((12, own.shape[-1]), F32)
     for t in range(2):
-        strip[1 + t, 0:12] = low3[t, 0:12]
-        strip[t, 12:16] = low3[t, 12:16]
-        strip[15 + t, 0:12] = high3[t, 0:12]
-        strip[16 + t, 12:16] = high3[t, 12:16]
+        rows = kept("gx", 3, low3[t])
+        strip[1 + t, 0:12] = rows[0:12]
+        strip[t, 12:16] = rows[12:16]
+        rows = kept("gx", -3, high3[t])
+        strip[15 + t, 0:12] = rows[0:12]
+        strip[16 + t, 12:16] = rows[12:16]
     for t in range(4):
-        strip[3 + t, 0:12] = low2[t, 0:12]
-        strip[2 + t, 12:16] = low2[t, 12:16]
+        rows = kept("gx", 2, low2[t])
+        strip[3 + t, 0:12] = rows[0:12]
+        strip[2 + t, 12:16] = rows[12:16]
         strip[7 + t, 0:12] = own[1 + t, 0:12]
-        strip[11 + t, 0:12] = high2[t, 0:12]
-        strip[12 + t, 12:16] = high2[t, 12:16]
+        rows = kept("gx", -2, high2[t])
+        strip[11 + t, 0:12] = rows[0:12]
+        strip[12 + t, 12:16] = rows[12:16]
     for t in range(6):
         strip[6 + t, 12:16] = own[t, 12:16]
     for plane, outer, mine in ((6, 5, 0), (11, 12, 5)):
@@ -409,26 +422,28 @@
 ):
     nz2, nz1, nz0 = mid.shape[-1], v1.shape[-1], v0.shape[-1]
     blank = jnp.zeros((4, nz2), F32)
+    sides = ((ym2, 2), (ym1, 1), (mid, 0), (yp1, -1), (yp2, -2))
     for j in range(18):
-        for n, side in enumerate((ym2, ym1, mid, yp1, yp2)):
-            eta2[j, 4 * n : 4 * n + 4] = side[j, 12:16]
+        for n, (side, step) in enumerate(sides):
+            rows = kept("gy", step, side[j]) if step else side[j]
+            eta2[j, 4 * n : 4 * n + 4] = rows[12:16]
+            if 1 <= j <= 16:
+                for c in range(3):
+                    g2[c, j - 1, 4 * n : 4 * n + 4] = rows[4 * c : 4 * c + 4]
         eta2[j, 20:24] = blank
-    for i in range(16):
-        for c in range(3):
-            for n, side in enumerate((ym2, ym1, mid, yp1, yp2)):
-                g2[c, i, 4 * n : 4 * n + 4] = side[i + 1, 4 * c : 4 * c + 4]
-            g2[c, i, 20:24] = blank
-    coefficients(eta2, cx2, cf2, 16, 0.0625)
-
-    def start(i, _):
+        if 1 <= j <= 16:
+            for c in range(3):
+                g2[c, j - 1, 20:24] = blank
+    coefficients(eta2, cx2, cf2, 16, 0.0625, U2)
+
+    def start(i):
         for c in range(3):
             va2[c, i] = cf2[EI, i] * g2[c, i]
-        return 0
-
-    lax.fori_loop(0, 16, start, 0)
+
+    planes(16, start, U2)
     source, target = va2, vb2
     for s in range(1, 6):
-        sweep(source, 0, g2, 0, cx2, cf2, 0, target, 0, s, 16 - s)
+        sweep(source, 0, g2, 0, cx2, cf2, 0, target, 0, s, 16 - s, U2)
         source, target = target, source
 
     for c in range(3):
@@ -441,8 +456,8 @@
     for c in range(3):
         for i in range(10):
             va1[c, i] = v1[c, i + 2] + get_plane(wide1, c * 6 + (i - 3) // 2 + 2)
-    sweep(va1, 3, g1, 4, cx1, cf1, 4, vb1, 3, -2, 6)
-    sweep(vb1, 3, g1, 4, cx1, cf1, 4, va1, 3, -1, 5)
+    sweep(va1, 3, g1, 4, cx1, cf1, 4, vb1, 3, -2, 6, U1)
+    sweep(vb1, 3, g1, 4, cx1, cf1, 4, va1, 3, -1, 5, U1)
 
     for c in range(3):
         for k in range(6):
@@ -452,24 +467,22 @@
         block = spread[n * 16 : n * 16 + 12]
         row_copies(wide0, n, block)
 
-    def correct(k, _):
+    def correct(k):
         for c in range(3):
             block = get_plane(wide0, c * 6 + k)
             va0[c, 2 * k] = v0[c, 2 * k] + block
             va0[c, 2 * k + 1] = v0[c, 2 * k + 1] + block
-        return 0
-
-    lax.fori_loop(0, 6, correct, 0)
-    sweep(va0, 2, g0, 3, cx0, cf0, 3, vb0, 2, -1, 9)
-
-    def final(x, _):
+
+    planes(6, correct, U0)
+    sweep(va0, 2, g0, 3, cx0, cf0, 3, vb0, 2, -1, 9, U0)
+
+    def final(x):
         for c in range(3):
             here, total = gather_sum(vb0, c, x + 2, cx0, cf0, x + 3)
             value = (1.0 / 3.0) * here + cf0[EI, x + 3] * (g0[c, x + 3] + total)
             out[c, x] = value[4:20]
-        return 0
-
-    lax.fori_loop(0, 8, final, 0)
+
+    planes(8, final, U0)
 
 
 def call(body, outs, *args, scratch=()):
@@ -486,10 +499,12 @@
 
 def moved(array, axis, step):
     size = lax.axis_size(axis)
-    pairs = [(i, i + step) for i in range(size) if 0 <= i + step < size]
-    if not pairs:
-        return jnp.zeros_like(array)
-    return lax.ppermute(array, axis, pairs)
+    return lax.ppermute(array, axis, [(i, i + step) for i in range(size) if 0 <= i + step < size])
+
+
+def cycled(array, axis, step):
+    size = lax.axis_size(axis)
+    return lax.ppermute(array, axis, [(i, (i + step) % size) for i in range(size)])
 
 
 def per_device(forcing, phase_ids):
@@ -505,20 +520,20 @@
         forcing, phase_ids, xlow, xhigh, ylow, yhigh,
         scratch=[(16, 24, z0), (3, 14, 24, z0), lane_blocks(18, z0), (144, z0)],
     )
-    xlow, xhigh = moved(up, "gx", 1), moved(down, "gx", -1)
+    xlow, xhigh = cycled(up, "gx", 1), cycled(down, "gx", -1)
     up, down = call(pack_middle_y, [(28, 8, z1)] * 2, f1, eta1, xlow, xhigh)
-    ylow, yhigh = moved(up, "gy", 1), moved(down, "gy", -1)
+    ylow, yhigh = cycled(up, "gy", 1), cycled(down, "gy", -1)
     v1, g1, cx1, cf1, own, up, down, far_up, far_down = call(
         middle_down,
         [(3, 14, 24, z1), (3, 12, 24, z1), (13, 24, z1), (6, 12, 24, z1), (6, 16, z2), (4, 16, z2), (4, 16, z2), (2, 16, z2), (2, 16, z2)],
         f1, eta1, xlow, xhigh, ylow, yhigh,
         scratch=[(14, 24, z1), (3, 14, 24, z1), lane_blocks(24, z1), (96, z1)],
     )
-    low2, high2 = moved(up, "gx", 2), moved(down, "gx", -2)
-    low3, high3 = moved(far_up, "gx", 3), moved(far_down, "gx", -3)
+    low2, high2 = cycled(up, "gx", 2), cycled(down, "gx", -2)
+    low3, high3 = cycled(far_up, "gx", 3), cycled(far_down, "gx", -3)
     (strip,) = call(pack_coarse_y, [(18, 16, z2)], own, low2, low3, high2, high3)
-    ym1, yp1 = moved(strip, "gy", 1), moved(strip, "gy", -1)
-    ym2, yp2 = moved(strip, "gy", 2), moved(strip, "gy", -2)
+    ym1, yp1 = cycled(strip, "gy", 1), cycled(strip, "gy", -1)
+    ym2, yp2 = cycled(strip, "gy", 2), cycled(strip, "gy", -2)
     (velocity,) = call(
         ascend,
         [forcing.shape],

time: 112 us -> 87.3 us (0.78)
  starting transfers between devices: 48.3 us -> 35.1 us
  Pallas kernels: 23.5 us -> 14.9 us
  waiting for transfers between devices: 36.8 us -> 33.4 us
    ppermute x16, starting transfers between devices: 48.3 us -> 35.1 us  [the longest x12 22.8 us: cycled(): lax.ppermute(array, axis, [(i, (i + step) % size) for i in range(size)])]
    pallas_call x7, Pallas kernels: 23.5 us -> 14.9 us  [call(): pl.pallas_call(body, out_shape=[jax.ShapeDtypeStruct(shape, F32) for shap...]
    ppermute x16, waiting for transfers between devices: 36.8 us -> 33.4 us  [the longest x4 18.5 us: moved(): lax.ppermute(array, axis, [(i, i + step) for i in range(size) if 0 <= i +...]
  transfers between devices with their start and end apart: 16 -> 16, of which waited for: 10 -> 11; matrix products, arithmetic and copies ran while one was open for 0% -> 0% of each run, Pallas kernels for 0% -> 0%
where the time goes in v2:
time: 87.3 us; the launch traced here: 85.6 us
  starting transfers between devices  35.1 us (40%)
  waiting for transfers between devices  33.4 us (38%)
  Pallas kernels  14.9 us (17%)
  local copies, waits for them, and re-layouts  2.08 us (2%)
    ppermute x12, starting transfers between devices, cycled(): lax.ppermute(array, axis, [(i, (i + step) % size) for i in range(size)])  22.8 us
    ppermute x4, waiting for transfers between devices, moved(): lax.ppermute(array, axis, [(i, i + step) for i in range(size) if 0 <= i +...  18.5 us
    ppermute x12, waiting for transfers between devices, cycled(): lax.ppermute(array, axis, [(i, (i + step) % size) for i in range(size)])  14.9 us
    pallas_call x7, Pallas kernels, call(): pl.pallas_call(body, out_shape=[jax.ShapeDtypeStruct(shape, F32) for shap...  14.9 us
    ppermute x4, starting transfers between devices, moved(): lax.ppermute(array, axis, [(i, i + step) for i in range(size) if 0 <= i +...  12.4 us
    unnamed x4, local copies, waits for them, and re-layouts  2.08 us
  transfers between devices with their start and end apart: 16, of which 11 were waited for; matrix products, arithmetic and copies ran while one was open for 0% of the time, Pallas kernels for 0%

profile of v2, /device:TPU:1, one launch (start us, length us, event | category | flops | bytes accessed | tf_op | source)
XLA Modules:
  0.0 85.6 jit_solution(17809985005355911060)
XLA Ops:
  0.0 0.0 copy-start
  0.0 1.1 %copy-done = f32[3,8,16,512]{3,2,1,0:T(8,128)S(1)} copy-done((f32[3,8,16,512]{3,2,1,0:T(8,128)S(1)}, f32[3,8,16,512]{3,2,1,0:T(8,128)}, u32[]{:S(2)}) %copy-start) | copy-done | bytes 786456
  1.1 0.0 copy-start.1
  1.1 0.9 %copy-done.1 = s32[8,16,512]{2,1,0:T(8,128)S(1)} copy-done((s32[8,16,512]{2,1,0:T(8,128)S(1)}, s32[8,16,512]{2,1,0:T(8,128)}, u32[]{:S(2)}) %copy-start.1) | copy-done | bytes 262168
  2.1 0.1 shard_map.28
  2.2 4.4 %collective-permute-start = (f32[13,16,512]{2,1,0:T(8,128)S(1)}, f32[13,16,512]{2,1,0:T(8,128)S(1)}, u32[]{:S(2)}, u32[]{:S(2)}) collective-permute-start(f32[13,16,512]{2,1,0:T(8,128)S(1)} %get-tuple-element.28), channel_id=1, source_target_pairs={{0,8},{8,16},{16,24},{24,32},{32,40},{40,48},{48,56},{56,64},{64,7... | collective-permute-start | bytes 1277960 | tf_op jit(solution)/shard_map/ppermute | solution.py:502
  6.6 1.3 %collective-permute-start.1 = (f32[13,16,512]{2,1,0:T(8,128)S(1)}, f32[13,16,512]{2,1,0:T(8,128)S(1)}, u32[]{:S(2)}, u32[]{:S(2)}) collective-permute-start(f32[13,16,512]{2,1,0:T(8,128)S(1)} %get-tuple-element.29), channel_id=1, source_target_pairs={{8,0},{16,8},{24,16},{32,24},{40,32},{48,40},{56,48},{64,56},{72,6... | collective-permute-start | bytes 1277960 | tf_op jit(solution)/shard_map/ppermute | solution.py:502
  7.9 7.1 %collective-permute-done.low.xlow = f32[13,16,512]{2,1,0:T(8,128)S(1)} collective-permute-done((f32[13,16,512]{2,1,0:T(8,128)S(1)}, f32[13,16,512]{2,1,0:T(8,128)S(1)}, u32[]{:S(2)}, u32[]{:S(2)}) %collective-permute-start) | collective-permute-done | bytes 426016 | tf_op jit(solution)/shard_map/ppermute | solution.py:502
  15.0 4.2 %collective-permute-done.1.high.xhigh = f32[13,16,512]{2,1,0:T(8,128)S(1)} collective-permute-done((f32[13,16,512]{2,1,0:T(8,128)S(1)}, f32[13,16,512]{2,1,0:T(8,128)S(1)}, u32[]{:S(2)}, u32[]{:S(2)}) %collective-permute-start.1) | collective-permute-done | bytes 426016 | tf_op jit(solution)/shard_map/ppermute | solution.py:502
  19.2 0.2 shard_map.29
  19.4 4.8 %collective-permute-start.2 = (f32[24,8,512]{2,1,0:T(8,128)S(1)}, f32[24,8,512]{2,1,0:T(8,128)S(1)}, u32[]{:S(2)}, u32[]{:S(2)}) collective-permute-start(f32[24,8,512]{2,1,0:T(8,128)S(1)} %get-tuple-element.30), channel_id=1, source_target_pairs={{0,1},{1,2},{2,3},{3,4},{4,5},{5,6},{6,7},{8,9},{9,10},{10,11},{11... | collective-permute-start | bytes 1179656 | tf_op jit(solution)/shard_map/ppermute | solution.py:502
  24.2 1.9 %collective-permute-start.3 = (f32[24,8,512]{2,1,0:T(8,128)S(1)}, f32[24,8,512]{2,1,0:T(8,128)S(1)}, u32[]{:S(2)}, u32[]{:S(2)}) collective-permute-start(f32[24,8,512]{2,1,0:T(8,128)S(1)} %get-tuple-element.31), channel_id=1, source_target_pairs={{1,0},{2,1},{3,2},{4,3},{5,4},{6,5},{7,6},{9,8},{10,9},{11,10},{12... | collective-permute-start | bytes 1179656 | tf_op jit(solution)/shard_map/ppermute | solution.py:502
  26.1 2.8 %collective-permute-done.2.ylow = f32[24,8,512]{2,1,0:T(8,128)S(1)} collective-permute-done((f32[24,8,512]{2,1,0:T(8,128)S(1)}, f32[24,8,512]{2,1,0:T(8,128)S(1)}, u32[]{:S(2)}, u32[]{:S(2)}) %collective-permute-start.2) | collective-permute-done | bytes 393248 | tf_op jit(solution)/shard_map/ppermute | solution.py:502
  28.9 4.4 %collective-permute-done.3.yhigh = f32[24,8,512]{2,1,0:T(8,128)S(1)} collective-permute-done((f32[24,8,512]{2,1,0:T(8,128)S(1)}, f32[24,8,512]{2,1,0:T(8,128)S(1)}, u32[]{:S(2)}, u32[]{:S(2)}) %collective-permute-start.3) | collective-permute-done | bytes 393248 | tf_op jit(solution)/shard_map/ppermute | solution.py:502
  33.3 5.0 %shard_map.30 = (f32[3,12,24,512]{3,2,1,0:T(8,128)S(1)}, f32[3,14,24,512]{3,2,1,0:T(8,128)S(1)}, f32[15,24,512]{2,1,0:T(8,128)S(1)}, f32[6,14,24,512]{3,2,1,0:T(...) custom-call(f32[3,8,16,512]{3,2,1,0:T(8,128)S(1)} %copy-done, ...), custom_call_target="tpu_custom_call" | custom-call | tf_op jit(solution)/shard_map/pallas_call | solution.py:490
  38.3 1.7 %collective-permute-start.4 = (f32[17,8,256]{2,1,0:T(8,128)S(1)}, f32[17,8,256]{2,1,0:T(8,128)S(1)}, u32[]{:S(2)}, u32[]{:S(2)}) collective-permute-start(f32[17,8,256]{2,1,0:T(8,128)S(1)} %get-tuple-element.34), channel_id=1, source_target_pairs={{0,8},{8,16},{16,24},{24,32},{32,40},{40,48},{48,56},{56,64},{64,7... | collective-permute-start | bytes 417800 | tf_op jit(solution)/shard_map/ppermute | solution.py:507
  40.0 3.7 %collective-permute-start.5 = (f32[17,8,256]{2,1,0:T(8,128)S(1)}, f32[17,8,256]{2,1,0:T(8,128)S(1)}, u32[]{:S(2)}, u32[]{:S(2)}) collective-permute-start(f32[17,8,256]{2,1,0:T(8,128)S(1)} %get-tuple-element.35), channel_id=1, source_target_pairs={{0,248},{8,0},{16,8},{24,16},{32,24},{40,32},{48,40},{56,48},{64,5... | collective-permute-start | bytes 417800 | tf_op jit(solution)/shard_map/ppermute | solution.py:507
  43.7 2.4 %collective-permute-done.4.low.xlow = f32[17,8,256]{2,1,0:T(8,128)S(1)} collective-permute-done((f32[17,8,256]{2,1,0:T(8,128)S(1)}, f32[17,8,256]{2,1,0:T(8,128)S(1)}, u32[]{:S(2)}, u32[]{:S(2)}) %collective-permute-start.4) | collective-permute-done | bytes 139296 | tf_op jit(solution)/shard_map/ppermute | solution.py:507
  46.1 0.0 collective-permute-done.5.high.xhigh
  46.1 0.1 shard_map.31
  46.1 1.0 %collective-permute-start.6 = (f32[28,8,256]{2,1,0:T(8,128)S(1)}, f32[28,8,256]{2,1,0:T(8,128)S(1)}, u32[]{:S(2)}, u32[]{:S(2)}) collective-permute-start(f32[28,8,256]{2,1,0:T(8,128)S(1)} %get-tuple-element.36), channel_id=1, source_target_pairs={{0,1},{1,2},{2,3},{3,4},{4,5},{5,6},{6,7},{7,0},{8,9},{9,10},{10,1... | collective-permute-start | bytes 688136 | tf_op jit(solution)/shard_map/ppermute | solution.py:507
  47.2 0.0 collective-permute-start.7
  47.2 3.0 %collective-permute-done.6.ylow = f32[28,8,256]{2,1,0:T(8,128)S(1)} collective-permute-done((f32[28,8,256]{2,1,0:T(8,128)S(1)}, f32[28,8,256]{2,1,0:T(8,128)S(1)}, u32[]{:S(2)}, u32[]{:S(2)}) %collective-permute-start.6) | collective-permute-done | bytes 229408 | tf_op jit(solution)/shard_map/ppermute | solution.py:507
  50.1 2.5 %collective-permute-done.7.yhigh = f32[28,8,256]{2,1,0:T(8,128)S(1)} collective-permute-done((f32[28,8,256]{2,1,0:T(8,128)S(1)}, f32[28,8,256]{2,1,0:T(8,128)S(1)}, u32[]{:S(2)}, u32[]{:S(2)}) %collective-permute-start.7) | collective-permute-done | bytes 229408 | tf_op jit(solution)/shard_map/ppermute | solution.py:507
  52.6 2.2 %shard_map.32 = (f32[3,14,24,256]{3,2,1,0:T(8,128)S(1)}, f32[3,12,24,256]{3,2,1,0:T(8,128)S(1)}, f32[13,24,256]{2,1,0:T(8,128)S(1)}, f32[6,12,24,256]{3,2,1,0:T(...) custom-call(f32[3,4,8,256]{3,2,1,0:T(8,128)S(1)} %get-tuple-element., ...), custom_call_target="tpu_custom_call" | custom-call | tf_op jit(solution)/shard_map/pallas_call | solution.py:490
  54.8 4.4 %collective-permute-start.8 = (f32[4,16,128]{2,1,0:T(8,128)S(1)}, f32[4,16,128]{2,1,0:T(8,128)S(1)}, u32[]{:S(2)}, u32[]{:S(2)}) collective-permute-start(f32[4,16,128]{2,1,0:T(8,128)S(1)} %get-tuple-element.39), channel_id=1, source_target_pairs={{0,16},{8,24},{16,32},{24,40},{32,48},{40,56},{48,64},{56,72},{64,... | collective-permute-start | bytes 98312 | tf_op jit(solution)/shard_map/ppermute | solution.py:507
  59.2 1.4 %collective-permute-start.10 = (f32[4,16,128]{2,1,0:T(8,128)S(1)}, f32[4,16,128]{2,1,0:T(8,128)S(1)}, u32[]{:S(2)}, u32[]{:S(2)}) collective-permute-start(f32[4,16,128]{2,1,0:T(8,128)S(1)} %get-tuple-element.41), channel_id=1, source_target_pairs={{0,240},{8,248},{16,0},{24,8},{32,16},{40,24},{48,32},{56,40},{64,... | collective-permute-start | bytes 98312 | tf_op jit(solution)/shard_map/ppermute | solution.py:507
  60.6 1.4 %collective-permute-start.9 = (f32[2,16,128]{2,1,0:T(8,128)S(1)}, f32[2,16,128]{2,1,0:T(8,128)S(1)}, u32[]{:S(2)}, u32[]{:S(2)}) collective-permute-start(f32[2,16,128]{2,1,0:T(8,128)S(1)} %get-tuple-element.40), channel_id=1, source_target_pairs={{0,24},{8,32},{16,40},{24,48},{32,56},{40,64},{48,72},{56,80},{64,... | collective-permute-start | bytes 49160 | tf_op jit(solution)/shard_map/ppermute | solution.py:507
  62.0 5.2 %collective-permute-start.11 = (f32[2,16,128]{2,1,0:T(8,128)S(1)}, f32[2,16,128]{2,1,0:T(8,128)S(1)}, u32[]{:S(2)}, u32[]{:S(2)}) collective-permute-start(f32[2,16,128]{2,1,0:T(8,128)S(1)} %get-tuple-element.42), channel_id=1, source_target_pairs={{0,232},{8,240},{16,248},{24,0},{32,8},{40,16},{48,24},{56,32},{64... | collective-permute-start | bytes 49160 | tf_op jit(solution)/shard_map/ppermute | solution.py:507
  67.2 1.1 %collective-permute-done.9.low3 = f32[2,16,128]{2,1,0:T(8,128)S(1)} collective-permute-done((f32[2,16,128]{2,1,0:T(8,128)S(1)}, f32[2,16,128]{2,1,0:T(8,128)S(1)}, u32[]{:S(2)}, u32[]{:S(2)}) %collective-permute-start.9) | collective-permute-done | bytes 16416 | tf_op jit(solution)/shard_map/ppermute | solution.py:507
  68.3 0.0 collective-permute-done.11.high3
  68.3 0.0 collective-permute-done.8.low2
  68.3 0.0 collective-permute-done.10.high2
  68.4 0.4 collective-permute-start.15
  68.8 2.9 %collective-permute-start.14 = (f32[18,16,128]{2,1,0:T(8,128)S(1)}, f32[18,16,128]{2,1,0:T(8,128)S(1)}, u32[]{:S(2)}, u32[]{:S(2)}) collective-permute-start(f32[18,16,128]{2,1,0:T(8,128)S(1)} %shard_map.33.mid), channel_id=1, source_target_pairs={{0,7},{1,0},{2,1},{3,2},{4,3},{5,4},{6,5},{7,6},{8,15},{9,8},{10,9... | collective-permute-start | bytes 442376 | tf_op jit(solution)/shard_map/ppermute | solution.py:507
  71.7 0.0 collective-permute-start.13
  71.7 0.7 collective-permute-start.12
  72.4 1.8 %collective-permute-done.15.yp2 = f32[18,16,128]{2,1,0:T(8,128)S(1)} collective-permute-done((f32[18,16,128]{2,1,0:T(8,128)S(1)}, f32[18,16,128]{2,1,0:T(8,128)S(1)}, u32[]{:S(2)}, u32[]{:S(2)}) %collective-permute-start.15) | collective-permute-done | bytes 147488 | tf_op jit(solution)/shard_map/ppermute | solution.py:507
  74.2 1.6 %collective-permute-done.14.yp1 = f32[18,16,128]{2,1,0:T(8,128)S(1)} collective-permute-done((f32[18,16,128]{2,1,0:T(8,128)S(1)}, f32[18,16,128]{2,1,0:T(8,128)S(1)}, u32[]{:S(2)}, u32[]{:S(2)}) %collective-permute-start.14) | collective-permute-done | bytes 147488 | tf_op jit(solution)/shard_map/ppermute | solution.py:507
  75.8 2.6 %collective-permute-done.13.ym2 = f32[18,16,128]{2,1,0:T(8,128)S(1)} collective-permute-done((f32[18,16,128]{2,1,0:T(8,128)S(1)}, f32[18,16,128]{2,1,0:T(8,128)S(1)}, u32[]{:S(2)}, u32[]{:S(2)}) %collective-permute-start.13) | collective-permute-done | bytes 147488 | tf_op jit(solution)/shard_map/ppermute | solution.py:507
  78.4 0.0 collective-permute-done.12.ym1
  78.4 7.2 %shard_map.34 = f32[3,8,16,512]{3,2,1,0:T(8,128)} custom-call(f32[18,16,128]{2,1,0:T(8,128)S(1)} %shard_map.33.mid, f32[18,16,128]{2,1,0:T(8,128)S(1)} %collective-permute-done.12.ym1, f32[18,16,128]{2,1,0:T(8,128)S(1)} %collective-permute-done.13.ym2, f32[18,16,128]{2,1,0:T(8,128)S(1)} %collective-permute-done.14.yp1, ...), custom_call_target="tpu_custom_call" | custom-call | tf_op jit(solution)/shard_map/pallas_call | solution.py:490
  (1 shorter events, 0.0 us)
Async XLA Ops:
  0.0 1.1 %copy-start = (f32[3,8,16,512]{3,2,1,0:T(8,128)S(1)}, f32[3,8,16,512]{3,2,1,0:T(8,128)}, u32[]{:S(2)}) copy-start(f32[3,8,16,512]{3,2,1,0:T(8,128)} %f.5) | copy-start | bytes 2359300
  1.1 0.9 %copy-start.1 = (s32[8,16,512]{2,1,0:T(8,128)S(1)}, s32[8,16,512]{2,1,0:T(8,128)}, u32[]{:S(2)}) copy-start(s32[8,16,512]{2,1,0:T(8,128)} %ids.5) | copy-start | bytes 786436
  2.2 12.8 %collective-permute-start = (f32[13,16,512]{2,1,0:T(8,128)S(1)}, f32[13,16,512]{2,1,0:T(8,128)S(1)}, u32[]{:S(2)}, u32[]{:S(2)}) collective-permute-start(f32[13,16,512]{2,1,0:T(8,128)S(1)} %get-tuple-element.28), channel_id=1, source_target_pairs={{0,8},{8,16},{16,24},{24,32},{32,40},{40,48},{48,56},{56,64},{64,7... | collective-permute-start | bytes 1277960 | tf_op jit(solution)/shard_map/ppermute | solution.py:502
  6.6 12.6 %collective-permute-start.1 = (f32[13,16,512]{2,1,0:T(8,128)S(1)}, f32[13,16,512]{2,1,0:T(8,128)S(1)}, u32[]{:S(2)}, u32[]{:S(2)}) collective-permute-start(f32[13,16,512]{2,1,0:T(8,128)S(1)} %get-tuple-element.29), channel_id=1, source_target_pairs={{8,0},{16,8},{24,16},{32,24},{40,32},{48,40},{56,48},{64,56},{72,6... | collective-permute-start | bytes 1277960 | tf_op jit(solution)/shard_map/ppermute | solution.py:502
  19.4 9.5 %collective-permute-start.2 = (f32[24,8,512]{2,1,0:T(8,128)S(1)}, f32[24,8,512]{2,1,0:T(8,128)S(1)}, u32[]{:S(2)}, u32[]{:S(2)}) collective-permute-start(f32[24,8,512]{2,1,0:T(8,128)S(1)} %get-tuple-element.30), channel_id=1, source_target_pairs={{0,1},{1,2},{2,3},{3,4},{4,5},{5,6},{6,7},{8,9},{9,10},{10,11},{11... | collective-permute-start | bytes 1179656 | tf_op jit(solution)/shard_map/ppermute | solution.py:502
  24.2 9.1 %collective-permute-start.3 = (f32[24,8,512]{2,1,0:T(8,128)S(1)}, f32[24,8,512]{2,1,0:T(8,128)S(1)}, u32[]{:S(2)}, u32[]{:S(2)}) collective-permute-start(f32[24,8,512]{2,1,0:T(8,128)S(1)} %get-tuple-element.31), channel_id=1, source_target_pairs={{1,0},{2,1},{3,2},{4,3},{5,4},{6,5},{7,6},{9,8},{10,9},{11,10},{12... | collective-permute-start | bytes 1179656 | tf_op jit(solution)/shard_map/ppermute | solution.py:502
  38.3 7.7 %collective-permute-start.4 = (f32[17,8,256]{2,1,0:T(8,128)S(1)}, f32[17,8,256]{2,1,0:T(8,128)S(1)}, u32[]{:S(2)}, u32[]{:S(2)}) collective-permute-start(f32[17,8,256]{2,1,0:T(8,128)S(1)} %get-tuple-element.34), channel_id=1, source_target_pairs={{0,8},{8,16},{16,24},{24,32},{32,40},{40,48},{48,56},{56,64},{64,7... | collective-permute-start | bytes 417800 | tf_op jit(solution)/shard_map/ppermute | solution.py:507
  40.0 6.0 %collective-permute-start.5 = (f32[17,8,256]{2,1,0:T(8,128)S(1)}, f32[17,8,256]{2,1,0:T(8,128)S(1)}, u32[]{:S(2)}, u32[]{:S(2)}) collective-permute-start(f32[17,8,256]{2,1,0:T(8,128)S(1)} %get-tuple-element.35), channel_id=1, source_target_pairs={{0,248},{8,0},{16,8},{24,16},{32,24},{40,32},{48,40},{56,48},{64,5... | collective-permute-start | bytes 417800 | tf_op jit(solution)/shard_map/ppermute | solution.py:507
  46.1 4.0 %collective-permute-start.6 = (f32[28,8,256]{2,1,0:T(8,128)S(1)}, f32[28,8,256]{2,1,0:T(8,128)S(1)}, u32[]{:S(2)}, u32[]{:S(2)}) collective-permute-start(f32[28,8,256]{2,1,0:T(8,128)S(1)} %get-tuple-element.36), channel_id=1, source_target_pairs={{0,1},{1,2},{2,3},{3,4},{4,5},{5,6},{6,7},{7,0},{8,9},{9,10},{10,1... | collective-permute-start | bytes 688136 | tf_op jit(solution)/shard_map/ppermute | solution.py:507
  47.2 5.4 %collective-permute-start.7 = (f32[28,8,256]{2,1,0:T(8,128)S(1)}, f32[28,8,256]{2,1,0:T(8,128)S(1)}, u32[]{:S(2)}, u32[]{:S(2)}) collective-permute-start(f32[28,8,256]{2,1,0:T(8,128)S(1)} %get-tuple-element.37), channel_id=1, source_target_pairs={{0,7},{1,0},{2,1},{3,2},{4,3},{5,4},{6,5},{7,6},{8,15},{9,8},{10,9... | collective-permute-start | bytes 688136 | tf_op jit(solution)/shard_map/ppermute | solution.py:507
  54.8 13.5 %collective-permute-start.8 = (f32[4,16,128]{2,1,0:T(8,128)S(1)}, f32[4,16,128]{2,1,0:T(8,128)S(1)}, u32[]{:S(2)}, u32[]{:S(2)}) collective-permute-start(f32[4,16,128]{2,1,0:T(8,128)S(1)} %get-tuple-element.39), channel_id=1, source_target_pairs={{0,16},{8,24},{16,32},{24,40},{32,48},{40,56},{48,64},{56,72},{64,... | collective-permute-start | bytes 98312 | tf_op jit(solution)/shard_map/ppermute | solution.py:507
  59.2 9.1 %collective-permute-start.10 = (f32[4,16,128]{2,1,0:T(8,128)S(1)}, f32[4,16,128]{2,1,0:T(8,128)S(1)}, u32[]{:S(2)}, u32[]{:S(2)}) collective-permute-start(f32[4,16,128]{2,1,0:T(8,128)S(1)} %get-tuple-element.41), channel_id=1, source_target_pairs={{0,240},{8,248},{16,0},{24,8},{32,16},{40,24},{48,32},{56,40},{64,... | collective-permute-start | bytes 98312 | tf_op jit(solution)/shard_map/ppermute | solution.py:507
  60.6 7.7 %collective-permute-start.9 = (f32[2,16,128]{2,1,0:T(8,128)S(1)}, f32[2,16,128]{2,1,0:T(8,128)S(1)}, u32[]{:S(2)}, u32[]{:S(2)}) collective-permute-start(f32[2,16,128]{2,1,0:T(8,128)S(1)} %get-tuple-element.40), channel_id=1, source_target_pairs={{0,24},{8,32},{16,40},{24,48},{32,56},{40,64},{48,72},{56,80},{64,... | collective-permute-start | bytes 49160 | tf_op jit(solution)/shard_map/ppermute | solution.py:507
  62.0 6.3 %collective-permute-start.11 = (f32[2,16,128]{2,1,0:T(8,128)S(1)}, f32[2,16,128]{2,1,0:T(8,128)S(1)}, u32[]{:S(2)}, u32[]{:S(2)}) collective-permute-start(f32[2,16,128]{2,1,0:T(8,128)S(1)} %get-tuple-element.42), channel_id=1, source_target_pairs={{0,232},{8,240},{16,248},{24,0},{32,8},{40,16},{48,24},{56,32},{64... | collective-permute-start | bytes 49160 | tf_op jit(solution)/shard_map/ppermute | solution.py:507
  68.4 5.8 %collective-permute-start.15 = (f32[18,16,128]{2,1,0:T(8,128)S(1)}, f32[18,16,128]{2,1,0:T(8,128)S(1)}, u32[]{:S(2)}, u32[]{:S(2)}) collective-permute-start(f32[18,16,128]{2,1,0:T(8,128)S(1)} %shard_map.33.mid), channel_id=1, source_target_pairs={{0,6},{1,7},{2,0},{3,1},{4,2},{5,3},{6,4},{7,5},{8,14},{9,15},{10,... | collective-permute-start | bytes 442376 | tf_op jit(solution)/shard_map/ppermute | solution.py:507
  68.8 7.0 %collective-permute-start.14 = (f32[18,16,128]{2,1,0:T(8,128)S(1)}, f32[18,16,128]{2,1,0:T(8,128)S(1)}, u32[]{:S(2)}, u32[]{:S(2)}) collective-permute-start(f32[18,16,128]{2,1,0:T(8,128)S(1)} %shard_map.33.mid), channel_id=1, source_target_pairs={{0,7},{1,0},{2,1},{3,2},{4,3},{5,4},{6,5},{7,6},{8,15},{9,8},{10,9... | collective-permute-start | bytes 442376 | tf_op jit(solution)/shard_map/ppermute | solution.py:507
  71.7 6.7 %collective-permute-start.13 = (f32[18,16,128]{2,1,0:T(8,128)S(1)}, f32[18,16,128]{2,1,0:T(8,128)S(1)}, u32[]{:S(2)}, u32[]{:S(2)}) collective-permute-start(f32[18,16,128]{2,1,0:T(8,128)S(1)} %shard_map.33.mid), channel_id=1, source_target_pairs={{0,2},{1,3},{2,4},{3,5},{4,6},{5,7},{6,0},{7,1},{8,10},{9,11},{10,... | collective-permute-start | bytes 442376 | tf_op jit(solution)/shard_map/ppermute | solution.py:507
  71.7 6.7 %collective-permute-start.12 = (f32[18,16,128]{2,1,0:T(8,128)S(1)}, f32[18,16,128]{2,1,0:T(8,128)S(1)}, u32[]{:S(2)}, u32[]{:S(2)}) collective-permute-start(f32[18,16,128]{2,1,0:T(8,128)S(1)} %shard_map.33.mid), channel_id=1, source_target_pairs={{0,1},{1,2},{2,3},{3,4},{4,5},{5,6},{6,7},{7,0},{8,9},{9,10},{10,1... | collective-permute-start | bytes 442376 | tf_op jit(solution)/shard_map/ppermute | solution.py:507

commit v3 on v2

--- a/solution.py
+++ b/solution.py
@@ -141,68 +141,92 @@
     return g[comp, x + go] - cf[DG, x + co] * here + total
 
 
-def pack_fine_x(f, ids, up, down):
+def pack_fine(f, ids, xup, xdown, yup, ydown):
     for c in range(3):
         for k in range(3):
-            up[3 * c + k] = f[c, 5 + k]
-            down[3 * c + k] = f[c, k]
-    for k in range(4):
-        up[9 + k] = materials(ids[4 + k])
-        down[9 + k] = materials(ids[k])
+            xup[3 * c + k] = f[c, 5 + k]
+            xdown[3 * c + k] = f[c, k]
+    for x in range(8):
+        eta = materials(ids[x])
+        if x < 4:
+            xdown[9 + x] = eta
+        else:
+            xup[9 + x - 4] = eta
+        for out, at, eta_at in ((yup, 13, 12), (ydown, 0, 0)):
+            pack_rows(out, x, 8, [f[c, x, at : at + 3] for c in range(3)])
+            put_eta_rows(out, 9, x, eta[eta_at : eta_at + 4])
+
+
+def pack_rows(out, n, spill, rows):
+    out[n, 0:3] = rows[0]
+    out[n, 3:6] = rows[1]
+    out[n, 6:8] = rows[2][0:2]
+    out[spill + n // 8, n % 8 : n % 8 + 1] = rows[2][2:3]
+
+
+def put_eta_rows(out, first, n, rows):
+    at = 4 * (n % 2)
+    out[first + n // 2, at : at + 4] = rows
 
 
 def fine_source(f, low, high, c, x):
     if x < 0:
-        return low[3 * c + x + 3]
+        return kept("gx", 1, low[3 * c + x + 3])
     if x < 8:
         return f[c, x]
-    return high[3 * c + x - 8]
+    return kept("gx", -1, high[3 * c + x - 8])
 
 
 def fine_eta(ids, low, high, x):
     if x < 0:
-        return low[9 + x + 4]
+        return kept("gx", 1, low[9 + x + 4])
     if x < 8:
         return materials(ids[x])
-    return high[9 + x - 8]
-
-
-def pack_fine_y(f, ids, low, high, up, down):
-    for i in range(14):
-        rows = [fine_source(f, low, high, c, i - 3) for c in range(3)]
+    return kept("gx", -1, high[9 + x - 8])
+
+
+def pack_corners(low, high, up, down):
+    for n, x in enumerate((-3, -2, -1, 8, 9, 10)):
+        rows = [fine_source(None, low, high, c, x) for c in range(3)]
         for out, at in ((up, 13), (down, 0)):
-            out[i, 0:3] = rows[0][at : at + 3]
-            out[i, 3:6] = rows[1][at : at + 3]
-            out[i, 6:8] = rows[2][at : at + 2]
-            out[14 + i // 8, i % 8 : i % 8 + 1] = rows[2][at + 2 : at + 3]
+            pack_rows(out, n, 6, [row[at : at + 3] for row in rows])
+    for n, x in enumerate((-4, -3, -2, -1, 8, 9, 10, 11)):
+        eta = fine_eta(None, low, high, x)
+        put_eta_rows(up, 7, n, eta[12:16])
+        put_eta_rows(down, 7, n, eta[0:4])
     for out in (up, down):
-        out[15, 6:8] = jnp.zeros((2, f.shape[-1]), F32)
-    for j in range(16):
-        eta = fine_eta(ids, low, high, j - 4)
-        at = 4 * (j % 2)
-        up[16 + j // 2, at : at + 4] = eta[12:16]
-        down[16 + j // 2, at : at + 4] = eta[0:4]
-
-
-def fine_down(f, ids, xlow, xhigh, ylow, yhigh, v0, g, cx, cf, f1, eta1, up, down, eta, va, pairs, rest):
+        out[6, 6:8] = jnp.zeros((2, low.shape[-1]), F32)
+
+
+def fine_down(f, ids, xlow, xhigh, ylow, yhigh, clow, chigh, v0, g, cx, cf, f1, eta1, up, down, eta, va, pairs, rest):
     nz = f.shape[-1]
     blank = jnp.zeros((1, nz), F32)
-    for c in range(3):
-        for i in range(14):
-            g[c, i, 4:20] = fine_source(f, xlow, xhigh, c, i - 3)
-            for side, at in ((ylow, 1), (yhigh, 20)):
-                if c < 2:
-                    g[c, i, at : at + 3] = side[i, 3 * c : 3 * c + 3]
-                else:
-                    g[c, i, at : at + 2] = side[i, 6:8]
-                    g[c, i, at + 2 : at + 3] = side[14 + i // 8, i % 8 : i % 8 + 1]
+    for i in range(14):
+        x = i - 3
+        for c in range(3):
+            g[c, i, 4:20] = fine_source(f, xlow, xhigh, c, x)
             g[c, i, 0:1] = blank
             g[c, i, 23:24] = blank
+        for own, corner, at, step in ((ylow, clow, 1, 1), (yhigh, chigh, 20, -1)):
+            if 0 <= x < 8:
+                side, n, spill = own, x, 8
+            else:
+                side, n, spill = corner, (i if x < 0 else x - 5), 6
+            tile = kept("gy", step, side[n])
+            g[0, i, at : at + 3] = tile[0:3]
+            g[1, i, at : at + 3] = tile[3:6]
+            g[2, i, at : at + 2] = tile[6:8]
+            g[2, i, at + 2 : at + 3] = kept("gy", step, side[spill, n : n + 1])
     for j in range(16):
-        eta[j, 4:20] = fine_eta(ids, xlow, xhigh, j - 4)
-        at = 4 * (j % 2)
-        eta[j, 0:4] = ylow[16 + j // 2, at : at + 4]
-        eta[j, 20:24] = yhigh[16 + j // 2, at : at + 4]
+        x = j - 4
+        eta[j, 4:20] = fine_eta(ids, xlow, xhigh, x)
+        for own, corner, row, step in ((ylow, clow, 0, 1), (yhigh, chigh, 20, -1)):
+            if 0 <= x < 8:
+                side, n, first = own, x, 9
+            else:
+                side, n, first = corner, (j if x < 0 else x - 4), 7
+            at = 4 * (n % 2)
+            eta[j, row : row + 4] = kept("gy", step, side[first + n // 2, at : at + 4])
 
     coefficients(eta, cx, cf, 14, 1.0, U0)
 
@@ -497,11 +521,6 @@
     )(*args)
 
 
-def moved(array, axis, step):
-    size = lax.axis_size(axis)
-    return lax.ppermute(array, axis, [(i, i + step) for i in range(size) if 0 <= i + step < size])
-
-
 def cycled(array, axis, step):
     size = lax.axis_size(axis)
     return lax.ppermute(array, axis, [(i, (i + step) % size) for i in range(size)])
@@ -510,14 +529,15 @@
 def per_device(forcing, phase_ids):
     z0 = forcing.shape[-1]
     z1, z2 = z0 // 2, z0 // 4
-    up, down = call(pack_fine_x, [(13, 16, z0)] * 2, forcing, phase_ids)
-    xlow, xhigh = moved(up, "gx", 1), moved(down, "gx", -1)
-    up, down = call(pack_fine_y, [(24, 8, z0)] * 2, forcing, phase_ids, xlow, xhigh)
-    ylow, yhigh = moved(up, "gy", 1), moved(down, "gy", -1)
+    xup, xdown, yup, ydown = call(pack_fine, [(13, 16, z0)] * 2 + [(13, 8, z0)] * 2, forcing, phase_ids)
+    xlow, xhigh = cycled(xup, "gx", 1), cycled(xdown, "gx", -1)
+    ylow, yhigh = cycled(yup, "gy", 1), cycled(ydown, "gy", -1)
+    up, down = call(pack_corners, [(11, 8, z0)] * 2, xlow, xhigh)
+    clow, chigh = cycled(up, "gy", 1), cycled(down, "gy", -1)
     v0, g0, cx0, cf0, f1, eta1, up, down = call(
         fine_down,
         [(3, 12, 24, z0), (3, 14, 24, z0), (15, 24, z0), (6, 14, 24, z0), (3, 4, 8, z1), (6, 8, z1), (17, 8, z1), (17, 8, z1)],
-        forcing, phase_ids, xlow, xhigh, ylow, yhigh,
+        forcing, phase_ids, xlow, xhigh, ylow, yhigh, clow, chigh,
         scratch=[(16, 24, z0), (3, 14, 24, z0), lane_blocks(18, z0), (144, z0)],
     )
     xlow, xhigh = cycled(up, "gx", 1), cycled(down, "gx", -1)

time: 87.3 us -> 81.4 us (0.932); the launches traced: 85.6 us -> 81.2 us
  waiting for transfers between devices: 33.4 us -> 27 us
  starting transfers between devices: 35.1 us -> 37.2 us
    ppermute x4 -> x0, waiting for transfers between devices: 18.5 us -> none  [moved(): lax.ppermute(array, axis, [(i, i + step) for i in range(size) if 0 <= i +...]
    ppermute x12 -> x18, starting transfers between devices: 22.8 us -> 37.2 us  [cycled(): lax.ppermute(array, axis, [(i, (i + step) % size) for i in range(size)])]
    ppermute x4 -> x0, starting transfers between devices: 12.4 us -> none  [moved(): lax.ppermute(array, axis, [(i, i + step) for i in range(size) if 0 <= i +...]
    ppermute x12 -> x18, waiting for transfers between devices: 14.9 us -> 27 us  [cycled(): lax.ppermute(array, axis, [(i, (i + step) % size) for i in range(size)])]
    unnamed x4 -> x8, local copies, waits for them, and re-layouts: 2.08 us -> 2.09 us
  transfers between devices with their start and end apart: 16 -> 18, of which waited for: 11 -> 10; matrix products, arithmetic and copies ran while one was open for 0% -> 0% of each run, Pallas kernels for 0% -> 0%
where the time goes in v3:
time: 81.4 us; the launch traced here: 81.2 us
  starting transfers between devices  37.2 us (46%)
  waiting for transfers between devices  27 us (33%)
  Pallas kernels  14.9 us (18%)
  local copies, waits for them, and re-layouts  2.09 us (3%)
    ppermute x18, starting transfers between devices, cycled(): lax.ppermute(array, axis, [(i, (i + step) % size) for i in range(size)])  37.2 us
    ppermute x18, waiting for transfers between devices, cycled(): lax.ppermute(array, axis, [(i, (i + step) % size) for i in range(size)])  27 us
    pallas_call x7, Pallas kernels, call(): pl.pallas_call(body, out_shape=[jax.ShapeDtypeStruct(shape, F32) for shap...  14.9 us
    unnamed x8, local copies, waits for them, and re-layouts  2.09 us
  transfers between devices with their start and end apart: 18, of which 10 were waited for; matrix products, arithmetic and copies ran while one was open for 0% of the time, Pallas kernels for 0%

profile of v3, /device:TPU:1, one launch (start us, length us, event | category | flops | bytes accessed | tf_op | source)
XLA Modules:
  0.0 81.2 jit_solution(14187229320609252574)
XLA Ops:
  0.0 0.0 copy-start
  0.0 1.1 %copy-done = f32[3,8,16,512]{3,2,1,0:T(8,128)S(1)} copy-done((f32[3,8,16,512]{3,2,1,0:T(8,128)S(1)}, f32[3,8,16,512]{3,2,1,0:T(8,128)}, u32[]{:S(2)}) %copy-start) | copy-done | bytes 786456
  1.1 0.0 copy-start.2
  1.1 0.9 %copy-done.2 = s32[8,16,512]{2,1,0:T(8,128)S(1)} copy-done((s32[8,16,512]{2,1,0:T(8,128)S(1)}, s32[8,16,512]{2,1,0:T(8,128)}, u32[]{:S(2)}) %copy-start.2) | copy-done | bytes 262168
  2.1 0.0 copy-start.1
  2.1 0.0 copy-start.3
  2.1 0.2 shard_map.28
  2.3 2.5 %collective-permute-start = (f32[13,16,512]{2,1,0:T(8,128)S(1)}, f32[13,16,512]{2,1,0:T(8,128)S(1)}, u32[]{:S(2)}, u32[]{:S(2)}) collective-permute-start(f32[13,16,512]{2,1,0:T(8,128)S(1)} %get-tuple-element.30), channel_id=1, source_target_pairs={{0,8},{8,16},{16,24},{24,32},{32,40},{40,48},{48,56},{56,64},{64,7... | collective-permute-start | bytes 1277960 | tf_op jit(solution)/shard_map/ppermute | solution.py:526
  4.8 6.2 %collective-permute-start.1 = (f32[13,16,512]{2,1,0:T(8,128)S(1)}, f32[13,16,512]{2,1,0:T(8,128)S(1)}, u32[]{:S(2)}, u32[]{:S(2)}) collective-permute-start(f32[13,16,512]{2,1,0:T(8,128)S(1)} %get-tuple-element.31), channel_id=1, source_target_pairs={{0,248},{8,0},{16,8},{24,16},{32,24},{40,32},{48,40},{56,48},{64,5... | collective-permute-start | bytes 1277960 | tf_op jit(solution)/shard_map/ppermute | solution.py:526
  11.1 2.1 %collective-permute-start.2 = (f32[13,8,512]{2,1,0:T(8,128)S(1)}, f32[13,8,512]{2,1,0:T(8,128)S(1)}, u32[]{:S(2)}, u32[]{:S(2)}) collective-permute-start(f32[13,8,512]{2,1,0:T(8,128)S(1)} %get-tuple-element.32), channel_id=1, source_target_pairs={{0,1},{1,2},{2,3},{3,4},{4,5},{5,6},{6,7},{7,0},{8,9},{9,10},{10,1... | collective-permute-start | bytes 638984 | tf_op jit(solution)/shard_map/ppermute | solution.py:526
  13.2 0.0 collective-permute-start.3
  13.2 7.3 %collective-permute-done.low.xlow = f32[13,16,512]{2,1,0:T(8,128)S(1)} collective-permute-done((f32[13,16,512]{2,1,0:T(8,128)S(1)}, f32[13,16,512]{2,1,0:T(8,128)S(1)}, u32[]{:S(2)}, u32[]{:S(2)}) %collective-permute-start) | collective-permute-done | bytes 426016 | tf_op jit(solution)/shard_map/ppermute | solution.py:526
  20.5 0.0 collective-permute-done.1.high.xhigh
  20.5 0.1 shard_map.29
  20.6 2.4 %collective-permute-start.4 = (f32[11,8,512]{2,1,0:T(8,128)S(1)}, f32[11,8,512]{2,1,0:T(8,128)S(1)}, u32[]{:S(2)}, u32[]{:S(2)}) collective-permute-start(f32[11,8,512]{2,1,0:T(8,128)S(1)} %get-tuple-element.34), channel_id=1, source_target_pairs={{0,1},{1,2},{2,3},{3,4},{4,5},{5,6},{6,7},{7,0},{8,9},{9,10},{10,1... | collective-permute-start | bytes 540680 | tf_op jit(solution)/shard_map/ppermute | solution.py:526
  23.1 0.0 collective-permute-start.5
  23.1 0.0 collective-permute-done.2.ylow
  23.1 0.0 collective-permute-done.3.yhigh
  23.1 2.4 %collective-permute-done.4.clow = f32[11,8,512]{2,1,0:T(8,128)S(1)} collective-permute-done((f32[11,8,512]{2,1,0:T(8,128)S(1)}, f32[11,8,512]{2,1,0:T(8,128)S(1)}, u32[]{:S(2)}, u32[]{:S(2)}) %collective-permute-start.4) | collective-permute-done | bytes 180256 | tf_op jit(solution)/shard_map/ppermute | solution.py:526
  25.5 2.5 %collective-permute-done.5.chigh = f32[11,8,512]{2,1,0:T(8,128)S(1)} collective-permute-done((f32[11,8,512]{2,1,0:T(8,128)S(1)}, f32[11,8,512]{2,1,0:T(8,128)S(1)}, u32[]{:S(2)}, u32[]{:S(2)}) %collective-permute-start.5) | collective-permute-done | bytes 180256 | tf_op jit(solution)/shard_map/ppermute | solution.py:526
  28.0 0.0 copy-done.1
  28.0 0.0 copy-done.3
  28.0 5.0 %shard_map.30 = (f32[3,12,24,512]{3,2,1,0:T(8,128)S(1)}, f32[3,14,24,512]{3,2,1,0:T(8,128)S(1)}, f32[15,24,512]{2,1,0:T(8,128)S(1)}, f32[6,14,24,512]{3,2,1,0:T(...) custom-call(f32[3,8,16,512]{3,2,1,0:T(8,128)S(1)} %copy-done.1, ...), custom_call_target="tpu_custom_call" | custom-call | tf_op jit(solution)/shard_map/pallas_call | solution.py:514
  33.0 0.1 collective-permute-start.6
  33.1 4.9 %collective-permute-start.7 = (f32[17,8,256]{2,1,0:T(8,128)S(1)}, f32[17,8,256]{2,1,0:T(8,128)S(1)}, u32[]{:S(2)}, u32[]{:S(2)}) collective-permute-start(f32[17,8,256]{2,1,0:T(8,128)S(1)} %get-tuple-element.39), channel_id=1, source_target_pairs={{0,248},{8,0},{16,8},{24,16},{32,24},{40,32},{48,40},{56,48},{64,5... | collective-permute-start | bytes 417800 | tf_op jit(solution)/shard_map/ppermute | solution.py:526
  38.0 3.8 %collective-permute-done.6.low.xlow = f32[17,8,256]{2,1,0:T(8,128)S(1)} collective-permute-done((f32[17,8,256]{2,1,0:T(8,128)S(1)}, f32[17,8,256]{2,1,0:T(8,128)S(1)}, u32[]{:S(2)}, u32[]{:S(2)}) %collective-permute-start.6) | collective-permute-done | bytes 139296 | tf_op jit(solution)/shard_map/ppermute | solution.py:526
  41.8 0.0 collective-permute-done.7.high.xhigh
  41.8 0.1 shard_map.31
  41.9 0.4 collective-permute-start.8
  42.3 0.4 collective-permute-start.9
  42.7 2.6 %collective-permute-done.8.ylow = f32[28,8,256]{2,1,0:T(8,128)S(1)} collective-permute-done((f32[28,8,256]{2,1,0:T(8,128)S(1)}, f32[28,8,256]{2,1,0:T(8,128)S(1)}, u32[]{:S(2)}, u32[]{:S(2)}) %collective-permute-start.8) | collective-permute-done | bytes 229408 | tf_op jit(solution)/shard_map/ppermute | solution.py:526
  45.2 2.8 %collective-permute-done.9.yhigh = f32[28,8,256]{2,1,0:T(8,128)S(1)} collective-permute-done((f32[28,8,256]{2,1,0:T(8,128)S(1)}, f32[28,8,256]{2,1,0:T(8,128)S(1)}, u32[]{:S(2)}, u32[]{:S(2)}) %collective-permute-start.9) | collective-permute-done | bytes 229408 | tf_op jit(solution)/shard_map/ppermute | solution.py:526
  48.0 2.2 %shard_map.32 = (f32[3,14,24,256]{3,2,1,0:T(8,128)S(1)}, f32[3,12,24,256]{3,2,1,0:T(8,128)S(1)}, f32[13,24,256]{2,1,0:T(8,128)S(1)}, f32[6,12,24,256]{3,2,1,0:T(...) custom-call(f32[3,4,8,256]{3,2,1,0:T(8,128)S(1)} %get-tuple-element., ...), custom_call_target="tpu_custom_call" | custom-call | tf_op jit(solution)/shard_map/pallas_call | solution.py:514
  50.2 0.1 collective-permute-start.10
  50.3 5.7 %collective-permute-start.12 = (f32[4,16,128]{2,1,0:T(8,128)S(1)}, f32[4,16,128]{2,1,0:T(8,128)S(1)}, u32[]{:S(2)}, u32[]{:S(2)}) collective-permute-start(f32[4,16,128]{2,1,0:T(8,128)S(1)} %get-tuple-element.45), channel_id=1, source_target_pairs={{0,240},{8,248},{16,0},{24,8},{32,16},{40,24},{48,32},{56,40},{64,... | collective-permute-start | bytes 98312 | tf_op jit(solution)/shard_map/ppermute | solution.py:526
  56.0 0.0 collective-permute-start.11
  56.0 6.6 %collective-permute-start.13 = (f32[2,16,128]{2,1,0:T(8,128)S(1)}, f32[2,16,128]{2,1,0:T(8,128)S(1)}, u32[]{:S(2)}, u32[]{:S(2)}) collective-permute-start(f32[2,16,128]{2,1,0:T(8,128)S(1)} %get-tuple-element.46), channel_id=1, source_target_pairs={{0,232},{8,240},{16,248},{24,0},{32,8},{40,16},{48,24},{56,32},{64... | collective-permute-start | bytes 49160 | tf_op jit(solution)/shard_map/ppermute | solution.py:526
  62.6 1.1 %collective-permute-done.11.low3 = f32[2,16,128]{2,1,0:T(8,128)S(1)} collective-permute-done((f32[2,16,128]{2,1,0:T(8,128)S(1)}, f32[2,16,128]{2,1,0:T(8,128)S(1)}, u32[]{:S(2)}, u32[]{:S(2)}) %collective-permute-start.11) | collective-permute-done | bytes 16416 | tf_op jit(solution)/shard_map/ppermute | solution.py:526
  63.7 0.0 collective-permute-done.13.high3
  63.7 0.0 collective-permute-done.10.low2
  63.7 0.0 collective-permute-done.12.high2
  63.8 3.9 %collective-permute-start.17 = (f32[18,16,128]{2,1,0:T(8,128)S(1)}, f32[18,16,128]{2,1,0:T(8,128)S(1)}, u32[]{:S(2)}, u32[]{:S(2)}) collective-permute-start(f32[18,16,128]{2,1,0:T(8,128)S(1)} %shard_map.33.mid), channel_id=1, source_target_pairs={{0,6},{1,7},{2,0},{3,1},{4,2},{5,3},{6,4},{7,5},{8,14},{9,15},{10,... | collective-permute-start | bytes 442376 | tf_op jit(solution)/shard_map/ppermute | solution.py:526
  67.7 0.0 collective-permute-start.16
  67.7 0.9 %collective-permute-start.15 = (f32[18,16,128]{2,1,0:T(8,128)S(1)}, f32[18,16,128]{2,1,0:T(8,128)S(1)}, u32[]{:S(2)}, u32[]{:S(2)}) collective-permute-start(f32[18,16,128]{2,1,0:T(8,128)S(1)} %shard_map.33.mid), channel_id=1, source_target_pairs={{0,2},{1,3},{2,4},{3,5},{4,6},{5,7},{6,0},{7,1},{8,10},{9,11},{10,... | collective-permute-start | bytes 442376 | tf_op jit(solution)/shard_map/ppermute | solution.py:526
  68.6 0.9 %collective-permute-start.14 = (f32[18,16,128]{2,1,0:T(8,128)S(1)}, f32[18,16,128]{2,1,0:T(8,128)S(1)}, u32[]{:S(2)}, u32[]{:S(2)}) collective-permute-start(f32[18,16,128]{2,1,0:T(8,128)S(1)} %shard_map.33.mid), channel_id=1, source_target_pairs={{0,1},{1,2},{2,3},{3,4},{4,5},{5,6},{6,7},{7,0},{8,9},{9,10},{10,1... | collective-permute-start | bytes 442376 | tf_op jit(solution)/shard_map/ppermute | solution.py:526
  69.5 1.9 %collective-permute-done.17.yp2 = f32[18,16,128]{2,1,0:T(8,128)S(1)} collective-permute-done((f32[18,16,128]{2,1,0:T(8,128)S(1)}, f32[18,16,128]{2,1,0:T(8,128)S(1)}, u32[]{:S(2)}, u32[]{:S(2)}) %collective-permute-start.17) | collective-permute-done | bytes 147488 | tf_op jit(solution)/shard_map/ppermute | solution.py:526
  71.4 1.8 %collective-permute-done.16.yp1 = f32[18,16,128]{2,1,0:T(8,128)S(1)} collective-permute-done((f32[18,16,128]{2,1,0:T(8,128)S(1)}, f32[18,16,128]{2,1,0:T(8,128)S(1)}, u32[]{:S(2)}, u32[]{:S(2)}) %collective-permute-start.16) | collective-permute-done | bytes 147488 | tf_op jit(solution)/shard_map/ppermute | solution.py:526
  73.2 0.7 collective-permute-done.15.ym2
  73.9 0.0 collective-permute-done.14.ym1
  73.9 7.2 %shard_map.34 = f32[3,8,16,512]{3,2,1,0:T(8,128)} custom-call(f32[18,16,128]{2,1,0:T(8,128)S(1)} %shard_map.33.mid, f32[18,16,128]{2,1,0:T(8,128)S(1)} %collective-permute-done.14.ym1, f32[18,16,128]{2,1,0:T(8,128)S(1)} %collective-permute-done.15.ym2, f32[18,16,128]{2,1,0:T(8,128)S(1)} %collective-permute-done.16.yp1, ...), custom_call_target="tpu_custom_call" | custom-call | tf_op jit(solution)/shard_map/pallas_call | solution.py:514
  (1 shorter events, 0.0 us)
Async XLA Ops:
  0.0 1.1 %copy-start = (f32[3,8,16,512]{3,2,1,0:T(8,128)S(1)}, f32[3,8,16,512]{3,2,1,0:T(8,128)}, u32[]{:S(2)}) copy-start(f32[3,8,16,512]{3,2,1,0:T(8,128)} %f.3) | copy-start | bytes 2359300
  1.1 0.9 %copy-start.2 = (s32[8,16,512]{2,1,0:T(8,128)S(1)}, s32[8,16,512]{2,1,0:T(8,128)}, u32[]{:S(2)}) copy-start(s32[8,16,512]{2,1,0:T(8,128)} %ids.3) | copy-start | bytes 786436
  2.1 25.9 %copy-start.1 = (f32[3,8,16,512]{3,2,1,0:T(8,128)S(1)}, f32[3,8,16,512]{3,2,1,0:T(8,128)}, u32[]{:S(2)}) copy-start(f32[3,8,16,512]{3,2,1,0:T(8,128)} %f.3) | copy-start | bytes 2359300
  2.1 25.9 %copy-start.3 = (s32[8,16,512]{2,1,0:T(8,128)S(1)}, s32[8,16,512]{2,1,0:T(8,128)}, u32[]{:S(2)}) copy-start(s32[8,16,512]{2,1,0:T(8,128)} %ids.3) | copy-start | bytes 786436
  2.3 18.2 %collective-permute-start = (f32[13,16,512]{2,1,0:T(8,128)S(1)}, f32[13,16,512]{2,1,0:T(8,128)S(1)}, u32[]{:S(2)}, u32[]{:S(2)}) collective-permute-start(f32[13,16,512]{2,1,0:T(8,128)S(1)} %get-tuple-element.30), channel_id=1, source_target_pairs={{0,8},{8,16},{16,24},{24,32},{32,40},{40,48},{48,56},{56,64},{64,7... | collective-permute-start | bytes 1277960 | tf_op jit(solution)/shard_map/ppermute | solution.py:526
  4.8 15.7 %collective-permute-start.1 = (f32[13,16,512]{2,1,0:T(8,128)S(1)}, f32[13,16,512]{2,1,0:T(8,128)S(1)}, u32[]{:S(2)}, u32[]{:S(2)}) collective-permute-start(f32[13,16,512]{2,1,0:T(8,128)S(1)} %get-tuple-element.31), channel_id=1, source_target_pairs={{0,248},{8,0},{16,8},{24,16},{32,24},{40,32},{48,40},{56,48},{64,5... | collective-permute-start | bytes 1277960 | tf_op jit(solution)/shard_map/ppermute | solution.py:526
  11.1 12.0 %collective-permute-start.2 = (f32[13,8,512]{2,1,0:T(8,128)S(1)}, f32[13,8,512]{2,1,0:T(8,128)S(1)}, u32[]{:S(2)}, u32[]{:S(2)}) collective-permute-start(f32[13,8,512]{2,1,0:T(8,128)S(1)} %get-tuple-element.32), channel_id=1, source_target_pairs={{0,1},{1,2},{2,3},{3,4},{4,5},{5,6},{6,7},{7,0},{8,9},{9,10},{10,1... | collective-permute-start | bytes 638984 | tf_op jit(solution)/shard_map/ppermute | solution.py:526
  13.2 9.9 %collective-permute-start.3 = (f32[13,8,512]{2,1,0:T(8,128)S(1)}, f32[13,8,512]{2,1,0:T(8,128)S(1)}, u32[]{:S(2)}, u32[]{:S(2)}) collective-permute-start(f32[13,8,512]{2,1,0:T(8,128)S(1)} %get-tuple-element.33), channel_id=1, source_target_pairs={{0,7},{1,0},{2,1},{3,2},{4,3},{5,4},{6,5},{7,6},{8,15},{9,8},{10,9... | collective-permute-start | bytes 638984 | tf_op jit(solution)/shard_map/ppermute | solution.py:526
  20.6 4.9 %collective-permute-start.4 = (f32[11,8,512]{2,1,0:T(8,128)S(1)}, f32[11,8,512]{2,1,0:T(8,128)S(1)}, u32[]{:S(2)}, u32[]{:S(2)}) collective-permute-start(f32[11,8,512]{2,1,0:T(8,128)S(1)} %get-tuple-element.34), channel_id=1, source_target_pairs={{0,1},{1,2},{2,3},{3,4},{4,5},{5,6},{6,7},{7,0},{8,9},{9,10},{10,1... | collective-permute-start | bytes 540680 | tf_op jit(solution)/shard_map/ppermute | solution.py:526
  23.1 4.9 %collective-permute-start.5 = (f32[11,8,512]{2,1,0:T(8,128)S(1)}, f32[11,8,512]{2,1,0:T(8,128)S(1)}, u32[]{:S(2)}, u32[]{:S(2)}) collective-permute-start(f32[11,8,512]{2,1,0:T(8,128)S(1)} %get-tuple-element.35), channel_id=1, source_target_pairs={{0,7},{1,0},{2,1},{3,2},{4,3},{5,4},{6,5},{7,6},{8,15},{9,8},{10,9... | collective-permute-start | bytes 540680 | tf_op jit(solution)/shard_map/ppermute | solution.py:526
  33.0 8.8 %collective-permute-start.6 = (f32[17,8,256]{2,1,0:T(8,128)S(1)}, f32[17,8,256]{2,1,0:T(8,128)S(1)}, u32[]{:S(2)}, u32[]{:S(2)}) collective-permute-start(f32[17,8,256]{2,1,0:T(8,128)S(1)} %get-tuple-element.38), channel_id=1, source_target_pairs={{0,8},{8,16},{16,24},{24,32},{32,40},{40,48},{48,56},{56,64},{64,7... | collective-permute-start | bytes 417800 | tf_op jit(solution)/shard_map/ppermute | solution.py:526
  33.1 8.7 %collective-permute-start.7 = (f32[17,8,256]{2,1,0:T(8,128)S(1)}, f32[17,8,256]{2,1,0:T(8,128)S(1)}, u32[]{:S(2)}, u32[]{:S(2)}) collective-permute-start(f32[17,8,256]{2,1,0:T(8,128)S(1)} %get-tuple-element.39), channel_id=1, source_target_pairs={{0,248},{8,0},{16,8},{24,16},{32,24},{40,32},{48,40},{56,48},{64,5... | collective-permute-start | bytes 417800 | tf_op jit(solution)/shard_map/ppermute | solution.py:526
  41.9 3.3 %collective-permute-start.8 = (f32[28,8,256]{2,1,0:T(8,128)S(1)}, f32[28,8,256]{2,1,0:T(8,128)S(1)}, u32[]{:S(2)}, u32[]{:S(2)}) collective-permute-start(f32[28,8,256]{2,1,0:T(8,128)S(1)} %get-tuple-element.40), channel_id=1, source_target_pairs={{0,1},{1,2},{2,3},{3,4},{4,5},{5,6},{6,7},{7,0},{8,9},{9,10},{10,1... | collective-permute-start | bytes 688136 | tf_op jit(solution)/shard_map/ppermute | solution.py:526
  42.3 5.7 %collective-permute-start.9 = (f32[28,8,256]{2,1,0:T(8,128)S(1)}, f32[28,8,256]{2,1,0:T(8,128)S(1)}, u32[]{:S(2)}, u32[]{:S(2)}) collective-permute-start(f32[28,8,256]{2,1,0:T(8,128)S(1)} %get-tuple-element.41), channel_id=1, source_target_pairs={{0,7},{1,0},{2,1},{3,2},{4,3},{5,4},{6,5},{7,6},{8,15},{9,8},{10,9... | collective-permute-start | bytes 688136 | tf_op jit(solution)/shard_map/ppermute | solution.py:526
  50.2 13.5 %collective-permute-start.10 = (f32[4,16,128]{2,1,0:T(8,128)S(1)}, f32[4,16,128]{2,1,0:T(8,128)S(1)}, u32[]{:S(2)}, u32[]{:S(2)}) collective-permute-start(f32[4,16,128]{2,1,0:T(8,128)S(1)} %get-tuple-element.43), channel_id=1, source_target_pairs={{0,16},{8,24},{16,32},{24,40},{32,48},{40,56},{48,64},{56,72},{64,... | collective-permute-start | bytes 98312 | tf_op jit(solution)/shard_map/ppermute | solution.py:526
  50.3 13.4 %collective-permute-start.12 = (f32[4,16,128]{2,1,0:T(8,128)S(1)}, f32[4,16,128]{2,1,0:T(8,128)S(1)}, u32[]{:S(2)}, u32[]{:S(2)}) collective-permute-start(f32[4,16,128]{2,1,0:T(8,128)S(1)} %get-tuple-element.45), channel_id=1, source_target_pairs={{0,240},{8,248},{16,0},{24,8},{32,16},{40,24},{48,32},{56,40},{64,... | collective-permute-start | bytes 98312 | tf_op jit(solution)/shard_map/ppermute | solution.py:526
  56.0 7.7 %collective-permute-start.11 = (f32[2,16,128]{2,1,0:T(8,128)S(1)}, f32[2,16,128]{2,1,0:T(8,128)S(1)}, u32[]{:S(2)}, u32[]{:S(2)}) collective-permute-start(f32[2,16,128]{2,1,0:T(8,128)S(1)} %get-tuple-element.44), channel_id=1, source_target_pairs={{0,24},{8,32},{16,40},{24,48},{32,56},{40,64},{48,72},{56,80},{64,... | collective-permute-start | bytes 49160 | tf_op jit(solution)/shard_map/ppermute | solution.py:526
  56.0 7.7 %collective-permute-start.13 = (f32[2,16,128]{2,1,0:T(8,128)S(1)}, f32[2,16,128]{2,1,0:T(8,128)S(1)}, u32[]{:S(2)}, u32[]{:S(2)}) collective-permute-start(f32[2,16,128]{2,1,0:T(8,128)S(1)} %get-tuple-element.46), channel_id=1, source_target_pairs={{0,232},{8,240},{16,248},{24,0},{32,8},{40,16},{48,24},{56,32},{64... | collective-permute-start | bytes 49160 | tf_op jit(solution)/shard_map/ppermute | solution.py:526
  63.8 7.6 %collective-permute-start.17 = (f32[18,16,128]{2,1,0:T(8,128)S(1)}, f32[18,16,128]{2,1,0:T(8,128)S(1)}, u32[]{:S(2)}, u32[]{:S(2)}) collective-permute-start(f32[18,16,128]{2,1,0:T(8,128)S(1)} %shard_map.33.mid), channel_id=1, source_target_pairs={{0,6},{1,7},{2,0},{3,1},{4,2},{5,3},{6,4},{7,5},{8,14},{9,15},{10,... | collective-permute-start | bytes 442376 | tf_op jit(solution)/shard_map/ppermute | solution.py:526
  67.7 5.5 %collective-permute-start.16 = (f32[18,16,128]{2,1,0:T(8,128)S(1)}, f32[18,16,128]{2,1,0:T(8,128)S(1)}, u32[]{:S(2)}, u32[]{:S(2)}) collective-permute-start(f32[18,16,128]{2,1,0:T(8,128)S(1)} %shard_map.33.mid), channel_id=1, source_target_pairs={{0,7},{1,0},{2,1},{3,2},{4,3},{5,4},{6,5},{7,6},{8,15},{9,8},{10,9... | collective-permute-start | bytes 442376 | tf_op jit(solution)/shard_map/ppermute | solution.py:526
  67.7 6.2 %collective-permute-start.15 = (f32[18,16,128]{2,1,0:T(8,128)S(1)}, f32[18,16,128]{2,1,0:T(8,128)S(1)}, u32[]{:S(2)}, u32[]{:S(2)}) collective-permute-start(f32[18,16,128]{2,1,0:T(8,128)S(1)} %shard_map.33.mid), channel_id=1, source_target_pairs={{0,2},{1,3},{2,4},{3,5},{4,6},{5,7},{6,0},{7,1},{8,10},{9,11},{10,... | collective-permute-start | bytes 442376 | tf_op jit(solution)/shard_map/ppermute | solution.py:526
  68.6 5.3 %collective-permute-start.14 = (f32[18,16,128]{2,1,0:T(8,128)S(1)}, f32[18,16,128]{2,1,0:T(8,128)S(1)}, u32[]{:S(2)}, u32[]{:S(2)}) collective-permute-start(f32[18,16,128]{2,1,0:T(8,128)S(1)} %shard_map.33.mid), channel_id=1, source_target_pairs={{0,1},{1,2},{2,3},{3,4},{4,5},{5,6},{6,7},{7,0},{8,9},{9,10},{10,1... | collective-permute-start | bytes 442376 | tf_op jit(solution)/shard_map/ppermute | solution.py:526

commit v4 on v3

--- a/solution.py
+++ b/solution.py
@@ -141,7 +141,13 @@
     return g[comp, x + go] - cf[DG, x + co] * here + total
 
 
-def pack_fine(f, ids, xup, xdown, yup, ydown):
+def pack_fine(f_in, ids_in, xup, xdown, yup, ydown, f, ids, arrived):
+    copies = [pltpu.make_async_copy(ids_in.at[x : x + 2], ids.at[x : x + 2], arrived.at[8 + x // 2]) for x in (0, 2, 4, 6)]
+    copies += [pltpu.make_async_copy(f_in.at[:, x], f.at[:, x], arrived.at[x]) for x in range(8)]
+    for copy in copies:
+        copy.start()
+    for copy in copies:
+        copy.wait()
     for c in range(3):
         for k in range(3):
             xup[3 * c + k] = f[c, 5 + k]
@@ -442,7 +448,7 @@
 
 def ascend(
     mid, ym1, ym2, yp1, yp2, v1, g1, cx1, cf1, v0, g0, cx0, cf0, out,
-    eta2, g2, cx2, cf2, va2, vb2, rows2, wide1, va1, vb1, rows1, wide0, va0, vb0,
+    eta2, g2, cx2, cf2, va2, vb2, rows2, wide1, va1, vb1, rows1, wide0, va0, vb0, result, sent,
 ):
     nz2, nz1, nz0 = mid.shape[-1], v1.shape[-1], v0.shape[-1]
     blank = jnp.zeros((4, nz2), F32)
@@ -504,19 +510,25 @@
         for c in range(3):
             here, total = gather_sum(vb0, c, x + 2, cx0, cf0, x + 3)
             value = (1.0 / 3.0) * here + cf0[EI, x + 3] * (g0[c, x + 3] + total)
-            out[c, x] = value[4:20]
+            result[c, x] = value[4:20]
+        pltpu.make_async_copy(result.at[:, x], out.at[:, x], sent.at[x]).start()
 
     planes(8, final, U0)
-
-
-def call(body, outs, *args, scratch=()):
-    vmem = pl.BlockSpec(memory_space=pltpu.VMEM)
+    for x in range(8):
+        pltpu.make_async_copy(result.at[:, x], out.at[:, x], sent.at[x]).wait()
+
+
+def call(body, outs, *args, scratch=(), copies=0, where_in=pltpu.VMEM, where_out=pltpu.VMEM):
+    outs = [out if isinstance(out, jax.ShapeDtypeStruct) else jax.ShapeDtypeStruct(out, F32) for out in outs]
+    scratch_shapes = [pltpu.VMEM(shape, F32) for shape in scratch]
+    if copies:
+        scratch_shapes.append(pltpu.SemaphoreType.DMA((copies,)))
     return pl.pallas_call(
         body,
-        out_shape=[jax.ShapeDtypeStruct(shape, F32) for shape in outs],
-        in_specs=[vmem] * len(args),
-        out_specs=[vmem] * len(outs),
-        scratch_shapes=[pltpu.VMEM(shape, F32) for shape in scratch],
+        out_shape=outs,
+        in_specs=[pl.BlockSpec(memory_space=where_in)] * len(args),
+        out_specs=[pl.BlockSpec(memory_space=where_out)] * len(outs),
+        scratch_shapes=scratch_shapes,
         compiler_params=pltpu.CompilerParams(vmem_limit_bytes=VMEM_LIMIT),
     )(*args)
 
@@ -529,7 +541,11 @@
 def per_device(forcing, phase_ids):
     z0 = forcing.shape[-1]
     z1, z2 = z0 // 2, z0 // 4
-    xup, xdown, yup, ydown = call(pack_fine, [(13, 16, z0)] * 2 + [(13, 8, z0)] * 2, forcing, phase_ids)
+    xup, xdown, yup, ydown, f0, ids0 = call(
+        pack_fine,
+        [(13, 16, z0)] * 2 + [(13, 8, z0)] * 2 + [forcing.shape, jax.ShapeDtypeStruct(phase_ids.shape, jnp.int32)],
+        *(pltpu.with_memory_space_constraint(a, pltpu.HBM) for a in (forcing, phase_ids)), copies=12, where_in=pltpu.HBM,
+    )
     xlow, xhigh = cycled(xup, "gx", 1), cycled(xdown, "gx", -1)
     ylow, yhigh = cycled(yup, "gy", 1), cycled(ydown, "gy", -1)
     up, down = call(pack_corners, [(11, 8, z0)] * 2, xlow, xhigh)
@@ -537,7 +553,7 @@
     v0, g0, cx0, cf0, f1, eta1, up, down = call(
         fine_down,
         [(3, 12, 24, z0), (3, 14, 24, z0), (15, 24, z0), (6, 14, 24, z0), (3, 4, 8, z1), (6, 8, z1), (17, 8, z1), (17, 8, z1)],
-        forcing, phase_ids, xlow, xhigh, ylow, yhigh, clow, chigh,
+        f0, ids0, xlow, xhigh, ylow, yhigh, clow, chigh,
         scratch=[(16, 24, z0), (3, 14, 24, z0), lane_blocks(18, z0), (144, z0)],
     )
     xlow, xhigh = cycled(up, "gx", 1), cycled(down, "gx", -1)
@@ -561,8 +577,10 @@
         scratch=[
             (18, 24, z2), (3, 16, 24, z2), (17, 24, z2), (6, 16, 24, z2), (3, 16, 24, z2), (3, 16, 24, z2),
             (288, z2), lane_blocks(18, z1), (3, 10, 24, z1), (3, 10, 24, z1),
-            (288, z1), lane_blocks(18, z0), (3, 12, 24, z0), (3, 12, 24, z0),
+            (288, z1), lane_blocks(18, z0), (3, 12, 24, z0), (3, 12, 24, z0), forcing.shape,
         ],
+        copies=8,
+        where_out=pltpu.HBM,
     )
     return velocity
 

time: 81.4 us -> 80.8 us (level)
  local copies, waits for them, and re-layouts: 2.09 us -> 0 us
  Pallas kernels: 14.9 us -> 16.2 us
    unnamed x8 -> x0, local copies, waits for them, and re-layouts: 2.09 us -> none
    pallas_call x7, Pallas kernels: 14.9 us -> 16.2 us  [call(): pl.pallas_call(body, out_shape=outs, in_specs=[pl.BlockSpec(memory_space=...]
where the time goes in v4:
time: 80.8 us; the launch traced here: 80.5 us
  starting transfers between devices  37.2 us (46%)
  waiting for transfers between devices  27 us (33%)
  Pallas kernels  16.2 us (20%)
    ppermute x18, starting transfers between devices, cycled(): lax.ppermute(array, axis, [(i, (i + step) % size) for i in range(size)])  37.2 us
    ppermute x18, waiting for transfers between devices, cycled(): lax.ppermute(array, axis, [(i, (i + step) % size) for i in range(size)])  27 us
    pallas_call x7, Pallas kernels, call(): pl.pallas_call(body, out_shape=outs, in_specs=[pl.BlockSpec(memory_space=...  16.2 us
  transfers between devices with their start and end apart: 18, of which 10 were waited for; matrix products, arithmetic and copies ran while one was open for 0% of the time, Pallas kernels for 0%

profile of v4, /device:TPU:1, one launch (start us, length us, event | category | flops | bytes accessed | tf_op | source)
XLA Modules:
  0.0 80.5 jit_solution(16925020787346134149)
XLA Ops:
  0.0 1.6 %shard_map.28 = (f32[13,16,512]{2,1,0:T(8,128)S(1)}, f32[13,16,512]{2,1,0:T(8,128)S(1)}, f32[13,8,512]{2,1,0:T(8,128)S(1)}, f32[13,8,512]{2,1,0:T(8,128)S(1)}, f...) custom-call(f32[3,8,16,512]{3,2,1,0:T(8,128)} %f_in.1, s32[8,16,512]{2,1,0:T(8,128)} %ids_in.1), custom_call_target="tpu_custom_call" | custom-call | tf_op jit(solution)/shard_map/pallas_call | solution.py:526
  1.6 2.5 %collective-permute-start = (f32[13,16,512]{2,1,0:T(8,128)S(1)}, f32[13,16,512]{2,1,0:T(8,128)S(1)}, u32[]{:S(2)}, u32[]{:S(2)}) collective-permute-start(f32[13,16,512]{2,1,0:T(8,128)S(1)} %get-tuple-element.34), channel_id=1, source_target_pairs={{0,8},{8,16},{16,24},{24,32},{32,40},{40,48},{48,56},{56,64},{64,7... | collective-permute-start | bytes 1277960 | tf_op jit(solution)/shard_map/ppermute | solution.py:538
  4.2 6.2 %collective-permute-start.1 = (f32[13,16,512]{2,1,0:T(8,128)S(1)}, f32[13,16,512]{2,1,0:T(8,128)S(1)}, u32[]{:S(2)}, u32[]{:S(2)}) collective-permute-start(f32[13,16,512]{2,1,0:T(8,128)S(1)} %get-tuple-element.35), channel_id=1, source_target_pairs={{0,248},{8,0},{16,8},{24,16},{32,24},{40,32},{48,40},{56,48},{64,5... | collective-permute-start | bytes 1277960 | tf_op jit(solution)/shard_map/ppermute | solution.py:538
  10.4 2.1 %collective-permute-start.2 = (f32[13,8,512]{2,1,0:T(8,128)S(1)}, f32[13,8,512]{2,1,0:T(8,128)S(1)}, u32[]{:S(2)}, u32[]{:S(2)}) collective-permute-start(f32[13,8,512]{2,1,0:T(8,128)S(1)} %get-tuple-element.36), channel_id=1, source_target_pairs={{0,1},{1,2},{2,3},{3,4},{4,5},{5,6},{6,7},{7,0},{8,9},{9,10},{10,1... | collective-permute-start | bytes 638984 | tf_op jit(solution)/shard_map/ppermute | solution.py:538
  12.5 0.0 collective-permute-start.3
  12.5 7.3 %collective-permute-done.low.xlow = f32[13,16,512]{2,1,0:T(8,128)S(1)} collective-permute-done((f32[13,16,512]{2,1,0:T(8,128)S(1)}, f32[13,16,512]{2,1,0:T(8,128)S(1)}, u32[]{:S(2)}, u32[]{:S(2)}) %collective-permute-start) | collective-permute-done | bytes 426016 | tf_op jit(solution)/shard_map/ppermute | solution.py:538
  19.8 0.0 collective-permute-done.1.high.xhigh
  19.8 0.1 shard_map.29
  20.0 2.4 %collective-permute-start.4 = (f32[11,8,512]{2,1,0:T(8,128)S(1)}, f32[11,8,512]{2,1,0:T(8,128)S(1)}, u32[]{:S(2)}, u32[]{:S(2)}) collective-permute-start(f32[11,8,512]{2,1,0:T(8,128)S(1)} %get-tuple-element.38), channel_id=1, source_target_pairs={{0,1},{1,2},{2,3},{3,4},{4,5},{5,6},{6,7},{7,0},{8,9},{9,10},{10,1... | collective-permute-start | bytes 540680 | tf_op jit(solution)/shard_map/ppermute | solution.py:538
  22.4 0.0 collective-permute-start.5
  22.4 0.0 collective-permute-done.2.ylow
  22.4 0.0 collective-permute-done.3.yhigh
  22.4 2.4 %collective-permute-done.4.clow = f32[11,8,512]{2,1,0:T(8,128)S(1)} collective-permute-done((f32[11,8,512]{2,1,0:T(8,128)S(1)}, f32[11,8,512]{2,1,0:T(8,128)S(1)}, u32[]{:S(2)}, u32[]{:S(2)}) %collective-permute-start.4) | collective-permute-done | bytes 180256 | tf_op jit(solution)/shard_map/ppermute | solution.py:538
  24.8 2.5 %collective-permute-done.5.chigh = f32[11,8,512]{2,1,0:T(8,128)S(1)} collective-permute-done((f32[11,8,512]{2,1,0:T(8,128)S(1)}, f32[11,8,512]{2,1,0:T(8,128)S(1)}, u32[]{:S(2)}, u32[]{:S(2)}) %collective-permute-start.5) | collective-permute-done | bytes 180256 | tf_op jit(solution)/shard_map/ppermute | solution.py:538
  27.3 5.0 %shard_map.30 = (f32[3,12,24,512]{3,2,1,0:T(8,128)S(1)}, f32[3,14,24,512]{3,2,1,0:T(8,128)S(1)}, f32[15,24,512]{2,1,0:T(8,128)S(1)}, f32[6,14,24,512]{3,2,1,0:T(...) custom-call(f32[3,8,16,512]{3,2,1,0:T(8,128)S(1)} %get-tuple-element, ...), custom_call_target="tpu_custom_call" | custom-call | tf_op jit(solution)/shard_map/pallas_call | solution.py:526
  32.3 0.1 collective-permute-start.6
  32.4 4.9 %collective-permute-start.7 = (f32[17,8,256]{2,1,0:T(8,128)S(1)}, f32[17,8,256]{2,1,0:T(8,128)S(1)}, u32[]{:S(2)}, u32[]{:S(2)}) collective-permute-start(f32[17,8,256]{2,1,0:T(8,128)S(1)} %get-tuple-element.43), channel_id=1, source_target_pairs={{0,248},{8,0},{16,8},{24,16},{32,24},{40,32},{48,40},{56,48},{64,5... | collective-permute-start | bytes 417800 | tf_op jit(solution)/shard_map/ppermute | solution.py:538
  37.3 3.8 %collective-permute-done.6.low.xlow = f32[17,8,256]{2,1,0:T(8,128)S(1)} collective-permute-done((f32[17,8,256]{2,1,0:T(8,128)S(1)}, f32[17,8,256]{2,1,0:T(8,128)S(1)}, u32[]{:S(2)}, u32[]{:S(2)}) %collective-permute-start.6) | collective-permute-done | bytes 139296 | tf_op jit(solution)/shard_map/ppermute | solution.py:538
  41.1 0.0 collective-permute-done.7.high.xhigh
  41.1 0.1 shard_map.31
  41.2 0.3 collective-permute-start.8
  41.5 0.4 collective-permute-start.9
  42.0 2.5 %collective-permute-done.8.ylow = f32[28,8,256]{2,1,0:T(8,128)S(1)} collective-permute-done((f32[28,8,256]{2,1,0:T(8,128)S(1)}, f32[28,8,256]{2,1,0:T(8,128)S(1)}, u32[]{:S(2)}, u32[]{:S(2)}) %collective-permute-start.8) | collective-permute-done | bytes 229408 | tf_op jit(solution)/shard_map/ppermute | solution.py:538
  44.5 2.8 %collective-permute-done.9.yhigh = f32[28,8,256]{2,1,0:T(8,128)S(1)} collective-permute-done((f32[28,8,256]{2,1,0:T(8,128)S(1)}, f32[28,8,256]{2,1,0:T(8,128)S(1)}, u32[]{:S(2)}, u32[]{:S(2)}) %collective-permute-start.9) | collective-permute-done | bytes 229408 | tf_op jit(solution)/shard_map/ppermute | solution.py:538
  47.3 2.2 %shard_map.32 = (f32[3,14,24,256]{3,2,1,0:T(8,128)S(1)}, f32[3,12,24,256]{3,2,1,0:T(8,128)S(1)}, f32[13,24,256]{2,1,0:T(8,128)S(1)}, f32[6,12,24,256]{3,2,1,0:T(...) custom-call(f32[3,4,8,256]{3,2,1,0:T(8,128)S(1)} %get-tuple-element., ...), custom_call_target="tpu_custom_call" | custom-call | tf_op jit(solution)/shard_map/pallas_call | solution.py:526
  49.5 0.1 collective-permute-start.10
  49.6 5.7 %collective-permute-start.12 = (f32[4,16,128]{2,1,0:T(8,128)S(1)}, f32[4,16,128]{2,1,0:T(8,128)S(1)}, u32[]{:S(2)}, u32[]{:S(2)}) collective-permute-start(f32[4,16,128]{2,1,0:T(8,128)S(1)} %get-tuple-element.49), channel_id=1, source_target_pairs={{0,240},{8,248},{16,0},{24,8},{32,16},{40,24},{48,32},{56,40},{64,... | collective-permute-start | bytes 98312 | tf_op jit(solution)/shard_map/ppermute | solution.py:538
  55.3 0.0 collective-permute-start.11
  55.3 6.6 %collective-permute-start.13 = (f32[2,16,128]{2,1,0:T(8,128)S(1)}, f32[2,16,128]{2,1,0:T(8,128)S(1)}, u32[]{:S(2)}, u32[]{:S(2)}) collective-permute-start(f32[2,16,128]{2,1,0:T(8,128)S(1)} %get-tuple-element.50), channel_id=1, source_target_pairs={{0,232},{8,240},{16,248},{24,0},{32,8},{40,16},{48,24},{56,32},{64... | collective-permute-start | bytes 49160 | tf_op jit(solution)/shard_map/ppermute | solution.py:538
  61.9 1.1 %collective-permute-done.11.low3 = f32[2,16,128]{2,1,0:T(8,128)S(1)} collective-permute-done((f32[2,16,128]{2,1,0:T(8,128)S(1)}, f32[2,16,128]{2,1,0:T(8,128)S(1)}, u32[]{:S(2)}, u32[]{:S(2)}) %collective-permute-start.11) | collective-permute-done | bytes 16416 | tf_op jit(solution)/shard_map/ppermute | solution.py:538
  63.0 0.0 collective-permute-done.13.high3
  63.0 0.0 collective-permute-done.10.low2
  63.0 0.0 collective-permute-done.12.high2
  63.0 4.0 %collective-permute-start.17 = (f32[18,16,128]{2,1,0:T(8,128)S(1)}, f32[18,16,128]{2,1,0:T(8,128)S(1)}, u32[]{:S(2)}, u32[]{:S(2)}) collective-permute-start(f32[18,16,128]{2,1,0:T(8,128)S(1)} %shard_map.33.mid), channel_id=1, source_target_pairs={{0,6},{1,7},{2,0},{3,1},{4,2},{5,3},{6,4},{7,5},{8,14},{9,15},{10,... | collective-permute-start | bytes 442376 | tf_op jit(solution)/shard_map/ppermute | solution.py:538
  67.0 0.0 collective-permute-start.16
  67.0 0.9 %collective-permute-start.15 = (f32[18,16,128]{2,1,0:T(8,128)S(1)}, f32[18,16,128]{2,1,0:T(8,128)S(1)}, u32[]{:S(2)}, u32[]{:S(2)}) collective-permute-start(f32[18,16,128]{2,1,0:T(8,128)S(1)} %shard_map.33.mid), channel_id=1, source_target_pairs={{0,2},{1,3},{2,4},{3,5},{4,6},{5,7},{6,0},{7,1},{8,10},{9,11},{10,... | collective-permute-start | bytes 442376 | tf_op jit(solution)/shard_map/ppermute | solution.py:538
  67.9 0.9 %collective-permute-start.14 = (f32[18,16,128]{2,1,0:T(8,128)S(1)}, f32[18,16,128]{2,1,0:T(8,128)S(1)}, u32[]{:S(2)}, u32[]{:S(2)}) collective-permute-start(f32[18,16,128]{2,1,0:T(8,128)S(1)} %shard_map.33.mid), channel_id=1, source_target_pairs={{0,1},{1,2},{2,3},{3,4},{4,5},{5,6},{6,7},{7,0},{8,9},{9,10},{10,1... | collective-permute-start | bytes 442376 | tf_op jit(solution)/shard_map/ppermute | solution.py:538
  68.8 1.9 %collective-permute-done.17.yp2 = f32[18,16,128]{2,1,0:T(8,128)S(1)} collective-permute-done((f32[18,16,128]{2,1,0:T(8,128)S(1)}, f32[18,16,128]{2,1,0:T(8,128)S(1)}, u32[]{:S(2)}, u32[]{:S(2)}) %collective-permute-start.17) | collective-permute-done | bytes 147488 | tf_op jit(solution)/shard_map/ppermute | solution.py:538
  70.7 1.8 %collective-permute-done.16.yp1 = f32[18,16,128]{2,1,0:T(8,128)S(1)} collective-permute-done((f32[18,16,128]{2,1,0:T(8,128)S(1)}, f32[18,16,128]{2,1,0:T(8,128)S(1)}, u32[]{:S(2)}, u32[]{:S(2)}) %collective-permute-start.16) | collective-permute-done | bytes 147488 | tf_op jit(solution)/shard_map/ppermute | solution.py:538
  72.5 0.7 collective-permute-done.15.ym2
  73.2 0.0 collective-permute-done.14.ym1
  73.2 7.1 %shard_map.34 = f32[3,8,16,512]{3,2,1,0:T(8,128)} custom-call(f32[18,16,128]{2,1,0:T(8,128)S(1)} %shard_map.33.mid, f32[18,16,128]{2,1,0:T(8,128)S(1)} %collective-permute-done.14.ym1, f32[18,16,128]{2,1,0:T(8,128)S(1)} %collective-permute-done.15.ym2, f32[18,16,128]{2,1,0:T(8,128)S(1)} %collective-permute-done.16.yp1, ...), custom_call_target="tpu_custom_call" | custom-call | tf_op jit(solution)/shard_map/pallas_call | solution.py:526
  (1 shorter events, 0.0 us)
Async XLA Ops:
  1.6 18.2 %collective-permute-start = (f32[13,16,512]{2,1,0:T(8,128)S(1)}, f32[13,16,512]{2,1,0:T(8,128)S(1)}, u32[]{:S(2)}, u32[]{:S(2)}) collective-permute-start(f32[13,16,512]{2,1,0:T(8,128)S(1)} %get-tuple-element.34), channel_id=1, source_target_pairs={{0,8},{8,16},{16,24},{24,32},{32,40},{40,48},{48,56},{56,64},{64,7... | collective-permute-start | bytes 1277960 | tf_op jit(solution)/shard_map/ppermute | solution.py:538
  4.2 15.7 %collective-permute-start.1 = (f32[13,16,512]{2,1,0:T(8,128)S(1)}, f32[13,16,512]{2,1,0:T(8,128)S(1)}, u32[]{:S(2)}, u32[]{:S(2)}) collective-permute-start(f32[13,16,512]{2,1,0:T(8,128)S(1)} %get-tuple-element.35), channel_id=1, source_target_pairs={{0,248},{8,0},{16,8},{24,16},{32,24},{40,32},{48,40},{56,48},{64,5... | collective-permute-start | bytes 1277960 | tf_op jit(solution)/shard_map/ppermute | solution.py:538
  10.4 12.0 %collective-permute-start.2 = (f32[13,8,512]{2,1,0:T(8,128)S(1)}, f32[13,8,512]{2,1,0:T(8,128)S(1)}, u32[]{:S(2)}, u32[]{:S(2)}) collective-permute-start(f32[13,8,512]{2,1,0:T(8,128)S(1)} %get-tuple-element.36), channel_id=1, source_target_pairs={{0,1},{1,2},{2,3},{3,4},{4,5},{5,6},{6,7},{7,0},{8,9},{9,10},{10,1... | collective-permute-start | bytes 638984 | tf_op jit(solution)/shard_map/ppermute | solution.py:538
  12.5 9.9 %collective-permute-start.3 = (f32[13,8,512]{2,1,0:T(8,128)S(1)}, f32[13,8,512]{2,1,0:T(8,128)S(1)}, u32[]{:S(2)}, u32[]{:S(2)}) collective-permute-start(f32[13,8,512]{2,1,0:T(8,128)S(1)} %get-tuple-element.37), channel_id=1, source_target_pairs={{0,7},{1,0},{2,1},{3,2},{4,3},{5,4},{6,5},{7,6},{8,15},{9,8},{10,9... | collective-permute-start | bytes 638984 | tf_op jit(solution)/shard_map/ppermute | solution.py:538
  20.0 4.9 %collective-permute-start.4 = (f32[11,8,512]{2,1,0:T(8,128)S(1)}, f32[11,8,512]{2,1,0:T(8,128)S(1)}, u32[]{:S(2)}, u32[]{:S(2)}) collective-permute-start(f32[11,8,512]{2,1,0:T(8,128)S(1)} %get-tuple-element.38), channel_id=1, source_target_pairs={{0,1},{1,2},{2,3},{3,4},{4,5},{5,6},{6,7},{7,0},{8,9},{9,10},{10,1... | collective-permute-start | bytes 540680 | tf_op jit(solution)/shard_map/ppermute | solution.py:538
  22.4 4.9 %collective-permute-start.5 = (f32[11,8,512]{2,1,0:T(8,128)S(1)}, f32[11,8,512]{2,1,0:T(8,128)S(1)}, u32[]{:S(2)}, u32[]{:S(2)}) collective-permute-start(f32[11,8,512]{2,1,0:T(8,128)S(1)} %get-tuple-element.39), channel_id=1, source_target_pairs={{0,7},{1,0},{2,1},{3,2},{4,3},{5,4},{6,5},{7,6},{8,15},{9,8},{10,9... | collective-permute-start | bytes 540680 | tf_op jit(solution)/shard_map/ppermute | solution.py:538
  32.3 8.8 %collective-permute-start.6 = (f32[17,8,256]{2,1,0:T(8,128)S(1)}, f32[17,8,256]{2,1,0:T(8,128)S(1)}, u32[]{:S(2)}, u32[]{:S(2)}) collective-permute-start(f32[17,8,256]{2,1,0:T(8,128)S(1)} %get-tuple-element.42), channel_id=1, source_target_pairs={{0,8},{8,16},{16,24},{24,32},{32,40},{40,48},{48,56},{56,64},{64,7... | collective-permute-start | bytes 417800 | tf_op jit(solution)/shard_map/ppermute | solution.py:538
  32.4 8.8 %collective-permute-start.7 = (f32[17,8,256]{2,1,0:T(8,128)S(1)}, f32[17,8,256]{2,1,0:T(8,128)S(1)}, u32[]{:S(2)}, u32[]{:S(2)}) collective-permute-start(f32[17,8,256]{2,1,0:T(8,128)S(1)} %get-tuple-element.43), channel_id=1, source_target_pairs={{0,248},{8,0},{16,8},{24,16},{32,24},{40,32},{48,40},{56,48},{64,5... | collective-permute-start | bytes 417800 | tf_op jit(solution)/shard_map/ppermute | solution.py:538
  41.2 3.3 %collective-permute-start.8 = (f32[28,8,256]{2,1,0:T(8,128)S(1)}, f32[28,8,256]{2,1,0:T(8,128)S(1)}, u32[]{:S(2)}, u32[]{:S(2)}) collective-permute-start(f32[28,8,256]{2,1,0:T(8,128)S(1)} %get-tuple-element.44), channel_id=1, source_target_pairs={{0,1},{1,2},{2,3},{3,4},{4,5},{5,6},{6,7},{7,0},{8,9},{9,10},{10,1... | collective-permute-start | bytes 688136 | tf_op jit(solution)/shard_map/ppermute | solution.py:538
  41.5 5.7 %collective-permute-start.9 = (f32[28,8,256]{2,1,0:T(8,128)S(1)}, f32[28,8,256]{2,1,0:T(8,128)S(1)}, u32[]{:S(2)}, u32[]{:S(2)}) collective-permute-start(f32[28,8,256]{2,1,0:T(8,128)S(1)} %get-tuple-element.45), channel_id=1, source_target_pairs={{0,7},{1,0},{2,1},{3,2},{4,3},{5,4},{6,5},{7,6},{8,15},{9,8},{10,9... | collective-permute-start | bytes 688136 | tf_op jit(solution)/shard_map/ppermute | solution.py:538
  49.5 13.5 %collective-permute-start.10 = (f32[4,16,128]{2,1,0:T(8,128)S(1)}, f32[4,16,128]{2,1,0:T(8,128)S(1)}, u32[]{:S(2)}, u32[]{:S(2)}) collective-permute-start(f32[4,16,128]{2,1,0:T(8,128)S(1)} %get-tuple-element.47), channel_id=1, source_target_pairs={{0,16},{8,24},{16,32},{24,40},{32,48},{40,56},{48,64},{56,72},{64,... | collective-permute-start | bytes 98312 | tf_op jit(solution)/shard_map/ppermute | solution.py:538
  49.6 13.4 %collective-permute-start.12 = (f32[4,16,128]{2,1,0:T(8,128)S(1)}, f32[4,16,128]{2,1,0:T(8,128)S(1)}, u32[]{:S(2)}, u32[]{:S(2)}) collective-permute-start(f32[4,16,128]{2,1,0:T(8,128)S(1)} %get-tuple-element.49), channel_id=1, source_target_pairs={{0,240},{8,248},{16,0},{24,8},{32,16},{40,24},{48,32},{56,40},{64,... | collective-permute-start | bytes 98312 | tf_op jit(solution)/shard_map/ppermute | solution.py:538
  55.3 7.7 %collective-permute-start.11 = (f32[2,16,128]{2,1,0:T(8,128)S(1)}, f32[2,16,128]{2,1,0:T(8,128)S(1)}, u32[]{:S(2)}, u32[]{:S(2)}) collective-permute-start(f32[2,16,128]{2,1,0:T(8,128)S(1)} %get-tuple-element.48), channel_id=1, source_target_pairs={{0,24},{8,32},{16,40},{24,48},{32,56},{40,64},{48,72},{56,80},{64,... | collective-permute-start | bytes 49160 | tf_op jit(solution)/shard_map/ppermute | solution.py:538
  55.3 7.7 %collective-permute-start.13 = (f32[2,16,128]{2,1,0:T(8,128)S(1)}, f32[2,16,128]{2,1,0:T(8,128)S(1)}, u32[]{:S(2)}, u32[]{:S(2)}) collective-permute-start(f32[2,16,128]{2,1,0:T(8,128)S(1)} %get-tuple-element.50), channel_id=1, source_target_pairs={{0,232},{8,240},{16,248},{24,0},{32,8},{40,16},{48,24},{56,32},{64... | collective-permute-start | bytes 49160 | tf_op jit(solution)/shard_map/ppermute | solution.py:538
  63.0 7.6 %collective-permute-start.17 = (f32[18,16,128]{2,1,0:T(8,128)S(1)}, f32[18,16,128]{2,1,0:T(8,128)S(1)}, u32[]{:S(2)}, u32[]{:S(2)}) collective-permute-start(f32[18,16,128]{2,1,0:T(8,128)S(1)} %shard_map.33.mid), channel_id=1, source_target_pairs={{0,6},{1,7},{2,0},{3,1},{4,2},{5,3},{6,4},{7,5},{8,14},{9,15},{10,... | collective-permute-start | bytes 442376 | tf_op jit(solution)/shard_map/ppermute | solution.py:538
  67.0 5.5 %collective-permute-start.16 = (f32[18,16,128]{2,1,0:T(8,128)S(1)}, f32[18,16,128]{2,1,0:T(8,128)S(1)}, u32[]{:S(2)}, u32[]{:S(2)}) collective-permute-start(f32[18,16,128]{2,1,0:T(8,128)S(1)} %shard_map.33.mid), channel_id=1, source_target_pairs={{0,7},{1,0},{2,1},{3,2},{4,3},{5,4},{6,5},{7,6},{8,15},{9,8},{10,9... | collective-permute-start | bytes 442376 | tf_op jit(solution)/shard_map/ppermute | solution.py:538
  67.0 6.2 %collective-permute-start.15 = (f32[18,16,128]{2,1,0:T(8,128)S(1)}, f32[18,16,128]{2,1,0:T(8,128)S(1)}, u32[]{:S(2)}, u32[]{:S(2)}) collective-permute-start(f32[18,16,128]{2,1,0:T(8,128)S(1)} %shard_map.33.mid), channel_id=1, source_target_pairs={{0,2},{1,3},{2,4},{3,5},{4,6},{5,7},{6,0},{7,1},{8,10},{9,11},{10,... | collective-permute-start | bytes 442376 | tf_op jit(solution)/shard_map/ppermute | solution.py:538
  67.9 5.3 %collective-permute-start.14 = (f32[18,16,128]{2,1,0:T(8,128)S(1)}, f32[18,16,128]{2,1,0:T(8,128)S(1)}, u32[]{:S(2)}, u32[]{:S(2)}) collective-permute-start(f32[18,16,128]{2,1,0:T(8,128)S(1)} %shard_map.33.mid), channel_id=1, source_target_pairs={{0,1},{1,2},{2,3},{3,4},{4,5},{5,6},{6,7},{7,0},{8,9},{9,10},{10,1... | collective-permute-start | bytes 442376 | tf_op jit(solution)/shard_map/ppermute | solution.py:538

commit v5 on v4

--- a/solution.py
+++ b/solution.py
@@ -85,6 +85,30 @@
 YP, YM, ZP, ZM, DG, EI = range(6)
 
 
+def plane_coefficients(below, here, above, scale):
+    half = 0.5 * scale
+    lane = lanes_of(here.shape)
+    first = lane == 0
+    final = lane == here.shape[1] - 1
+    yp, ym = next_row(here), last_row(here)
+    zp, zm = next_lane(here), last_lane(here)
+
+    def ghost(q):
+        return jnp.where(q > 0.0, q, here)
+
+    around = ghost(yp) + ghost(ym) + ghost(below) + ghost(above)
+    around = around + jnp.where(final, here, zp) + jnp.where(first, here, zm)
+    diag = scale * (3.0 * here + 0.5 * around)
+    return (
+        half * (here + yp),
+        half * (here + ym),
+        jnp.where(final, 0.0, half * (here + zp)),
+        jnp.where(first, 0.0, half * (here + zm)),
+        diag,
+        jnp.where(here > 0.0, WEIGHT / diag, 0.0),
+    )
+
+
 def coefficients(eta, cx, cf, layers, scale, unroll):
     half = 0.5 * scale
 
@@ -94,25 +118,9 @@
     planes(layers + 1, face, unroll)
 
     def body(i):
-        here = eta[i + 1]
-        lane = lanes_of(here.shape)
-        first = lane == 0
-        final = lane == here.shape[1] - 1
-        yp, ym = next_row(here), last_row(here)
-        zp, zm = next_lane(here), last_lane(here)
-        cf[YP, i] = half * (here + yp)
-        cf[YM, i] = half * (here + ym)
-        cf[ZP, i] = jnp.where(final, 0.0, half * (here + zp))
-        cf[ZM, i] = jnp.where(first, 0.0, half * (here + zm))
-
-        def ghost(q):
-            return jnp.where(q > 0.0, q, here)
-
-        around = ghost(yp) + ghost(ym) + ghost(eta[i]) + ghost(eta[i + 2])
-        around = around + jnp.where(final, here, zp) + jnp.where(first, here, zm)
-        diag = scale * (3.0 * here + 0.5 * around)
-        cf[DG, i] = diag
-        cf[EI, i] = jnp.where(here > 0.0, WEIGHT / diag, 0.0)
+        made = plane_coefficients(eta[i], eta[i + 1], eta[i + 2], scale)
+        for n, value in enumerate(made):
+            cf[n, i] = value
 
     planes(layers, body, unroll)
 
@@ -149,15 +157,15 @@
     for copy in copies:
         copy.wait()
     for c in range(3):
-        for k in range(3):
-            xup[3 * c + k] = f[c, 5 + k]
-            xdown[3 * c + k] = f[c, k]
+        for k in range(2):
+            xup[2 * c + k] = f[c, 6 + k]
+            xdown[2 * c + k] = f[c, k]
     for x in range(8):
         eta = materials(ids[x])
-        if x < 4:
-            xdown[9 + x] = eta
-        else:
-            xup[9 + x - 4] = eta
+        if x < 3:
+            xdown[6 + x] = eta
+        if x > 4:
+            xup[6 + x - 5] = eta
         for out, at, eta_at in ((yup, 13, 12), (ydown, 0, 0)):
             pack_rows(out, x, 8, [f[c, x, at : at + 3] for c in range(3)])
             put_eta_rows(out, 9, x, eta[eta_at : eta_at + 4])
@@ -177,38 +185,38 @@
 
 def fine_source(f, low, high, c, x):
     if x < 0:
-        return kept("gx", 1, low[3 * c + x + 3])
+        return kept("gx", 1, low[2 * c + x + 2])
     if x < 8:
         return f[c, x]
-    return kept("gx", -1, high[3 * c + x - 8])
+    return kept("gx", -1, high[2 * c + x - 8])
 
 
 def fine_eta(ids, low, high, x):
     if x < 0:
-        return kept("gx", 1, low[9 + x + 4])
+        return kept("gx", 1, low[6 + x + 3])
     if x < 8:
         return materials(ids[x])
-    return kept("gx", -1, high[9 + x - 8])
+    return kept("gx", -1, high[6 + x - 8])
 
 
 def pack_corners(low, high, up, down):
-    for n, x in enumerate((-3, -2, -1, 8, 9, 10)):
+    for n, x in enumerate((-2, -1, 8, 9)):
         rows = [fine_source(None, low, high, c, x) for c in range(3)]
         for out, at in ((up, 13), (down, 0)):
-            pack_rows(out, n, 6, [row[at : at + 3] for row in rows])
-    for n, x in enumerate((-4, -3, -2, -1, 8, 9, 10, 11)):
+            pack_rows(out, n, 4, [row[at : at + 3] for row in rows])
+    for n, x in enumerate((-3, -2, -1, 8, 9, 10)):
         eta = fine_eta(None, low, high, x)
-        put_eta_rows(up, 7, n, eta[12:16])
-        put_eta_rows(down, 7, n, eta[0:4])
+        put_eta_rows(up, 5, n, eta[12:16])
+        put_eta_rows(down, 5, n, eta[0:4])
     for out in (up, down):
-        out[6, 6:8] = jnp.zeros((2, low.shape[-1]), F32)
-
-
-def fine_down(f, ids, xlow, xhigh, ylow, yhigh, clow, chigh, v0, g, cx, cf, f1, eta1, up, down, eta, va, pairs, rest):
+        out[4, 4:8] = jnp.zeros((4, low.shape[-1]), F32)
+
+
+def fine_down(f, ids, xlow, xhigh, ylow, yhigh, clow, chigh, v0, va, g, eta, cx, cf, f1, eta1, up, down, pairs, rest):
     nz = f.shape[-1]
     blank = jnp.zeros((1, nz), F32)
-    for i in range(14):
-        x = i - 3
+    for i in range(12):
+        x = i - 2
         for c in range(3):
             g[c, i, 4:20] = fine_source(f, xlow, xhigh, c, x)
             g[c, i, 0:1] = blank
@@ -217,42 +225,42 @@
             if 0 <= x < 8:
                 side, n, spill = own, x, 8
             else:
-                side, n, spill = corner, (i if x < 0 else x - 5), 6
+                side, n, spill = corner, (i if x < 0 else x - 6), 4
             tile = kept("gy", step, side[n])
             g[0, i, at : at + 3] = tile[0:3]
             g[1, i, at : at + 3] = tile[3:6]
             g[2, i, at : at + 2] = tile[6:8]
             g[2, i, at + 2 : at + 3] = kept("gy", step, side[spill, n : n + 1])
-    for j in range(16):
-        x = j - 4
+    for j in range(14):
+        x = j - 3
         eta[j, 4:20] = fine_eta(ids, xlow, xhigh, x)
         for own, corner, row, step in ((ylow, clow, 0, 1), (yhigh, chigh, 20, -1)):
             if 0 <= x < 8:
                 side, n, first = own, x, 9
             else:
-                side, n, first = corner, (j if x < 0 else x - 4), 7
+                side, n, first = corner, (j if x < 0 else x - 5), 5
             at = 4 * (n % 2)
             eta[j, row : row + 4] = kept("gy", step, side[first + n // 2, at : at + 4])
 
-    coefficients(eta, cx, cf, 14, 1.0, U0)
+    coefficients(eta, cx, cf, 12, 1.0, U0)
 
     def start(i):
         for c in range(3):
             va[c, i] = cf[EI, i] * g[c, i]
 
-    planes(14, start, U0)
-    sweep(va, 3, g, 3, cx, cf, 3, v0, 2, -2, 10, U0)
+    planes(12, start, U0)
+    sweep(va, 2, g, 2, cx, cf, 2, v0, 1, -1, 9, U0)
 
     def down_pair(k):
         for c in range(3):
             x = 2 * k
-            total = residual(v0, 2, g, 3, cx, cf, 3, c, x) + residual(v0, 2, g, 3, cx, cf, 3, c, x + 1)
+            total = residual(v0, 1, g, 2, cx, cf, 2, c, x) + residual(v0, 1, g, 2, cx, cf, 2, c, x + 1)
             put_plane(pairs, c * 4 + k, total)
 
     planes(4, down_pair, U0)
 
     def eta_pair(k):
-        put_plane(pairs, 12 + k, eta[2 * k + 2] + eta[2 * k + 3])
+        put_plane(pairs, 12 + k, eta[2 * k + 1] + eta[2 * k + 2])
 
     planes(6, eta_pair, U0)
     for n in range(18):
@@ -303,7 +311,29 @@
     return jnp.concatenate([ref[n, b] for b in range(ref.shape[1])], axis=1)
 
 
-def pack_middle_y(f1, eta1, low, high, up, down):
+def fine_rim(low, high, va, g, eta, cx, cf, rim):
+    nz = low.shape[-1]
+    blank = jnp.zeros((4, nz), F32)
+
+    for n, (side, step) in enumerate(((low, 1), (high, -1))):
+        rows = [jnp.concatenate([blank, kept("gx", step, side[k]), blank], axis=0) for k in range(4)]
+        edge, k, inner, face, far = ((0, 0, 1, 1, 0), (13, 11, 10, 11, 12))[n]
+        weight = plane_coefficients(rows[3], eta[edge], eta[1 if n == 0 else 12], 1.0)[EI]
+        for c in range(3):
+            here = va[c, k]
+            total = cx[far] * (weight * rows[c]) + cx[face] * va[c, inner]
+            total = total + cf[YP, k] * next_row(here) + cf[YM, k] * last_row(here)
+            total = total + cf[ZP, k] * next_lane(here) + cf[ZM, k] * last_lane(here)
+            rim[c, n] = (1.0 / 3.0) * here + cf[EI, k] * (g[c, k] + total)
+
+
+def pack_middle_y(f1, eta1, low, high, f, ids, up, down, late_up, late_down):
+    for c in range(3):
+        late_up[c] = f[c, 5]
+        late_down[c] = f[c, 2]
+    late_up[3] = materials(ids[4])
+    late_down[3] = materials(ids[3])
+
     def source(c, x):
         if x < 0:
             return kept("gx", 1, low[4 * c + x + 4])
@@ -447,7 +477,7 @@
 
 
 def ascend(
-    mid, ym1, ym2, yp1, yp2, v1, g1, cx1, cf1, v0, g0, cx0, cf0, out,
+    mid, ym1, ym2, yp1, yp2, v1, g1, cx1, cf1, v0, rim, g0, cx0, cf0, out,
     eta2, g2, cx2, cf2, va2, vb2, rows2, wide1, va1, vb1, rows1, wide0, va0, vb0, result, sent,
 ):
     nz2, nz1, nz0 = mid.shape[-1], v1.shape[-1], v0.shape[-1]
@@ -497,19 +527,17 @@
         block = spread[n * 16 : n * 16 + 12]
         row_copies(wide0, n, block)
 
-    def correct(k):
+    for k in range(6):
         for c in range(3):
             block = get_plane(wide0, c * 6 + k)
-            va0[c, 2 * k] = v0[c, 2 * k] + block
-            va0[c, 2 * k + 1] = v0[c, 2 * k + 1] + block
-
-    planes(6, correct, U0)
-    sweep(va0, 2, g0, 3, cx0, cf0, 3, vb0, 2, -1, 9, U0)
+            va0[c, 2 * k] = (v0[c, 2 * k - 1] if k > 0 else rim[c, 0]) + block
+            va0[c, 2 * k + 1] = (v0[c, 2 * k] if k < 5 else rim[c, 1]) + block
+    sweep(va0, 2, g0, 2, cx0, cf0, 2, vb0, 2, -1, 9, U0)
 
     def final(x):
         for c in range(3):
-            here, total = gather_sum(vb0, c, x + 2, cx0, cf0, x + 3)
-            value = (1.0 / 3.0) * here + cf0[EI, x + 3] * (g0[c, x + 3] + total)
+            here, total = gather_sum(vb0, c, x + 2, cx0, cf0, x + 2)
+            value = (1.0 / 3.0) * here + cf0[EI, x + 2] * (g0[c, x + 2] + total)
             result[c, x] = value[4:20]
         pltpu.make_async_copy(result.at[:, x], out.at[:, x], sent.at[x]).start()
 
@@ -543,22 +571,26 @@
     z1, z2 = z0 // 2, z0 // 4
     xup, xdown, yup, ydown, f0, ids0 = call(
         pack_fine,
-        [(13, 16, z0)] * 2 + [(13, 8, z0)] * 2 + [forcing.shape, jax.ShapeDtypeStruct(phase_ids.shape, jnp.int32)],
+        [(9, 16, z0)] * 2 + [(13, 8, z0)] * 2 + [forcing.shape, jax.ShapeDtypeStruct(phase_ids.shape, jnp.int32)],
         *(pltpu.with_memory_space_constraint(a, pltpu.HBM) for a in (forcing, phase_ids)), copies=12, where_in=pltpu.HBM,
     )
     xlow, xhigh = cycled(xup, "gx", 1), cycled(xdown, "gx", -1)
     ylow, yhigh = cycled(yup, "gy", 1), cycled(ydown, "gy", -1)
-    up, down = call(pack_corners, [(11, 8, z0)] * 2, xlow, xhigh)
+    up, down = call(pack_corners, [(8, 8, z0)] * 2, xlow, xhigh)
     clow, chigh = cycled(up, "gy", 1), cycled(down, "gy", -1)
-    v0, g0, cx0, cf0, f1, eta1, up, down = call(
+    v0, va, g0, eta0, cx0, cf0, f1, eta1, up, down = call(
         fine_down,
-        [(3, 12, 24, z0), (3, 14, 24, z0), (15, 24, z0), (6, 14, 24, z0), (3, 4, 8, z1), (6, 8, z1), (17, 8, z1), (17, 8, z1)],
+        [(3, 10, 24, z0), (3, 12, 24, z0), (3, 12, 24, z0), (14, 24, z0), (13, 24, z0), (6, 12, 24, z0), (3, 4, 8, z1), (6, 8, z1), (17, 8, z1), (17, 8, z1)],
         f0, ids0, xlow, xhigh, ylow, yhigh, clow, chigh,
-        scratch=[(16, 24, z0), (3, 14, 24, z0), lane_blocks(18, z0), (144, z0)],
+        scratch=[lane_blocks(18, z0), (144, z0)],
     )
     xlow, xhigh = cycled(up, "gx", 1), cycled(down, "gx", -1)
-    up, down = call(pack_middle_y, [(28, 8, z1)] * 2, f1, eta1, xlow, xhigh)
+    up, down, late_up, late_down = call(
+        pack_middle_y, [(28, 8, z1)] * 2 + [(4, 16, z0)] * 2, f1, eta1, xlow, xhigh, f0, ids0
+    )
     ylow, yhigh = cycled(up, "gy", 1), cycled(down, "gy", -1)
+    late_low, late_high = cycled(late_up, "gx", 1), cycled(late_down, "gx", -1)
+    (rim,) = call(fine_rim, [(3, 2, 24, z0)], late_low, late_high, va, g0, eta0, cx0, cf0)
     v1, g1, cx1, cf1, own, up, down, far_up, far_down = call(
         middle_down,
         [(3, 14, 24, z1), (3, 12, 24, z1), (13, 24, z1), (6, 12, 24, z1), (6, 16, z2), (4, 16, z2), (4, 16, z2), (2, 16, z2), (2, 16, z2)],
@@ -573,7 +605,7 @@
     (velocity,) = call(
         ascend,
         [forcing.shape],
-        strip, ym1, ym2, yp1, yp2, v1, g1, cx1, cf1, v0, g0, cx0, cf0,
+        strip, ym1, ym2, yp1, yp2, v1, g1, cx1, cf1, v0, rim, g0, cx0, cf0,
         scratch=[
             (18, 24, z2), (3, 16, 24, z2), (17, 24, z2), (6, 16, 24, z2), (3, 16, 24, z2), (3, 16, 24, z2),
             (288, z2), lane_blocks(18, z1), (3, 10, 24, z1), (3, 10, 24, z1),

time: 80.8 us -> 76.7 us (0.949)
  waiting for transfers between devices: 27 us -> 22.3 us
  starting transfers between devices: 37.2 us -> 38.7 us
  Pallas kernels: 16.2 us -> 15.2 us
    ppermute x18 -> x20, waiting for transfers between devices: 27 us -> 22.3 us  [cycled(): lax.ppermute(array, axis, [(i, (i + step) % size) for i in range(size)])]
    ppermute x18 -> x20, starting transfers between devices: 37.2 us -> 38.7 us  [cycled(): lax.ppermute(array, axis, [(i, (i + step) % size) for i in range(size)])]
    pallas_call x7 -> x8, Pallas kernels: 16.2 us -> 15.2 us  [call(): pl.pallas_call(body, out_shape=outs, in_specs=[pl.BlockSpec(memory_space=...]
  transfers between devices with their start and end apart: 18 -> 20, of which waited for: 10 -> 8; matrix products, arithmetic and copies ran while one was open for 0% -> 0% of each run, Pallas kernels for 0% -> 3%
where the time goes in v5:
time: 76.7 us; the launch traced here: 76.6 us
  starting transfers between devices  38.7 us (50%)
  waiting for transfers between devices  22.3 us (29%)
  Pallas kernels  15.2 us (20%)
    ppermute x20, starting transfers between devices, cycled(): lax.ppermute(array, axis, [(i, (i + step) % size) for i in range(size)])  38.7 us
    ppermute x20, waiting for transfers between devices, cycled(): lax.ppermute(array, axis, [(i, (i + step) % size) for i in range(size)])  22.3 us
    pallas_call x8, Pallas kernels, call(): pl.pallas_call(body, out_shape=outs, in_specs=[pl.BlockSpec(memory_space=...  15.2 us
  transfers between devices with their start and end apart: 20, of which 8 were waited for; matrix products, arithmetic and copies ran while one was open for 0% of the time, Pallas kernels for 3%

profile of v5, /device:TPU:1, one launch (start us, length us, event | category | flops | bytes accessed | tf_op | source)
XLA Modules:
  0.0 76.6 jit_solution(15188339733193079095)
XLA Ops:
  0.0 1.6 %shard_map.28 = (f32[9,16,512]{2,1,0:T(8,128)S(1)}, f32[9,16,512]{2,1,0:T(8,128)S(1)}, f32[13,8,512]{2,1,0:T(8,128)S(1)}, f32[13,8,512]{2,1,0:T(8,128)S(1)}, f32...) custom-call(f32[3,8,16,512]{3,2,1,0:T(8,128)} %f_in.1, s32[8,16,512]{2,1,0:T(8,128)} %ids_in.1), custom_call_target="tpu_custom_call" | custom-call | tf_op jit(solution)/shard_map/pallas_call | solution.py:554
  1.6 2.5 %collective-permute-start = (f32[9,16,512]{2,1,0:T(8,128)S(1)}, f32[9,16,512]{2,1,0:T(8,128)S(1)}, u32[]{:S(2)}, u32[]{:S(2)}) collective-permute-start(f32[9,16,512]{2,1,0:T(8,128)S(1)} %get-tuple-element.38), channel_id=1, source_target_pairs={{0,8},{8,16},{16,24},{24,32},{32,40},{40,48},{48,56},{56,64},{64,7... | collective-permute-start | bytes 884744 | tf_op jit(solution)/shard_map/ppermute | solution.py:566
  4.1 6.2 %collective-permute-start.1 = (f32[9,16,512]{2,1,0:T(8,128)S(1)}, f32[9,16,512]{2,1,0:T(8,128)S(1)}, u32[]{:S(2)}, u32[]{:S(2)}) collective-permute-start(f32[9,16,512]{2,1,0:T(8,128)S(1)} %get-tuple-element.39), channel_id=1, source_target_pairs={{0,248},{8,0},{16,8},{24,16},{32,24},{40,32},{48,40},{56,48},{64,5... | collective-permute-start | bytes 884744 | tf_op jit(solution)/shard_map/ppermute | solution.py:566
  10.4 2.1 %collective-permute-start.2 = (f32[13,8,512]{2,1,0:T(8,128)S(1)}, f32[13,8,512]{2,1,0:T(8,128)S(1)}, u32[]{:S(2)}, u32[]{:S(2)}) collective-permute-start(f32[13,8,512]{2,1,0:T(8,128)S(1)} %get-tuple-element.40), channel_id=1, source_target_pairs={{0,1},{1,2},{2,3},{3,4},{4,5},{5,6},{6,7},{7,0},{8,9},{9,10},{10,1... | collective-permute-start | bytes 638984 | tf_op jit(solution)/shard_map/ppermute | solution.py:566
  12.5 0.0 collective-permute-start.3
  12.5 4.5 %collective-permute-done.low.xlow = f32[9,16,512]{2,1,0:T(8,128)S(1)} collective-permute-done((f32[9,16,512]{2,1,0:T(8,128)S(1)}, f32[9,16,512]{2,1,0:T(8,128)S(1)}, u32[]{:S(2)}, u32[]{:S(2)}) %collective-permute-start) | collective-permute-done | bytes 294944 | tf_op jit(solution)/shard_map/ppermute | solution.py:566
  17.0 0.0 collective-permute-done.1.high.xhigh
  17.0 0.1 shard_map.29
  17.1 2.4 %collective-permute-start.4 = (f32[8,8,512]{2,1,0:T(8,128)S(1)}, f32[8,8,512]{2,1,0:T(8,128)S(1)}, u32[]{:S(2)}, u32[]{:S(2)}) collective-permute-start(f32[8,8,512]{2,1,0:T(8,128)S(1)} %get-tuple-element.42), channel_id=1, source_target_pairs={{0,1},{1,2},{2,3},{3,4},{4,5},{5,6},{6,7},{7,0},{8,9},{9,10},{10,1... | collective-permute-start | bytes 393224 | tf_op jit(solution)/shard_map/ppermute | solution.py:566
  19.5 0.0 collective-permute-start.5
  19.5 0.0 collective-permute-done.2.ylow
  19.5 0.0 collective-permute-done.3.yhigh
  19.5 1.9 %collective-permute-done.4.clow = f32[8,8,512]{2,1,0:T(8,128)S(1)} collective-permute-done((f32[8,8,512]{2,1,0:T(8,128)S(1)}, f32[8,8,512]{2,1,0:T(8,128)S(1)}, u32[]{:S(2)}, u32[]{:S(2)}) %collective-permute-start.4) | collective-permute-done | bytes 131104 | tf_op jit(solution)/shard_map/ppermute | solution.py:566
  21.5 2.4 %collective-permute-done.5.chigh = f32[8,8,512]{2,1,0:T(8,128)S(1)} collective-permute-done((f32[8,8,512]{2,1,0:T(8,128)S(1)}, f32[8,8,512]{2,1,0:T(8,128)S(1)}, u32[]{:S(2)}, u32[]{:S(2)}) %collective-permute-start.5) | collective-permute-done | bytes 131104 | tf_op jit(solution)/shard_map/ppermute | solution.py:566
  23.9 4.0 %shard_map.30 = (f32[3,10,24,512]{3,2,1,0:T(8,128)S(1)}, f32[3,12,24,512]{3,2,1,0:T(8,128)S(1)}, f32[3,12,24,512]{3,2,1,0:T(8,128)S(1)}, f32[14,24,512]{2,1,0:T(...) custom-call(f32[3,8,16,512]{3,2,1,0:T(8,128)S(1)} %get-tuple-element, ...), custom_call_target="tpu_custom_call" | custom-call | tf_op jit(solution)/shard_map/pallas_call | solution.py:554
  28.0 0.1 collective-permute-start.6
  28.0 4.9 %collective-permute-start.7 = (f32[17,8,256]{2,1,0:T(8,128)S(1)}, f32[17,8,256]{2,1,0:T(8,128)S(1)}, u32[]{:S(2)}, u32[]{:S(2)}) collective-permute-start(f32[17,8,256]{2,1,0:T(8,128)S(1)} %get-tuple-element.47), channel_id=1, source_target_pairs={{0,248},{8,0},{16,8},{24,16},{32,24},{40,32},{48,40},{56,48},{64,5... | collective-permute-start | bytes 417800 | tf_op jit(solution)/shard_map/ppermute | solution.py:566
  33.0 3.8 %collective-permute-done.6.low.xlow = f32[17,8,256]{2,1,0:T(8,128)S(1)} collective-permute-done((f32[17,8,256]{2,1,0:T(8,128)S(1)}, f32[17,8,256]{2,1,0:T(8,128)S(1)}, u32[]{:S(2)}, u32[]{:S(2)}) %collective-permute-start.6) | collective-permute-done | bytes 139296 | tf_op jit(solution)/shard_map/ppermute | solution.py:566
  36.8 0.0 collective-permute-done.7.high.xhigh
  36.8 0.1 shard_map.31
  36.9 0.3 collective-permute-start.8
  37.2 0.4 collective-permute-start.9
  37.7 0.0 collective-permute-start.18
  37.7 2.5 %collective-permute-done.8.ylow = f32[28,8,256]{2,1,0:T(8,128)S(1)} collective-permute-done((f32[28,8,256]{2,1,0:T(8,128)S(1)}, f32[28,8,256]{2,1,0:T(8,128)S(1)}, u32[]{:S(2)}, u32[]{:S(2)}) %collective-permute-start.8) | collective-permute-done | bytes 229408 | tf_op jit(solution)/shard_map/ppermute | solution.py:566
  40.2 2.8 %collective-permute-done.9.yhigh = f32[28,8,256]{2,1,0:T(8,128)S(1)} collective-permute-done((f32[28,8,256]{2,1,0:T(8,128)S(1)}, f32[28,8,256]{2,1,0:T(8,128)S(1)}, u32[]{:S(2)}, u32[]{:S(2)}) %collective-permute-start.9) | collective-permute-done | bytes 229408 | tf_op jit(solution)/shard_map/ppermute | solution.py:566
  43.0 2.1 %shard_map.32 = (f32[3,14,24,256]{3,2,1,0:T(8,128)S(1)}, f32[3,12,24,256]{3,2,1,0:T(8,128)S(1)}, f32[13,24,256]{2,1,0:T(8,128)S(1)}, f32[6,12,24,256]{3,2,1,0:T(...) custom-call(f32[3,4,8,256]{3,2,1,0:T(8,128)S(1)} %get-tuple-element., ...), custom_call_target="tpu_custom_call" | custom-call | tf_op jit(solution)/shard_map/pallas_call | solution.py:554
  45.1 0.1 collective-permute-start.10
  45.2 5.7 %collective-permute-start.12 = (f32[4,16,128]{2,1,0:T(8,128)S(1)}, f32[4,16,128]{2,1,0:T(8,128)S(1)}, u32[]{:S(2)}, u32[]{:S(2)}) collective-permute-start(f32[4,16,128]{2,1,0:T(8,128)S(1)} %get-tuple-element.53), channel_id=1, source_target_pairs={{0,240},{8,248},{16,0},{24,8},{32,16},{40,24},{48,32},{56,40},{64,... | collective-permute-start | bytes 98312 | tf_op jit(solution)/shard_map/ppermute | solution.py:566
  50.9 0.0 collective-permute-start.11
  50.9 6.6 %collective-permute-start.13 = (f32[2,16,128]{2,1,0:T(8,128)S(1)}, f32[2,16,128]{2,1,0:T(8,128)S(1)}, u32[]{:S(2)}, u32[]{:S(2)}) collective-permute-start(f32[2,16,128]{2,1,0:T(8,128)S(1)} %get-tuple-element.54), channel_id=1, source_target_pairs={{0,232},{8,240},{16,248},{24,0},{32,8},{40,16},{48,24},{56,32},{64... | collective-permute-start | bytes 49160 | tf_op jit(solution)/shard_map/ppermute | solution.py:566
  57.5 1.1 %collective-permute-done.11.low3 = f32[2,16,128]{2,1,0:T(8,128)S(1)} collective-permute-done((f32[2,16,128]{2,1,0:T(8,128)S(1)}, f32[2,16,128]{2,1,0:T(8,128)S(1)}, u32[]{:S(2)}, u32[]{:S(2)}) %collective-permute-start.11) | collective-permute-done | bytes 16416 | tf_op jit(solution)/shard_map/ppermute | solution.py:566
  58.6 0.0 collective-permute-done.13.high3
  58.6 0.0 collective-permute-done.10.low2
  58.6 0.0 collective-permute-done.12.high2
  58.6 4.0 %collective-permute-start.17 = (f32[18,16,128]{2,1,0:T(8,128)S(1)}, f32[18,16,128]{2,1,0:T(8,128)S(1)}, u32[]{:S(2)}, u32[]{:S(2)}) collective-permute-start(f32[18,16,128]{2,1,0:T(8,128)S(1)} %shard_map.33.mid), channel_id=1, source_target_pairs={{0,6},{1,7},{2,0},{3,1},{4,2},{5,3},{6,4},{7,5},{8,14},{9,15},{10,... | collective-permute-start | bytes 442376 | tf_op jit(solution)/shard_map/ppermute | solution.py:566
  62.6 0.0 collective-permute-start.16
  62.6 0.9 %collective-permute-start.15 = (f32[18,16,128]{2,1,0:T(8,128)S(1)}, f32[18,16,128]{2,1,0:T(8,128)S(1)}, u32[]{:S(2)}, u32[]{:S(2)}) collective-permute-start(f32[18,16,128]{2,1,0:T(8,128)S(1)} %shard_map.33.mid), channel_id=1, source_target_pairs={{0,2},{1,3},{2,4},{3,5},{4,6},{5,7},{6,0},{7,1},{8,10},{9,11},{10,... | collective-permute-start | bytes 442376 | tf_op jit(solution)/shard_map/ppermute | solution.py:566
  63.5 0.9 %collective-permute-start.14 = (f32[18,16,128]{2,1,0:T(8,128)S(1)}, f32[18,16,128]{2,1,0:T(8,128)S(1)}, u32[]{:S(2)}, u32[]{:S(2)}) collective-permute-start(f32[18,16,128]{2,1,0:T(8,128)S(1)} %shard_map.33.mid), channel_id=1, source_target_pairs={{0,1},{1,2},{2,3},{3,4},{4,5},{5,6},{6,7},{7,0},{8,9},{9,10},{10,1... | collective-permute-start | bytes 442376 | tf_op jit(solution)/shard_map/ppermute | solution.py:566
  64.4 0.0 collective-permute-done.18.low
  64.4 1.5 %collective-permute-start.19 = (f32[4,16,512]{2,1,0:T(8,128)S(1)}, f32[4,16,512]{2,1,0:T(8,128)S(1)}, u32[]{:S(2)}, u32[]{:S(2)}) collective-permute-start(f32[4,16,512]{2,1,0:T(8,128)S(1)} %get-tuple-element.61), channel_id=1, source_target_pairs={{0,248},{8,0},{16,8},{24,16},{32,24},{40,32},{48,40},{56,48},{64,5... | collective-permute-start | bytes 393224 | tf_op jit(solution)/shard_map/ppermute | solution.py:566
  65.9 3.2 %collective-permute-done.19.high = f32[4,16,512]{2,1,0:T(8,128)S(1)} collective-permute-done((f32[4,16,512]{2,1,0:T(8,128)S(1)}, f32[4,16,512]{2,1,0:T(8,128)S(1)}, u32[]{:S(2)}, u32[]{:S(2)}) %collective-permute-start.19) | collective-permute-done | bytes 131104 | tf_op jit(solution)/shard_map/ppermute | solution.py:566
  69.1 0.4 shard_map.34.rim
  69.5 0.0 collective-permute-done.17.yp2
  69.5 0.0 collective-permute-done.16.yp1
  69.5 0.0 collective-permute-done.15.ym2
  69.5 0.0 collective-permute-done.14.ym1
  69.5 6.9 %shard_map.35 = f32[3,8,16,512]{3,2,1,0:T(8,128)} custom-call(f32[18,16,128]{2,1,0:T(8,128)S(1)} %shard_map.33.mid, f32[18,16,128]{2,1,0:T(8,128)S(1)} %collective-permute-done.14.ym1, f32[18,16,128]{2,1,0:T(8,128)S(1)} %collective-permute-done.15.ym2, f32[18,16,128]{2,1,0:T(8,128)S(1)} %collective-permute-done.16.yp1, ...), custom_call_target="tpu_custom_call" | custom-call | tf_op jit(solution)/shard_map/pallas_call | solution.py:554
  (1 shorter events, 0.0 us)
Async XLA Ops:
  1.6 15.4 %collective-permute-start = (f32[9,16,512]{2,1,0:T(8,128)S(1)}, f32[9,16,512]{2,1,0:T(8,128)S(1)}, u32[]{:S(2)}, u32[]{:S(2)}) collective-permute-start(f32[9,16,512]{2,1,0:T(8,128)S(1)} %get-tuple-element.38), channel_id=1, source_target_pairs={{0,8},{8,16},{16,24},{24,32},{32,40},{40,48},{48,56},{56,64},{64,7... | collective-permute-start | bytes 884744 | tf_op jit(solution)/shard_map/ppermute | solution.py:566
  4.1 12.9 %collective-permute-start.1 = (f32[9,16,512]{2,1,0:T(8,128)S(1)}, f32[9,16,512]{2,1,0:T(8,128)S(1)}, u32[]{:S(2)}, u32[]{:S(2)}) collective-permute-start(f32[9,16,512]{2,1,0:T(8,128)S(1)} %get-tuple-element.39), channel_id=1, source_target_pairs={{0,248},{8,0},{16,8},{24,16},{32,24},{40,32},{48,40},{56,48},{64,5... | collective-permute-start | bytes 884744 | tf_op jit(solution)/shard_map/ppermute | solution.py:566
  10.4 9.2 %collective-permute-start.2 = (f32[13,8,512]{2,1,0:T(8,128)S(1)}, f32[13,8,512]{2,1,0:T(8,128)S(1)}, u32[]{:S(2)}, u32[]{:S(2)}) collective-permute-start(f32[13,8,512]{2,1,0:T(8,128)S(1)} %get-tuple-element.40), channel_id=1, source_target_pairs={{0,1},{1,2},{2,3},{3,4},{4,5},{5,6},{6,7},{7,0},{8,9},{9,10},{10,1... | collective-permute-start | bytes 638984 | tf_op jit(solution)/shard_map/ppermute | solution.py:566
  12.5 7.0 %collective-permute-start.3 = (f32[13,8,512]{2,1,0:T(8,128)S(1)}, f32[13,8,512]{2,1,0:T(8,128)S(1)}, u32[]{:S(2)}, u32[]{:S(2)}) collective-permute-start(f32[13,8,512]{2,1,0:T(8,128)S(1)} %get-tuple-element.41), channel_id=1, source_target_pairs={{0,7},{1,0},{2,1},{3,2},{4,3},{5,4},{6,5},{7,6},{8,15},{9,8},{10,9... | collective-permute-start | bytes 638984 | tf_op jit(solution)/shard_map/ppermute | solution.py:566
  17.1 4.4 %collective-permute-start.4 = (f32[8,8,512]{2,1,0:T(8,128)S(1)}, f32[8,8,512]{2,1,0:T(8,128)S(1)}, u32[]{:S(2)}, u32[]{:S(2)}) collective-permute-start(f32[8,8,512]{2,1,0:T(8,128)S(1)} %get-tuple-element.42), channel_id=1, source_target_pairs={{0,1},{1,2},{2,3},{3,4},{4,5},{5,6},{6,7},{7,0},{8,9},{9,10},{10,1... | collective-permute-start | bytes 393224 | tf_op jit(solution)/shard_map/ppermute | solution.py:566
  19.5 4.4 %collective-permute-start.5 = (f32[8,8,512]{2,1,0:T(8,128)S(1)}, f32[8,8,512]{2,1,0:T(8,128)S(1)}, u32[]{:S(2)}, u32[]{:S(2)}) collective-permute-start(f32[8,8,512]{2,1,0:T(8,128)S(1)} %get-tuple-element.43), channel_id=1, source_target_pairs={{0,7},{1,0},{2,1},{3,2},{4,3},{5,4},{6,5},{7,6},{8,15},{9,8},{10,9... | collective-permute-start | bytes 393224 | tf_op jit(solution)/shard_map/ppermute | solution.py:566
  28.0 8.8 %collective-permute-start.6 = (f32[17,8,256]{2,1,0:T(8,128)S(1)}, f32[17,8,256]{2,1,0:T(8,128)S(1)}, u32[]{:S(2)}, u32[]{:S(2)}) collective-permute-start(f32[17,8,256]{2,1,0:T(8,128)S(1)} %get-tuple-element.46), channel_id=1, source_target_pairs={{0,8},{8,16},{16,24},{24,32},{32,40},{40,48},{48,56},{56,64},{64,7... | collective-permute-start | bytes 417800 | tf_op jit(solution)/shard_map/ppermute | solution.py:566
  28.0 8.8 %collective-permute-start.7 = (f32[17,8,256]{2,1,0:T(8,128)S(1)}, f32[17,8,256]{2,1,0:T(8,128)S(1)}, u32[]{:S(2)}, u32[]{:S(2)}) collective-permute-start(f32[17,8,256]{2,1,0:T(8,128)S(1)} %get-tuple-element.47), channel_id=1, source_target_pairs={{0,248},{8,0},{16,8},{24,16},{32,24},{40,32},{48,40},{56,48},{64,5... | collective-permute-start | bytes 417800 | tf_op jit(solution)/shard_map/ppermute | solution.py:566
  36.9 3.3 %collective-permute-start.8 = (f32[28,8,256]{2,1,0:T(8,128)S(1)}, f32[28,8,256]{2,1,0:T(8,128)S(1)}, u32[]{:S(2)}, u32[]{:S(2)}) collective-permute-start(f32[28,8,256]{2,1,0:T(8,128)S(1)} %get-tuple-element.48), channel_id=1, source_target_pairs={{0,1},{1,2},{2,3},{3,4},{4,5},{5,6},{6,7},{7,0},{8,9},{9,10},{10,1... | collective-permute-start | bytes 688136 | tf_op jit(solution)/shard_map/ppermute | solution.py:566
  37.2 5.7 %collective-permute-start.9 = (f32[28,8,256]{2,1,0:T(8,128)S(1)}, f32[28,8,256]{2,1,0:T(8,128)S(1)}, u32[]{:S(2)}, u32[]{:S(2)}) collective-permute-start(f32[28,8,256]{2,1,0:T(8,128)S(1)} %get-tuple-element.49), channel_id=1, source_target_pairs={{0,7},{1,0},{2,1},{3,2},{4,3},{5,4},{6,5},{7,6},{8,15},{9,8},{10,9... | collective-permute-start | bytes 688136 | tf_op jit(solution)/shard_map/ppermute | solution.py:566
  37.7 26.7 %collective-permute-start.18 = (f32[4,16,512]{2,1,0:T(8,128)S(1)}, f32[4,16,512]{2,1,0:T(8,128)S(1)}, u32[]{:S(2)}, u32[]{:S(2)}) collective-permute-start(f32[4,16,512]{2,1,0:T(8,128)S(1)} %get-tuple-element.60), channel_id=1, source_target_pairs={{0,8},{8,16},{16,24},{24,32},{32,40},{40,48},{48,56},{56,64},{64,7... | collective-permute-start | bytes 393224 | tf_op jit(solution)/shard_map/ppermute | solution.py:566
  45.1 13.5 %collective-permute-start.10 = (f32[4,16,128]{2,1,0:T(8,128)S(1)}, f32[4,16,128]{2,1,0:T(8,128)S(1)}, u32[]{:S(2)}, u32[]{:S(2)}) collective-permute-start(f32[4,16,128]{2,1,0:T(8,128)S(1)} %get-tuple-element.51), channel_id=1, source_target_pairs={{0,16},{8,24},{16,32},{24,40},{32,48},{40,56},{48,64},{56,72},{64,... | collective-permute-start | bytes 98312 | tf_op jit(solution)/shard_map/ppermute | solution.py:566
  45.2 13.4 %collective-permute-start.12 = (f32[4,16,128]{2,1,0:T(8,128)S(1)}, f32[4,16,128]{2,1,0:T(8,128)S(1)}, u32[]{:S(2)}, u32[]{:S(2)}) collective-permute-start(f32[4,16,128]{2,1,0:T(8,128)S(1)} %get-tuple-element.53), channel_id=1, source_target_pairs={{0,240},{8,248},{16,0},{24,8},{32,16},{40,24},{48,32},{56,40},{64,... | collective-permute-start | bytes 98312 | tf_op jit(solution)/shard_map/ppermute | solution.py:566
  50.9 7.7 %collective-permute-start.11 = (f32[2,16,128]{2,1,0:T(8,128)S(1)}, f32[2,16,128]{2,1,0:T(8,128)S(1)}, u32[]{:S(2)}, u32[]{:S(2)}) collective-permute-start(f32[2,16,128]{2,1,0:T(8,128)S(1)} %get-tuple-element.52), channel_id=1, source_target_pairs={{0,24},{8,32},{16,40},{24,48},{32,56},{40,64},{48,72},{56,80},{64,... | collective-permute-start | bytes 49160 | tf_op jit(solution)/shard_map/ppermute | solution.py:566
  50.9 7.7 %collective-permute-start.13 = (f32[2,16,128]{2,1,0:T(8,128)S(1)}, f32[2,16,128]{2,1,0:T(8,128)S(1)}, u32[]{:S(2)}, u32[]{:S(2)}) collective-permute-start(f32[2,16,128]{2,1,0:T(8,128)S(1)} %get-tuple-element.54), channel_id=1, source_target_pairs={{0,232},{8,240},{16,248},{24,0},{32,8},{40,16},{48,24},{56,32},{64... | collective-permute-start | bytes 49160 | tf_op jit(solution)/shard_map/ppermute | solution.py:566
  58.6 10.8 %collective-permute-start.17 = (f32[18,16,128]{2,1,0:T(8,128)S(1)}, f32[18,16,128]{2,1,0:T(8,128)S(1)}, u32[]{:S(2)}, u32[]{:S(2)}) collective-permute-start(f32[18,16,128]{2,1,0:T(8,128)S(1)} %shard_map.33.mid), channel_id=1, source_target_pairs={{0,6},{1,7},{2,0},{3,1},{4,2},{5,3},{6,4},{7,5},{8,14},{9,15},{10,... | collective-permute-start | bytes 442376 | tf_op jit(solution)/shard_map/ppermute | solution.py:566
  62.6 6.9 %collective-permute-start.16 = (f32[18,16,128]{2,1,0:T(8,128)S(1)}, f32[18,16,128]{2,1,0:T(8,128)S(1)}, u32[]{:S(2)}, u32[]{:S(2)}) collective-permute-start(f32[18,16,128]{2,1,0:T(8,128)S(1)} %shard_map.33.mid), channel_id=1, source_target_pairs={{0,7},{1,0},{2,1},{3,2},{4,3},{5,4},{6,5},{7,6},{8,15},{9,8},{10,9... | collective-permute-start | bytes 442376 | tf_op jit(solution)/shard_map/ppermute | solution.py:566
  62.6 6.9 %collective-permute-start.15 = (f32[18,16,128]{2,1,0:T(8,128)S(1)}, f32[18,16,128]{2,1,0:T(8,128)S(1)}, u32[]{:S(2)}, u32[]{:S(2)}) collective-permute-start(f32[18,16,128]{2,1,0:T(8,128)S(1)} %shard_map.33.mid), channel_id=1, source_target_pairs={{0,2},{1,3},{2,4},{3,5},{4,6},{5,7},{6,0},{7,1},{8,10},{9,11},{10,... | collective-permute-start | bytes 442376 | tf_op jit(solution)/shard_map/ppermute | solution.py:566
  63.5 6.0 %collective-permute-start.14 = (f32[18,16,128]{2,1,0:T(8,128)S(1)}, f32[18,16,128]{2,1,0:T(8,128)S(1)}, u32[]{:S(2)}, u32[]{:S(2)}) collective-permute-start(f32[18,16,128]{2,1,0:T(8,128)S(1)} %shard_map.33.mid), channel_id=1, source_target_pairs={{0,1},{1,2},{2,3},{3,4},{4,5},{5,6},{6,7},{7,0},{8,9},{9,10},{10,1... | collective-permute-start | bytes 442376 | tf_op jit(solution)/shard_map/ppermute | solution.py:566
  64.4 4.7 %collective-permute-start.19 = (f32[4,16,512]{2,1,0:T(8,128)S(1)}, f32[4,16,512]{2,1,0:T(8,128)S(1)}, u32[]{:S(2)}, u32[]{:S(2)}) collective-permute-start(f32[4,16,512]{2,1,0:T(8,128)S(1)} %get-tuple-element.61), channel_id=1, source_target_pairs={{0,248},{8,0},{16,8},{24,16},{32,24},{40,32},{48,40},{56,48},{64,5... | collective-permute-start | bytes 393224 | tf_op jit(solution)/shard_map/ppermute | solution.py:566

commit v6 on v5

--- a/solution.py
+++ b/solution.py
@@ -11,7 +11,7 @@
 BF16 = jnp.bfloat16
 WEIGHT = 2.0 / 3.0
 VMEM_LIMIT = 40 * 1024 * 1024
-U0, U1, U2 = 2, 4, 16
+U0, U1, U2 = 12, 12, 16
 
 
 def materials(ids):
@@ -449,7 +449,7 @@
             far_down[t - 2, 12:16] = own[t + 2, 12:16]
 
 
-def pack_coarse_y(own, low2, low3, high2, high3, strip):
+def pack_coarse_y(own, low2, low3, high2, high3, rim, strip):
     strip[0, 0:12] = jnp.zeros((12, own.shape[-1]), F32)
     strip[17, 0:12] = jnp.zeros((12, own.shape[-1]), F32)
     for t in range(2):
@@ -599,7 +599,7 @@
     )
     low2, high2 = cycled(up, "gx", 2), cycled(down, "gx", -2)
     low3, high3 = cycled(far_up, "gx", 3), cycled(far_down, "gx", -3)
-    (strip,) = call(pack_coarse_y, [(18, 16, z2)], own, low2, low3, high2, high3)
+    (strip,) = call(pack_coarse_y, [(18, 16, z2)], own, low2, low3, high2, high3, rim)
     ym1, yp1 = cycled(strip, "gy", 1), cycled(strip, "gy", -1)
     ym2, yp2 = cycled(strip, "gy", 2), cycled(strip, "gy", -2)
     (velocity,) = call(

time: 76.7 us -> 77.1 us (level)
  starting transfers between devices: 38.7 us -> 42.8 us
  waiting for transfers between devices: 22.3 us -> 19.5 us
  Pallas kernels: 15.2 us -> 14.4 us
    ppermute x20, starting transfers between devices: 38.7 us -> 42.8 us  [cycled(): lax.ppermute(array, axis, [(i, (i + step) % size) for i in range(size)])]
    ppermute x20, waiting for transfers between devices: 22.3 us -> 19.5 us  [cycled(): lax.ppermute(array, axis, [(i, (i + step) % size) for i in range(size)])]
    pallas_call x8, Pallas kernels: 15.2 us -> 14.4 us  [call(): pl.pallas_call(body, out_shape=outs, in_specs=[pl.BlockSpec(memory_space=...]
where the time goes in v6:
time: 77.1 us; the launch traced here: 76.9 us
  starting transfers between devices  42.8 us (56%)
  waiting for transfers between devices  19.5 us (25%)
  Pallas kernels  14.4 us (19%)
    ppermute x20, starting transfers between devices, cycled(): lax.ppermute(array, axis, [(i, (i + step) % size) for i in range(size)])  42.8 us
    ppermute x20, waiting for transfers between devices, cycled(): lax.ppermute(array, axis, [(i, (i + step) % size) for i in range(size)])  19.5 us
    pallas_call x8, Pallas kernels, call(): pl.pallas_call(body, out_shape=outs, in_specs=[pl.BlockSpec(memory_space=...  14.4 us
  transfers between devices with their start and end apart: 20, of which 8 were waited for; matrix products, arithmetic and copies ran while one was open for 0% of the time, Pallas kernels for 3%

profile of v6, /device:TPU:1, one launch (start us, length us, event | category | flops | bytes accessed | tf_op | source)
XLA Modules:
  0.0 76.9 jit_solution(17340737801071733707)
XLA Ops:
  0.0 1.6 %shard_map.28 = (f32[9,16,512]{2,1,0:T(8,128)S(1)}, f32[9,16,512]{2,1,0:T(8,128)S(1)}, f32[13,8,512]{2,1,0:T(8,128)S(1)}, f32[13,8,512]{2,1,0:T(8,128)S(1)}, f32...) custom-call(f32[3,8,16,512]{3,2,1,0:T(8,128)} %f_in.1, s32[8,16,512]{2,1,0:T(8,128)} %ids_in.1), custom_call_target="tpu_custom_call" | custom-call | tf_op jit(solution)/shard_map/pallas_call | solution.py:554
  1.6 2.5 %collective-permute-start = (f32[9,16,512]{2,1,0:T(8,128)S(1)}, f32[9,16,512]{2,1,0:T(8,128)S(1)}, u32[]{:S(2)}, u32[]{:S(2)}) collective-permute-start(f32[9,16,512]{2,1,0:T(8,128)S(1)} %get-tuple-element.38), channel_id=1, source_target_pairs={{0,8},{8,16},{16,24},{24,32},{32,40},{40,48},{48,56},{56,64},{64,7... | collective-permute-start | bytes 884744 | tf_op jit(solution)/shard_map/ppermute | solution.py:566
  4.1 6.2 %collective-permute-start.1 = (f32[9,16,512]{2,1,0:T(8,128)S(1)}, f32[9,16,512]{2,1,0:T(8,128)S(1)}, u32[]{:S(2)}, u32[]{:S(2)}) collective-permute-start(f32[9,16,512]{2,1,0:T(8,128)S(1)} %get-tuple-element.39), channel_id=1, source_target_pairs={{0,248},{8,0},{16,8},{24,16},{32,24},{40,32},{48,40},{56,48},{64,5... | collective-permute-start | bytes 884744 | tf_op jit(solution)/shard_map/ppermute | solution.py:566
  10.4 2.1 %collective-permute-start.2 = (f32[13,8,512]{2,1,0:T(8,128)S(1)}, f32[13,8,512]{2,1,0:T(8,128)S(1)}, u32[]{:S(2)}, u32[]{:S(2)}) collective-permute-start(f32[13,8,512]{2,1,0:T(8,128)S(1)} %get-tuple-element.40), channel_id=1, source_target_pairs={{0,1},{1,2},{2,3},{3,4},{4,5},{5,6},{6,7},{7,0},{8,9},{9,10},{10,1... | collective-permute-start | bytes 638984 | tf_op jit(solution)/shard_map/ppermute | solution.py:566
  12.5 0.0 collective-permute-start.3
  12.5 4.5 %collective-permute-done.low.xlow = f32[9,16,512]{2,1,0:T(8,128)S(1)} collective-permute-done((f32[9,16,512]{2,1,0:T(8,128)S(1)}, f32[9,16,512]{2,1,0:T(8,128)S(1)}, u32[]{:S(2)}, u32[]{:S(2)}) %collective-permute-start) | collective-permute-done | bytes 294944 | tf_op jit(solution)/shard_map/ppermute | solution.py:566
  17.0 0.0 collective-permute-done.1.high.xhigh
  17.0 0.1 shard_map.29
  17.1 2.4 %collective-permute-start.4 = (f32[8,8,512]{2,1,0:T(8,128)S(1)}, f32[8,8,512]{2,1,0:T(8,128)S(1)}, u32[]{:S(2)}, u32[]{:S(2)}) collective-permute-start(f32[8,8,512]{2,1,0:T(8,128)S(1)} %get-tuple-element.42), channel_id=1, source_target_pairs={{0,1},{1,2},{2,3},{3,4},{4,5},{5,6},{6,7},{7,0},{8,9},{9,10},{10,1... | collective-permute-start | bytes 393224 | tf_op jit(solution)/shard_map/ppermute | solution.py:566
  19.5 0.0 collective-permute-start.5
  19.5 0.0 collective-permute-done.2.ylow
  19.5 0.0 collective-permute-done.3.yhigh
  19.5 1.9 %collective-permute-done.4.clow = f32[8,8,512]{2,1,0:T(8,128)S(1)} collective-permute-done((f32[8,8,512]{2,1,0:T(8,128)S(1)}, f32[8,8,512]{2,1,0:T(8,128)S(1)}, u32[]{:S(2)}, u32[]{:S(2)}) %collective-permute-start.4) | collective-permute-done | bytes 131104 | tf_op jit(solution)/shard_map/ppermute | solution.py:566
  21.5 2.4 %collective-permute-done.5.chigh = f32[8,8,512]{2,1,0:T(8,128)S(1)} collective-permute-done((f32[8,8,512]{2,1,0:T(8,128)S(1)}, f32[8,8,512]{2,1,0:T(8,128)S(1)}, u32[]{:S(2)}, u32[]{:S(2)}) %collective-permute-start.5) | collective-permute-done | bytes 131104 | tf_op jit(solution)/shard_map/ppermute | solution.py:566
  23.9 4.1 %shard_map.30 = (f32[3,10,24,512]{3,2,1,0:T(8,128)S(1)}, f32[3,12,24,512]{3,2,1,0:T(8,128)S(1)}, f32[3,12,24,512]{3,2,1,0:T(8,128)S(1)}, f32[14,24,512]{2,1,0:T(...) custom-call(f32[3,8,16,512]{3,2,1,0:T(8,128)S(1)} %get-tuple-element, ...), custom_call_target="tpu_custom_call" | custom-call | tf_op jit(solution)/shard_map/pallas_call | solution.py:554
  28.0 0.1 collective-permute-start.6
  28.1 4.9 %collective-permute-start.7 = (f32[17,8,256]{2,1,0:T(8,128)S(1)}, f32[17,8,256]{2,1,0:T(8,128)S(1)}, u32[]{:S(2)}, u32[]{:S(2)}) collective-permute-start(f32[17,8,256]{2,1,0:T(8,128)S(1)} %get-tuple-element.47), channel_id=1, source_target_pairs={{0,248},{8,0},{16,8},{24,16},{32,24},{40,32},{48,40},{56,48},{64,5... | collective-permute-start | bytes 417800 | tf_op jit(solution)/shard_map/ppermute | solution.py:566
  33.0 3.8 %collective-permute-done.6.low.xlow = f32[17,8,256]{2,1,0:T(8,128)S(1)} collective-permute-done((f32[17,8,256]{2,1,0:T(8,128)S(1)}, f32[17,8,256]{2,1,0:T(8,128)S(1)}, u32[]{:S(2)}, u32[]{:S(2)}) %collective-permute-start.6) | collective-permute-done | bytes 139296 | tf_op jit(solution)/shard_map/ppermute | solution.py:566
  36.9 0.0 collective-permute-done.7.high.xhigh
  36.9 0.1 shard_map.31
  37.0 0.3 collective-permute-start.8
  37.3 0.4 collective-permute-start.9
  37.7 0.0 collective-permute-start.14
  37.7 4.9 %collective-permute-start.15 = (f32[4,16,512]{2,1,0:T(8,128)S(1)}, f32[4,16,512]{2,1,0:T(8,128)S(1)}, u32[]{:S(2)}, u32[]{:S(2)}) collective-permute-start(f32[4,16,512]{2,1,0:T(8,128)S(1)} %get-tuple-element.56), channel_id=1, source_target_pairs={{0,248},{8,0},{16,8},{24,16},{32,24},{40,32},{48,40},{56,48},{64,5... | collective-permute-start | bytes 393224 | tf_op jit(solution)/shard_map/ppermute | solution.py:566
  42.6 0.0 collective-permute-done.8.ylow
  42.6 0.4 collective-permute-done.9.yhigh
  43.0 1.9 %shard_map.32 = (f32[3,14,24,256]{3,2,1,0:T(8,128)S(1)}, f32[3,12,24,256]{3,2,1,0:T(8,128)S(1)}, f32[13,24,256]{2,1,0:T(8,128)S(1)}, f32[6,12,24,256]{3,2,1,0:T(...) custom-call(f32[3,4,8,256]{3,2,1,0:T(8,128)S(1)} %get-tuple-element., ...), custom_call_target="tpu_custom_call" | custom-call | tf_op jit(solution)/shard_map/pallas_call | solution.py:554
  45.0 0.1 collective-permute-start.10
  45.1 5.7 %collective-permute-start.12 = (f32[4,16,128]{2,1,0:T(8,128)S(1)}, f32[4,16,128]{2,1,0:T(8,128)S(1)}, u32[]{:S(2)}, u32[]{:S(2)}) collective-permute-start(f32[4,16,128]{2,1,0:T(8,128)S(1)} %get-tuple-element.53), channel_id=1, source_target_pairs={{0,240},{8,248},{16,0},{24,8},{32,16},{40,24},{48,32},{56,40},{64,... | collective-permute-start | bytes 98312 | tf_op jit(solution)/shard_map/ppermute | solution.py:566
  50.8 0.0 collective-permute-start.11
  50.8 0.0 collective-permute-done.14.low
  50.8 6.6 %collective-permute-start.13 = (f32[2,16,128]{2,1,0:T(8,128)S(1)}, f32[2,16,128]{2,1,0:T(8,128)S(1)}, u32[]{:S(2)}, u32[]{:S(2)}) collective-permute-start(f32[2,16,128]{2,1,0:T(8,128)S(1)} %get-tuple-element.54), channel_id=1, source_target_pairs={{0,232},{8,240},{16,248},{24,0},{32,8},{40,16},{48,24},{56,32},{64... | collective-permute-start | bytes 49160 | tf_op jit(solution)/shard_map/ppermute | solution.py:566
  57.3 0.0 collective-permute-done.15.high
  57.3 0.4 shard_map.33.rim
  57.7 0.8 %collective-permute-done.11.low3 = f32[2,16,128]{2,1,0:T(8,128)S(1)} collective-permute-done((f32[2,16,128]{2,1,0:T(8,128)S(1)}, f32[2,16,128]{2,1,0:T(8,128)S(1)}, u32[]{:S(2)}, u32[]{:S(2)}) %collective-permute-start.11) | collective-permute-done | bytes 16416 | tf_op jit(solution)/shard_map/ppermute | solution.py:566
  58.5 0.0 collective-permute-done.13.high3
  58.5 0.0 collective-permute-done.10.low2
  58.5 0.0 collective-permute-done.12.high2
  58.6 3.9 %collective-permute-start.19 = (f32[18,16,128]{2,1,0:T(8,128)S(1)}, f32[18,16,128]{2,1,0:T(8,128)S(1)}, u32[]{:S(2)}, u32[]{:S(2)}) collective-permute-start(f32[18,16,128]{2,1,0:T(8,128)S(1)} %shard_map.34.mid), channel_id=1, source_target_pairs={{0,6},{1,7},{2,0},{3,1},{4,2},{5,3},{6,4},{7,5},{8,14},{9,15},{10,... | collective-permute-start | bytes 442376 | tf_op jit(solution)/shard_map/ppermute | solution.py:566
  62.5 1.4 %collective-permute-start.18 = (f32[18,16,128]{2,1,0:T(8,128)S(1)}, f32[18,16,128]{2,1,0:T(8,128)S(1)}, u32[]{:S(2)}, u32[]{:S(2)}) collective-permute-start(f32[18,16,128]{2,1,0:T(8,128)S(1)} %shard_map.34.mid), channel_id=1, source_target_pairs={{0,7},{1,0},{2,1},{3,2},{4,3},{5,4},{6,5},{7,6},{8,15},{9,8},{10,9... | collective-permute-start | bytes 442376 | tf_op jit(solution)/shard_map/ppermute | solution.py:566
  63.9 1.1 %collective-permute-start.17 = (f32[18,16,128]{2,1,0:T(8,128)S(1)}, f32[18,16,128]{2,1,0:T(8,128)S(1)}, u32[]{:S(2)}, u32[]{:S(2)}) collective-permute-start(f32[18,16,128]{2,1,0:T(8,128)S(1)} %shard_map.34.mid), channel_id=1, source_target_pairs={{0,2},{1,3},{2,4},{3,5},{4,6},{5,7},{6,0},{7,1},{8,10},{9,11},{10,... | collective-permute-start | bytes 442376 | tf_op jit(solution)/shard_map/ppermute | solution.py:566
  65.0 0.0 collective-permute-start.16
  65.0 0.0 collective-permute-done.19.yp2
  65.0 4.6 %collective-permute-done.18.yp1 = f32[18,16,128]{2,1,0:T(8,128)S(1)} collective-permute-done((f32[18,16,128]{2,1,0:T(8,128)S(1)}, f32[18,16,128]{2,1,0:T(8,128)S(1)}, u32[]{:S(2)}, u32[]{:S(2)}) %collective-permute-start.18) | collective-permute-done | bytes 147488 | tf_op jit(solution)/shard_map/ppermute | solution.py:566
  69.6 1.0 %collective-permute-done.17.ym2 = f32[18,16,128]{2,1,0:T(8,128)S(1)} collective-permute-done((f32[18,16,128]{2,1,0:T(8,128)S(1)}, f32[18,16,128]{2,1,0:T(8,128)S(1)}, u32[]{:S(2)}, u32[]{:S(2)}) %collective-permute-start.17) | collective-permute-done | bytes 147488 | tf_op jit(solution)/shard_map/ppermute | solution.py:566
  70.6 0.0 collective-permute-done.16.ym1
  70.6 6.2 %shard_map.35 = f32[3,8,16,512]{3,2,1,0:T(8,128)} custom-call(f32[18,16,128]{2,1,0:T(8,128)S(1)} %shard_map.34.mid, f32[18,16,128]{2,1,0:T(8,128)S(1)} %collective-permute-done.16.ym1, f32[18,16,128]{2,1,0:T(8,128)S(1)} %collective-permute-done.17.ym2, f32[18,16,128]{2,1,0:T(8,128)S(1)} %collective-permute-done.18.yp1, ...), custom_call_target="tpu_custom_call" | custom-call | tf_op jit(solution)/shard_map/pallas_call | solution.py:554
  (1 shorter events, 0.0 us)
Async XLA Ops:
  1.6 15.4 %collective-permute-start = (f32[9,16,512]{2,1,0:T(8,128)S(1)}, f32[9,16,512]{2,1,0:T(8,128)S(1)}, u32[]{:S(2)}, u32[]{:S(2)}) collective-permute-start(f32[9,16,512]{2,1,0:T(8,128)S(1)} %get-tuple-element.38), channel_id=1, source_target_pairs={{0,8},{8,16},{16,24},{24,32},{32,40},{40,48},{48,56},{56,64},{64,7... | collective-permute-start | bytes 884744 | tf_op jit(solution)/shard_map/ppermute | solution.py:566
  4.1 12.9 %collective-permute-start.1 = (f32[9,16,512]{2,1,0:T(8,128)S(1)}, f32[9,16,512]{2,1,0:T(8,128)S(1)}, u32[]{:S(2)}, u32[]{:S(2)}) collective-permute-start(f32[9,16,512]{2,1,0:T(8,128)S(1)} %get-tuple-element.39), channel_id=1, source_target_pairs={{0,248},{8,0},{16,8},{24,16},{32,24},{40,32},{48,40},{56,48},{64,5... | collective-permute-start | bytes 884744 | tf_op jit(solution)/shard_map/ppermute | solution.py:566
  10.4 9.2 %collective-permute-start.2 = (f32[13,8,512]{2,1,0:T(8,128)S(1)}, f32[13,8,512]{2,1,0:T(8,128)S(1)}, u32[]{:S(2)}, u32[]{:S(2)}) collective-permute-start(f32[13,8,512]{2,1,0:T(8,128)S(1)} %get-tuple-element.40), channel_id=1, source_target_pairs={{0,1},{1,2},{2,3},{3,4},{4,5},{5,6},{6,7},{7,0},{8,9},{9,10},{10,1... | collective-permute-start | bytes 638984 | tf_op jit(solution)/shard_map/ppermute | solution.py:566
  12.5 7.0 %collective-permute-start.3 = (f32[13,8,512]{2,1,0:T(8,128)S(1)}, f32[13,8,512]{2,1,0:T(8,128)S(1)}, u32[]{:S(2)}, u32[]{:S(2)}) collective-permute-start(f32[13,8,512]{2,1,0:T(8,128)S(1)} %get-tuple-element.41), channel_id=1, source_target_pairs={{0,7},{1,0},{2,1},{3,2},{4,3},{5,4},{6,5},{7,6},{8,15},{9,8},{10,9... | collective-permute-start | bytes 638984 | tf_op jit(solution)/shard_map/ppermute | solution.py:566
  17.1 4.4 %collective-permute-start.4 = (f32[8,8,512]{2,1,0:T(8,128)S(1)}, f32[8,8,512]{2,1,0:T(8,128)S(1)}, u32[]{:S(2)}, u32[]{:S(2)}) collective-permute-start(f32[8,8,512]{2,1,0:T(8,128)S(1)} %get-tuple-element.42), channel_id=1, source_target_pairs={{0,1},{1,2},{2,3},{3,4},{4,5},{5,6},{6,7},{7,0},{8,9},{9,10},{10,1... | collective-permute-start | bytes 393224 | tf_op jit(solution)/shard_map/ppermute | solution.py:566
  19.5 4.4 %collective-permute-start.5 = (f32[8,8,512]{2,1,0:T(8,128)S(1)}, f32[8,8,512]{2,1,0:T(8,128)S(1)}, u32[]{:S(2)}, u32[]{:S(2)}) collective-permute-start(f32[8,8,512]{2,1,0:T(8,128)S(1)} %get-tuple-element.43), channel_id=1, source_target_pairs={{0,7},{1,0},{2,1},{3,2},{4,3},{5,4},{6,5},{7,6},{8,15},{9,8},{10,9... | collective-permute-start | bytes 393224 | tf_op jit(solution)/shard_map/ppermute | solution.py:566
  28.0 8.8 %collective-permute-start.6 = (f32[17,8,256]{2,1,0:T(8,128)S(1)}, f32[17,8,256]{2,1,0:T(8,128)S(1)}, u32[]{:S(2)}, u32[]{:S(2)}) collective-permute-start(f32[17,8,256]{2,1,0:T(8,128)S(1)} %get-tuple-element.46), channel_id=1, source_target_pairs={{0,8},{8,16},{16,24},{24,32},{32,40},{40,48},{48,56},{56,64},{64,7... | collective-permute-start | bytes 417800 | tf_op jit(solution)/shard_map/ppermute | solution.py:566
  28.1 8.8 %collective-permute-start.7 = (f32[17,8,256]{2,1,0:T(8,128)S(1)}, f32[17,8,256]{2,1,0:T(8,128)S(1)}, u32[]{:S(2)}, u32[]{:S(2)}) collective-permute-start(f32[17,8,256]{2,1,0:T(8,128)S(1)} %get-tuple-element.47), channel_id=1, source_target_pairs={{0,248},{8,0},{16,8},{24,16},{32,24},{40,32},{48,40},{56,48},{64,5... | collective-permute-start | bytes 417800 | tf_op jit(solution)/shard_map/ppermute | solution.py:566
  37.0 5.6 %collective-permute-start.8 = (f32[28,8,256]{2,1,0:T(8,128)S(1)}, f32[28,8,256]{2,1,0:T(8,128)S(1)}, u32[]{:S(2)}, u32[]{:S(2)}) collective-permute-start(f32[28,8,256]{2,1,0:T(8,128)S(1)} %get-tuple-element.48), channel_id=1, source_target_pairs={{0,1},{1,2},{2,3},{3,4},{4,5},{5,6},{6,7},{7,0},{8,9},{9,10},{10,1... | collective-permute-start | bytes 688136 | tf_op jit(solution)/shard_map/ppermute | solution.py:566
  37.3 5.7 %collective-permute-start.9 = (f32[28,8,256]{2,1,0:T(8,128)S(1)}, f32[28,8,256]{2,1,0:T(8,128)S(1)}, u32[]{:S(2)}, u32[]{:S(2)}) collective-permute-start(f32[28,8,256]{2,1,0:T(8,128)S(1)} %get-tuple-element.49), channel_id=1, source_target_pairs={{0,7},{1,0},{2,1},{3,2},{4,3},{5,4},{6,5},{7,6},{8,15},{9,8},{10,9... | collective-permute-start | bytes 688136 | tf_op jit(solution)/shard_map/ppermute | solution.py:566
  37.7 13.0 %collective-permute-start.14 = (f32[4,16,512]{2,1,0:T(8,128)S(1)}, f32[4,16,512]{2,1,0:T(8,128)S(1)}, u32[]{:S(2)}, u32[]{:S(2)}) collective-permute-start(f32[4,16,512]{2,1,0:T(8,128)S(1)} %get-tuple-element.55), channel_id=1, source_target_pairs={{0,8},{8,16},{16,24},{24,32},{32,40},{40,48},{48,56},{56,64},{64,7... | collective-permute-start | bytes 393224 | tf_op jit(solution)/shard_map/ppermute | solution.py:566
  37.7 19.6 %collective-permute-start.15 = (f32[4,16,512]{2,1,0:T(8,128)S(1)}, f32[4,16,512]{2,1,0:T(8,128)S(1)}, u32[]{:S(2)}, u32[]{:S(2)}) collective-permute-start(f32[4,16,512]{2,1,0:T(8,128)S(1)} %get-tuple-element.56), channel_id=1, source_target_pairs={{0,248},{8,0},{16,8},{24,16},{32,24},{40,32},{48,40},{56,48},{64,5... | collective-permute-start | bytes 393224 | tf_op jit(solution)/shard_map/ppermute | solution.py:566
  45.0 13.5 %collective-permute-start.10 = (f32[4,16,128]{2,1,0:T(8,128)S(1)}, f32[4,16,128]{2,1,0:T(8,128)S(1)}, u32[]{:S(2)}, u32[]{:S(2)}) collective-permute-start(f32[4,16,128]{2,1,0:T(8,128)S(1)} %get-tuple-element.51), channel_id=1, source_target_pairs={{0,16},{8,24},{16,32},{24,40},{32,48},{40,56},{48,64},{56,72},{64,... | collective-permute-start | bytes 98312 | tf_op jit(solution)/shard_map/ppermute | solution.py:566
  45.1 13.4 %collective-permute-start.12 = (f32[4,16,128]{2,1,0:T(8,128)S(1)}, f32[4,16,128]{2,1,0:T(8,128)S(1)}, u32[]{:S(2)}, u32[]{:S(2)}) collective-permute-start(f32[4,16,128]{2,1,0:T(8,128)S(1)} %get-tuple-element.53), channel_id=1, source_target_pairs={{0,240},{8,248},{16,0},{24,8},{32,16},{40,24},{48,32},{56,40},{64,... | collective-permute-start | bytes 98312 | tf_op jit(solution)/shard_map/ppermute | solution.py:566
  50.8 7.8 %collective-permute-start.11 = (f32[2,16,128]{2,1,0:T(8,128)S(1)}, f32[2,16,128]{2,1,0:T(8,128)S(1)}, u32[]{:S(2)}, u32[]{:S(2)}) collective-permute-start(f32[2,16,128]{2,1,0:T(8,128)S(1)} %get-tuple-element.52), channel_id=1, source_target_pairs={{0,24},{8,32},{16,40},{24,48},{32,56},{40,64},{48,72},{56,80},{64,... | collective-permute-start | bytes 49160 | tf_op jit(solution)/shard_map/ppermute | solution.py:566
  50.8 7.8 %collective-permute-start.13 = (f32[2,16,128]{2,1,0:T(8,128)S(1)}, f32[2,16,128]{2,1,0:T(8,128)S(1)}, u32[]{:S(2)}, u32[]{:S(2)}) collective-permute-start(f32[2,16,128]{2,1,0:T(8,128)S(1)} %get-tuple-element.54), channel_id=1, source_target_pairs={{0,232},{8,240},{16,248},{24,0},{32,8},{40,16},{48,24},{56,32},{64... | collective-permute-start | bytes 49160 | tf_op jit(solution)/shard_map/ppermute | solution.py:566
  58.6 6.5 %collective-permute-start.19 = (f32[18,16,128]{2,1,0:T(8,128)S(1)}, f32[18,16,128]{2,1,0:T(8,128)S(1)}, u32[]{:S(2)}, u32[]{:S(2)}) collective-permute-start(f32[18,16,128]{2,1,0:T(8,128)S(1)} %shard_map.34.mid), channel_id=1, source_target_pairs={{0,6},{1,7},{2,0},{3,1},{4,2},{5,3},{6,4},{7,5},{8,14},{9,15},{10,... | collective-permute-start | bytes 442376 | tf_op jit(solution)/shard_map/ppermute | solution.py:566
  62.5 7.1 %collective-permute-start.18 = (f32[18,16,128]{2,1,0:T(8,128)S(1)}, f32[18,16,128]{2,1,0:T(8,128)S(1)}, u32[]{:S(2)}, u32[]{:S(2)}) collective-permute-start(f32[18,16,128]{2,1,0:T(8,128)S(1)} %shard_map.34.mid), channel_id=1, source_target_pairs={{0,7},{1,0},{2,1},{3,2},{4,3},{5,4},{6,5},{7,6},{8,15},{9,8},{10,9... | collective-permute-start | bytes 442376 | tf_op jit(solution)/shard_map/ppermute | solution.py:566
  63.9 6.7 %collective-permute-start.17 = (f32[18,16,128]{2,1,0:T(8,128)S(1)}, f32[18,16,128]{2,1,0:T(8,128)S(1)}, u32[]{:S(2)}, u32[]{:S(2)}) collective-permute-start(f32[18,16,128]{2,1,0:T(8,128)S(1)} %shard_map.34.mid), channel_id=1, source_target_pairs={{0,2},{1,3},{2,4},{3,5},{4,6},{5,7},{6,0},{7,1},{8,10},{9,11},{10,... | collective-permute-start | bytes 442376 | tf_op jit(solution)/shard_map/ppermute | solution.py:566
  65.0 5.6 %collective-permute-start.16 = (f32[18,16,128]{2,1,0:T(8,128)S(1)}, f32[18,16,128]{2,1,0:T(8,128)S(1)}, u32[]{:S(2)}, u32[]{:S(2)}) collective-permute-start(f32[18,16,128]{2,1,0:T(8,128)S(1)} %shard_map.34.mid), channel_id=1, source_target_pairs={{0,1},{1,2},{2,3},{3,4},{4,5},{5,6},{6,7},{7,0},{8,9},{9,10},{10,1... | collective-permute-start | bytes 442376 | tf_op jit(solution)/shard_map/ppermute | solution.py:566

commit v7 on v5

--- a/solution.py
+++ b/solution.py
@@ -11,7 +11,7 @@
 BF16 = jnp.bfloat16
 WEIGHT = 2.0 / 3.0
 VMEM_LIMIT = 40 * 1024 * 1024
-U0, U1, U2 = 2, 4, 16
+U0, U1, U2 = 12, 12, 16
 
 
 def materials(ids):
@@ -149,23 +149,37 @@
     return g[comp, x + go] - cf[DG, x + co] * here + total
 
 
-def pack_fine(f_in, ids_in, xup, xdown, yup, ydown, f, ids, arrived):
-    copies = [pltpu.make_async_copy(ids_in.at[x : x + 2], ids.at[x : x + 2], arrived.at[8 + x // 2]) for x in (0, 2, 4, 6)]
-    copies += [pltpu.make_async_copy(f_in.at[:, x], f.at[:, x], arrived.at[x]) for x in range(8)]
+def copied(copies):
     for copy in copies:
         copy.start()
     for copy in copies:
         copy.wait()
-    for c in range(3):
-        for k in range(2):
-            xup[2 * c + k] = f[c, 6 + k]
-            xdown[2 * c + k] = f[c, k]
+
+
+def pack_fine_x(f_in, ids_in, xup, xdown, f, ids, arrived):
+    copied(
+        [pltpu.make_async_copy(ids_in.at[5 * k : 5 * k + 3], ids.at[3 * k : 3 * k + 3], arrived.at[k]) for k in range(2)]
+        + [
+            pltpu.make_async_copy(f_in.at[:, 6 * k + n], f.at[:, 2 * k + n], arrived.at[2 + 2 * k + n])
+            for k in range(2)
+            for n in range(2)
+        ]
+    )
+    for n, out in enumerate((xdown, xup)):
+        for c in range(3):
+            for k in range(2):
+                out[2 * c + k] = f[c, 2 * n + k]
+        for k in range(3):
+            out[6 + k] = materials(ids[3 * n + k])
+
+
+def pack_fine_y(f_in, ids_in, yup, ydown, f, ids, arrived):
+    copied(
+        [pltpu.make_async_copy(ids_in.at[x : x + 2], ids.at[x : x + 2], arrived.at[8 + x // 2]) for x in (0, 2, 4, 6)]
+        + [pltpu.make_async_copy(f_in.at[:, x], f.at[:, x], arrived.at[x]) for x in range(8)]
+    )
     for x in range(8):
         eta = materials(ids[x])
-        if x < 3:
-            xdown[6 + x] = eta
-        if x > 4:
-            xup[6 + x - 5] = eta
         for out, at, eta_at in ((yup, 13, 12), (ydown, 0, 0)):
             pack_rows(out, x, 8, [f[c, x, at : at + 3] for c in range(3)])
             put_eta_rows(out, 9, x, eta[eta_at : eta_at + 4])
@@ -546,9 +560,13 @@
         pltpu.make_async_copy(result.at[:, x], out.at[:, x], sent.at[x]).wait()
 
 
+def typed(shape):
+    return shape if isinstance(shape, jax.ShapeDtypeStruct) else jax.ShapeDtypeStruct(shape, F32)
+
+
 def call(body, outs, *args, scratch=(), copies=0, where_in=pltpu.VMEM, where_out=pltpu.VMEM):
-    outs = [out if isinstance(out, jax.ShapeDtypeStruct) else jax.ShapeDtypeStruct(out, F32) for out in outs]
-    scratch_shapes = [pltpu.VMEM(shape, F32) for shape in scratch]
+    outs = [typed(out) for out in outs]
+    scratch_shapes = [pltpu.VMEM(typed(shape).shape, typed(shape).dtype) for shape in scratch]
     if copies:
         scratch_shapes.append(pltpu.SemaphoreType.DMA((copies,)))
     return pl.pallas_call(
@@ -569,10 +587,15 @@
 def per_device(forcing, phase_ids):
     z0 = forcing.shape[-1]
     z1, z2 = z0 // 2, z0 // 4
-    xup, xdown, yup, ydown, f0, ids0 = call(
-        pack_fine,
-        [(9, 16, z0)] * 2 + [(13, 8, z0)] * 2 + [forcing.shape, jax.ShapeDtypeStruct(phase_ids.shape, jnp.int32)],
-        *(pltpu.with_memory_space_constraint(a, pltpu.HBM) for a in (forcing, phase_ids)), copies=12, where_in=pltpu.HBM,
+    inputs = [pltpu.with_memory_space_constraint(a, pltpu.HBM) for a in (forcing, phase_ids)]
+    xup, xdown = call(
+        pack_fine_x, [(9, 16, z0)] * 2, *inputs,
+        scratch=[(3, 4, 16, z0), jax.ShapeDtypeStruct((6, 16, z0), jnp.int32)], copies=6, where_in=pltpu.HBM,
+    )
+    yup, ydown, f0, ids0 = call(
+        pack_fine_y,
+        [(13, 8, z0)] * 2 + [forcing.shape, jax.ShapeDtypeStruct(phase_ids.shape, jnp.int32)],
+        *inputs, copies=12, where_in=pltpu.HBM,
     )
     xlow, xhigh = cycled(xup, "gx", 1), cycled(xdown, "gx", -1)
     ylow, yhigh = cycled(yup, "gy", 1), cycled(ydown, "gy", -1)

time: 76.7 us -> 75.6 us (0.986)
  waiting for transfers between devices: 22.3 us -> 20.8 us
    ppermute x20, waiting for transfers between devices: 22.3 us -> 20.8 us  [cycled(): lax.ppermute(array, axis, [(i, (i + step) % size) for i in range(size)])]
    pallas_call x8 -> x9, Pallas kernels: 15.2 us -> 15.6 us  [call(): pl.pallas_call(body, out_shape=outs, in_specs=[pl.BlockSpec(memory_space=...]
  transfers between devices with their start and end apart: 20 -> 20, of which waited for: 8 -> 8; matrix products, arithmetic and copies ran while one was open for 0% -> 0% of each run, Pallas kernels for 3% -> 5%
where the time goes in v7:
time: 75.6 us; the launch traced here: 75.4 us
  starting transfers between devices  38.7 us (51%)
  waiting for transfers between devices  20.8 us (28%)
  Pallas kernels  15.6 us (21%)
    ppermute x20, starting transfers between devices, cycled(): lax.ppermute(array, axis, [(i, (i + step) % size) for i in range(size)])  38.7 us
    ppermute x20, waiting for transfers between devices, cycled(): lax.ppermute(array, axis, [(i, (i + step) % size) for i in range(size)])  20.8 us
    pallas_call x9, Pallas kernels, call(): pl.pallas_call(body, out_shape=outs, in_specs=[pl.BlockSpec(memory_space=...  15.6 us
  transfers between devices with their start and end apart: 20, of which 8 were waited for; matrix products, arithmetic and copies ran while one was open for 0% of the time, Pallas kernels for 5%

profile of v7, /device:TPU:1, one launch (start us, length us, event | category | flops | bytes accessed | tf_op | source)
XLA Modules:
  0.0 75.4 jit_solution(12315425869599714412)
XLA Ops:
  0.0 1.3 %shard_map.29 = (f32[9,16,512]{2,1,0:T(8,128)S(1)}, f32[9,16,512]{2,1,0:T(8,128)S(1)}) custom-call(f32[3,8,16,512]{3,2,1,0:T(8,128)} %f_in.3, s32[8,16,512]{2,1,0:T(8,128)} %ids_in.3), custom_call_target="tpu_custom_call" | custom-call | tf_op jit(solution)/shard_map/pallas_call | solution.py:572
  1.3 2.5 %collective-permute-start = (f32[9,16,512]{2,1,0:T(8,128)S(1)}, f32[9,16,512]{2,1,0:T(8,128)S(1)}, u32[]{:S(2)}, u32[]{:S(2)}) collective-permute-start(f32[9,16,512]{2,1,0:T(8,128)S(1)} %get-tuple-element.38), channel_id=1, source_target_pairs={{0,8},{8,16},{16,24},{24,32},{32,40},{40,48},{48,56},{56,64},{64,7... | collective-permute-start | bytes 884744 | tf_op jit(solution)/shard_map/ppermute | solution.py:584
  3.8 6.2 %collective-permute-start.1 = (f32[9,16,512]{2,1,0:T(8,128)S(1)}, f32[9,16,512]{2,1,0:T(8,128)S(1)}, u32[]{:S(2)}, u32[]{:S(2)}) collective-permute-start(f32[9,16,512]{2,1,0:T(8,128)S(1)} %get-tuple-element.39), channel_id=1, source_target_pairs={{0,248},{8,0},{16,8},{24,16},{32,24},{40,32},{48,40},{56,48},{64,5... | collective-permute-start | bytes 884744 | tf_op jit(solution)/shard_map/ppermute | solution.py:584
  10.0 1.6 %shard_map.28 = (f32[13,8,512]{2,1,0:T(8,128)S(1)}, f32[13,8,512]{2,1,0:T(8,128)S(1)}, f32[3,8,16,512]{3,2,1,0:T(8,128)S(1)}, s32[8,16,512]{2,1,0:T(8,128)S(1)}) custom-call(f32[3,8,16,512]{3,2,1,0:T(8,128)} %f_in.3, s32[8,16,512]{2,1,0:T(8,128)} %ids_in.3), custom_call_target="tpu_custom_call" | custom-call | tf_op jit(solution)/shard_map/pallas_call | solution.py:572
  11.6 2.1 %collective-permute-start.2 = (f32[13,8,512]{2,1,0:T(8,128)S(1)}, f32[13,8,512]{2,1,0:T(8,128)S(1)}, u32[]{:S(2)}, u32[]{:S(2)}) collective-permute-start(f32[13,8,512]{2,1,0:T(8,128)S(1)} %get-tuple-element.40), channel_id=1, source_target_pairs={{0,1},{1,2},{2,3},{3,4},{4,5},{5,6},{6,7},{7,0},{8,9},{9,10},{10,1... | collective-permute-start | bytes 638984 | tf_op jit(solution)/shard_map/ppermute | solution.py:584
  13.8 0.0 collective-permute-start.3
  13.8 2.9 %collective-permute-done.low.xlow = f32[9,16,512]{2,1,0:T(8,128)S(1)} collective-permute-done((f32[9,16,512]{2,1,0:T(8,128)S(1)}, f32[9,16,512]{2,1,0:T(8,128)S(1)}, u32[]{:S(2)}, u32[]{:S(2)}) %collective-permute-start) | collective-permute-done | bytes 294944 | tf_op jit(solution)/shard_map/ppermute | solution.py:584
  16.7 0.0 collective-permute-done.1.high.xhigh
  16.7 0.1 shard_map.30
  16.8 2.4 %collective-permute-start.4 = (f32[8,8,512]{2,1,0:T(8,128)S(1)}, f32[8,8,512]{2,1,0:T(8,128)S(1)}, u32[]{:S(2)}, u32[]{:S(2)}) collective-permute-start(f32[8,8,512]{2,1,0:T(8,128)S(1)} %get-tuple-element.42), channel_id=1, source_target_pairs={{0,1},{1,2},{2,3},{3,4},{4,5},{5,6},{6,7},{7,0},{8,9},{9,10},{10,1... | collective-permute-start | bytes 393224 | tf_op jit(solution)/shard_map/ppermute | solution.py:584
  19.2 0.0 collective-permute-start.5
  19.2 0.0 collective-permute-done.2.ylow
  19.2 0.0 collective-permute-done.3.yhigh
  19.2 1.9 %collective-permute-done.4.clow = f32[8,8,512]{2,1,0:T(8,128)S(1)} collective-permute-done((f32[8,8,512]{2,1,0:T(8,128)S(1)}, f32[8,8,512]{2,1,0:T(8,128)S(1)}, u32[]{:S(2)}, u32[]{:S(2)}) %collective-permute-start.4) | collective-permute-done | bytes 131104 | tf_op jit(solution)/shard_map/ppermute | solution.py:584
  21.1 2.4 %collective-permute-done.5.chigh = f32[8,8,512]{2,1,0:T(8,128)S(1)} collective-permute-done((f32[8,8,512]{2,1,0:T(8,128)S(1)}, f32[8,8,512]{2,1,0:T(8,128)S(1)}, u32[]{:S(2)}, u32[]{:S(2)}) %collective-permute-start.5) | collective-permute-done | bytes 131104 | tf_op jit(solution)/shard_map/ppermute | solution.py:584
  23.6 4.1 %shard_map.31 = (f32[3,10,24,512]{3,2,1,0:T(8,128)S(1)}, f32[3,12,24,512]{3,2,1,0:T(8,128)S(1)}, f32[3,12,24,512]{3,2,1,0:T(8,128)S(1)}, f32[14,24,512]{2,1,0:T(...) custom-call(f32[3,8,16,512]{3,2,1,0:T(8,128)S(1)} %get-tuple-element, ...), custom_call_target="tpu_custom_call" | custom-call | tf_op jit(solution)/shard_map/pallas_call | solution.py:572
  27.7 0.1 collective-permute-start.6
  27.8 4.9 %collective-permute-start.7 = (f32[17,8,256]{2,1,0:T(8,128)S(1)}, f32[17,8,256]{2,1,0:T(8,128)S(1)}, u32[]{:S(2)}, u32[]{:S(2)}) collective-permute-start(f32[17,8,256]{2,1,0:T(8,128)S(1)} %get-tuple-element.47), channel_id=1, source_target_pairs={{0,248},{8,0},{16,8},{24,16},{32,24},{40,32},{48,40},{56,48},{64,5... | collective-permute-start | bytes 417800 | tf_op jit(solution)/shard_map/ppermute | solution.py:584
  32.7 3.8 %collective-permute-done.6.low.xlow = f32[17,8,256]{2,1,0:T(8,128)S(1)} collective-permute-done((f32[17,8,256]{2,1,0:T(8,128)S(1)}, f32[17,8,256]{2,1,0:T(8,128)S(1)}, u32[]{:S(2)}, u32[]{:S(2)}) %collective-permute-start.6) | collective-permute-done | bytes 139296 | tf_op jit(solution)/shard_map/ppermute | solution.py:584
  36.5 0.0 collective-permute-done.7.high.xhigh
  36.5 0.1 shard_map.32
  36.6 0.3 collective-permute-start.8
  37.0 0.4 collective-permute-start.9
  37.4 0.0 collective-permute-start.18
  37.4 2.5 %collective-permute-done.8.ylow = f32[28,8,256]{2,1,0:T(8,128)S(1)} collective-permute-done((f32[28,8,256]{2,1,0:T(8,128)S(1)}, f32[28,8,256]{2,1,0:T(8,128)S(1)}, u32[]{:S(2)}, u32[]{:S(2)}) %collective-permute-start.8) | collective-permute-done | bytes 229408 | tf_op jit(solution)/shard_map/ppermute | solution.py:584
  39.9 2.8 %collective-permute-done.9.yhigh = f32[28,8,256]{2,1,0:T(8,128)S(1)} collective-permute-done((f32[28,8,256]{2,1,0:T(8,128)S(1)}, f32[28,8,256]{2,1,0:T(8,128)S(1)}, u32[]{:S(2)}, u32[]{:S(2)}) %collective-permute-start.9) | collective-permute-done | bytes 229408 | tf_op jit(solution)/shard_map/ppermute | solution.py:584
  42.7 1.9 %shard_map.33 = (f32[3,14,24,256]{3,2,1,0:T(8,128)S(1)}, f32[3,12,24,256]{3,2,1,0:T(8,128)S(1)}, f32[13,24,256]{2,1,0:T(8,128)S(1)}, f32[6,12,24,256]{3,2,1,0:T(...) custom-call(f32[3,4,8,256]{3,2,1,0:T(8,128)S(1)} %get-tuple-element., ...), custom_call_target="tpu_custom_call" | custom-call | tf_op jit(solution)/shard_map/pallas_call | solution.py:572
  44.7 0.1 collective-permute-start.10
  44.7 5.7 %collective-permute-start.12 = (f32[4,16,128]{2,1,0:T(8,128)S(1)}, f32[4,16,128]{2,1,0:T(8,128)S(1)}, u32[]{:S(2)}, u32[]{:S(2)}) collective-permute-start(f32[4,16,128]{2,1,0:T(8,128)S(1)} %get-tuple-element.53), channel_id=1, source_target_pairs={{0,240},{8,248},{16,0},{24,8},{32,16},{40,24},{48,32},{56,40},{64,... | collective-permute-start | bytes 98312 | tf_op jit(solution)/shard_map/ppermute | solution.py:584
  50.4 0.0 collective-permute-start.11
  50.4 6.6 %collective-permute-start.13 = (f32[2,16,128]{2,1,0:T(8,128)S(1)}, f32[2,16,128]{2,1,0:T(8,128)S(1)}, u32[]{:S(2)}, u32[]{:S(2)}) collective-permute-start(f32[2,16,128]{2,1,0:T(8,128)S(1)} %get-tuple-element.54), channel_id=1, source_target_pairs={{0,232},{8,240},{16,248},{24,0},{32,8},{40,16},{48,24},{56,32},{64... | collective-permute-start | bytes 49160 | tf_op jit(solution)/shard_map/ppermute | solution.py:584
  57.0 1.1 %collective-permute-done.11.low3 = f32[2,16,128]{2,1,0:T(8,128)S(1)} collective-permute-done((f32[2,16,128]{2,1,0:T(8,128)S(1)}, f32[2,16,128]{2,1,0:T(8,128)S(1)}, u32[]{:S(2)}, u32[]{:S(2)}) %collective-permute-start.11) | collective-permute-done | bytes 16416 | tf_op jit(solution)/shard_map/ppermute | solution.py:584
  58.1 0.0 collective-permute-done.13.high3
  58.1 0.0 collective-permute-done.10.low2
  58.1 0.0 collective-permute-done.12.high2
  58.2 4.0 %collective-permute-start.17 = (f32[18,16,128]{2,1,0:T(8,128)S(1)}, f32[18,16,128]{2,1,0:T(8,128)S(1)}, u32[]{:S(2)}, u32[]{:S(2)}) collective-permute-start(f32[18,16,128]{2,1,0:T(8,128)S(1)} %shard_map.34.mid), channel_id=1, source_target_pairs={{0,6},{1,7},{2,0},{3,1},{4,2},{5,3},{6,4},{7,5},{8,14},{9,15},{10,... | collective-permute-start | bytes 442376 | tf_op jit(solution)/shard_map/ppermute | solution.py:584
  62.1 0.0 collective-permute-start.16
  62.1 0.9 %collective-permute-start.15 = (f32[18,16,128]{2,1,0:T(8,128)S(1)}, f32[18,16,128]{2,1,0:T(8,128)S(1)}, u32[]{:S(2)}, u32[]{:S(2)}) collective-permute-start(f32[18,16,128]{2,1,0:T(8,128)S(1)} %shard_map.34.mid), channel_id=1, source_target_pairs={{0,2},{1,3},{2,4},{3,5},{4,6},{5,7},{6,0},{7,1},{8,10},{9,11},{10,... | collective-permute-start | bytes 442376 | tf_op jit(solution)/shard_map/ppermute | solution.py:584
  63.0 0.9 %collective-permute-start.14 = (f32[18,16,128]{2,1,0:T(8,128)S(1)}, f32[18,16,128]{2,1,0:T(8,128)S(1)}, u32[]{:S(2)}, u32[]{:S(2)}) collective-permute-start(f32[18,16,128]{2,1,0:T(8,128)S(1)} %shard_map.34.mid), channel_id=1, source_target_pairs={{0,1},{1,2},{2,3},{3,4},{4,5},{5,6},{6,7},{7,0},{8,9},{9,10},{10,1... | collective-permute-start | bytes 442376 | tf_op jit(solution)/shard_map/ppermute | solution.py:584
  63.9 0.0 collective-permute-done.18.low
  63.9 1.5 %collective-permute-start.19 = (f32[4,16,512]{2,1,0:T(8,128)S(1)}, f32[4,16,512]{2,1,0:T(8,128)S(1)}, u32[]{:S(2)}, u32[]{:S(2)}) collective-permute-start(f32[4,16,512]{2,1,0:T(8,128)S(1)} %get-tuple-element.61), channel_id=1, source_target_pairs={{0,248},{8,0},{16,8},{24,16},{32,24},{40,32},{48,40},{56,48},{64,5... | collective-permute-start | bytes 393224 | tf_op jit(solution)/shard_map/ppermute | solution.py:584
  65.5 3.2 %collective-permute-done.19.high = f32[4,16,512]{2,1,0:T(8,128)S(1)} collective-permute-done((f32[4,16,512]{2,1,0:T(8,128)S(1)}, f32[4,16,512]{2,1,0:T(8,128)S(1)}, u32[]{:S(2)}, u32[]{:S(2)}) %collective-permute-start.19) | collective-permute-done | bytes 131104 | tf_op jit(solution)/shard_map/ppermute | solution.py:584
  68.6 0.4 shard_map.35.rim
  69.0 0.0 collective-permute-done.17.yp2
  69.0 0.0 collective-permute-done.16.yp1
  69.0 0.0 collective-permute-done.15.ym2
  69.0 0.0 collective-permute-done.14.ym1
  69.1 6.2 %shard_map.36 = f32[3,8,16,512]{3,2,1,0:T(8,128)} custom-call(f32[18,16,128]{2,1,0:T(8,128)S(1)} %shard_map.34.mid, f32[18,16,128]{2,1,0:T(8,128)S(1)} %collective-permute-done.14.ym1, f32[18,16,128]{2,1,0:T(8,128)S(1)} %collective-permute-done.15.ym2, f32[18,16,128]{2,1,0:T(8,128)S(1)} %collective-permute-done.16.yp1, ...), custom_call_target="tpu_custom_call" | custom-call | tf_op jit(solution)/shard_map/pallas_call | solution.py:572
  (1 shorter events, 0.0 us)
Async XLA Ops:
  1.3 15.4 %collective-permute-start = (f32[9,16,512]{2,1,0:T(8,128)S(1)}, f32[9,16,512]{2,1,0:T(8,128)S(1)}, u32[]{:S(2)}, u32[]{:S(2)}) collective-permute-start(f32[9,16,512]{2,1,0:T(8,128)S(1)} %get-tuple-element.38), channel_id=1, source_target_pairs={{0,8},{8,16},{16,24},{24,32},{32,40},{40,48},{48,56},{56,64},{64,7... | collective-permute-start | bytes 884744 | tf_op jit(solution)/shard_map/ppermute | solution.py:584
  3.8 12.9 %collective-permute-start.1 = (f32[9,16,512]{2,1,0:T(8,128)S(1)}, f32[9,16,512]{2,1,0:T(8,128)S(1)}, u32[]{:S(2)}, u32[]{:S(2)}) collective-permute-start(f32[9,16,512]{2,1,0:T(8,128)S(1)} %get-tuple-element.39), channel_id=1, source_target_pairs={{0,248},{8,0},{16,8},{24,16},{32,24},{40,32},{48,40},{56,48},{64,5... | collective-permute-start | bytes 884744 | tf_op jit(solution)/shard_map/ppermute | solution.py:584
  11.6 7.6 %collective-permute-start.2 = (f32[13,8,512]{2,1,0:T(8,128)S(1)}, f32[13,8,512]{2,1,0:T(8,128)S(1)}, u32[]{:S(2)}, u32[]{:S(2)}) collective-permute-start(f32[13,8,512]{2,1,0:T(8,128)S(1)} %get-tuple-element.40), channel_id=1, source_target_pairs={{0,1},{1,2},{2,3},{3,4},{4,5},{5,6},{6,7},{7,0},{8,9},{9,10},{10,1... | collective-permute-start | bytes 638984 | tf_op jit(solution)/shard_map/ppermute | solution.py:584
  13.8 5.4 %collective-permute-start.3 = (f32[13,8,512]{2,1,0:T(8,128)S(1)}, f32[13,8,512]{2,1,0:T(8,128)S(1)}, u32[]{:S(2)}, u32[]{:S(2)}) collective-permute-start(f32[13,8,512]{2,1,0:T(8,128)S(1)} %get-tuple-element.41), channel_id=1, source_target_pairs={{0,7},{1,0},{2,1},{3,2},{4,3},{5,4},{6,5},{7,6},{8,15},{9,8},{10,9... | collective-permute-start | bytes 638984 | tf_op jit(solution)/shard_map/ppermute | solution.py:584
  16.8 4.4 %collective-permute-start.4 = (f32[8,8,512]{2,1,0:T(8,128)S(1)}, f32[8,8,512]{2,1,0:T(8,128)S(1)}, u32[]{:S(2)}, u32[]{:S(2)}) collective-permute-start(f32[8,8,512]{2,1,0:T(8,128)S(1)} %get-tuple-element.42), channel_id=1, source_target_pairs={{0,1},{1,2},{2,3},{3,4},{4,5},{5,6},{6,7},{7,0},{8,9},{9,10},{10,1... | collective-permute-start | bytes 393224 | tf_op jit(solution)/shard_map/ppermute | solution.py:584
  19.2 4.4 %collective-permute-start.5 = (f32[8,8,512]{2,1,0:T(8,128)S(1)}, f32[8,8,512]{2,1,0:T(8,128)S(1)}, u32[]{:S(2)}, u32[]{:S(2)}) collective-permute-start(f32[8,8,512]{2,1,0:T(8,128)S(1)} %get-tuple-element.43), channel_id=1, source_target_pairs={{0,7},{1,0},{2,1},{3,2},{4,3},{5,4},{6,5},{7,6},{8,15},{9,8},{10,9... | collective-permute-start | bytes 393224 | tf_op jit(solution)/shard_map/ppermute | solution.py:584
  27.7 8.9 %collective-permute-start.6 = (f32[17,8,256]{2,1,0:T(8,128)S(1)}, f32[17,8,256]{2,1,0:T(8,128)S(1)}, u32[]{:S(2)}, u32[]{:S(2)}) collective-permute-start(f32[17,8,256]{2,1,0:T(8,128)S(1)} %get-tuple-element.46), channel_id=1, source_target_pairs={{0,8},{8,16},{16,24},{24,32},{32,40},{40,48},{48,56},{56,64},{64,7... | collective-permute-start | bytes 417800 | tf_op jit(solution)/shard_map/ppermute | solution.py:584
  27.8 8.8 %collective-permute-start.7 = (f32[17,8,256]{2,1,0:T(8,128)S(1)}, f32[17,8,256]{2,1,0:T(8,128)S(1)}, u32[]{:S(2)}, u32[]{:S(2)}) collective-permute-start(f32[17,8,256]{2,1,0:T(8,128)S(1)} %get-tuple-element.47), channel_id=1, source_target_pairs={{0,248},{8,0},{16,8},{24,16},{32,24},{40,32},{48,40},{56,48},{64,5... | collective-permute-start | bytes 417800 | tf_op jit(solution)/shard_map/ppermute | solution.py:584
  36.6 3.3 %collective-permute-start.8 = (f32[28,8,256]{2,1,0:T(8,128)S(1)}, f32[28,8,256]{2,1,0:T(8,128)S(1)}, u32[]{:S(2)}, u32[]{:S(2)}) collective-permute-start(f32[28,8,256]{2,1,0:T(8,128)S(1)} %get-tuple-element.48), channel_id=1, source_target_pairs={{0,1},{1,2},{2,3},{3,4},{4,5},{5,6},{6,7},{7,0},{8,9},{9,10},{10,1... | collective-permute-start | bytes 688136 | tf_op jit(solution)/shard_map/ppermute | solution.py:584
  37.0 5.7 %collective-permute-start.9 = (f32[28,8,256]{2,1,0:T(8,128)S(1)}, f32[28,8,256]{2,1,0:T(8,128)S(1)}, u32[]{:S(2)}, u32[]{:S(2)}) collective-permute-start(f32[28,8,256]{2,1,0:T(8,128)S(1)} %get-tuple-element.49), channel_id=1, source_target_pairs={{0,7},{1,0},{2,1},{3,2},{4,3},{5,4},{6,5},{7,6},{8,15},{9,8},{10,9... | collective-permute-start | bytes 688136 | tf_op jit(solution)/shard_map/ppermute | solution.py:584
  37.4 26.5 %collective-permute-start.18 = (f32[4,16,512]{2,1,0:T(8,128)S(1)}, f32[4,16,512]{2,1,0:T(8,128)S(1)}, u32[]{:S(2)}, u32[]{:S(2)}) collective-permute-start(f32[4,16,512]{2,1,0:T(8,128)S(1)} %get-tuple-element.60), channel_id=1, source_target_pairs={{0,8},{8,16},{16,24},{24,32},{32,40},{40,48},{48,56},{56,64},{64,7... | collective-permute-start | bytes 393224 | tf_op jit(solution)/shard_map/ppermute | solution.py:584
  44.7 13.5 %collective-permute-start.10 = (f32[4,16,128]{2,1,0:T(8,128)S(1)}, f32[4,16,128]{2,1,0:T(8,128)S(1)}, u32[]{:S(2)}, u32[]{:S(2)}) collective-permute-start(f32[4,16,128]{2,1,0:T(8,128)S(1)} %get-tuple-element.51), channel_id=1, source_target_pairs={{0,16},{8,24},{16,32},{24,40},{32,48},{40,56},{48,64},{56,72},{64,... | collective-permute-start | bytes 98312 | tf_op jit(solution)/shard_map/ppermute | solution.py:584
  44.7 13.4 %collective-permute-start.12 = (f32[4,16,128]{2,1,0:T(8,128)S(1)}, f32[4,16,128]{2,1,0:T(8,128)S(1)}, u32[]{:S(2)}, u32[]{:S(2)}) collective-permute-start(f32[4,16,128]{2,1,0:T(8,128)S(1)} %get-tuple-element.53), channel_id=1, source_target_pairs={{0,240},{8,248},{16,0},{24,8},{32,16},{40,24},{48,32},{56,40},{64,... | collective-permute-start | bytes 98312 | tf_op jit(solution)/shard_map/ppermute | solution.py:584
  50.4 7.7 %collective-permute-start.11 = (f32[2,16,128]{2,1,0:T(8,128)S(1)}, f32[2,16,128]{2,1,0:T(8,128)S(1)}, u32[]{:S(2)}, u32[]{:S(2)}) collective-permute-start(f32[2,16,128]{2,1,0:T(8,128)S(1)} %get-tuple-element.52), channel_id=1, source_target_pairs={{0,24},{8,32},{16,40},{24,48},{32,56},{40,64},{48,72},{56,80},{64,... | collective-permute-start | bytes 49160 | tf_op jit(solution)/shard_map/ppermute | solution.py:584
  50.4 7.7 %collective-permute-start.13 = (f32[2,16,128]{2,1,0:T(8,128)S(1)}, f32[2,16,128]{2,1,0:T(8,128)S(1)}, u32[]{:S(2)}, u32[]{:S(2)}) collective-permute-start(f32[2,16,128]{2,1,0:T(8,128)S(1)} %get-tuple-element.54), channel_id=1, source_target_pairs={{0,232},{8,240},{16,248},{24,0},{32,8},{40,16},{48,24},{56,32},{64... | collective-permute-start | bytes 49160 | tf_op jit(solution)/shard_map/ppermute | solution.py:584
  58.2 10.8 %collective-permute-start.17 = (f32[18,16,128]{2,1,0:T(8,128)S(1)}, f32[18,16,128]{2,1,0:T(8,128)S(1)}, u32[]{:S(2)}, u32[]{:S(2)}) collective-permute-start(f32[18,16,128]{2,1,0:T(8,128)S(1)} %shard_map.34.mid), channel_id=1, source_target_pairs={{0,6},{1,7},{2,0},{3,1},{4,2},{5,3},{6,4},{7,5},{8,14},{9,15},{10,... | collective-permute-start | bytes 442376 | tf_op jit(solution)/shard_map/ppermute | solution.py:584
  62.1 6.9 %collective-permute-start.16 = (f32[18,16,128]{2,1,0:T(8,128)S(1)}, f32[18,16,128]{2,1,0:T(8,128)S(1)}, u32[]{:S(2)}, u32[]{:S(2)}) collective-permute-start(f32[18,16,128]{2,1,0:T(8,128)S(1)} %shard_map.34.mid), channel_id=1, source_target_pairs={{0,7},{1,0},{2,1},{3,2},{4,3},{5,4},{6,5},{7,6},{8,15},{9,8},{10,9... | collective-permute-start | bytes 442376 | tf_op jit(solution)/shard_map/ppermute | solution.py:584
  62.1 6.9 %collective-permute-start.15 = (f32[18,16,128]{2,1,0:T(8,128)S(1)}, f32[18,16,128]{2,1,0:T(8,128)S(1)}, u32[]{:S(2)}, u32[]{:S(2)}) collective-permute-start(f32[18,16,128]{2,1,0:T(8,128)S(1)} %shard_map.34.mid), channel_id=1, source_target_pairs={{0,2},{1,3},{2,4},{3,5},{4,6},{5,7},{6,0},{7,1},{8,10},{9,11},{10,... | collective-permute-start | bytes 442376 | tf_op jit(solution)/shard_map/ppermute | solution.py:584
  63.0 6.0 %collective-permute-start.14 = (f32[18,16,128]{2,1,0:T(8,128)S(1)}, f32[18,16,128]{2,1,0:T(8,128)S(1)}, u32[]{:S(2)}, u32[]{:S(2)}) collective-permute-start(f32[18,16,128]{2,1,0:T(8,128)S(1)} %shard_map.34.mid), channel_id=1, source_target_pairs={{0,1},{1,2},{2,3},{3,4},{4,5},{5,6},{6,7},{7,0},{8,9},{9,10},{10,1... | collective-permute-start | bytes 442376 | tf_op jit(solution)/shard_map/ppermute | solution.py:584
  63.9 4.7 %collective-permute-start.19 = (f32[4,16,512]{2,1,0:T(8,128)S(1)}, f32[4,16,512]{2,1,0:T(8,128)S(1)}, u32[]{:S(2)}, u32[]{:S(2)}) collective-permute-start(f32[4,16,512]{2,1,0:T(8,128)S(1)} %get-tuple-element.61), channel_id=1, source_target_pairs={{0,248},{8,0},{16,8},{24,16},{32,24},{40,32},{48,40},{56,48},{64,5... | collective-permute-start | bytes 393224 | tf_op jit(solution)/shard_map/ppermute | solution.py:584

commit v8 on v7

--- a/solution.py
+++ b/solution.py
@@ -10,7 +10,7 @@
 F32 = jnp.float32
 BF16 = jnp.bfloat16
 WEIGHT = 2.0 / 3.0
-VMEM_LIMIT = 40 * 1024 * 1024
+VMEM_LIMIT = 24 * 1024 * 1024
 U0, U1, U2 = 12, 12, 16
 
 
@@ -58,6 +58,31 @@
 def kept(axis, step, value):
     place = lax.axis_index(axis) - step
     return jnp.where((place >= 0) & (place < lax.axis_size(axis)), value, 0.0)
+
+
+class Spliced:
+    def __init__(self, middle, outer, first, count, flat=False):
+        self.middle, self.outer, self.first, self.count, self.flat = middle, outer, first, count, flat
+
+    def place(self, key):
+        lead, i = ((), key) if self.flat else ((key[0],), key[1])
+        rest = () if self.flat else tuple(key[2:])
+        if self.first <= i < self.first + self.count:
+            return self.middle, lead + (i - self.first,) + rest
+        return self.outer, lead + (i if i < self.first else i - self.count,) + rest
+
+    def __getitem__(self, key):
+        ref, at = self.place(key)
+        return ref[at]
+
+    def __setitem__(self, key, value):
+        ref, at = self.place(key)
+        ref[at] = value
+
+
+def fine_set(inner, outer):
+    spans = ((3, 4), (3, 6), (2, 8), (3, 8), (3, 7), (3, 6))
+    return [Spliced(a, b, *span, flat=n in (3, 4)) for n, (a, b, span) in enumerate(zip(inner, outer, spans))]
 
 
 def split_dot(rows, matrix):
@@ -110,19 +135,18 @@
 
 
 def coefficients(eta, cx, cf, layers, scale, unroll):
-    half = 0.5 * scale
-
-    def face(i):
-        cx[i] = half * (eta[i] + eta[i + 1])
-
-    planes(layers + 1, face, unroll)
-
-    def body(i):
-        made = plane_coefficients(eta[i], eta[i + 1], eta[i + 2], scale)
-        for n, value in enumerate(made):
-            cf[n, i] = value
-
-    planes(layers, body, unroll)
+    planes(layers + 1, lambda i: face_plane(eta, cx, i, scale), unroll)
+    planes(layers, lambda i: cell_plane(eta, cf, i, scale), unroll)
+
+
+def face_plane(eta, cx, i, scale):
+    cx[i] = (0.5 * scale) * (eta[i] + eta[i + 1])
+
+
+def cell_plane(eta, cf, i, scale):
+    made = plane_coefficients(eta[i], eta[i + 1], eta[i + 2], scale)
+    for n, value in enumerate(made):
+        cf[n, i] = value
 
 
 def gather_sum(v, comp, i, cx, cf, k):
@@ -226,44 +250,63 @@
         out[4, 4:8] = jnp.zeros((4, low.shape[-1]), F32)
 
 
-def fine_down(f, ids, xlow, xhigh, ylow, yhigh, clow, chigh, v0, va, g, eta, cx, cf, f1, eta1, up, down, pairs, rest):
-    nz = f.shape[-1]
-    blank = jnp.zeros((1, nz), F32)
-    for i in range(12):
-        x = i - 2
-        for c in range(3):
-            g[c, i, 4:20] = fine_source(f, xlow, xhigh, c, x)
+def fine_rows(g, eta, i, source, viscosity, low, high, n, spill, first):
+    blank = jnp.zeros((1, source[0].shape[-1]), F32) if source else None
+    if source:
+        for c in range(3):
+            g[c, i, 4:20] = source[c]
             g[c, i, 0:1] = blank
             g[c, i, 23:24] = blank
-        for own, corner, at, step in ((ylow, clow, 1, 1), (yhigh, chigh, 20, -1)):
-            if 0 <= x < 8:
-                side, n, spill = own, x, 8
-            else:
-                side, n, spill = corner, (i if x < 0 else x - 6), 4
-            tile = kept("gy", step, side[n])
+    for side, at, row, step in ((low, 1, 0, 1), (high, 20, 20, -1)):
+        if source:
+            tile = kept("gy", step, side[n, 0:8])
             g[0, i, at : at + 3] = tile[0:3]
             g[1, i, at : at + 3] = tile[3:6]
             g[2, i, at : at + 2] = tile[6:8]
             g[2, i, at + 2 : at + 3] = kept("gy", step, side[spill, n : n + 1])
-    for j in range(14):
-        x = j - 3
-        eta[j, 4:20] = fine_eta(ids, xlow, xhigh, x)
-        for own, corner, row, step in ((ylow, clow, 0, 1), (yhigh, chigh, 20, -1)):
-            if 0 <= x < 8:
-                side, n, first = own, x, 9
-            else:
-                side, n, first = corner, (j if x < 0 else x - 5), 5
-            at = 4 * (n % 2)
-            eta[j, row : row + 4] = kept("gy", step, side[first + n // 2, at : at + 4])
-
-    coefficients(eta, cx, cf, 12, 1.0, U0)
-
-    def start(i):
-        for c in range(3):
-            va[c, i] = cf[EI, i] * g[c, i]
-
-    planes(12, start, U0)
-    sweep(va, 2, g, 2, cx, cf, 2, v0, 1, -1, 9, U0)
+        else:
+            part = 4 * (n % 2)
+            eta[i, row : row + 4] = kept("gy", step, side[first + n // 2, part : part + 4])
+    if viscosity is not None:
+        eta[i, 4:20] = viscosity
+
+
+def fine_first(va, g, cf, i):
+    for c in range(3):
+        va[c, i] = cf[EI, i] * g[c, i]
+
+
+def fine_inner(f, ids, ylow, yhigh, v0, va, g, eta, cx, cf):
+    for x in range(8):
+        fine_rows(g, eta, x, [f[c, x] for c in range(3)], None, ylow, yhigh, x, 8, 9)
+        fine_rows(g, eta, x, None, materials(ids[x]), ylow, yhigh, x, 8, 9)
+    for i in range(7):
+        face_plane(eta, cx, i, 1.0)
+    for i in range(6):
+        cell_plane(eta, cf, i, 1.0)
+        for c in range(3):
+            va[c, i] = cf[EI, i] * g[c, i + 1]
+    sweep(va, 0, g, 1, cx, cf, 0, v0, -1, 1, 5, U0)
+
+
+def fine_down(*refs):
+    xlow, xhigh, clow, chigh = refs[0:4]
+    inner, outer = refs[4:10], refs[10:16]
+    f1, eta1, up, down, pairs, rest = refs[16:22]
+    v0, va, g, eta, cx, cf = fine_set(inner, outer)
+    nz = xlow.shape[-1]
+    for n, x in enumerate((-2, -1, 8, 9)):
+        rows = [fine_source(None, xlow, xhigh, c, x) for c in range(3)]
+        fine_rows(outer[2], None, n, rows, None, clow, chigh, n, 4, 5)
+    for n, x in enumerate((-3, -2, -1, 8, 9, 10)):
+        fine_rows(None, outer[3], n, None, fine_eta(None, xlow, xhigh, x), clow, chigh, n, 4, 5)
+    for i in (0, 1, 2, 10, 11, 12):
+        face_plane(eta, cx, i, 1.0)
+    for i in (0, 1, 2, 9, 10, 11):
+        cell_plane(eta, cf, i, 1.0)
+        fine_first(va, g, cf, i)
+    sweep(va, 2, g, 2, cx, cf, 2, v0, 1, -1, 2, U0)
+    sweep(va, 2, g, 2, cx, cf, 2, v0, 1, 6, 9, U0)
 
     def down_pair(k):
         for c in range(3):
@@ -325,10 +368,11 @@
     return jnp.concatenate([ref[n, b] for b in range(ref.shape[1])], axis=1)
 
 
-def fine_rim(low, high, va, g, eta, cx, cf, rim):
+def fine_rim(low, high, *refs):
+    _, va, g, eta, cx, cf = fine_set(refs[0:6], refs[6:12])
+    rim = refs[12]
     nz = low.shape[-1]
     blank = jnp.zeros((4, nz), F32)
-
     for n, (side, step) in enumerate(((low, 1), (high, -1))):
         rows = [jnp.concatenate([blank, kept("gx", step, side[k]), blank], axis=0) for k in range(4)]
         edge, k, inner, face, far = ((0, 0, 1, 1, 0), (13, 11, 10, 11, 12))[n]
@@ -491,10 +535,12 @@
 
 
 def ascend(
-    mid, ym1, ym2, yp1, yp2, v1, g1, cx1, cf1, v0, rim, g0, cx0, cf0, out,
+    mid, ym1, ym2, yp1, yp2, v1, g1, cx1, cf1, rim,
+    v0i, vai, g0i, eta0i, cx0i, cf0i, v0o, vao, g0o, eta0o, cx0o, cf0o, out,
     eta2, g2, cx2, cf2, va2, vb2, rows2, wide1, va1, vb1, rows1, wide0, va0, vb0, result, sent,
 ):
-    nz2, nz1, nz0 = mid.shape[-1], v1.shape[-1], v0.shape[-1]
+    v0, _, g0, _, cx0, cf0 = fine_set((v0i, vai, g0i, eta0i, cx0i, cf0i), (v0o, vao, g0o, eta0o, cx0o, cf0o))
+    nz2, nz1 = mid.shape[-1], v1.shape[-1]
     blank = jnp.zeros((4, nz2), F32)
     sides = ((ym2, 2), (ym1, 1), (mid, 0), (yp1, -1), (yp2, -2))
     for j in range(18):
@@ -601,10 +647,15 @@
     ylow, yhigh = cycled(yup, "gy", 1), cycled(ydown, "gy", -1)
     up, down = call(pack_corners, [(8, 8, z0)] * 2, xlow, xhigh)
     clow, chigh = cycled(up, "gy", 1), cycled(down, "gy", -1)
-    v0, va, g0, eta0, cx0, cf0, f1, eta1, up, down = call(
+    inner = call(
+        fine_inner,
+        [(3, 4, 24, z0), (3, 6, 24, z0), (3, 8, 24, z0), (8, 24, z0), (7, 24, z0), (6, 6, 24, z0)],
+        f0, ids0, ylow, yhigh,
+    )
+    *outer, f1, eta1, up, down = call(
         fine_down,
-        [(3, 10, 24, z0), (3, 12, 24, z0), (3, 12, 24, z0), (14, 24, z0), (13, 24, z0), (6, 12, 24, z0), (3, 4, 8, z1), (6, 8, z1), (17, 8, z1), (17, 8, z1)],
-        f0, ids0, xlow, xhigh, ylow, yhigh, clow, chigh,
+        [(3, 6, 24, z0), (3, 6, 24, z0), (3, 4, 24, z0), (6, 24, z0), (6, 24, z0), (6, 6, 24, z0), (3, 4, 8, z1), (6, 8, z1), (17, 8, z1), (17, 8, z1)],
+        xlow, xhigh, clow, chigh, *inner,
         scratch=[lane_blocks(18, z0), (144, z0)],
     )
     xlow, xhigh = cycled(up, "gx", 1), cycled(down, "gx", -1)
@@ -613,7 +664,7 @@
     )
     ylow, yhigh = cycled(up, "gy", 1), cycled(down, "gy", -1)
     late_low, late_high = cycled(late_up, "gx", 1), cycled(late_down, "gx", -1)
-    (rim,) = call(fine_rim, [(3, 2, 24, z0)], late_low, late_high, va, g0, eta0, cx0, cf0)
+    (rim,) = call(fine_rim, [(3, 2, 24, z0)], late_low, late_high, *inner, *outer)
     v1, g1, cx1, cf1, own, up, down, far_up, far_down = call(
         middle_down,
         [(3, 14, 24, z1), (3, 12, 24, z1), (13, 24, z1), (6, 12, 24, z1), (6, 16, z2), (4, 16, z2), (4, 16, z2), (2, 16, z2), (2, 16, z2)],
@@ -628,7 +679,7 @@
     (velocity,) = call(
         ascend,
         [forcing.shape],
-        strip, ym1, ym2, yp1, yp2, v1, g1, cx1, cf1, v0, rim, g0, cx0, cf0,
+        strip, ym1, ym2, yp1, yp2, v1, g1, cx1, cf1, rim, *inner, *outer,
         scratch=[
             (18, 24, z2), (3, 16, 24, z2), (17, 24, z2), (6, 16, 24, z2), (3, 16, 24, z2), (3, 16, 24, z2),
             (288, z2), lane_blocks(18, z1), (3, 10, 24, z1), (3, 10, 24, z1),

time: 75.6 us -> 75.1 us (level)
  waiting for transfers between devices: 20.8 us -> 19.5 us
  Pallas kernels: 15.6 us -> 16.4 us
    ppermute x20, waiting for transfers between devices: 20.8 us -> 19.5 us  [cycled(): lax.ppermute(array, axis, [(i, (i + step) % size) for i in range(size)])]
    pallas_call x9 -> x10, Pallas kernels: 15.6 us -> 16.4 us  [call(): pl.pallas_call(body, out_shape=outs, in_specs=[pl.BlockSpec(memory_space=...]
  transfers between devices with their start and end apart: 20 -> 20, of which waited for: 8 -> 8; matrix products, arithmetic and copies ran while one was open for 0% -> 0% of each run, Pallas kernels for 5% -> 7%
where the time goes in v8:
time: 75.1 us; the launch traced here: 74.9 us
  starting transfers between devices  38.7 us (52%)
  waiting for transfers between devices  19.5 us (26%)
  Pallas kernels  16.4 us (22%)
    ppermute x20, starting transfers between devices, cycled(): lax.ppermute(array, axis, [(i, (i + step) % size) for i in range(size)])  38.7 us
    ppermute x20, waiting for transfers between devices, cycled(): lax.ppermute(array, axis, [(i, (i + step) % size) for i in range(size)])  19.5 us
    pallas_call x10, Pallas kernels, call(): pl.pallas_call(body, out_shape=outs, in_specs=[pl.BlockSpec(memory_space=...  16.4 us
  transfers between devices with their start and end apart: 20, of which 8 were waited for; matrix products, arithmetic and copies ran while one was open for 0% of the time, Pallas kernels for 7%

profile of v8, /device:TPU:1, one launch (start us, length us, event | category | flops | bytes accessed | tf_op | source)
XLA Modules:
  0.0 74.9 jit_solution(3682761747520826910)
XLA Ops:
  0.0 1.3 %shard_map.28 = (f32[9,16,512]{2,1,0:T(8,128)S(1)}, f32[9,16,512]{2,1,0:T(8,128)S(1)}) custom-call(f32[3,8,16,512]{3,2,1,0:T(8,128)} %f_in.3, s32[8,16,512]{2,1,0:T(8,128)} %ids_in.3), custom_call_target="tpu_custom_call" | custom-call | tf_op jit(solution)/shard_map/pallas_call | solution.py:618
  1.3 2.5 %collective-permute-start = (f32[9,16,512]{2,1,0:T(8,128)S(1)}, f32[9,16,512]{2,1,0:T(8,128)S(1)}, u32[]{:S(2)}, u32[]{:S(2)}) collective-permute-start(f32[9,16,512]{2,1,0:T(8,128)S(1)} %get-tuple-element.42), channel_id=1, source_target_pairs={{0,8},{8,16},{16,24},{24,32},{32,40},{40,48},{48,56},{56,64},{64,7... | collective-permute-start | bytes 884744 | tf_op jit(solution)/shard_map/ppermute | solution.py:630
  3.8 6.2 %collective-permute-start.1 = (f32[9,16,512]{2,1,0:T(8,128)S(1)}, f32[9,16,512]{2,1,0:T(8,128)S(1)}, u32[]{:S(2)}, u32[]{:S(2)}) collective-permute-start(f32[9,16,512]{2,1,0:T(8,128)S(1)} %get-tuple-element.43), channel_id=1, source_target_pairs={{0,248},{8,0},{16,8},{24,16},{32,24},{40,32},{48,40},{56,48},{64,5... | collective-permute-start | bytes 884744 | tf_op jit(solution)/shard_map/ppermute | solution.py:630
  10.0 1.6 %shard_map.30 = (f32[13,8,512]{2,1,0:T(8,128)S(1)}, f32[13,8,512]{2,1,0:T(8,128)S(1)}, f32[3,8,16,512]{3,2,1,0:T(8,128)S(1)}, s32[8,16,512]{2,1,0:T(8,128)S(1)}) custom-call(f32[3,8,16,512]{3,2,1,0:T(8,128)} %f_in.3, s32[8,16,512]{2,1,0:T(8,128)} %ids_in.3), custom_call_target="tpu_custom_call" | custom-call | tf_op jit(solution)/shard_map/pallas_call | solution.py:618
  11.6 2.1 %collective-permute-start.4 = (f32[13,8,512]{2,1,0:T(8,128)S(1)}, f32[13,8,512]{2,1,0:T(8,128)S(1)}, u32[]{:S(2)}, u32[]{:S(2)}) collective-permute-start(f32[13,8,512]{2,1,0:T(8,128)S(1)} %get-tuple-element.48), channel_id=1, source_target_pairs={{0,1},{1,2},{2,3},{3,4},{4,5},{5,6},{6,7},{7,0},{8,9},{9,10},{10,1... | collective-permute-start | bytes 638984 | tf_op jit(solution)/shard_map/ppermute | solution.py:630
  13.8 0.0 collective-permute-start.5
  13.8 2.9 %collective-permute-done.low.refs_0_ = f32[9,16,512]{2,1,0:T(8,128)S(1)} collective-permute-done((f32[9,16,512]{2,1,0:T(8,128)S(1)}, f32[9,16,512]{2,1,0:T(8,128)S(1)}, u32[]{:S(2)}, u32[]{:S(2)}) %collective-permute-start) | collective-permute-done | bytes 294944 | tf_op jit(solution)/shard_map/ppermute | solution.py:630
  16.7 0.0 collective-permute-done.1.high.refs_1_
  16.7 0.1 shard_map.29
  16.8 2.4 %collective-permute-start.2 = (f32[8,8,512]{2,1,0:T(8,128)S(1)}, f32[8,8,512]{2,1,0:T(8,128)S(1)}, u32[]{:S(2)}, u32[]{:S(2)}) collective-permute-start(f32[8,8,512]{2,1,0:T(8,128)S(1)} %get-tuple-element.44), channel_id=1, source_target_pairs={{0,1},{1,2},{2,3},{3,4},{4,5},{5,6},{6,7},{7,0},{8,9},{9,10},{10,1... | collective-permute-start | bytes 393224 | tf_op jit(solution)/shard_map/ppermute | solution.py:630
  19.2 0.0 collective-permute-start.3
  19.2 0.0 collective-permute-done.4.ylow
  19.2 0.0 collective-permute-done.5.yhigh
  19.2 1.3 %shard_map.31 = (f32[3,4,24,512]{3,2,1,0:T(8,128)S(1)}, f32[3,6,24,512]{3,2,1,0:T(8,128)S(1)}, f32[3,8,24,512]{3,2,1,0:T(8,128)S(1)}, f32[8,24,512]{2,1,0:T(8,12...) custom-call(f32[3,8,16,512]{3,2,1,0:T(8,128)S(1)} %get-tuple-element.46.f, ...), custom_call_target="tpu_custom_call" | custom-call | tf_op jit(solution)/shard_map/pallas_call | solution.py:618
  20.5 0.6 collective-permute-done.2.refs_2_
  21.1 2.4 %collective-permute-done.3.refs_3_ = f32[8,8,512]{2,1,0:T(8,128)S(1)} collective-permute-done((f32[8,8,512]{2,1,0:T(8,128)S(1)}, f32[8,8,512]{2,1,0:T(8,128)S(1)}, u32[]{:S(2)}, u32[]{:S(2)}) %collective-permute-start.3) | collective-permute-done | bytes 131104 | tf_op jit(solution)/shard_map/ppermute | solution.py:630
  23.6 3.0 %shard_map.32 = (f32[3,6,24,512]{3,2,1,0:T(8,128)S(1)}, f32[3,6,24,512]{3,2,1,0:T(8,128)S(1)}, f32[3,4,24,512]{3,2,1,0:T(8,128)S(1)}, f32[6,24,512]{2,1,0:T(8,12...) custom-call(f32[9,16,512]{2,1,0:T(8,128)S(1)} %collective-permute-do, ...), custom_call_target="tpu_custom_call" | custom-call | tf_op jit(solution)/shard_map/pallas_call | solution.py:618
  26.6 0.1 collective-permute-start.6
  26.7 4.9 %collective-permute-start.7 = (f32[17,8,256]{2,1,0:T(8,128)S(1)}, f32[17,8,256]{2,1,0:T(8,128)S(1)}, u32[]{:S(2)}, u32[]{:S(2)}) collective-permute-start(f32[17,8,256]{2,1,0:T(8,128)S(1)} %get-tuple-element.59), channel_id=1, source_target_pairs={{0,248},{8,0},{16,8},{24,16},{32,24},{40,32},{48,40},{56,48},{64,5... | collective-permute-start | bytes 417800 | tf_op jit(solution)/shard_map/ppermute | solution.py:630
  31.7 3.8 %collective-permute-done.6.low.xlow = f32[17,8,256]{2,1,0:T(8,128)S(1)} collective-permute-done((f32[17,8,256]{2,1,0:T(8,128)S(1)}, f32[17,8,256]{2,1,0:T(8,128)S(1)}, u32[]{:S(2)}, u32[]{:S(2)}) %collective-permute-start.6) | collective-permute-done | bytes 139296 | tf_op jit(solution)/shard_map/ppermute | solution.py:630
  35.5 0.0 collective-permute-done.7.high.xhigh
  35.5 0.1 shard_map.33
  35.6 0.3 collective-permute-start.8
  35.9 0.4 collective-permute-start.9
  36.3 0.0 collective-permute-start.18
  36.3 2.5 %collective-permute-done.8.ylow = f32[28,8,256]{2,1,0:T(8,128)S(1)} collective-permute-done((f32[28,8,256]{2,1,0:T(8,128)S(1)}, f32[28,8,256]{2,1,0:T(8,128)S(1)}, u32[]{:S(2)}, u32[]{:S(2)}) %collective-permute-start.8) | collective-permute-done | bytes 229408 | tf_op jit(solution)/shard_map/ppermute | solution.py:630
  38.9 2.8 %collective-permute-done.9.yhigh = f32[28,8,256]{2,1,0:T(8,128)S(1)} collective-permute-done((f32[28,8,256]{2,1,0:T(8,128)S(1)}, f32[28,8,256]{2,1,0:T(8,128)S(1)}, u32[]{:S(2)}, u32[]{:S(2)}) %collective-permute-start.9) | collective-permute-done | bytes 229408 | tf_op jit(solution)/shard_map/ppermute | solution.py:630
  41.7 2.0 %shard_map.34 = (f32[3,14,24,256]{3,2,1,0:T(8,128)S(1)}, f32[3,12,24,256]{3,2,1,0:T(8,128)S(1)}, f32[13,24,256]{2,1,0:T(8,128)S(1)}, f32[6,12,24,256]{3,2,1,0:T(...) custom-call(f32[3,4,8,256]{3,2,1,0:T(8,128)S(1)} %get-tuple-element., ...), custom_call_target="tpu_custom_call" | custom-call | tf_op jit(solution)/shard_map/pallas_call | solution.py:618
  43.7 0.1 collective-permute-start.10
  43.8 5.7 %collective-permute-start.12 = (f32[4,16,128]{2,1,0:T(8,128)S(1)}, f32[4,16,128]{2,1,0:T(8,128)S(1)}, u32[]{:S(2)}, u32[]{:S(2)}) collective-permute-start(f32[4,16,128]{2,1,0:T(8,128)S(1)} %get-tuple-element.65), channel_id=1, source_target_pairs={{0,240},{8,248},{16,0},{24,8},{32,16},{40,24},{48,32},{56,40},{64,... | collective-permute-start | bytes 98312 | tf_op jit(solution)/shard_map/ppermute | solution.py:630
  49.4 0.0 collective-permute-start.11
  49.4 6.6 %collective-permute-start.13 = (f32[2,16,128]{2,1,0:T(8,128)S(1)}, f32[2,16,128]{2,1,0:T(8,128)S(1)}, u32[]{:S(2)}, u32[]{:S(2)}) collective-permute-start(f32[2,16,128]{2,1,0:T(8,128)S(1)} %get-tuple-element.66), channel_id=1, source_target_pairs={{0,232},{8,240},{16,248},{24,0},{32,8},{40,16},{48,24},{56,32},{64... | collective-permute-start | bytes 49160 | tf_op jit(solution)/shard_map/ppermute | solution.py:630
  56.0 1.1 %collective-permute-done.11.low3 = f32[2,16,128]{2,1,0:T(8,128)S(1)} collective-permute-done((f32[2,16,128]{2,1,0:T(8,128)S(1)}, f32[2,16,128]{2,1,0:T(8,128)S(1)}, u32[]{:S(2)}, u32[]{:S(2)}) %collective-permute-start.11) | collective-permute-done | bytes 16416 | tf_op jit(solution)/shard_map/ppermute | solution.py:630
  57.1 0.0 collective-permute-done.13.high3
  57.1 0.0 collective-permute-done.10.low2
  57.1 0.0 collective-permute-done.12.high2
  57.2 4.0 %collective-permute-start.17 = (f32[18,16,128]{2,1,0:T(8,128)S(1)}, f32[18,16,128]{2,1,0:T(8,128)S(1)}, u32[]{:S(2)}, u32[]{:S(2)}) collective-permute-start(f32[18,16,128]{2,1,0:T(8,128)S(1)} %shard_map.35.mid), channel_id=1, source_target_pairs={{0,6},{1,7},{2,0},{3,1},{4,2},{5,3},{6,4},{7,5},{8,14},{9,15},{10,... | collective-permute-start | bytes 442376 | tf_op jit(solution)/shard_map/ppermute | solution.py:630
  61.1 0.0 collective-permute-start.16
  61.1 0.9 %collective-permute-start.15 = (f32[18,16,128]{2,1,0:T(8,128)S(1)}, f32[18,16,128]{2,1,0:T(8,128)S(1)}, u32[]{:S(2)}, u32[]{:S(2)}) collective-permute-start(f32[18,16,128]{2,1,0:T(8,128)S(1)} %shard_map.35.mid), channel_id=1, source_target_pairs={{0,2},{1,3},{2,4},{3,5},{4,6},{5,7},{6,0},{7,1},{8,10},{9,11},{10,... | collective-permute-start | bytes 442376 | tf_op jit(solution)/shard_map/ppermute | solution.py:630
  62.0 0.9 %collective-permute-start.14 = (f32[18,16,128]{2,1,0:T(8,128)S(1)}, f32[18,16,128]{2,1,0:T(8,128)S(1)}, u32[]{:S(2)}, u32[]{:S(2)}) collective-permute-start(f32[18,16,128]{2,1,0:T(8,128)S(1)} %shard_map.35.mid), channel_id=1, source_target_pairs={{0,1},{1,2},{2,3},{3,4},{4,5},{5,6},{6,7},{7,0},{8,9},{9,10},{10,1... | collective-permute-start | bytes 442376 | tf_op jit(solution)/shard_map/ppermute | solution.py:630
  62.9 0.0 collective-permute-done.18.low
  62.9 1.5 %collective-permute-start.19 = (f32[4,16,512]{2,1,0:T(8,128)S(1)}, f32[4,16,512]{2,1,0:T(8,128)S(1)}, u32[]{:S(2)}, u32[]{:S(2)}) collective-permute-start(f32[4,16,512]{2,1,0:T(8,128)S(1)} %get-tuple-element.72), channel_id=1, source_target_pairs={{0,248},{8,0},{16,8},{24,16},{32,24},{40,32},{48,40},{56,48},{64,5... | collective-permute-start | bytes 393224 | tf_op jit(solution)/shard_map/ppermute | solution.py:630
  64.5 3.2 %collective-permute-done.19.high = f32[4,16,512]{2,1,0:T(8,128)S(1)} collective-permute-done((f32[4,16,512]{2,1,0:T(8,128)S(1)}, f32[4,16,512]{2,1,0:T(8,128)S(1)}, u32[]{:S(2)}, u32[]{:S(2)}) %collective-permute-start.19) | collective-permute-done | bytes 131104 | tf_op jit(solution)/shard_map/ppermute | solution.py:630
  67.6 0.4 shard_map.36.rim
  68.1 0.0 collective-permute-done.17.yp2
  68.1 0.0 collective-permute-done.16.yp1
  68.1 0.0 collective-permute-done.15.ym2
  68.1 0.0 collective-permute-done.14.ym1
  68.1 6.6 %shard_map.37 = f32[3,8,16,512]{3,2,1,0:T(8,128)} custom-call(f32[18,16,128]{2,1,0:T(8,128)S(1)} %shard_map.35.mid, f32[18,16,128]{2,1,0:T(8,128)S(1)} %collective-permute-done.14.ym1, f32[18,16,128]{2,1,0:T(8,128)S(1)} %collective-permute-done.15.ym2, f32[18,16,128]{2,1,0:T(8,128)S(1)} %collective-permute-done.16.yp1, ...), custom_call_target="tpu_custom_call" | custom-call | tf_op jit(solution)/shard_map/pallas_call | solution.py:618
  (1 shorter events, 0.0 us)
Async XLA Ops:
  1.3 15.4 %collective-permute-start = (f32[9,16,512]{2,1,0:T(8,128)S(1)}, f32[9,16,512]{2,1,0:T(8,128)S(1)}, u32[]{:S(2)}, u32[]{:S(2)}) collective-permute-start(f32[9,16,512]{2,1,0:T(8,128)S(1)} %get-tuple-element.42), channel_id=1, source_target_pairs={{0,8},{8,16},{16,24},{24,32},{32,40},{40,48},{48,56},{56,64},{64,7... | collective-permute-start | bytes 884744 | tf_op jit(solution)/shard_map/ppermute | solution.py:630
  3.8 12.9 %collective-permute-start.1 = (f32[9,16,512]{2,1,0:T(8,128)S(1)}, f32[9,16,512]{2,1,0:T(8,128)S(1)}, u32[]{:S(2)}, u32[]{:S(2)}) collective-permute-start(f32[9,16,512]{2,1,0:T(8,128)S(1)} %get-tuple-element.43), channel_id=1, source_target_pairs={{0,248},{8,0},{16,8},{24,16},{32,24},{40,32},{48,40},{56,48},{64,5... | collective-permute-start | bytes 884744 | tf_op jit(solution)/shard_map/ppermute | solution.py:630
  11.6 7.6 %collective-permute-start.4 = (f32[13,8,512]{2,1,0:T(8,128)S(1)}, f32[13,8,512]{2,1,0:T(8,128)S(1)}, u32[]{:S(2)}, u32[]{:S(2)}) collective-permute-start(f32[13,8,512]{2,1,0:T(8,128)S(1)} %get-tuple-element.48), channel_id=1, source_target_pairs={{0,1},{1,2},{2,3},{3,4},{4,5},{5,6},{6,7},{7,0},{8,9},{9,10},{10,1... | collective-permute-start | bytes 638984 | tf_op jit(solution)/shard_map/ppermute | solution.py:630
  13.8 5.4 %collective-permute-start.5 = (f32[13,8,512]{2,1,0:T(8,128)S(1)}, f32[13,8,512]{2,1,0:T(8,128)S(1)}, u32[]{:S(2)}, u32[]{:S(2)}) collective-permute-start(f32[13,8,512]{2,1,0:T(8,128)S(1)} %get-tuple-element.49), channel_id=1, source_target_pairs={{0,7},{1,0},{2,1},{3,2},{4,3},{5,4},{6,5},{7,6},{8,15},{9,8},{10,9... | collective-permute-start | bytes 638984 | tf_op jit(solution)/shard_map/ppermute | solution.py:630
  16.8 4.4 %collective-permute-start.2 = (f32[8,8,512]{2,1,0:T(8,128)S(1)}, f32[8,8,512]{2,1,0:T(8,128)S(1)}, u32[]{:S(2)}, u32[]{:S(2)}) collective-permute-start(f32[8,8,512]{2,1,0:T(8,128)S(1)} %get-tuple-element.44), channel_id=1, source_target_pairs={{0,1},{1,2},{2,3},{3,4},{4,5},{5,6},{6,7},{7,0},{8,9},{9,10},{10,1... | collective-permute-start | bytes 393224 | tf_op jit(solution)/shard_map/ppermute | solution.py:630
  19.2 4.4 %collective-permute-start.3 = (f32[8,8,512]{2,1,0:T(8,128)S(1)}, f32[8,8,512]{2,1,0:T(8,128)S(1)}, u32[]{:S(2)}, u32[]{:S(2)}) collective-permute-start(f32[8,8,512]{2,1,0:T(8,128)S(1)} %get-tuple-element.45), channel_id=1, source_target_pairs={{0,7},{1,0},{2,1},{3,2},{4,3},{5,4},{6,5},{7,6},{8,15},{9,8},{10,9... | collective-permute-start | bytes 393224 | tf_op jit(solution)/shard_map/ppermute | solution.py:630
  26.6 8.9 %collective-permute-start.6 = (f32[17,8,256]{2,1,0:T(8,128)S(1)}, f32[17,8,256]{2,1,0:T(8,128)S(1)}, u32[]{:S(2)}, u32[]{:S(2)}) collective-permute-start(f32[17,8,256]{2,1,0:T(8,128)S(1)} %get-tuple-element.58), channel_id=1, source_target_pairs={{0,8},{8,16},{16,24},{24,32},{32,40},{40,48},{48,56},{56,64},{64,7... | collective-permute-start | bytes 417800 | tf_op jit(solution)/shard_map/ppermute | solution.py:630
  26.7 8.8 %collective-permute-start.7 = (f32[17,8,256]{2,1,0:T(8,128)S(1)}, f32[17,8,256]{2,1,0:T(8,128)S(1)}, u32[]{:S(2)}, u32[]{:S(2)}) collective-permute-start(f32[17,8,256]{2,1,0:T(8,128)S(1)} %get-tuple-element.59), channel_id=1, source_target_pairs={{0,248},{8,0},{16,8},{24,16},{32,24},{40,32},{48,40},{56,48},{64,5... | collective-permute-start | bytes 417800 | tf_op jit(solution)/shard_map/ppermute | solution.py:630
  35.6 3.3 %collective-permute-start.8 = (f32[28,8,256]{2,1,0:T(8,128)S(1)}, f32[28,8,256]{2,1,0:T(8,128)S(1)}, u32[]{:S(2)}, u32[]{:S(2)}) collective-permute-start(f32[28,8,256]{2,1,0:T(8,128)S(1)} %get-tuple-element.60), channel_id=1, source_target_pairs={{0,1},{1,2},{2,3},{3,4},{4,5},{5,6},{6,7},{7,0},{8,9},{9,10},{10,1... | collective-permute-start | bytes 688136 | tf_op jit(solution)/shard_map/ppermute | solution.py:630
  35.9 5.7 %collective-permute-start.9 = (f32[28,8,256]{2,1,0:T(8,128)S(1)}, f32[28,8,256]{2,1,0:T(8,128)S(1)}, u32[]{:S(2)}, u32[]{:S(2)}) collective-permute-start(f32[28,8,256]{2,1,0:T(8,128)S(1)} %get-tuple-element.61), channel_id=1, source_target_pairs={{0,7},{1,0},{2,1},{3,2},{4,3},{5,4},{6,5},{7,6},{8,15},{9,8},{10,9... | collective-permute-start | bytes 688136 | tf_op jit(solution)/shard_map/ppermute | solution.py:630
  36.3 26.6 %collective-permute-start.18 = (f32[4,16,512]{2,1,0:T(8,128)S(1)}, f32[4,16,512]{2,1,0:T(8,128)S(1)}, u32[]{:S(2)}, u32[]{:S(2)}) collective-permute-start(f32[4,16,512]{2,1,0:T(8,128)S(1)} %get-tuple-element.71), channel_id=1, source_target_pairs={{0,8},{8,16},{16,24},{24,32},{32,40},{40,48},{48,56},{56,64},{64,7... | collective-permute-start | bytes 393224 | tf_op jit(solution)/shard_map/ppermute | solution.py:630
  43.7 13.5 %collective-permute-start.10 = (f32[4,16,128]{2,1,0:T(8,128)S(1)}, f32[4,16,128]{2,1,0:T(8,128)S(1)}, u32[]{:S(2)}, u32[]{:S(2)}) collective-permute-start(f32[4,16,128]{2,1,0:T(8,128)S(1)} %get-tuple-element.63), channel_id=1, source_target_pairs={{0,16},{8,24},{16,32},{24,40},{32,48},{40,56},{48,64},{56,72},{64,... | collective-permute-start | bytes 98312 | tf_op jit(solution)/shard_map/ppermute | solution.py:630
  43.8 13.4 %collective-permute-start.12 = (f32[4,16,128]{2,1,0:T(8,128)S(1)}, f32[4,16,128]{2,1,0:T(8,128)S(1)}, u32[]{:S(2)}, u32[]{:S(2)}) collective-permute-start(f32[4,16,128]{2,1,0:T(8,128)S(1)} %get-tuple-element.65), channel_id=1, source_target_pairs={{0,240},{8,248},{16,0},{24,8},{32,16},{40,24},{48,32},{56,40},{64,... | collective-permute-start | bytes 98312 | tf_op jit(solution)/shard_map/ppermute | solution.py:630
  49.4 7.7 %collective-permute-start.11 = (f32[2,16,128]{2,1,0:T(8,128)S(1)}, f32[2,16,128]{2,1,0:T(8,128)S(1)}, u32[]{:S(2)}, u32[]{:S(2)}) collective-permute-start(f32[2,16,128]{2,1,0:T(8,128)S(1)} %get-tuple-element.64), channel_id=1, source_target_pairs={{0,24},{8,32},{16,40},{24,48},{32,56},{40,64},{48,72},{56,80},{64,... | collective-permute-start | bytes 49160 | tf_op jit(solution)/shard_map/ppermute | solution.py:630
  49.4 7.7 %collective-permute-start.13 = (f32[2,16,128]{2,1,0:T(8,128)S(1)}, f32[2,16,128]{2,1,0:T(8,128)S(1)}, u32[]{:S(2)}, u32[]{:S(2)}) collective-permute-start(f32[2,16,128]{2,1,0:T(8,128)S(1)} %get-tuple-element.66), channel_id=1, source_target_pairs={{0,232},{8,240},{16,248},{24,0},{32,8},{40,16},{48,24},{56,32},{64... | collective-permute-start | bytes 49160 | tf_op jit(solution)/shard_map/ppermute | solution.py:630
  57.2 10.9 %collective-permute-start.17 = (f32[18,16,128]{2,1,0:T(8,128)S(1)}, f32[18,16,128]{2,1,0:T(8,128)S(1)}, u32[]{:S(2)}, u32[]{:S(2)}) collective-permute-start(f32[18,16,128]{2,1,0:T(8,128)S(1)} %shard_map.35.mid), channel_id=1, source_target_pairs={{0,6},{1,7},{2,0},{3,1},{4,2},{5,3},{6,4},{7,5},{8,14},{9,15},{10,... | collective-permute-start | bytes 442376 | tf_op jit(solution)/shard_map/ppermute | solution.py:630
  61.1 6.9 %collective-permute-start.16 = (f32[18,16,128]{2,1,0:T(8,128)S(1)}, f32[18,16,128]{2,1,0:T(8,128)S(1)}, u32[]{:S(2)}, u32[]{:S(2)}) collective-permute-start(f32[18,16,128]{2,1,0:T(8,128)S(1)} %shard_map.35.mid), channel_id=1, source_target_pairs={{0,7},{1,0},{2,1},{3,2},{4,3},{5,4},{6,5},{7,6},{8,15},{9,8},{10,9... | collective-permute-start | bytes 442376 | tf_op jit(solution)/shard_map/ppermute | solution.py:630
  61.1 6.9 %collective-permute-start.15 = (f32[18,16,128]{2,1,0:T(8,128)S(1)}, f32[18,16,128]{2,1,0:T(8,128)S(1)}, u32[]{:S(2)}, u32[]{:S(2)}) collective-permute-start(f32[18,16,128]{2,1,0:T(8,128)S(1)} %shard_map.35.mid), channel_id=1, source_target_pairs={{0,2},{1,3},{2,4},{3,5},{4,6},{5,7},{6,0},{7,1},{8,10},{9,11},{10,... | collective-permute-start | bytes 442376 | tf_op jit(solution)/shard_map/ppermute | solution.py:630
  62.0 6.1 %collective-permute-start.14 = (f32[18,16,128]{2,1,0:T(8,128)S(1)}, f32[18,16,128]{2,1,0:T(8,128)S(1)}, u32[]{:S(2)}, u32[]{:S(2)}) collective-permute-start(f32[18,16,128]{2,1,0:T(8,128)S(1)} %shard_map.35.mid), channel_id=1, source_target_pairs={{0,1},{1,2},{2,3},{3,4},{4,5},{5,6},{6,7},{7,0},{8,9},{9,10},{10,1... | collective-permute-start | bytes 442376 | tf_op jit(solution)/shard_map/ppermute | solution.py:630
  62.9 4.7 %collective-permute-start.19 = (f32[4,16,512]{2,1,0:T(8,128)S(1)}, f32[4,16,512]{2,1,0:T(8,128)S(1)}, u32[]{:S(2)}, u32[]{:S(2)}) collective-permute-start(f32[4,16,512]{2,1,0:T(8,128)S(1)} %get-tuple-element.72), channel_id=1, source_target_pairs={{0,248},{8,0},{16,8},{24,16},{32,24},{40,32},{48,40},{56,48},{64,5... | collective-permute-start | bytes 393224 | tf_op jit(solution)/shard_map/ppermute | solution.py:630

commit v9 on v8

--- a/solution.py
+++ b/solution.py
@@ -507,7 +507,7 @@
             far_down[t - 2, 12:16] = own[t + 2, 12:16]
 
 
-def pack_coarse_y(own, low2, low3, high2, high3, strip):
+def pack_coarse_y(own, low2, low3, high2, high3, rim, strip):
     strip[0, 0:12] = jnp.zeros((12, own.shape[-1]), F32)
     strip[17, 0:12] = jnp.zeros((12, own.shape[-1]), F32)
     for t in range(2):
@@ -673,7 +673,7 @@
     )
     low2, high2 = cycled(up, "gx", 2), cycled(down, "gx", -2)
     low3, high3 = cycled(far_up, "gx", 3), cycled(far_down, "gx", -3)
-    (strip,) = call(pack_coarse_y, [(18, 16, z2)], own, low2, low3, high2, high3)
+    (strip,) = call(pack_coarse_y, [(18, 16, z2)], own, low2, low3, high2, high3, rim)
     ym1, yp1 = cycled(strip, "gy", 1), cycled(strip, "gy", -1)
     ym2, yp2 = cycled(strip, "gy", 2), cycled(strip, "gy", -2)
     (velocity,) = call(

time: 75.1 us -> 76.2 us (1.015)
  starting transfers between devices: 38.7 us -> 42.8 us
  waiting for transfers between devices: 19.5 us -> 16.6 us
    ppermute x20, starting transfers between devices: 38.7 us -> 42.8 us  [cycled(): lax.ppermute(array, axis, [(i, (i + step) % size) for i in range(size)])]
    ppermute x20, waiting for transfers between devices: 19.5 us -> 16.6 us  [cycled(): lax.ppermute(array, axis, [(i, (i + step) % size) for i in range(size)])]
where the time goes in v9:
time: 76.2 us; the launch traced here: 76 us
  starting transfers between devices  42.8 us (56%)
  waiting for transfers between devices  16.6 us (22%)
  Pallas kernels  16.4 us (22%)
    ppermute x20, starting transfers between devices, cycled(): lax.ppermute(array, axis, [(i, (i + step) % size) for i in range(size)])  42.8 us
    ppermute x20, waiting for transfers between devices, cycled(): lax.ppermute(array, axis, [(i, (i + step) % size) for i in range(size)])  16.6 us
    pallas_call x10, Pallas kernels, call(): pl.pallas_call(body, out_shape=outs, in_specs=[pl.BlockSpec(memory_space=...  16.4 us
  transfers between devices with their start and end apart: 20, of which 8 were waited for; matrix products, arithmetic and copies ran while one was open for 0% of the time, Pallas kernels for 7%

profile of v9, /device:TPU:1, one launch (start us, length us, event | category | flops | bytes accessed | tf_op | source)
XLA Modules:
  0.0 76.0 jit_solution(8237349819917440388)
XLA Ops:
  0.0 1.3 %shard_map.28 = (f32[9,16,512]{2,1,0:T(8,128)S(1)}, f32[9,16,512]{2,1,0:T(8,128)S(1)}) custom-call(f32[3,8,16,512]{3,2,1,0:T(8,128)} %f_in.3, s32[8,16,512]{2,1,0:T(8,128)} %ids_in.3), custom_call_target="tpu_custom_call" | custom-call | tf_op jit(solution)/shard_map/pallas_call | solution.py:618
  1.3 2.5 %collective-permute-start = (f32[9,16,512]{2,1,0:T(8,128)S(1)}, f32[9,16,512]{2,1,0:T(8,128)S(1)}, u32[]{:S(2)}, u32[]{:S(2)}) collective-permute-start(f32[9,16,512]{2,1,0:T(8,128)S(1)} %get-tuple-element.42), channel_id=1, source_target_pairs={{0,8},{8,16},{16,24},{24,32},{32,40},{40,48},{48,56},{56,64},{64,7... | collective-permute-start | bytes 884744 | tf_op jit(solution)/shard_map/ppermute | solution.py:630
  3.8 6.2 %collective-permute-start.1 = (f32[9,16,512]{2,1,0:T(8,128)S(1)}, f32[9,16,512]{2,1,0:T(8,128)S(1)}, u32[]{:S(2)}, u32[]{:S(2)}) collective-permute-start(f32[9,16,512]{2,1,0:T(8,128)S(1)} %get-tuple-element.43), channel_id=1, source_target_pairs={{0,248},{8,0},{16,8},{24,16},{32,24},{40,32},{48,40},{56,48},{64,5... | collective-permute-start | bytes 884744 | tf_op jit(solution)/shard_map/ppermute | solution.py:630
  10.0 1.6 %shard_map.30 = (f32[13,8,512]{2,1,0:T(8,128)S(1)}, f32[13,8,512]{2,1,0:T(8,128)S(1)}, f32[3,8,16,512]{3,2,1,0:T(8,128)S(1)}, s32[8,16,512]{2,1,0:T(8,128)S(1)}) custom-call(f32[3,8,16,512]{3,2,1,0:T(8,128)} %f_in.3, s32[8,16,512]{2,1,0:T(8,128)} %ids_in.3), custom_call_target="tpu_custom_call" | custom-call | tf_op jit(solution)/shard_map/pallas_call | solution.py:618
  11.6 2.1 %collective-permute-start.4 = (f32[13,8,512]{2,1,0:T(8,128)S(1)}, f32[13,8,512]{2,1,0:T(8,128)S(1)}, u32[]{:S(2)}, u32[]{:S(2)}) collective-permute-start(f32[13,8,512]{2,1,0:T(8,128)S(1)} %get-tuple-element.48), channel_id=1, source_target_pairs={{0,1},{1,2},{2,3},{3,4},{4,5},{5,6},{6,7},{7,0},{8,9},{9,10},{10,1... | collective-permute-start | bytes 638984 | tf_op jit(solution)/shard_map/ppermute | solution.py:630
  13.8 0.0 collective-permute-start.5
  13.8 2.9 %collective-permute-done.low.refs_0_ = f32[9,16,512]{2,1,0:T(8,128)S(1)} collective-permute-done((f32[9,16,512]{2,1,0:T(8,128)S(1)}, f32[9,16,512]{2,1,0:T(8,128)S(1)}, u32[]{:S(2)}, u32[]{:S(2)}) %collective-permute-start) | collective-permute-done | bytes 294944 | tf_op jit(solution)/shard_map/ppermute | solution.py:630
  16.7 0.0 collective-permute-done.1.high.refs_1_
  16.7 0.1 shard_map.29
  16.8 2.4 %collective-permute-start.2 = (f32[8,8,512]{2,1,0:T(8,128)S(1)}, f32[8,8,512]{2,1,0:T(8,128)S(1)}, u32[]{:S(2)}, u32[]{:S(2)}) collective-permute-start(f32[8,8,512]{2,1,0:T(8,128)S(1)} %get-tuple-element.44), channel_id=1, source_target_pairs={{0,1},{1,2},{2,3},{3,4},{4,5},{5,6},{6,7},{7,0},{8,9},{9,10},{10,1... | collective-permute-start | bytes 393224 | tf_op jit(solution)/shard_map/ppermute | solution.py:630
  19.2 0.0 collective-permute-start.3
  19.2 0.0 collective-permute-done.4.ylow
  19.2 0.0 collective-permute-done.5.yhigh
  19.2 1.3 %shard_map.31 = (f32[3,4,24,512]{3,2,1,0:T(8,128)S(1)}, f32[3,6,24,512]{3,2,1,0:T(8,128)S(1)}, f32[3,8,24,512]{3,2,1,0:T(8,128)S(1)}, f32[8,24,512]{2,1,0:T(8,12...) custom-call(f32[3,8,16,512]{3,2,1,0:T(8,128)S(1)} %get-tuple-element.46.f, ...), custom_call_target="tpu_custom_call" | custom-call | tf_op jit(solution)/shard_map/pallas_call | solution.py:618
  20.5 0.6 collective-permute-done.2.refs_2_
  21.1 2.4 %collective-permute-done.3.refs_3_ = f32[8,8,512]{2,1,0:T(8,128)S(1)} collective-permute-done((f32[8,8,512]{2,1,0:T(8,128)S(1)}, f32[8,8,512]{2,1,0:T(8,128)S(1)}, u32[]{:S(2)}, u32[]{:S(2)}) %collective-permute-start.3) | collective-permute-done | bytes 131104 | tf_op jit(solution)/shard_map/ppermute | solution.py:630
  23.6 3.0 %shard_map.32 = (f32[3,6,24,512]{3,2,1,0:T(8,128)S(1)}, f32[3,6,24,512]{3,2,1,0:T(8,128)S(1)}, f32[3,4,24,512]{3,2,1,0:T(8,128)S(1)}, f32[6,24,512]{2,1,0:T(8,12...) custom-call(f32[9,16,512]{2,1,0:T(8,128)S(1)} %collective-permute-do, ...), custom_call_target="tpu_custom_call" | custom-call | tf_op jit(solution)/shard_map/pallas_call | solution.py:618
  26.6 0.1 collective-permute-start.6
  26.7 4.9 %collective-permute-start.7 = (f32[17,8,256]{2,1,0:T(8,128)S(1)}, f32[17,8,256]{2,1,0:T(8,128)S(1)}, u32[]{:S(2)}, u32[]{:S(2)}) collective-permute-start(f32[17,8,256]{2,1,0:T(8,128)S(1)} %get-tuple-element.59), channel_id=1, source_target_pairs={{0,248},{8,0},{16,8},{24,16},{32,24},{40,32},{48,40},{56,48},{64,5... | collective-permute-start | bytes 417800 | tf_op jit(solution)/shard_map/ppermute | solution.py:630
  31.7 3.8 %collective-permute-done.6.low.xlow = f32[17,8,256]{2,1,0:T(8,128)S(1)} collective-permute-done((f32[17,8,256]{2,1,0:T(8,128)S(1)}, f32[17,8,256]{2,1,0:T(8,128)S(1)}, u32[]{:S(2)}, u32[]{:S(2)}) %collective-permute-start.6) | collective-permute-done | bytes 139296 | tf_op jit(solution)/shard_map/ppermute | solution.py:630
  35.5 0.0 collective-permute-done.7.high.xhigh
  35.5 0.1 shard_map.33
  35.6 0.3 collective-permute-start.8
  35.9 0.4 collective-permute-start.9
  36.3 0.0 collective-permute-start.14
  36.3 4.9 %collective-permute-start.15 = (f32[4,16,512]{2,1,0:T(8,128)S(1)}, f32[4,16,512]{2,1,0:T(8,128)S(1)}, u32[]{:S(2)}, u32[]{:S(2)}) collective-permute-start(f32[4,16,512]{2,1,0:T(8,128)S(1)} %get-tuple-element.68), channel_id=1, source_target_pairs={{0,248},{8,0},{16,8},{24,16},{32,24},{40,32},{48,40},{56,48},{64,5... | collective-permute-start | bytes 393224 | tf_op jit(solution)/shard_map/ppermute | solution.py:630
  41.2 0.0 collective-permute-done.8.ylow
  41.2 0.4 collective-permute-done.9.yhigh
  41.7 2.0 %shard_map.34 = (f32[3,14,24,256]{3,2,1,0:T(8,128)S(1)}, f32[3,12,24,256]{3,2,1,0:T(8,128)S(1)}, f32[13,24,256]{2,1,0:T(8,128)S(1)}, f32[6,12,24,256]{3,2,1,0:T(...) custom-call(f32[3,4,8,256]{3,2,1,0:T(8,128)S(1)} %get-tuple-element., ...), custom_call_target="tpu_custom_call" | custom-call | tf_op jit(solution)/shard_map/pallas_call | solution.py:618
  43.7 0.1 collective-permute-start.10
  43.8 5.7 %collective-permute-start.12 = (f32[4,16,128]{2,1,0:T(8,128)S(1)}, f32[4,16,128]{2,1,0:T(8,128)S(1)}, u32[]{:S(2)}, u32[]{:S(2)}) collective-permute-start(f32[4,16,128]{2,1,0:T(8,128)S(1)} %get-tuple-element.65), channel_id=1, source_target_pairs={{0,240},{8,248},{16,0},{24,8},{32,16},{40,24},{48,32},{56,40},{64,... | collective-permute-start | bytes 98312 | tf_op jit(solution)/shard_map/ppermute | solution.py:630
  49.4 0.0 collective-permute-start.11
  49.4 0.0 collective-permute-done.14.low
  49.4 6.6 %collective-permute-start.13 = (f32[2,16,128]{2,1,0:T(8,128)S(1)}, f32[2,16,128]{2,1,0:T(8,128)S(1)}, u32[]{:S(2)}, u32[]{:S(2)}) collective-permute-start(f32[2,16,128]{2,1,0:T(8,128)S(1)} %get-tuple-element.66), channel_id=1, source_target_pairs={{0,232},{8,240},{16,248},{24,0},{32,8},{40,16},{48,24},{56,32},{64... | collective-permute-start | bytes 49160 | tf_op jit(solution)/shard_map/ppermute | solution.py:630
  56.0 0.0 collective-permute-done.15.high
  56.0 0.4 shard_map.35.rim
  56.4 0.7 collective-permute-done.11.low3
  57.2 0.0 collective-permute-done.13.high3
  57.2 0.0 collective-permute-done.10.low2
  57.2 0.0 collective-permute-done.12.high2
  57.2 3.9 %collective-permute-start.19 = (f32[18,16,128]{2,1,0:T(8,128)S(1)}, f32[18,16,128]{2,1,0:T(8,128)S(1)}, u32[]{:S(2)}, u32[]{:S(2)}) collective-permute-start(f32[18,16,128]{2,1,0:T(8,128)S(1)} %shard_map.36.mid), channel_id=1, source_target_pairs={{0,6},{1,7},{2,0},{3,1},{4,2},{5,3},{6,4},{7,5},{8,14},{9,15},{10,... | collective-permute-start | bytes 442376 | tf_op jit(solution)/shard_map/ppermute | solution.py:630
  61.1 1.4 %collective-permute-start.18 = (f32[18,16,128]{2,1,0:T(8,128)S(1)}, f32[18,16,128]{2,1,0:T(8,128)S(1)}, u32[]{:S(2)}, u32[]{:S(2)}) collective-permute-start(f32[18,16,128]{2,1,0:T(8,128)S(1)} %shard_map.36.mid), channel_id=1, source_target_pairs={{0,7},{1,0},{2,1},{3,2},{4,3},{5,4},{6,5},{7,6},{8,15},{9,8},{10,9... | collective-permute-start | bytes 442376 | tf_op jit(solution)/shard_map/ppermute | solution.py:630
  62.6 1.1 %collective-permute-start.17 = (f32[18,16,128]{2,1,0:T(8,128)S(1)}, f32[18,16,128]{2,1,0:T(8,128)S(1)}, u32[]{:S(2)}, u32[]{:S(2)}) collective-permute-start(f32[18,16,128]{2,1,0:T(8,128)S(1)} %shard_map.36.mid), channel_id=1, source_target_pairs={{0,2},{1,3},{2,4},{3,5},{4,6},{5,7},{6,0},{7,1},{8,10},{9,11},{10,... | collective-permute-start | bytes 442376 | tf_op jit(solution)/shard_map/ppermute | solution.py:630
  63.7 0.0 collective-permute-start.16
  63.7 0.0 collective-permute-done.19.yp2
  63.7 4.6 %collective-permute-done.18.yp1 = f32[18,16,128]{2,1,0:T(8,128)S(1)} collective-permute-done((f32[18,16,128]{2,1,0:T(8,128)S(1)}, f32[18,16,128]{2,1,0:T(8,128)S(1)}, u32[]{:S(2)}, u32[]{:S(2)}) %collective-permute-start.18) | collective-permute-done | bytes 147488 | tf_op jit(solution)/shard_map/ppermute | solution.py:630
  68.3 1.0 %collective-permute-done.17.ym2 = f32[18,16,128]{2,1,0:T(8,128)S(1)} collective-permute-done((f32[18,16,128]{2,1,0:T(8,128)S(1)}, f32[18,16,128]{2,1,0:T(8,128)S(1)}, u32[]{:S(2)}, u32[]{:S(2)}) %collective-permute-start.17) | collective-permute-done | bytes 147488 | tf_op jit(solution)/shard_map/ppermute | solution.py:630
  69.2 0.0 collective-permute-done.16.ym1
  69.2 6.6 %shard_map.37 = f32[3,8,16,512]{3,2,1,0:T(8,128)} custom-call(f32[18,16,128]{2,1,0:T(8,128)S(1)} %shard_map.36.mid, f32[18,16,128]{2,1,0:T(8,128)S(1)} %collective-permute-done.16.ym1, f32[18,16,128]{2,1,0:T(8,128)S(1)} %collective-permute-done.17.ym2, f32[18,16,128]{2,1,0:T(8,128)S(1)} %collective-permute-done.18.yp1, ...), custom_call_target="tpu_custom_call" | custom-call | tf_op jit(solution)/shard_map/pallas_call | solution.py:618
  (1 shorter events, 0.0 us)
Async XLA Ops:
  1.3 15.4 %collective-permute-start = (f32[9,16,512]{2,1,0:T(8,128)S(1)}, f32[9,16,512]{2,1,0:T(8,128)S(1)}, u32[]{:S(2)}, u32[]{:S(2)}) collective-permute-start(f32[9,16,512]{2,1,0:T(8,128)S(1)} %get-tuple-element.42), channel_id=1, source_target_pairs={{0,8},{8,16},{16,24},{24,32},{32,40},{40,48},{48,56},{56,64},{64,7... | collective-permute-start | bytes 884744 | tf_op jit(solution)/shard_map/ppermute | solution.py:630
  3.8 12.9 %collective-permute-start.1 = (f32[9,16,512]{2,1,0:T(8,128)S(1)}, f32[9,16,512]{2,1,0:T(8,128)S(1)}, u32[]{:S(2)}, u32[]{:S(2)}) collective-permute-start(f32[9,16,512]{2,1,0:T(8,128)S(1)} %get-tuple-element.43), channel_id=1, source_target_pairs={{0,248},{8,0},{16,8},{24,16},{32,24},{40,32},{48,40},{56,48},{64,5... | collective-permute-start | bytes 884744 | tf_op jit(solution)/shard_map/ppermute | solution.py:630
  11.6 7.6 %collective-permute-start.4 = (f32[13,8,512]{2,1,0:T(8,128)S(1)}, f32[13,8,512]{2,1,0:T(8,128)S(1)}, u32[]{:S(2)}, u32[]{:S(2)}) collective-permute-start(f32[13,8,512]{2,1,0:T(8,128)S(1)} %get-tuple-element.48), channel_id=1, source_target_pairs={{0,1},{1,2},{2,3},{3,4},{4,5},{5,6},{6,7},{7,0},{8,9},{9,10},{10,1... | collective-permute-start | bytes 638984 | tf_op jit(solution)/shard_map/ppermute | solution.py:630
  13.8 5.4 %collective-permute-start.5 = (f32[13,8,512]{2,1,0:T(8,128)S(1)}, f32[13,8,512]{2,1,0:T(8,128)S(1)}, u32[]{:S(2)}, u32[]{:S(2)}) collective-permute-start(f32[13,8,512]{2,1,0:T(8,128)S(1)} %get-tuple-element.49), channel_id=1, source_target_pairs={{0,7},{1,0},{2,1},{3,2},{4,3},{5,4},{6,5},{7,6},{8,15},{9,8},{10,9... | collective-permute-start | bytes 638984 | tf_op jit(solution)/shard_map/ppermute | solution.py:630
  16.8 4.4 %collective-permute-start.2 = (f32[8,8,512]{2,1,0:T(8,128)S(1)}, f32[8,8,512]{2,1,0:T(8,128)S(1)}, u32[]{:S(2)}, u32[]{:S(2)}) collective-permute-start(f32[8,8,512]{2,1,0:T(8,128)S(1)} %get-tuple-element.44), channel_id=1, source_target_pairs={{0,1},{1,2},{2,3},{3,4},{4,5},{5,6},{6,7},{7,0},{8,9},{9,10},{10,1... | collective-permute-start | bytes 393224 | tf_op jit(solution)/shard_map/ppermute | solution.py:630
  19.2 4.4 %collective-permute-start.3 = (f32[8,8,512]{2,1,0:T(8,128)S(1)}, f32[8,8,512]{2,1,0:T(8,128)S(1)}, u32[]{:S(2)}, u32[]{:S(2)}) collective-permute-start(f32[8,8,512]{2,1,0:T(8,128)S(1)} %get-tuple-element.45), channel_id=1, source_target_pairs={{0,7},{1,0},{2,1},{3,2},{4,3},{5,4},{6,5},{7,6},{8,15},{9,8},{10,9... | collective-permute-start | bytes 393224 | tf_op jit(solution)/shard_map/ppermute | solution.py:630
  26.6 8.9 %collective-permute-start.6 = (f32[17,8,256]{2,1,0:T(8,128)S(1)}, f32[17,8,256]{2,1,0:T(8,128)S(1)}, u32[]{:S(2)}, u32[]{:S(2)}) collective-permute-start(f32[17,8,256]{2,1,0:T(8,128)S(1)} %get-tuple-element.58), channel_id=1, source_target_pairs={{0,8},{8,16},{16,24},{24,32},{32,40},{40,48},{48,56},{56,64},{64,7... | collective-permute-start | bytes 417800 | tf_op jit(solution)/shard_map/ppermute | solution.py:630
  26.7 8.8 %collective-permute-start.7 = (f32[17,8,256]{2,1,0:T(8,128)S(1)}, f32[17,8,256]{2,1,0:T(8,128)S(1)}, u32[]{:S(2)}, u32[]{:S(2)}) collective-permute-start(f32[17,8,256]{2,1,0:T(8,128)S(1)} %get-tuple-element.59), channel_id=1, source_target_pairs={{0,248},{8,0},{16,8},{24,16},{32,24},{40,32},{48,40},{56,48},{64,5... | collective-permute-start | bytes 417800 | tf_op jit(solution)/shard_map/ppermute | solution.py:630
  35.6 5.6 %collective-permute-start.8 = (f32[28,8,256]{2,1,0:T(8,128)S(1)}, f32[28,8,256]{2,1,0:T(8,128)S(1)}, u32[]{:S(2)}, u32[]{:S(2)}) collective-permute-start(f32[28,8,256]{2,1,0:T(8,128)S(1)} %get-tuple-element.60), channel_id=1, source_target_pairs={{0,1},{1,2},{2,3},{3,4},{4,5},{5,6},{6,7},{7,0},{8,9},{9,10},{10,1... | collective-permute-start | bytes 688136 | tf_op jit(solution)/shard_map/ppermute | solution.py:630
  35.9 5.7 %collective-permute-start.9 = (f32[28,8,256]{2,1,0:T(8,128)S(1)}, f32[28,8,256]{2,1,0:T(8,128)S(1)}, u32[]{:S(2)}, u32[]{:S(2)}) collective-permute-start(f32[28,8,256]{2,1,0:T(8,128)S(1)} %get-tuple-element.61), channel_id=1, source_target_pairs={{0,7},{1,0},{2,1},{3,2},{4,3},{5,4},{6,5},{7,6},{8,15},{9,8},{10,9... | collective-permute-start | bytes 688136 | tf_op jit(solution)/shard_map/ppermute | solution.py:630
  36.3 13.1 %collective-permute-start.14 = (f32[4,16,512]{2,1,0:T(8,128)S(1)}, f32[4,16,512]{2,1,0:T(8,128)S(1)}, u32[]{:S(2)}, u32[]{:S(2)}) collective-permute-start(f32[4,16,512]{2,1,0:T(8,128)S(1)} %get-tuple-element.67), channel_id=1, source_target_pairs={{0,8},{8,16},{16,24},{24,32},{32,40},{40,48},{48,56},{56,64},{64,7... | collective-permute-start | bytes 393224 | tf_op jit(solution)/shard_map/ppermute | solution.py:630
  36.3 19.7 %collective-permute-start.15 = (f32[4,16,512]{2,1,0:T(8,128)S(1)}, f32[4,16,512]{2,1,0:T(8,128)S(1)}, u32[]{:S(2)}, u32[]{:S(2)}) collective-permute-start(f32[4,16,512]{2,1,0:T(8,128)S(1)} %get-tuple-element.68), channel_id=1, source_target_pairs={{0,248},{8,0},{16,8},{24,16},{32,24},{40,32},{48,40},{56,48},{64,5... | collective-permute-start | bytes 393224 | tf_op jit(solution)/shard_map/ppermute | solution.py:630
  43.7 13.5 %collective-permute-start.10 = (f32[4,16,128]{2,1,0:T(8,128)S(1)}, f32[4,16,128]{2,1,0:T(8,128)S(1)}, u32[]{:S(2)}, u32[]{:S(2)}) collective-permute-start(f32[4,16,128]{2,1,0:T(8,128)S(1)} %get-tuple-element.63), channel_id=1, source_target_pairs={{0,16},{8,24},{16,32},{24,40},{32,48},{40,56},{48,64},{56,72},{64,... | collective-permute-start | bytes 98312 | tf_op jit(solution)/shard_map/ppermute | solution.py:630
  43.8 13.4 %collective-permute-start.12 = (f32[4,16,128]{2,1,0:T(8,128)S(1)}, f32[4,16,128]{2,1,0:T(8,128)S(1)}, u32[]{:S(2)}, u32[]{:S(2)}) collective-permute-start(f32[4,16,128]{2,1,0:T(8,128)S(1)} %get-tuple-element.65), channel_id=1, source_target_pairs={{0,240},{8,248},{16,0},{24,8},{32,16},{40,24},{48,32},{56,40},{64,... | collective-permute-start | bytes 98312 | tf_op jit(solution)/shard_map/ppermute | solution.py:630
  49.4 7.8 %collective-permute-start.11 = (f32[2,16,128]{2,1,0:T(8,128)S(1)}, f32[2,16,128]{2,1,0:T(8,128)S(1)}, u32[]{:S(2)}, u32[]{:S(2)}) collective-permute-start(f32[2,16,128]{2,1,0:T(8,128)S(1)} %get-tuple-element.64), channel_id=1, source_target_pairs={{0,24},{8,32},{16,40},{24,48},{32,56},{40,64},{48,72},{56,80},{64,... | collective-permute-start | bytes 49160 | tf_op jit(solution)/shard_map/ppermute | solution.py:630
  49.4 7.8 %collective-permute-start.13 = (f32[2,16,128]{2,1,0:T(8,128)S(1)}, f32[2,16,128]{2,1,0:T(8,128)S(1)}, u32[]{:S(2)}, u32[]{:S(2)}) collective-permute-start(f32[2,16,128]{2,1,0:T(8,128)S(1)} %get-tuple-element.66), channel_id=1, source_target_pairs={{0,232},{8,240},{16,248},{24,0},{32,8},{40,16},{48,24},{56,32},{64... | collective-permute-start | bytes 49160 | tf_op jit(solution)/shard_map/ppermute | solution.py:630
  57.2 6.5 %collective-permute-start.19 = (f32[18,16,128]{2,1,0:T(8,128)S(1)}, f32[18,16,128]{2,1,0:T(8,128)S(1)}, u32[]{:S(2)}, u32[]{:S(2)}) collective-permute-start(f32[18,16,128]{2,1,0:T(8,128)S(1)} %shard_map.36.mid), channel_id=1, source_target_pairs={{0,6},{1,7},{2,0},{3,1},{4,2},{5,3},{6,4},{7,5},{8,14},{9,15},{10,... | collective-permute-start | bytes 442376 | tf_op jit(solution)/shard_map/ppermute | solution.py:630
  61.1 7.1 %collective-permute-start.18 = (f32[18,16,128]{2,1,0:T(8,128)S(1)}, f32[18,16,128]{2,1,0:T(8,128)S(1)}, u32[]{:S(2)}, u32[]{:S(2)}) collective-permute-start(f32[18,16,128]{2,1,0:T(8,128)S(1)} %shard_map.36.mid), channel_id=1, source_target_pairs={{0,7},{1,0},{2,1},{3,2},{4,3},{5,4},{6,5},{7,6},{8,15},{9,8},{10,9... | collective-permute-start | bytes 442376 | tf_op jit(solution)/shard_map/ppermute | solution.py:630
  62.6 6.7 %collective-permute-start.17 = (f32[18,16,128]{2,1,0:T(8,128)S(1)}, f32[18,16,128]{2,1,0:T(8,128)S(1)}, u32[]{:S(2)}, u32[]{:S(2)}) collective-permute-start(f32[18,16,128]{2,1,0:T(8,128)S(1)} %shard_map.36.mid), channel_id=1, source_target_pairs={{0,2},{1,3},{2,4},{3,5},{4,6},{5,7},{6,0},{7,1},{8,10},{9,11},{10,... | collective-permute-start | bytes 442376 | tf_op jit(solution)/shard_map/ppermute | solution.py:630
  63.7 5.6 %collective-permute-start.16 = (f32[18,16,128]{2,1,0:T(8,128)S(1)}, f32[18,16,128]{2,1,0:T(8,128)S(1)}, u32[]{:S(2)}, u32[]{:S(2)}) collective-permute-start(f32[18,16,128]{2,1,0:T(8,128)S(1)} %shard_map.36.mid), channel_id=1, source_target_pairs={{0,1},{1,2},{2,3},{3,4},{4,5},{5,6},{6,7},{7,0},{8,9},{9,10},{10,1... | collective-permute-start | bytes 442376 | tf_op jit(solution)/shard_map/ppermute | solution.py:630

commit v10 on v8

--- a/solution.py
+++ b/solution.py
@@ -180,19 +180,15 @@
         copy.wait()
 
 
-def pack_fine_x(f_in, ids_in, xup, xdown, f, ids, arrived):
-    copied(
-        [pltpu.make_async_copy(ids_in.at[5 * k : 5 * k + 3], ids.at[3 * k : 3 * k + 3], arrived.at[k]) for k in range(2)]
-        + [
-            pltpu.make_async_copy(f_in.at[:, 6 * k + n], f.at[:, 2 * k + n], arrived.at[2 + 2 * k + n])
-            for k in range(2)
-            for n in range(2)
-        ]
-    )
+def pack_fine_x(f_in, ids_in, xup, xdown, ids, arrived):
+    copies = [pltpu.make_async_copy(ids_in.at[5 * k : 5 * k + 3], ids.at[3 * k : 3 * k + 3], arrived.at[k]) for k in range(2)]
+    for c in range(3):
+        for k, out in enumerate((xdown, xup)):
+            copies.append(
+                pltpu.make_async_copy(f_in.at[c, 6 * k : 6 * k + 2], out.at[2 * c : 2 * c + 2], arrived.at[2 + 2 * c + k])
+            )
+    copied(copies)
     for n, out in enumerate((xdown, xup)):
-        for c in range(3):
-            for k in range(2):
-                out[2 * c + k] = f[c, 2 * n + k]
         for k in range(3):
             out[6 + k] = materials(ids[3 * n + k])
 
@@ -636,7 +632,7 @@
     inputs = [pltpu.with_memory_space_constraint(a, pltpu.HBM) for a in (forcing, phase_ids)]
     xup, xdown = call(
         pack_fine_x, [(9, 16, z0)] * 2, *inputs,
-        scratch=[(3, 4, 16, z0), jax.ShapeDtypeStruct((6, 16, z0), jnp.int32)], copies=6, where_in=pltpu.HBM,
+        scratch=[jax.ShapeDtypeStruct((6, 16, z0), jnp.int32)], copies=8, where_in=pltpu.HBM,
     )
     yup, ydown, f0, ids0 = call(
         pack_fine_y,

time: 75.1 us -> 75 us (level)
  no operation moved by 1% of the time
where the time goes in v10:
time: 75 us; the launch traced here: 74.9 us
  starting transfers between devices  38.7 us (52%)
  waiting for transfers between devices  19.5 us (26%)
  Pallas kernels  16.4 us (22%)
    ppermute x20, starting transfers between devices, cycled(): lax.ppermute(array, axis, [(i, (i + step) % size) for i in range(size)])  38.7 us
    ppermute x20, waiting for transfers between devices, cycled(): lax.ppermute(array, axis, [(i, (i + step) % size) for i in range(size)])  19.5 us
    pallas_call x10, Pallas kernels, call(): pl.pallas_call(body, out_shape=outs, in_specs=[pl.BlockSpec(memory_space=...  16.4 us
  transfers between devices with their start and end apart: 20, of which 8 were waited for; matrix products, arithmetic and copies ran while one was open for 0% of the time, Pallas kernels for 7%

profile of v10, /device:TPU:1, one launch (start us, length us, event | category | flops | bytes accessed | tf_op | source)
XLA Modules:
  0.0 74.9 jit_solution(16174179963773328917)
XLA Ops:
  0.0 1.2 %shard_map.28 = (f32[9,16,512]{2,1,0:T(8,128)S(1)}, f32[9,16,512]{2,1,0:T(8,128)S(1)}) custom-call(f32[3,8,16,512]{3,2,1,0:T(8,128)} %f_in.3, s32[8,16,512]{2,1,0:T(8,128)} %ids_in.3), custom_call_target="tpu_custom_call" | custom-call | tf_op jit(solution)/shard_map/pallas_call | solution.py:614
  1.2 2.5 %collective-permute-start = (f32[9,16,512]{2,1,0:T(8,128)S(1)}, f32[9,16,512]{2,1,0:T(8,128)S(1)}, u32[]{:S(2)}, u32[]{:S(2)}) collective-permute-start(f32[9,16,512]{2,1,0:T(8,128)S(1)} %get-tuple-element.42), channel_id=1, source_target_pairs={{0,8},{8,16},{16,24},{24,32},{32,40},{40,48},{48,56},{56,64},{64,7... | collective-permute-start | bytes 884744 | tf_op jit(solution)/shard_map/ppermute | solution.py:626
  3.8 6.2 %collective-permute-start.1 = (f32[9,16,512]{2,1,0:T(8,128)S(1)}, f32[9,16,512]{2,1,0:T(8,128)S(1)}, u32[]{:S(2)}, u32[]{:S(2)}) collective-permute-start(f32[9,16,512]{2,1,0:T(8,128)S(1)} %get-tuple-element.43), channel_id=1, source_target_pairs={{0,248},{8,0},{16,8},{24,16},{32,24},{40,32},{48,40},{56,48},{64,5... | collective-permute-start | bytes 884744 | tf_op jit(solution)/shard_map/ppermute | solution.py:626
  10.0 1.6 %shard_map.30 = (f32[13,8,512]{2,1,0:T(8,128)S(1)}, f32[13,8,512]{2,1,0:T(8,128)S(1)}, f32[3,8,16,512]{3,2,1,0:T(8,128)S(1)}, s32[8,16,512]{2,1,0:T(8,128)S(1)}) custom-call(f32[3,8,16,512]{3,2,1,0:T(8,128)} %f_in.3, s32[8,16,512]{2,1,0:T(8,128)} %ids_in.3), custom_call_target="tpu_custom_call" | custom-call | tf_op jit(solution)/shard_map/pallas_call | solution.py:614
  11.6 2.1 %collective-permute-start.4 = (f32[13,8,512]{2,1,0:T(8,128)S(1)}, f32[13,8,512]{2,1,0:T(8,128)S(1)}, u32[]{:S(2)}, u32[]{:S(2)}) collective-permute-start(f32[13,8,512]{2,1,0:T(8,128)S(1)} %get-tuple-element.48), channel_id=1, source_target_pairs={{0,1},{1,2},{2,3},{3,4},{4,5},{5,6},{6,7},{7,0},{8,9},{9,10},{10,1... | collective-permute-start | bytes 638984 | tf_op jit(solution)/shard_map/ppermute | solution.py:626
  13.7 0.0 collective-permute-start.5
  13.7 2.9 %collective-permute-done.low.refs_0_ = f32[9,16,512]{2,1,0:T(8,128)S(1)} collective-permute-done((f32[9,16,512]{2,1,0:T(8,128)S(1)}, f32[9,16,512]{2,1,0:T(8,128)S(1)}, u32[]{:S(2)}, u32[]{:S(2)}) %collective-permute-start) | collective-permute-done | bytes 294944 | tf_op jit(solution)/shard_map/ppermute | solution.py:626
  16.6 0.0 collective-permute-done.1.high.refs_1_
  16.6 0.1 shard_map.29
  16.7 2.4 %collective-permute-start.2 = (f32[8,8,512]{2,1,0:T(8,128)S(1)}, f32[8,8,512]{2,1,0:T(8,128)S(1)}, u32[]{:S(2)}, u32[]{:S(2)}) collective-permute-start(f32[8,8,512]{2,1,0:T(8,128)S(1)} %get-tuple-element.44), channel_id=1, source_target_pairs={{0,1},{1,2},{2,3},{3,4},{4,5},{5,6},{6,7},{7,0},{8,9},{9,10},{10,1... | collective-permute-start | bytes 393224 | tf_op jit(solution)/shard_map/ppermute | solution.py:626
  19.1 0.0 collective-permute-start.3
  19.1 0.0 collective-permute-done.4.ylow
  19.1 0.0 collective-permute-done.5.yhigh
  19.1 1.3 %shard_map.31 = (f32[3,4,24,512]{3,2,1,0:T(8,128)S(1)}, f32[3,6,24,512]{3,2,1,0:T(8,128)S(1)}, f32[3,8,24,512]{3,2,1,0:T(8,128)S(1)}, f32[8,24,512]{2,1,0:T(8,12...) custom-call(f32[3,8,16,512]{3,2,1,0:T(8,128)S(1)} %get-tuple-element.46.f, ...), custom_call_target="tpu_custom_call" | custom-call | tf_op jit(solution)/shard_map/pallas_call | solution.py:614
  20.5 0.6 collective-permute-done.2.refs_2_
  21.1 2.4 %collective-permute-done.3.refs_3_ = f32[8,8,512]{2,1,0:T(8,128)S(1)} collective-permute-done((f32[8,8,512]{2,1,0:T(8,128)S(1)}, f32[8,8,512]{2,1,0:T(8,128)S(1)}, u32[]{:S(2)}, u32[]{:S(2)}) %collective-permute-start.3) | collective-permute-done | bytes 131104 | tf_op jit(solution)/shard_map/ppermute | solution.py:626
  23.5 3.0 %shard_map.32 = (f32[3,6,24,512]{3,2,1,0:T(8,128)S(1)}, f32[3,6,24,512]{3,2,1,0:T(8,128)S(1)}, f32[3,4,24,512]{3,2,1,0:T(8,128)S(1)}, f32[6,24,512]{2,1,0:T(8,12...) custom-call(f32[9,16,512]{2,1,0:T(8,128)S(1)} %collective-permute-do, ...), custom_call_target="tpu_custom_call" | custom-call | tf_op jit(solution)/shard_map/pallas_call | solution.py:614
  26.6 0.1 collective-permute-start.6
  26.7 4.9 %collective-permute-start.7 = (f32[17,8,256]{2,1,0:T(8,128)S(1)}, f32[17,8,256]{2,1,0:T(8,128)S(1)}, u32[]{:S(2)}, u32[]{:S(2)}) collective-permute-start(f32[17,8,256]{2,1,0:T(8,128)S(1)} %get-tuple-element.59), channel_id=1, source_target_pairs={{0,248},{8,0},{16,8},{24,16},{32,24},{40,32},{48,40},{56,48},{64,5... | collective-permute-start | bytes 417800 | tf_op jit(solution)/shard_map/ppermute | solution.py:626
  31.6 3.8 %collective-permute-done.6.low.xlow = f32[17,8,256]{2,1,0:T(8,128)S(1)} collective-permute-done((f32[17,8,256]{2,1,0:T(8,128)S(1)}, f32[17,8,256]{2,1,0:T(8,128)S(1)}, u32[]{:S(2)}, u32[]{:S(2)}) %collective-permute-start.6) | collective-permute-done | bytes 139296 | tf_op jit(solution)/shard_map/ppermute | solution.py:626
  35.4 0.0 collective-permute-done.7.high.xhigh
  35.4 0.1 shard_map.33
  35.5 0.3 collective-permute-start.8
  35.9 0.4 collective-permute-start.9
  36.3 0.0 collective-permute-start.18
  36.3 2.5 %collective-permute-done.8.ylow = f32[28,8,256]{2,1,0:T(8,128)S(1)} collective-permute-done((f32[28,8,256]{2,1,0:T(8,128)S(1)}, f32[28,8,256]{2,1,0:T(8,128)S(1)}, u32[]{:S(2)}, u32[]{:S(2)}) %collective-permute-start.8) | collective-permute-done | bytes 229408 | tf_op jit(solution)/shard_map/ppermute | solution.py:626
  38.8 2.8 %collective-permute-done.9.yhigh = f32[28,8,256]{2,1,0:T(8,128)S(1)} collective-permute-done((f32[28,8,256]{2,1,0:T(8,128)S(1)}, f32[28,8,256]{2,1,0:T(8,128)S(1)}, u32[]{:S(2)}, u32[]{:S(2)}) %collective-permute-start.9) | collective-permute-done | bytes 229408 | tf_op jit(solution)/shard_map/ppermute | solution.py:626
  41.6 2.0 %shard_map.34 = (f32[3,14,24,256]{3,2,1,0:T(8,128)S(1)}, f32[3,12,24,256]{3,2,1,0:T(8,128)S(1)}, f32[13,24,256]{2,1,0:T(8,128)S(1)}, f32[6,12,24,256]{3,2,1,0:T(...) custom-call(f32[3,4,8,256]{3,2,1,0:T(8,128)S(1)} %get-tuple-element., ...), custom_call_target="tpu_custom_call" | custom-call | tf_op jit(solution)/shard_map/pallas_call | solution.py:614
  43.6 0.1 collective-permute-start.10
  43.7 5.7 %collective-permute-start.12 = (f32[4,16,128]{2,1,0:T(8,128)S(1)}, f32[4,16,128]{2,1,0:T(8,128)S(1)}, u32[]{:S(2)}, u32[]{:S(2)}) collective-permute-start(f32[4,16,128]{2,1,0:T(8,128)S(1)} %get-tuple-element.65), channel_id=1, source_target_pairs={{0,240},{8,248},{16,0},{24,8},{32,16},{40,24},{48,32},{56,40},{64,... | collective-permute-start | bytes 98312 | tf_op jit(solution)/shard_map/ppermute | solution.py:626
  49.4 0.0 collective-permute-start.11
  49.4 6.6 %collective-permute-start.13 = (f32[2,16,128]{2,1,0:T(8,128)S(1)}, f32[2,16,128]{2,1,0:T(8,128)S(1)}, u32[]{:S(2)}, u32[]{:S(2)}) collective-permute-start(f32[2,16,128]{2,1,0:T(8,128)S(1)} %get-tuple-element.66), channel_id=1, source_target_pairs={{0,232},{8,240},{16,248},{24,0},{32,8},{40,16},{48,24},{56,32},{64... | collective-permute-start | bytes 49160 | tf_op jit(solution)/shard_map/ppermute | solution.py:626
  56.0 1.1 %collective-permute-done.11.low3 = f32[2,16,128]{2,1,0:T(8,128)S(1)} collective-permute-done((f32[2,16,128]{2,1,0:T(8,128)S(1)}, f32[2,16,128]{2,1,0:T(8,128)S(1)}, u32[]{:S(2)}, u32[]{:S(2)}) %collective-permute-start.11) | collective-permute-done | bytes 16416 | tf_op jit(solution)/shard_map/ppermute | solution.py:626
  57.1 0.0 collective-permute-done.13.high3
  57.1 0.0 collective-permute-done.10.low2
  57.1 0.0 collective-permute-done.12.high2
  57.1 4.0 %collective-permute-start.17 = (f32[18,16,128]{2,1,0:T(8,128)S(1)}, f32[18,16,128]{2,1,0:T(8,128)S(1)}, u32[]{:S(2)}, u32[]{:S(2)}) collective-permute-start(f32[18,16,128]{2,1,0:T(8,128)S(1)} %shard_map.35.mid), channel_id=1, source_target_pairs={{0,6},{1,7},{2,0},{3,1},{4,2},{5,3},{6,4},{7,5},{8,14},{9,15},{10,... | collective-permute-start | bytes 442376 | tf_op jit(solution)/shard_map/ppermute | solution.py:626
  61.1 0.0 collective-permute-start.16
  61.1 0.9 %collective-permute-start.15 = (f32[18,16,128]{2,1,0:T(8,128)S(1)}, f32[18,16,128]{2,1,0:T(8,128)S(1)}, u32[]{:S(2)}, u32[]{:S(2)}) collective-permute-start(f32[18,16,128]{2,1,0:T(8,128)S(1)} %shard_map.35.mid), channel_id=1, source_target_pairs={{0,2},{1,3},{2,4},{3,5},{4,6},{5,7},{6,0},{7,1},{8,10},{9,11},{10,... | collective-permute-start | bytes 442376 | tf_op jit(solution)/shard_map/ppermute | solution.py:626
  62.0 0.9 %collective-permute-start.14 = (f32[18,16,128]{2,1,0:T(8,128)S(1)}, f32[18,16,128]{2,1,0:T(8,128)S(1)}, u32[]{:S(2)}, u32[]{:S(2)}) collective-permute-start(f32[18,16,128]{2,1,0:T(8,128)S(1)} %shard_map.35.mid), channel_id=1, source_target_pairs={{0,1},{1,2},{2,3},{3,4},{4,5},{5,6},{6,7},{7,0},{8,9},{9,10},{10,1... | collective-permute-start | bytes 442376 | tf_op jit(solution)/shard_map/ppermute | solution.py:626
  62.9 0.0 collective-permute-done.18.low
  62.9 1.5 %collective-permute-start.19 = (f32[4,16,512]{2,1,0:T(8,128)S(1)}, f32[4,16,512]{2,1,0:T(8,128)S(1)}, u32[]{:S(2)}, u32[]{:S(2)}) collective-permute-start(f32[4,16,512]{2,1,0:T(8,128)S(1)} %get-tuple-element.72), channel_id=1, source_target_pairs={{0,248},{8,0},{16,8},{24,16},{32,24},{40,32},{48,40},{56,48},{64,5... | collective-permute-start | bytes 393224 | tf_op jit(solution)/shard_map/ppermute | solution.py:626
  64.4 3.2 %collective-permute-done.19.high = f32[4,16,512]{2,1,0:T(8,128)S(1)} collective-permute-done((f32[4,16,512]{2,1,0:T(8,128)S(1)}, f32[4,16,512]{2,1,0:T(8,128)S(1)}, u32[]{:S(2)}, u32[]{:S(2)}) %collective-permute-start.19) | collective-permute-done | bytes 131104 | tf_op jit(solution)/shard_map/ppermute | solution.py:626
  67.6 0.4 shard_map.36.rim
  68.0 0.0 collective-permute-done.17.yp2
  68.0 0.0 collective-permute-done.16.yp1
  68.0 0.0 collective-permute-done.15.ym2
  68.0 0.0 collective-permute-done.14.ym1
  68.1 6.6 %shard_map.37 = f32[3,8,16,512]{3,2,1,0:T(8,128)} custom-call(f32[18,16,128]{2,1,0:T(8,128)S(1)} %shard_map.35.mid, f32[18,16,128]{2,1,0:T(8,128)S(1)} %collective-permute-done.14.ym1, f32[18,16,128]{2,1,0:T(8,128)S(1)} %collective-permute-done.15.ym2, f32[18,16,128]{2,1,0:T(8,128)S(1)} %collective-permute-done.16.yp1, ...), custom_call_target="tpu_custom_call" | custom-call | tf_op jit(solution)/shard_map/pallas_call | solution.py:614
  (1 shorter events, 0.0 us)
Async XLA Ops:
  1.2 15.4 %collective-permute-start = (f32[9,16,512]{2,1,0:T(8,128)S(1)}, f32[9,16,512]{2,1,0:T(8,128)S(1)}, u32[]{:S(2)}, u32[]{:S(2)}) collective-permute-start(f32[9,16,512]{2,1,0:T(8,128)S(1)} %get-tuple-element.42), channel_id=1, source_target_pairs={{0,8},{8,16},{16,24},{24,32},{32,40},{40,48},{48,56},{56,64},{64,7... | collective-permute-start | bytes 884744 | tf_op jit(solution)/shard_map/ppermute | solution.py:626
  3.8 12.9 %collective-permute-start.1 = (f32[9,16,512]{2,1,0:T(8,128)S(1)}, f32[9,16,512]{2,1,0:T(8,128)S(1)}, u32[]{:S(2)}, u32[]{:S(2)}) collective-permute-start(f32[9,16,512]{2,1,0:T(8,128)S(1)} %get-tuple-element.43), channel_id=1, source_target_pairs={{0,248},{8,0},{16,8},{24,16},{32,24},{40,32},{48,40},{56,48},{64,5... | collective-permute-start | bytes 884744 | tf_op jit(solution)/shard_map/ppermute | solution.py:626
  11.6 7.6 %collective-permute-start.4 = (f32[13,8,512]{2,1,0:T(8,128)S(1)}, f32[13,8,512]{2,1,0:T(8,128)S(1)}, u32[]{:S(2)}, u32[]{:S(2)}) collective-permute-start(f32[13,8,512]{2,1,0:T(8,128)S(1)} %get-tuple-element.48), channel_id=1, source_target_pairs={{0,1},{1,2},{2,3},{3,4},{4,5},{5,6},{6,7},{7,0},{8,9},{9,10},{10,1... | collective-permute-start | bytes 638984 | tf_op jit(solution)/shard_map/ppermute | solution.py:626
  13.7 5.4 %collective-permute-start.5 = (f32[13,8,512]{2,1,0:T(8,128)S(1)}, f32[13,8,512]{2,1,0:T(8,128)S(1)}, u32[]{:S(2)}, u32[]{:S(2)}) collective-permute-start(f32[13,8,512]{2,1,0:T(8,128)S(1)} %get-tuple-element.49), channel_id=1, source_target_pairs={{0,7},{1,0},{2,1},{3,2},{4,3},{5,4},{6,5},{7,6},{8,15},{9,8},{10,9... | collective-permute-start | bytes 638984 | tf_op jit(solution)/shard_map/ppermute | solution.py:626
  16.7 4.4 %collective-permute-start.2 = (f32[8,8,512]{2,1,0:T(8,128)S(1)}, f32[8,8,512]{2,1,0:T(8,128)S(1)}, u32[]{:S(2)}, u32[]{:S(2)}) collective-permute-start(f32[8,8,512]{2,1,0:T(8,128)S(1)} %get-tuple-element.44), channel_id=1, source_target_pairs={{0,1},{1,2},{2,3},{3,4},{4,5},{5,6},{6,7},{7,0},{8,9},{9,10},{10,1... | collective-permute-start | bytes 393224 | tf_op jit(solution)/shard_map/ppermute | solution.py:626
  19.1 4.4 %collective-permute-start.3 = (f32[8,8,512]{2,1,0:T(8,128)S(1)}, f32[8,8,512]{2,1,0:T(8,128)S(1)}, u32[]{:S(2)}, u32[]{:S(2)}) collective-permute-start(f32[8,8,512]{2,1,0:T(8,128)S(1)} %get-tuple-element.45), channel_id=1, source_target_pairs={{0,7},{1,0},{2,1},{3,2},{4,3},{5,4},{6,5},{7,6},{8,15},{9,8},{10,9... | collective-permute-start | bytes 393224 | tf_op jit(solution)/shard_map/ppermute | solution.py:626
  26.6 8.9 %collective-permute-start.6 = (f32[17,8,256]{2,1,0:T(8,128)S(1)}, f32[17,8,256]{2,1,0:T(8,128)S(1)}, u32[]{:S(2)}, u32[]{:S(2)}) collective-permute-start(f32[17,8,256]{2,1,0:T(8,128)S(1)} %get-tuple-element.58), channel_id=1, source_target_pairs={{0,8},{8,16},{16,24},{24,32},{32,40},{40,48},{48,56},{56,64},{64,7... | collective-permute-start | bytes 417800 | tf_op jit(solution)/shard_map/ppermute | solution.py:626
  26.7 8.8 %collective-permute-start.7 = (f32[17,8,256]{2,1,0:T(8,128)S(1)}, f32[17,8,256]{2,1,0:T(8,128)S(1)}, u32[]{:S(2)}, u32[]{:S(2)}) collective-permute-start(f32[17,8,256]{2,1,0:T(8,128)S(1)} %get-tuple-element.59), channel_id=1, source_target_pairs={{0,248},{8,0},{16,8},{24,16},{32,24},{40,32},{48,40},{56,48},{64,5... | collective-permute-start | bytes 417800 | tf_op jit(solution)/shard_map/ppermute | solution.py:626
  35.5 3.3 %collective-permute-start.8 = (f32[28,8,256]{2,1,0:T(8,128)S(1)}, f32[28,8,256]{2,1,0:T(8,128)S(1)}, u32[]{:S(2)}, u32[]{:S(2)}) collective-permute-start(f32[28,8,256]{2,1,0:T(8,128)S(1)} %get-tuple-element.60), channel_id=1, source_target_pairs={{0,1},{1,2},{2,3},{3,4},{4,5},{5,6},{6,7},{7,0},{8,9},{9,10},{10,1... | collective-permute-start | bytes 688136 | tf_op jit(solution)/shard_map/ppermute | solution.py:626
  35.9 5.7 %collective-permute-start.9 = (f32[28,8,256]{2,1,0:T(8,128)S(1)}, f32[28,8,256]{2,1,0:T(8,128)S(1)}, u32[]{:S(2)}, u32[]{:S(2)}) collective-permute-start(f32[28,8,256]{2,1,0:T(8,128)S(1)} %get-tuple-element.61), channel_id=1, source_target_pairs={{0,7},{1,0},{2,1},{3,2},{4,3},{5,4},{6,5},{7,6},{8,15},{9,8},{10,9... | collective-permute-start | bytes 688136 | tf_op jit(solution)/shard_map/ppermute | solution.py:626
  36.3 26.6 %collective-permute-start.18 = (f32[4,16,512]{2,1,0:T(8,128)S(1)}, f32[4,16,512]{2,1,0:T(8,128)S(1)}, u32[]{:S(2)}, u32[]{:S(2)}) collective-permute-start(f32[4,16,512]{2,1,0:T(8,128)S(1)} %get-tuple-element.71), channel_id=1, source_target_pairs={{0,8},{8,16},{16,24},{24,32},{32,40},{40,48},{48,56},{56,64},{64,7... | collective-permute-start | bytes 393224 | tf_op jit(solution)/shard_map/ppermute | solution.py:626
  43.6 13.5 %collective-permute-start.10 = (f32[4,16,128]{2,1,0:T(8,128)S(1)}, f32[4,16,128]{2,1,0:T(8,128)S(1)}, u32[]{:S(2)}, u32[]{:S(2)}) collective-permute-start(f32[4,16,128]{2,1,0:T(8,128)S(1)} %get-tuple-element.63), channel_id=1, source_target_pairs={{0,16},{8,24},{16,32},{24,40},{32,48},{40,56},{48,64},{56,72},{64,... | collective-permute-start | bytes 98312 | tf_op jit(solution)/shard_map/ppermute | solution.py:626
  43.7 13.4 %collective-permute-start.12 = (f32[4,16,128]{2,1,0:T(8,128)S(1)}, f32[4,16,128]{2,1,0:T(8,128)S(1)}, u32[]{:S(2)}, u32[]{:S(2)}) collective-permute-start(f32[4,16,128]{2,1,0:T(8,128)S(1)} %get-tuple-element.65), channel_id=1, source_target_pairs={{0,240},{8,248},{16,0},{24,8},{32,16},{40,24},{48,32},{56,40},{64,... | collective-permute-start | bytes 98312 | tf_op jit(solution)/shard_map/ppermute | solution.py:626
  49.4 7.7 %collective-permute-start.11 = (f32[2,16,128]{2,1,0:T(8,128)S(1)}, f32[2,16,128]{2,1,0:T(8,128)S(1)}, u32[]{:S(2)}, u32[]{:S(2)}) collective-permute-start(f32[2,16,128]{2,1,0:T(8,128)S(1)} %get-tuple-element.64), channel_id=1, source_target_pairs={{0,24},{8,32},{16,40},{24,48},{32,56},{40,64},{48,72},{56,80},{64,... | collective-permute-start | bytes 49160 | tf_op jit(solution)/shard_map/ppermute | solution.py:626
  49.4 7.7 %collective-permute-start.13 = (f32[2,16,128]{2,1,0:T(8,128)S(1)}, f32[2,16,128]{2,1,0:T(8,128)S(1)}, u32[]{:S(2)}, u32[]{:S(2)}) collective-permute-start(f32[2,16,128]{2,1,0:T(8,128)S(1)} %get-tuple-element.66), channel_id=1, source_target_pairs={{0,232},{8,240},{16,248},{24,0},{32,8},{40,16},{48,24},{56,32},{64... | collective-permute-start | bytes 49160 | tf_op jit(solution)/shard_map/ppermute | solution.py:626
  57.1 10.9 %collective-permute-start.17 = (f32[18,16,128]{2,1,0:T(8,128)S(1)}, f32[18,16,128]{2,1,0:T(8,128)S(1)}, u32[]{:S(2)}, u32[]{:S(2)}) collective-permute-start(f32[18,16,128]{2,1,0:T(8,128)S(1)} %shard_map.35.mid), channel_id=1, source_target_pairs={{0,6},{1,7},{2,0},{3,1},{4,2},{5,3},{6,4},{7,5},{8,14},{9,15},{10,... | collective-permute-start | bytes 442376 | tf_op jit(solution)/shard_map/ppermute | solution.py:626
  61.1 6.9 %collective-permute-start.16 = (f32[18,16,128]{2,1,0:T(8,128)S(1)}, f32[18,16,128]{2,1,0:T(8,128)S(1)}, u32[]{:S(2)}, u32[]{:S(2)}) collective-permute-start(f32[18,16,128]{2,1,0:T(8,128)S(1)} %shard_map.35.mid), channel_id=1, source_target_pairs={{0,7},{1,0},{2,1},{3,2},{4,3},{5,4},{6,5},{7,6},{8,15},{9,8},{10,9... | collective-permute-start | bytes 442376 | tf_op jit(solution)/shard_map/ppermute | solution.py:626
  61.1 6.9 %collective-permute-start.15 = (f32[18,16,128]{2,1,0:T(8,128)S(1)}, f32[18,16,128]{2,1,0:T(8,128)S(1)}, u32[]{:S(2)}, u32[]{:S(2)}) collective-permute-start(f32[18,16,128]{2,1,0:T(8,128)S(1)} %shard_map.35.mid), channel_id=1, source_target_pairs={{0,2},{1,3},{2,4},{3,5},{4,6},{5,7},{6,0},{7,1},{8,10},{9,11},{10,... | collective-permute-start | bytes 442376 | tf_op jit(solution)/shard_map/ppermute | solution.py:626
  62.0 6.1 %collective-permute-start.14 = (f32[18,16,128]{2,1,0:T(8,128)S(1)}, f32[18,16,128]{2,1,0:T(8,128)S(1)}, u32[]{:S(2)}, u32[]{:S(2)}) collective-permute-start(f32[18,16,128]{2,1,0:T(8,128)S(1)} %shard_map.35.mid), channel_id=1, source_target_pairs={{0,1},{1,2},{2,3},{3,4},{4,5},{5,6},{6,7},{7,0},{8,9},{9,10},{10,1... | collective-permute-start | bytes 442376 | tf_op jit(solution)/shard_map/ppermute | solution.py:626
  62.9 4.7 %collective-permute-start.19 = (f32[4,16,512]{2,1,0:T(8,128)S(1)}, f32[4,16,512]{2,1,0:T(8,128)S(1)}, u32[]{:S(2)}, u32[]{:S(2)}) collective-permute-start(f32[4,16,512]{2,1,0:T(8,128)S(1)} %get-tuple-element.72), channel_id=1, source_target_pairs={{0,248},{8,0},{16,8},{24,16},{32,24},{40,32},{48,40},{56,48},{64,5... | collective-permute-start | bytes 393224 | tf_op jit(solution)/shard_map/ppermute | solution.py:626
